TPU v7x, 256 devices: a whole 4x4x8 slice. The times are simulated.
256 devices in a mesh: frame: 32 (over y_lo, z, core), head: 8 (over x, y_hi).
Axes of the slice: x: 4, y: 4 (y_hi: 2, y_lo: 2; y = y_hi * 2 + y_lo), z: 8, core: 2. Of those that a mesh axis runs over, the one named last changes fastest.
Arguments:
- video: bfloat16 [3, 4096, 3072], P(None, 'frame', 'head'), may hold values from -6 to 6
- w_qkv: bfloat16 [3072, 3, 3072], P(None, None, 'head'), may hold values from -0.5 to 0.5
- w_out: bfloat16 [3072, 3072], P('head'), may hold values from -0.15625 to 0.15625
- text_kv: bfloat16 [2, 3, 256, 3072], P(None, None, None, 'head'), may hold values from -16 to 16
- text_lengths: int32 [3], replicated, may hold values from 1 to 256
- norm_gains: float32 [2, 128], replicated, may hold values from 1.3 to 5
- mod_table: float32 [32, 3, 3072], P(None, None, 'head'), may hold values from -4 to 4
- timestep_ids: int32 [32], replicated, may hold values from 0 to 31
- queue_shift: int32 [1], replicated, may hold values from 0 to 31
Outputs:
- video_out: bfloat16 [3, 4096, 3072], P(None, 'frame', 'head')
All inputs are finite; a program needn't handle non-finite values.
Results may differ from a plain program's by a relative error of at most 0.015.
Values may be sent and summed in bfloat16 or wider, within the bound.
No kernel may reach another device: no remote copies, remote signals or barrier semaphores. Data moves between devices by JAX's collectives and lax.ppermute only.
A program may use at most 128 MiB of HBM per device.

v0:
```python
import jax
import jax.numpy as jnp
from jax import lax
from jax.sharding import PartitionSpec as P

HD = 128
FRAME_TOK = 128
LAT_W = 16


rope_base = 256.0
norm_eps = 1e-06


def rope_angles(token_index):
    time_dims = HD // 8
    space_dims = (HD - time_dims) // 2
    in_frame = token_index % FRAME_TOK
    sections = [
        (token_index // FRAME_TOK, time_dims),
        (in_frame // LAT_W, space_dims),
        (in_frame % LAT_W, space_dims),
    ]
    angle_parts = []
    for position, sec_width in sections:
        frequency = rope_base ** (-jnp.arange(0, sec_width, 2).astype(jnp.float32) / sec_width)
        angle_parts.append(position.astype(jnp.float32)[:, None] * frequency[None, :])
    angles = jnp.concatenate(angle_parts, axis=1)
    return (jnp.cos(angles), jnp.sin(angles))


def rotate(inputs, cosine, sine_table):
    paired = inputs.reshape(inputs.shape[:-1] + (inputs.shape[-1] // 2, 2))
    even_part = paired[..., 0]
    odd_part = paired[..., 1]
    cosine = cosine[:, None, :]
    sine_table = sine_table[:, None, :]
    rotated = jnp.stack(
        [even_part * cosine - odd_part * sine_table, even_part * sine_table + odd_part * cosine],
        axis=-1,
    )
    return rotated.reshape(inputs.shape)


def rms_norm(inputs, gain_row):
    return (
        inputs * lax.rsqrt(jnp.mean(inputs * inputs, axis=-1, keepdims=True) + norm_eps) * gain_row
    )


def layer_norm(widened, row_mean, row_var):
    return (widened - row_mean) * lax.rsqrt(row_var + norm_eps)


def make_absorb(query_part, state, arrived):
    row_top, row_total, mixed_sum = state
    block_keys, block_values = arrived
    scores = jnp.einsum(
        "bqhd,bkhd->bhqk", query_part, block_keys, preferred_element_type=jnp.float32
    ) * HD ** (-0.5)
    new_top = jnp.maximum(row_top, jnp.max(scores, axis=-1))
    decay = jnp.exp(row_top - new_top)
    weights = jnp.exp(scores - new_top[..., None])
    added = jnp.einsum(
        "bhqk,bkhd->bhqd",
        weights.astype(jnp.bfloat16),
        block_values,
        preferred_element_type=jnp.float32,
    )
    return (
        new_top,
        row_total * decay + jnp.sum(weights, axis=-1),
        mixed_sum * decay[..., None] + added,
    )


def body(
    video, w_qkv, w_out, text_kv, text_lengths, norm_gains, mod_table, timestep_ids, queue_shift
):
    branches, rows, dshard = video.shape
    frame_count = rows // FRAME_TOK
    frames_all = timestep_ids.shape[0]
    first_frame = lax.axis_index("frame") * frame_count
    local_frames = first_frame + jnp.arange(frame_count, dtype=jnp.int32)
    queue_slot = (local_frames + queue_shift[0]) % frames_all
    slot_match = jnp.arange(frames_all, dtype=jnp.int32)[None, :] == queue_slot[:, None]
    noise_level = jnp.sum(jnp.where(slot_match, timestep_ids[None, :], 0), axis=1)
    level_count = mod_table.shape[0]
    level_hot = (jnp.arange(level_count, dtype=jnp.int32)[None, :] == noise_level[:, None]).astype(
        jnp.float32
    )
    looked = jnp.dot(
        level_hot, mod_table.reshape(level_count, -1), precision=lax.Precision.HIGHEST
    ).reshape(frame_count, 3, dshard)
    per_token = jnp.repeat(looked, FRAME_TOK, axis=0)
    widened = video.astype(jnp.float32)
    w_flat = w_qkv.reshape(w_qkv.shape[0], -1)
    sums = lax.psum((jnp.sum(widened, axis=-1), jnp.sum(widened * widened, axis=-1)), "head")
    full_width = dshard * lax.axis_size("head")
    row_mean = sums[0][..., None] / full_width
    row_var = sums[1][..., None] / full_width - row_mean * row_mean
    normed = layer_norm(widened, row_mean, row_var)
    modded = (normed * (1.0 + per_token[:, 1]) + per_token[:, 0]).astype(jnp.bfloat16)
    arrived = lax.all_gather(modded, "head", axis=2, tiled=True)
    projected = jnp.dot(
        arrived.reshape(-1, arrived.shape[2]), w_flat, preferred_element_type=jnp.float32
    )
    heads_here = w_qkv.shape[2] // HD
    projected = projected.reshape(branches, rows, 3, heads_here, HD)
    cosine, sine_table = rope_angles(first_frame * FRAME_TOK + jnp.arange(rows, dtype=jnp.int32))
    query = rotate(rms_norm(projected[:, :, 0], norm_gains[0]), cosine, sine_table).astype(
        jnp.bfloat16
    )
    key_rot = rotate(rms_norm(projected[:, :, 1], norm_gains[1]), cosine, sine_table).astype(
        jnp.bfloat16
    )
    value = projected[:, :, 2].astype(jnp.bfloat16)
    text_keys = text_kv[0].reshape(branches, -1, heads_here, HD)
    text_values = text_kv[1].reshape(branches, -1, heads_here, HD)
    text_valid = jnp.arange(text_keys.shape[1], dtype=jnp.int32)[None, :] < text_lengths[:, None]
    scores = jnp.einsum(
        "bqhd,bkhd->bhqk", query, text_keys, preferred_element_type=jnp.float32
    ) * HD ** (-0.5)
    scores = jnp.where(text_valid[:, None, None, :], scores, -jnp.inf)
    row_top = jnp.max(scores, axis=-1)
    weights = jnp.exp(scores - row_top[..., None])
    text_mixed = jnp.einsum(
        "bhqk,bkhd->bhqd",
        weights.astype(jnp.bfloat16),
        text_values,
        preferred_element_type=jnp.float32,
    )
    start_state = (row_top, jnp.sum(weights, axis=-1), text_mixed)
    results = []
    for branch in range(branches):
        branch_state = tuple((item[branch : branch + 1] for item in start_state))
        results.append(
            make_absorb(
                query[branch : branch + 1],
                branch_state,
                (
                    lax.all_gather(key_rot[branch : branch + 1], "frame", axis=1, tiled=True),
                    lax.all_gather(value[branch : branch + 1], "frame", axis=1, tiled=True),
                ),
            )
        )
    state = tuple(
        (jnp.concatenate([result[member] for result in results], axis=0) for member in range(3))
    )
    mixed_out = (state[2] / state[1][..., None]).astype(jnp.bfloat16)
    attention = mixed_out.transpose(0, 2, 1, 3).reshape(branches * rows, heads_here * HD)
    partial_proj = jnp.dot(attention, w_out, preferred_element_type=jnp.float32).reshape(
        branches, rows, -1
    )
    summed = lax.psum_scatter(
        partial_proj.astype(jnp.bfloat16), "head", scatter_dimension=2, tiled=True
    ).astype(jnp.float32)
    return (widened + per_token[:, 2] * summed).astype(jnp.bfloat16)


def solution(mesh):
    in_specs = (
        P(None, "frame", "head"),
        P(None, None, "head"),
        P("head", None),
        P(None, None, None, "head"),
        P(),
        P(),
        P(None, None, "head"),
        P(),
        P(),
    )
    out_specs = P(None, "frame", "head")
    return jax.shard_map(body, mesh=mesh, in_specs=in_specs, out_specs=out_specs, check_vma=False)
```

profile of v0, /device:TPU:6, one launch (start us, length us, event | category | flops | bytes accessed | tf_op | source)
XLA Modules:
  0.0 631.1 jit_solution(16202687310776871154)
XLA Ops:
  7.4 1.4 fusion.83
  8.7 1.8 fusion.67
  11.1 1.1 convert_reduce_fusion
  12.3 20.9 %all-reduce = (f32[3,128]{1,0:T(4,128)S(1)}, f32[3,128]{1,0:T(4,128)S(1)}) all-reduce(f32[3,128]{1,0:T(4,128)S(1)} %get-tuple-element.8, f32[3,128]{1,0:T(4,128)S(1)} %get-tuple-element.7), channel_id=1, replica_groups=mesh['frame'=32,'head'=8] {'head'}, use_global_device_ids=true, to_apply=%region_4.5 | all-reduce | flops 768 | bytes 6144 | tf_op jit(solution)/shard_map/psum | solution.py:98
  33.2 1.9 fusion.60
  35.2 10.3 %copy.33 = bf16[3072,3,384]{0,2,1:T(8,128)(2,1)} copy(bf16[3072,3,384]{2,0,1:T(8,128)(2,1)} %param.10) | data formatting | bytes 14155776 | tf_op args[1]
  46.1 55.3 %all-gather.11.cloned.1.call-done = bf16[3,128,3072]{2,1,0:T(8,128)(2,1)} async-done(((bf16[3,128,384]{2,1,0:T(8,128)(2,1)}), bf16[3,128,3072]{2,1,0:T(8,128)(2,1)}) %all-gather.11.cloned.1.call-update) | async-done | bytes 2359312 | tf_op jit(solution)/shard_map/all_gather | solution.py:104
  101.4 7.6 %fusion.94 = (bf16[3,128,3,3,128]{1,4,3,2,0:T(8,128)(2,1)}, f32[3,128,3,3,128]{1,4,3,2,0:T(8,128)S(1)}) fusion(bf16[3,3,128,3072,1]{3,2,1,0,4:T(8,128)(2,1)} %bitcast.170, bf16[3,128,3072]{2,1,0:T(8,128)(2,1)} %all-gather.11.cloned.1.call-done), kind=kOutput, calls=%fused_computation.140 | convolution fusion | flops 2718351360 | bytes 12091392 | tf_op jit(solution)/shard_map/dot_general | solution.py:105
  109.8 1.6 subtract_convert_fusion
  114.6 1.7 fusion.93
  117.9 2.2 fusion.92
  121.1 1.3 copy.37
  122.5 1.4 slice_maximum_fusion.2
  124.6 1.5 fusion.96
  126.9 51.4 %all-gather.15.cloned.1.call-done = bf16[1,4096,3,128]{3,1,2,0:T(8,128)(2,1)} async-done(((bf16[1,128,3,128]{3,1,2,0:T(8,128)(2,1)}), bf16[1,4096,3,128]{3,1,2,0:T(8,128)(2,1)}) %all-gather.15.cloned.1.call-update) | async-done | bytes 3145744 | tf_op jit(solution)/shard_map/all_gather | solution.py:142
  178.3 5.7 fusion.98
  184.0 62.1 %all-gather.13.cloned.1.call-done = bf16[1,4096,3,128]{3,1,2,0:T(8,128)(2,1)} async-done(((bf16[1,128,3,128]{3,1,2,0:T(8,128)(2,1)}), bf16[1,4096,3,128]{3,1,2,0:T(8,128)(2,1)}) %all-gather.13.cloned.1.call-update) | async-done | bytes 3145744 | tf_op jit(solution)/shard_map/all_gather | solution.py:142
  246.1 5.6 fusion.95
  251.6 61.9 %all-gather.17.cloned.1.call-done = bf16[1,4096,3,128]{3,1,2,0:T(8,128)(2,1)} async-done(((bf16[1,128,3,128]{3,1,2,0:T(8,128)(2,1)}), bf16[1,4096,3,128]{3,1,2,0:T(8,128)(2,1)}) %all-gather.17.cloned.1.call-update) | async-done | bytes 3145744 | tf_op jit(solution)/shard_map/all_gather | solution.py:142
  313.5 3.2 fusion.97
  316.7 6.1 fusion.2
  324.8 58.8 %all-gather.19.cloned.1.call-done = bf16[1,4096,1,3,128]{1,4,3,2,0:T(8,128)(2,1)} async-done(((bf16[1,128,1,3,128]{1,4,3,2,0:T(8,128)(2,1)}), bf16[1,4096,1,3,128]{1,4,3,2,0:T(8,128)(2,1)}) %all-gather.19.cloned.1.call-update) | async-done | bytes 3145744 | tf_op jit(solution)/shard_map/all_gather | solution.py:143
  383.6 4.9 fusion.50
  388.5 64.7 %all-gather.21.cloned.1.call-done = bf16[1,4096,1,3,128]{1,4,3,2,0:T(8,128)(2,1)} async-done(((bf16[1,128,1,3,128]{1,4,3,2,0:T(8,128)(2,1)}), bf16[1,4096,1,3,128]{1,4,3,2,0:T(8,128)(2,1)}) %all-gather.21.cloned.1.call-update) | async-done | bytes 3145744 | tf_op jit(solution)/shard_map/all_gather | solution.py:143
  453.2 4.9 fusion.45
  458.2 64.8 %all-gather.23.cloned.1.call-done = bf16[1,4096,1,3,128]{1,4,3,2,0:T(8,128)(2,1)} async-done(((bf16[1,128,1,3,128]{1,4,3,2,0:T(8,128)(2,1)}), bf16[1,4096,1,3,128]{1,4,3,2,0:T(8,128)(2,1)}) %all-gather.23.cloned.1.call-update) | async-done | bytes 3145744 | tf_op jit(solution)/shard_map/all_gather | solution.py:143
  523.0 5.2 fusion.40
  528.3 2.9 convolution_convert_fusion
  531.2 5.7 copy.54
  536.8 3.7 copy.69
  540.6 81.2 %reduce-scatter.4.cloned.1.call-done = bf16[384,384]{1,0:T(8,128)(2,1)} async-done(((bf16[3072,384]{1,0:T(8,128)(2,1)}), bf16[384,384]{1,0:T(8,128)(2,1)}) %reduce-scatter.4.cloned.1.call-update) | async-done | bytes 294928
  621.8 1.3 reshape.399
  (71 shorter events, 12.6 us)
Async XLA Ops:
  6.5 521.7 %copy-start = (bf16[384,3072]{1,0:T(8,128)(2,1)S(1)}, bf16[384,3072]{1,0:T(8,128)(2,1)}, u32[]{:S(2)}) copy-start(bf16[384,3072]{1,0:T(8,128)(2,1)} %param.11) | copy-start | bytes 7077892
  6.5 94.9 %all-gather.11.cloned.1.call-start = ((), (), s32[]{:S(2)}) async-start(), calls=%async_computation.1 | async-start | bytes 2654208 | tf_op jit(solution)/shard_map/all_gather | solution.py:104
  35.1 10.3 %copy-start.6 = (f32[2,128]{1,0:T(2,128)S(1)}, f32[2,128]{1,0:T(2,128)}, u32[]{:S(2)}) copy-start(f32[2,128]{1,0:T(2,128)} %param.14) | copy-start | bytes 3076
  35.1 143.2 %all-gather.15.cloned.1.call-start = ((), (), s32[]{:S(2)}) async-start(), calls=%async_computation.3 | async-start | bytes 3244032 | tf_op jit(solution)/shard_map/all_gather | solution.py:142
  112.9 9.6 %copy-start.7 = (s32[3]{0:T(128)S(1)}, s32[3]{0:T(128)}, u32[]{:S(2)}) copy-start(s32[3]{0:T(128)} %param.13) | copy-start | bytes 40
  112.9 133.1 %all-gather.13.cloned.1.call-start = ((), (), s32[]{:S(2)}) async-start(), calls=%async_computation.2 | async-start | bytes 3244032 | tf_op jit(solution)/shard_map/all_gather | solution.py:142
  113.7 199.8 %all-gather.17.cloned.1.call-start = ((), (), s32[]{:S(2)}) async-start(), calls=%async_computation.4 | async-start | bytes 3244032 | tf_op jit(solution)/shard_map/all_gather | solution.py:142
  114.6 269.1 %all-gather.19.cloned.1.call-start = ((), (), s32[]{:S(2)}) async-start(), calls=%async_computation.5 | async-start | bytes 3244032 | tf_op jit(solution)/shard_map/all_gather | solution.py:143
  116.3 336.9 %all-gather.21.cloned.1.call-start = ((), (), s32[]{:S(2)}) async-start(), calls=%async_computation.6 | async-start | bytes 3244032 | tf_op jit(solution)/shard_map/all_gather | solution.py:143
  116.9 406.1 %all-gather.23.cloned.1.call-start = ((), (), s32[]{:S(2)}) async-start(), calls=%async_computation.7 | async-start | bytes 3244032 | tf_op jit(solution)/shard_map/all_gather | solution.py:143
  117.7 504.1 %reduce-scatter.4.cloned.1.call-start = ((), (), s32[]{:S(2)}) async-start(), calls=%async_computation.8 | async-start | bytes 2654208
  178.3 67.8 %copy-start.4 = (bf16[1,128,3,64,2]{1,4,3,2,0:T(2,128)(2,1)S(1)}, bf16[1,128,3,64,2]{1,4,3,2,0:T(2,128)(2,1)}, u32[]{:S(2)}) copy-start(bf16[1,128,3,64,2]{1,4,3,2,0:T(2,128)(2,1)} %get-tuple-element.30) | copy-start | bytes 294916
  246.1 67.5 %copy-start.3 = (bf16[1,128,3,64,2]{1,4,3,2,0:T(2,128)(2,1)S(1)}, bf16[1,128,3,64,2]{1,4,3,2,0:T(2,128)(2,1)}, u32[]{:S(2)}) copy-start(bf16[1,128,3,64,2]{1,4,3,2,0:T(2,128)(2,1)} %get-tuple-element.32) | copy-start | bytes 294916
  313.5 10.2 %slice-start = ((s8[6291456]{0:T(1024)(128)(4,1)}), s8[4194304]{0:T(1024)(128)(4,1)S(1)}, s32[]{:S(2)}) async-start(s8[6291456]{0:T(1024)(128)(4,1)} %bitcast.166), calls=%async_computation.9 | async-start | bytes 8388608
  316.7 6.1 copy-start.1
  316.7 7.1 %slice-start.1 = ((s8[6291456]{0:T(1024)(128)(4,1)}), s8[2097152]{0:T(1024)(128)(4,1)S(1)}, s32[]{:S(2)}) async-start(s8[6291456]{0:T(1024)(128)(4,1)} %bitcast.166), calls=%async_computation.10 | async-start | bytes 4194304
  540.6 82.8 %copy-start.2 = (bf16[3,128,384]{2,1,0:T(8,128)(2,1)S(1)}, bf16[3,128,384]{2,1,0:T(8,128)(2,1)}, u32[]{:S(2)}) copy-start(bf16[3,128,384]{2,1,0:T(8,128)(2,1)} %param.9) | copy-start | bytes 884740
  540.6 82.8 %copy-start.5 = (f32[384]{0:T(512)S(1)}, f32[384]{0:T(512)}, u32[]{:S(2)}) copy-start(f32[384]{0:T(512)} %get-tuple-element.9) | copy-start | bytes 4612
Sparse Core Ops, SparseCore 0:
  35.2 66.1 all-gather.10
  113.0 65.2 all-gather.14
  180.2 65.8 all-gather.12
  247.8 65.7 all-gather.16
  315.2 68.4 all-gather.18
  385.2 67.9 all-gather.20
  455.0 67.9 all-gather.22
  540.7 81.0 reduce-scatter.3
where the time goes:
time: 632 us; the launch traced here: 631 us
  waiting for transfers between devices  501 us (79%)
  matrix products  43.6 us (7%)
  local copies, waits for them, and re-layouts  30.1 us (5%)
  blocking collectives  20.9 us (3%)
  other arithmetic  19.9 us (3%)
  between operations  14.6 us (2%)
    all_gather x3, waiting for transfers between devices, body(): lax.all_gather(value[branch:branch + 1], 'frame', axis=1, tiled=True)  188 us
    all_gather x3, waiting for transfers between devices, body(): lax.all_gather(key_rot[branch:branch + 1], 'frame', axis=1, tiled=True)  175 us
    unnamed x9, waiting for transfers between devices  82.5 us
    all_gather x1, waiting for transfers between devices, body(): arrived = lax.all_gather(modded, 'head', axis=2, tiled=True)  55.3 us
    unnamed x26, local copies, waits for them, and re-layouts  22.4 us
    psum x1, blocking collectives, body(): lax.psum((jnp.sum(widened, axis=-1), jnp.sum(widened * widened, axis=-1))...  20.9 us
    dot_general x3, matrix products, make_absorb(): jnp.einsum('bhqk,bkhd->bhqd', weights.astype(jnp.bfloat16), block_values,...  15 us
    dot_general x3, matrix products, make_absorb(): jnp.einsum('bqhd,bkhd->bhqk', query_part, block_keys, preferred_element_t...  14.4 us
  transfers between devices with their start and end apart: 8, of which 8 were waited for; matrix products, arithmetic and copies ran while one was open for 9% of the time, Pallas kernels for 0%

commit v1 on v0

v1 whole, which is shorter than its diff:
```python
import jax
import jax.numpy as jnp
import numpy as np
from jax import lax
from jax.experimental import pallas as pl
from jax.experimental.pallas import tpu as pltpu
from jax.sharding import PartitionSpec as P

HD = 128
TOK = 128
LAT_W = 16
FRAMES = 32
HEAD_AXIS = 8
BRANCH = 3
HEADS_HERE = 3
PAIRS = BRANCH * HEADS_HERE
DSH = 384
TXT = 256
RING = 8
ROWS = BRANCH * TOK
MOD_ROWS = 16
SENT = ROWS + MOD_ROWS
LAST = PAIRS - 1
STAT_ROWS = 16
LAST_ROWS = TOK + STAT_ROWS
RETURN = TOK + LAST_ROWS
WIDE = 3 * DSH
rope_base = 256.0
norm_eps = 1e-06
LOG2E = float(np.log2(np.e))
EXP_SCALE = float(HD ** (-0.5) * np.log2(np.e))
MIB = 1024 * 1024


def whole(shape):
    return pl.BlockSpec(shape, lambda *_: (0,) * len(shape))


def limbs_of(value):
    limbs = []
    for _ in range(3):
        limb = value.astype(jnp.bfloat16).astype(jnp.float32)
        limbs.append(limb)
        value = value - limb
    return limbs


def rope_tables(frame):
    time_dims = HD // 8
    space_dims = (HD - time_dims) // 2
    freq = np.concatenate(
        [
            np.repeat(rope_base ** (-np.arange(0, z, 2, dtype=np.float64) / z), 2)
            for z in (time_dims, space_dims, space_dims)
        ]
    ).astype(np.float32)
    section = np.repeat(np.arange(3), (time_dims, space_dims, space_dims))
    token = jnp.arange(TOK, dtype=jnp.int32)[:, None]
    section = jnp.asarray(section)[None, :]
    position = jnp.where(
        section == 0, frame, jnp.where(section == 1, token // LAT_W, token % LAT_W)
    )
    angle = position.astype(jnp.float32) * jnp.asarray(freq)[None, :]
    sign = jnp.asarray(np.tile(np.array([-1.0, 1.0], np.float32), HD // 2))
    return jnp.cos(angle), jnp.sin(angle) * sign[None, :]


def prep_kernel(
    frame_ref, head_ref, shift_ref, ids_ref, lengths_ref, video_ref, table_ref,
    own_ref, gate_ref, place_ref, where_ref,
):
    head = head_ref[0]
    for s, step in enumerate((0, 0, 2, -2, 2, -2, 4, 4)):
        near = lax.rem(head + step + HEAD_AXIS, HEAD_AXIS)
        place_ref[s] = near if s in (0, 2, 3, 6) else near + 1 - 2 * lax.rem(near, 2)
    slab = lax.rem(lax.div(frame_ref[0], 2), RING)
    branch = lax.div(slab, HEADS_HERE)
    text_block = jnp.minimum(slab, 1)
    where_ref[0] = branch
    where_ref[1] = lax.rem(slab, HEADS_HERE)
    where_ref[2] = lengths_ref[branch]
    where_ref[3] = jnp.where(slab < 2, lengths_ref[BRANCH - 1] - 128 * text_block, 0)
    where_ref[4] = text_block
    level = ids_ref[lax.rem(frame_ref[0] + shift_ref[0], FRAMES)]
    looked = [table_ref[part, pl.ds(level, 1), :] for part in range(3)]
    gate_ref[...] = looked[2]
    limbs = limbs_of(looked[0]) + limbs_of(looked[1])
    limbs.append(jnp.zeros((MOD_ROWS - 6, DSH), jnp.float32))
    for b in range(BRANCH):
        own_ref[b * TOK : (b + 1) * TOK, :] = video_ref[b]
    own_ref[ROWS:SENT, :] = jnp.concatenate(limbs, axis=0).astype(jnp.bfloat16)


def prep(frame, head, queue_shift, timestep_ids, lengths, video, table):
    return pl.pallas_call(
        prep_kernel,
        out_shape=(
            jax.ShapeDtypeStruct((SENT, DSH), jnp.bfloat16),
            jax.ShapeDtypeStruct((1, DSH), jnp.float32),
            jax.ShapeDtypeStruct((HEAD_AXIS,), jnp.int32),
            jax.ShapeDtypeStruct((5,), jnp.int32),
        ),
        grid_spec=pltpu.PrefetchScalarGridSpec(
            num_scalar_prefetch=5,
            grid=(1,),
            in_specs=[whole((BRANCH, TOK, DSH)), whole((3, FRAMES, DSH))],
            out_specs=(
                whole((SENT, DSH)),
                whole((1, DSH)),
                pl.BlockSpec(memory_space=pltpu.SMEM),
                pl.BlockSpec(memory_space=pltpu.SMEM),
            ),
        ),
        compiler_params=pltpu.CompilerParams(vmem_limit_bytes=16 * MIB),
        name="prep",
    )(frame, head, queue_shift, timestep_ids, lengths, video, table)


def project_kernel(place_ref, *refs):
    blocks = refs[:HEAD_AXIS]
    (
        w_hbm, gain_ref, cos_ref, sin_ref, out_ref, last_ref, mod_ref, acc_ref, w_ref, sems,
    ) = refs[HEAD_AXIS:]
    copies = [
        pltpu.make_async_copy(w_hbm.at[n], w_ref.at[:, pl.ds(n * DSH, DSH)], sems.at[n])
        for n in range(3)
    ]
    for copy in copies:
        copy.start()
    step = 64

    def chunk(n, carry):
        here = pl.ds(pl.multiple_of(n * step, step), step)
        total = jnp.zeros((step, 128), jnp.float32)
        square = jnp.zeros((step, 128), jnp.float32)
        for block in blocks:
            for lane in range(0, DSH, 128):
                x = block[here, lane : lane + 128].astype(jnp.float32)
                total += x
                square += x * x
        mean = jnp.sum(total, axis=1, keepdims=True) / (HEAD_AXIS * DSH)
        var = jnp.sum(square, axis=1, keepdims=True) / (HEAD_AXIS * DSH) - mean * mean
        inv = lax.rsqrt(var + norm_eps)
        for s, block in enumerate(blocks):
            limbs = block[ROWS:SENT, :].astype(jnp.float32)
            shift = limbs[0:1] + limbs[1:2] + limbs[2:3]
            scale = limbs[3:4] + limbs[4:5] + limbs[5:6]
            x = block[here, :].astype(jnp.float32)
            y = (x - mean) * inv * (1.0 + scale) + shift
            start = pl.multiple_of(place_ref[s] * DSH, DSH)
            mod_ref[here, pl.ds(start, DSH)] = y.astype(jnp.bfloat16)
        return carry

    lax.fori_loop(0, ROWS // step, chunk, 0)

    def piece(part, p):
        b, hd = divmod(p, HEADS_HERE)
        lane = part * DSH + hd * HD
        return acc_ref[b * TOK : (b + 1) * TOK, lane : lane + HD]

    def turned(part, p):
        t = piece(part, p)
        t = t * lax.rsqrt(jnp.mean(t * t, axis=1, keepdims=True) + norm_eps)
        t = t * gain_ref[part : part + 1, :]
        even = lax.broadcasted_iota(jnp.int32, t.shape, 1) % 2 == 0
        other = jnp.where(even, pltpu.roll(t, HD - 1, 1), pltpu.roll(t, 1, 1))
        return (t * cos_ref[...] + other * sin_ref[...]).astype(jnp.bfloat16)

    for copy in copies:
        copy.wait()
    acc_ref[...] = jnp.dot(mod_ref[...], w_ref[...], preferred_element_type=jnp.float32)
    for part in range(3):
        for p in range(PAIRS):
            if part == 2:
                result = piece(part, p).astype(jnp.bfloat16)
            else:
                result = turned(part, p)
            if part == 0 and p == LAST:
                for n in range(RING):
                    out_ref[n, 3 * TOK : 4 * TOK, :] = result
            elif part == 0:
                out_ref[p, 2 * TOK : 3 * TOK, :] = result
            elif p == LAST:
                last_ref[(part - 1) * TOK : part * TOK, :] = result
            else:
                out_ref[p, (part - 1) * TOK : part * TOK, :] = result


def project(places, blocks, w, gains, cosine, sine):
    return pl.pallas_call(
        project_kernel,
        out_shape=(
            jax.ShapeDtypeStruct((RING, 4 * TOK, HD), jnp.bfloat16),
            jax.ShapeDtypeStruct((2 * TOK, HD), jnp.bfloat16),
        ),
        grid_spec=pltpu.PrefetchScalarGridSpec(
            num_scalar_prefetch=1,
            grid=(1,),
            in_specs=[whole((SENT, DSH)) for _ in blocks]
            + [
                pl.BlockSpec(memory_space=pltpu.HBM),
                whole((2, HD)),
                whole((TOK, HD)),
                whole((TOK, HD)),
            ],
            out_specs=(whole((RING, 4 * TOK, HD)), whole((2 * TOK, HD))),
            scratch_shapes=[
                pltpu.VMEM((ROWS, HEAD_AXIS * DSH), jnp.bfloat16),
                pltpu.VMEM((ROWS, WIDE), jnp.float32),
                pltpu.VMEM((HEAD_AXIS * DSH, WIDE), jnp.bfloat16),
                pltpu.SemaphoreType.DMA((3,)),
            ],
        ),
        compiler_params=pltpu.CompilerParams(vmem_limit_bytes=28 * MIB),
        cost_estimate=pl.CostEstimate(
            flops=2 * ROWS * HEAD_AXIS * DSH * 3 * DSH, bytes_accessed=12_000_000, transcendentals=0
        ),
        name="project",
    )(places, *blocks, w, gains, cosine, sine)


QUAD = 4
TILE = QUAD * TOK
SET = RING * TOK
DIMS = (((1,), (1,)), ((), ()))


def score_keys(q, keys, score_ref, column, top):
    scores = lax.dot_general(q, keys, DIMS, preferred_element_type=jnp.float32)
    score_ref[:, column : column + scores.shape[1]] = scores
    for lane in range(0, scores.shape[1], 128):
        top = jnp.maximum(top, scores[:, lane : lane + 128])
    return top


def score_text(q, keys, valid, score_ref, column, top):
    scores = lax.dot_general(q, keys, DIMS, preferred_element_type=jnp.float32)
    index = lax.broadcasted_iota(jnp.int32, scores.shape, 1)
    scores = jnp.where(index < valid, scores, -jnp.inf)
    score_ref[:, column : column + scores.shape[1]] = scores
    for lane in range(0, scores.shape[1], 128):
        top = jnp.maximum(top, scores[:, lane : lane + 128])
    return top


def mix(score_ref, value_ref, top, count):
    mixed = jnp.zeros((TILE, 2 * HD), jnp.float32)
    for first in range(0, count, SET):
        stop = min(first + SET, count)
        weights = jnp.exp2(score_ref[:, first:stop] * EXP_SCALE - top).astype(jnp.bfloat16)
        mixed += jnp.dot(weights, value_ref[first:stop, :], preferred_element_type=jnp.float32)
    return mixed


def lay_values(value_ref, pieces):
    lane = lax.broadcasted_iota(jnp.int32, (value_ref.shape[0], HD), 1)
    value_ref[:, HD:] = jnp.where(lane == 0, 1.0, 0.0).astype(jnp.bfloat16)
    row = 0
    for piece in pieces:
        value_ref[row : row + piece.shape[0], :HD] = piece
        row += piece.shape[0]


def set_keys(ref):
    return ref[:, 0:TOK, :].reshape(SET, HD)


def set_values(ref):
    return ref[:, TOK : 2 * TOK, :].reshape(SET, HD)


def first_step():
    return pl.program_id(0) == 0


def tile_rows():
    return pl.ds(pl.multiple_of(pl.program_id(0) * TILE, TILE), TILE)


IN_VMEM = pl.BlockSpec(memory_space=pltpu.VMEM)


def attend_near_kernel(
    where_ref, q_ref, own_ref, core_ref, text_ref, w_hbm,
    mixed_ref, top_ref, w_ref, score_ref, value_ref, sem,
):
    copy = pltpu.make_async_copy(w_hbm, w_ref, sem)

    @pl.when(first_step())
    def _():
        copy.start()
        lay_values(value_ref, [set_values(own_ref), set_values(core_ref), text_ref[1, 0]])

    q = q_ref[...].reshape(TILE, HD)
    top = jnp.full((TILE, 128), -jnp.inf, jnp.float32)
    for n, ref in enumerate((own_ref, core_ref)):
        top = score_keys(q, set_keys(ref), score_ref, n * SET, top)
    top = score_text(q, text_ref[0, 0], where_ref[2], score_ref, 2 * SET, top)
    top = jnp.max(top, axis=1, keepdims=True) * EXP_SCALE
    here = tile_rows()
    mixed_ref[here, :] = mix(score_ref, value_ref, top, 2 * SET + TXT)
    top_ref[here, :] = jnp.broadcast_to(top, (TILE, 128))

    @pl.when(pl.program_id(0) == SET // TILE - 1)
    def _():
        copy.wait()


def attend_near(where, received, own, core, text_kv, w_out):
    return pl.pallas_call(
        attend_near_kernel,
        out_shape=(
            pltpu.VMEM((SET, 2 * HD), jnp.float32),
            pltpu.VMEM((SET, 128), jnp.float32),
            pltpu.VMEM(w_out.shape, w_out.dtype),
        ),
        grid_spec=pltpu.PrefetchScalarGridSpec(
            num_scalar_prefetch=1,
            grid=(SET // TILE,),
            in_specs=[
                pl.BlockSpec((QUAD, TOK, HD), lambda i, w: (i, 2, 0)),
                whole((RING, 2 * TOK, HD)),
                whole((RING, 2 * TOK, HD)),
                pl.BlockSpec((2, 1, TXT, HD), lambda i, w: (0, w[0], 0, w[1])),
                pl.BlockSpec(memory_space=pltpu.HBM),
            ],
            out_specs=(IN_VMEM, IN_VMEM, IN_VMEM),
            scratch_shapes=[
                pltpu.VMEM((TILE, 2 * SET + TXT), jnp.float32),
                pltpu.VMEM((2 * SET + TXT, 2 * HD), jnp.bfloat16),
                pltpu.SemaphoreType.DMA(()),
            ],
        ),
        compiler_params=pltpu.CompilerParams(vmem_limit_bytes=18 * MIB),
        cost_estimate=pl.CostEstimate(
            flops=4 * SET * 2304 * HD, bytes_accessed=3_000_000, transcendentals=SET * 2304
        ),
        name="attend_near",
    )(where, received, own, core, text_kv, w_out)


LAST_KEYS = QUAD * TOK + 128


def lay_last_kernel(where_ref, *refs):
    last_refs = refs[:QUAD]
    text_ref, keys_ref, value_ref = refs[QUAD:]
    for n, ref in enumerate(last_refs):
        keys_ref[n * TOK : (n + 1) * TOK, :] = ref[0:TOK, :]
    keys_ref[QUAD * TOK :, :] = text_ref[0, 0]
    lay_values(value_ref, [ref[TOK : 2 * TOK, :] for ref in last_refs] + [text_ref[1, 0]])


def lay_last(where, lasts, text_kv):
    return pl.pallas_call(
        lay_last_kernel,
        out_shape=(
            jax.ShapeDtypeStruct((LAST_KEYS, HD), jnp.bfloat16),
            jax.ShapeDtypeStruct((LAST_KEYS, 2 * HD), jnp.bfloat16),
        ),
        grid_spec=pltpu.PrefetchScalarGridSpec(
            num_scalar_prefetch=1,
            grid=(1,),
            in_specs=[whole((2 * TOK, HD)) for _ in lasts]
            + [
                pl.BlockSpec(
                    (2, 1, 128, HD), lambda i, w: (0, BRANCH - 1, w[4], HEADS_HERE - 1)
                )
            ],
            out_specs=(whole((LAST_KEYS, HD)), whole((LAST_KEYS, 2 * HD))),
        ),
        compiler_params=pltpu.CompilerParams(vmem_limit_bytes=16 * MIB),
        cost_estimate=pl.CostEstimate(
            flops=10_000_000_000, bytes_accessed=10_000_000, transcendentals=0
        ),
        name="lay_last",
    )(where, *lasts, text_kv)


def attend_last_kernel(where_ref, q_ref, keys_ref, value_ref, out_ref, score_ref):
    video_keys = QUAD * TOK
    q = q_ref[...].reshape(TILE, HD)
    top = jnp.full((TILE, 128), -jnp.inf, jnp.float32)
    top = score_keys(q, keys_ref[0:video_keys, :], score_ref, 0, top)
    top = score_text(q, keys_ref[video_keys:, :], where_ref[3], score_ref, video_keys, top)
    top = jnp.max(top, axis=1, keepdims=True) * EXP_SCALE
    mixed = mix(score_ref, value_ref, top, LAST_KEYS)
    total = mixed[:, HD : HD + 1]
    result = mixed[:, :HD] / total
    out_ref[:, 0:TOK, :] = result.astype(jnp.bfloat16).reshape(QUAD, TOK, HD)
    level = jnp.broadcast_to(top + jnp.log(total) * LOG2E, (TILE, HD))
    for f in range(QUAD):
        row = jnp.transpose(level[f * TOK : (f + 1) * TOK])[0:1]
        stats = limbs_of(row) + [jnp.zeros((STAT_ROWS - 3, HD), jnp.float32)]
        out_ref[f, TOK:LAST_ROWS, :] = jnp.concatenate(stats, axis=0).astype(jnp.bfloat16)


def attend_last(where, received, keys, values):
    return pl.pallas_call(
        attend_last_kernel,
        out_shape=jax.ShapeDtypeStruct((RING, LAST_ROWS, HD), jnp.bfloat16),
        grid_spec=pltpu.PrefetchScalarGridSpec(
            num_scalar_prefetch=1,
            grid=(SET // TILE,),
            in_specs=[
                pl.BlockSpec((QUAD, TOK, HD), lambda i, w: (i, 3, 0)),
                whole((LAST_KEYS, HD)),
                whole((LAST_KEYS, 2 * HD)),
            ],
            out_specs=pl.BlockSpec((QUAD, LAST_ROWS, HD), lambda i, w: (i, 0, 0)),
            scratch_shapes=[pltpu.VMEM((TILE, LAST_KEYS), jnp.float32)],
        ),
        compiler_params=pltpu.CompilerParams(vmem_limit_bytes=16 * MIB),
        cost_estimate=pl.CostEstimate(
            flops=4 * SET * 640 * HD, bytes_accessed=1_000_000, transcendentals=SET * 640
        ),
        name="attend_last",
    )(where, received, keys, values)


def attend_far_kernel(
    q_ref, y_ref, diagonal_ref, last_ref, mixed_ref, top_ref, out_ref, score_ref, value_ref
):
    @pl.when(first_step())
    def _():
        lay_values(value_ref, [set_values(y_ref), set_values(diagonal_ref)])

    q = q_ref[...].reshape(TILE, HD)
    top = jnp.full((TILE, 128), -jnp.inf, jnp.float32)
    for n, ref in enumerate((y_ref, diagonal_ref)):
        top = score_keys(q, set_keys(ref), score_ref, n * SET, top)
    here = tile_rows()
    before = top_ref[here, 0:1]
    top = jnp.maximum(jnp.max(top, axis=1, keepdims=True) * EXP_SCALE, before)
    mixed = mix(score_ref, value_ref, top, 2 * SET) + mixed_ref[here, :] * jnp.exp2(before - top)
    result = mixed[:, :HD] / mixed[:, HD : HD + 1]
    out_ref[:, 0:TOK, :] = result.astype(jnp.bfloat16).reshape(QUAD, TOK, HD)
    out_ref[:, TOK:RETURN, :] = last_ref[...]


def in_vmem(x):
    return pltpu.with_memory_space_constraint(x, pltpu.VMEM)


def in_hbm(x):
    return pltpu.with_memory_space_constraint(x, pltpu.HBM)


def attend_far(received, over_y, diagonal, last, mixed, top):
    return pl.pallas_call(
        attend_far_kernel,
        out_shape=jax.ShapeDtypeStruct((RING, RETURN, HD), jnp.bfloat16),
        grid=(SET // TILE,),
        in_specs=[
            pl.BlockSpec((QUAD, TOK, HD), lambda i: (i, 2, 0)),
            whole((RING, 2 * TOK, HD)),
            whole((RING, 2 * TOK, HD)),
            pl.BlockSpec((QUAD, LAST_ROWS, HD), lambda i: (i, 0, 0)),
            IN_VMEM,
            IN_VMEM,
        ],
        out_specs=pl.BlockSpec((QUAD, RETURN, HD), lambda i: (i, 0, 0)),
        scratch_shapes=[
            pltpu.VMEM((TILE, 2 * SET), jnp.float32),
            pltpu.VMEM((2 * SET, 2 * HD), jnp.bfloat16),
        ],
        compiler_params=pltpu.CompilerParams(vmem_limit_bytes=18 * MIB),
        cost_estimate=pl.CostEstimate(
            flops=4 * SET * 2048 * HD, bytes_accessed=4_000_000, transcendentals=SET * 2048
        ),
        name="attend_far",
    )(received, over_y, diagonal, last, in_vmem(mixed), in_vmem(top))


def output_kernel(place_ref, back_ref, w_ref, *refs):
    out_refs, attn_ref = refs[:HEAD_AXIS], refs[HEAD_AXIS]
    for p in range(RING):
        b, hd = divmod(p, HEADS_HERE)
        attn_ref[b * TOK : (b + 1) * TOK, hd * HD : (hd + 1) * HD] = back_ref[p, 0:TOK, :]
    levels = []
    for p in range(RING):
        stats = back_ref[p, 2 * TOK : RETURN, :].astype(jnp.float32)
        row = stats[0:1] + stats[1:2] + stats[2:3]
        levels.append(jnp.transpose(jnp.broadcast_to(row, (TOK, HD))))
    top = levels[0]
    for level in levels[1:]:
        top = jnp.maximum(top, level)
    total = jnp.zeros((TOK, HD), jnp.float32)
    mixed = jnp.zeros((TOK, HD), jnp.float32)
    for p, level in enumerate(levels):
        weight = jnp.exp2(level - top)
        total += weight
        mixed += weight * back_ref[p, TOK : 2 * TOK, :].astype(jnp.float32)
    attn_ref[(BRANCH - 1) * TOK :, (HEADS_HERE - 1) * HD :] = (mixed / total).astype(jnp.bfloat16)
    for s in range(HEAD_AXIS):
        start = pl.multiple_of(place_ref[s] * DSH, DSH)
        out_refs[s][...] = jnp.dot(
            attn_ref[...], w_ref[:, pl.ds(start, DSH)], preferred_element_type=jnp.float32
        ).astype(jnp.bfloat16)


def output(places, back, w_out):
    return pl.pallas_call(
        output_kernel,
        out_shape=tuple(
            jax.ShapeDtypeStruct((ROWS, DSH), jnp.bfloat16) for _ in range(HEAD_AXIS)
        ),
        grid_spec=pltpu.PrefetchScalarGridSpec(
            num_scalar_prefetch=1,
            grid=(1,),
            in_specs=[
                whole((RING, RETURN, HD)),
                IN_VMEM,
            ],
            out_specs=tuple(whole((ROWS, DSH)) for _ in range(HEAD_AXIS)),
            scratch_shapes=[pltpu.VMEM((ROWS, DSH), jnp.bfloat16)],
        ),
        compiler_params=pltpu.CompilerParams(vmem_limit_bytes=24 * MIB),
        cost_estimate=pl.CostEstimate(
            flops=2 * ROWS * DSH * DSH * HEAD_AXIS, bytes_accessed=5_000_000, transcendentals=0
        ),
        name="output",
    )(places, back, in_vmem(w_out))


def head_move(x, step):
    return lax.ppermute(x, "head", [(i, (i + step) % HEAD_AXIS) for i in range(HEAD_AXIS)])


def head_partner(x):
    return lax.ppermute(x, "head", [(i, i ^ 1) for i in range(HEAD_AXIS)])


def frame_move(x, flip):
    return lax.ppermute(x, "frame", [(i, i ^ flip) for i in range(FRAMES)])


def gather_head(own):
    partner = head_partner(own)
    opposite = head_move(own, 4)
    ahead = head_move(own, -2)
    behind = head_move(own, 2)
    return [
        own,
        partner,
        ahead,
        behind,
        head_move(partner, -2),
        head_move(partner, 2),
        opposite,
        head_partner(opposite),
    ]


def add(*terms):
    total = terms[0].astype(jnp.float32)
    for term in terms[1:]:
        total += term.astype(jnp.float32)
    return total


def scatter_head(parts):
    for_opposite = head_partner(parts[7])
    for_partner = [head_move(parts[4], 2), head_move(parts[5], -2)]
    direct = [head_move(parts[2], 2), head_move(parts[3], -2)]
    over_y = head_partner(add(parts[1], *for_partner).astype(jnp.bfloat16))
    across = head_move(add(parts[6], for_opposite).astype(jnp.bfloat16), 4)
    return add(parts[0], *direct, over_y, across)


def body(
    video, w_qkv, w_out, text_kv, text_lengths, norm_gains, mod_table, timestep_ids, queue_shift
):
    text_kv = in_hbm(text_kv)
    frame = lax.axis_index("frame").astype(jnp.int32)
    head = lax.axis_index("head").astype(jnp.int32)
    own, gate, places, where = prep(
        frame.reshape(1),
        head.reshape(1),
        queue_shift,
        in_hbm(timestep_ids),
        in_hbm(text_lengths),
        in_hbm(video),
        in_hbm(mod_table.transpose(1, 0, 2)),
    )
    cosine, sine = rope_tables(frame)
    blocks = gather_head(own)
    weights = in_hbm(w_qkv.transpose(1, 0, 2))
    send, last = project(places, blocks, weights, in_hbm(norm_gains), cosine, sine)
    rings = [[(y * RING + z) * 2 + core for z in range(RING)] for y in range(2) for core in range(2)]

    def over_rings(x):
        return lax.all_to_all(x, "frame", 0, 0, axis_index_groups=rings, tiled=True)

    received = over_rings(send)
    flips = (1, FRAMES // 2, FRAMES // 2 + 1)
    lasts = [last] + [frame_move(last, flip) for flip in flips]
    last_keys, last_values = lay_last(where, lasts, text_kv)
    near = received[:, : 2 * TOK]
    over_y = frame_move(near, FRAMES // 2)
    over_core = frame_move(near, 1)
    ninth = attend_last(where, received, last_keys, last_values)
    mixed, top, w_held = attend_near(where, received, near, over_core, text_kv, in_hbm(w_out))
    over_y, _, _ = lax.optimization_barrier((over_y, mixed, ninth))
    diagonal = frame_move(over_y, 1)
    returned = attend_far(received, over_y, diagonal, ninth, mixed, top)
    partial = output(places, over_rings(returned), w_held)
    proj = scatter_head(partial).reshape(video.shape)
    return (video.astype(jnp.float32) + gate * proj).astype(jnp.bfloat16)


def solution(mesh):
    in_specs = (
        P(None, "frame", "head"),
        P(None, None, "head"),
        P("head", None),
        P(None, None, None, "head"),
        P(),
        P(),
        P(None, None, "head"),
        P(),
        P(),
    )
    out_specs = P(None, "frame", "head")
    return jax.shard_map(body, mesh=mesh, in_specs=in_specs, out_specs=out_specs, check_vma=False)
```

time: 632 us -> 146 us (0.23)
  waiting for transfers between devices: 501 us -> 58.3 us
  matrix products: 43.6 us -> 0 us
  starting transfers between devices: 0.47 us -> 32 us
  Pallas kernels: 0 us -> 30.5 us
  local copies, waits for them, and re-layouts: 30.1 us -> 0.04 us
  other arithmetic: 19.9 us -> 2.22 us
  between operations: 14.6 us -> 0.77 us
    all_gather x7 -> x0, waiting for transfers between devices: 419 us -> none  [the longest x3 188 us: body(): lax.all_gather(value[branch:branch + 1], 'frame', axis=1, tiled=True)]
    unnamed x9 -> x0, waiting for transfers between devices: 82.5 us -> none
    dot_general x11 -> x0, matrix products: 43.6 us -> none  [the longest x3 15 us: make_absorb(): jnp.einsum('bhqk,bkhd->bhqd', weights.astype(jnp.bfloat16), block_values,...]
    ppermute x0 -> x20, waiting for transfers between devices: none -> 31.5 us  [the longest x10 25.1 us: head_move(): lax.ppermute(x, 'head', [(i, (i + step) % HEAD_AXIS) for i in range(HEAD_...]
    pallas_call x0 -> x7, Pallas kernels: none -> 30.5 us  [the longest x1 8.58 us: project(): pl.pallas_call(project_kernel, out_shape=(jax.ShapeDtypeStruct((RING, 4 *...]
    all_to_all x0 -> x1, waiting for transfers between devices: none -> 26.8 us  [over_rings(): return lax.all_to_all(x, 'frame', 0, 0, axis_index_groups=rings, tiled=True)]
    ppermute x0 -> x20, starting transfers between devices: none -> 23.5 us  [the longest x10 13.9 us: head_move(): lax.ppermute(x, 'head', [(i, (i + step) % HEAD_AXIS) for i in range(HEAD_...]
    unnamed x26 -> x2, local copies, waits for them, and re-layouts: 22.4 us -> 0.01 us
  transfers between devices with their start and end apart: 8 -> 21, of which waited for: 8 -> 11; matrix products, arithmetic and copies ran while one was open for 9% -> 1% of each run, Pallas kernels for 0% -> 8%
where the time goes in v1:
time: 146 us; the launch traced here: 145 us
  waiting for transfers between devices  58.3 us (40%)
  starting transfers between devices  32 us (22%)
  Pallas kernels  30.5 us (21%)
  blocking collectives  21.2 us (15%)
  other arithmetic  2.22 us (2%)
    all_to_all x1, waiting for transfers between devices, over_rings(): return lax.all_to_all(x, 'frame', 0, 0, axis_index_groups=rings, tiled=True)  26.8 us
    ppermute x10, waiting for transfers between devices, head_move(): lax.ppermute(x, 'head', [(i, (i + step) % HEAD_AXIS) for i in range(HEAD_...  25.1 us
    all_to_all x1, blocking collectives, over_rings(): return lax.all_to_all(x, 'frame', 0, 0, axis_index_groups=rings, tiled=True)  21.2 us
    ppermute x10, starting transfers between devices, head_move(): lax.ppermute(x, 'head', [(i, (i + step) % HEAD_AXIS) for i in range(HEAD_...  13.9 us
    pallas_call x1, Pallas kernels, project(): pl.pallas_call(project_kernel, out_shape=(jax.ShapeDtypeStruct((RING, 4 *...  8.58 us
    all_to_all x1, starting transfers between devices, over_rings(): return lax.all_to_all(x, 'frame', 0, 0, axis_index_groups=rings, tiled=True)  8.48 us
    pallas_call x1, Pallas kernels, attend_near(): pl.pallas_call(attend_near_kernel, out_shape=(pltpu.VMEM((SET, 2 * HD), j...  7.08 us
    ppermute x4, starting transfers between devices, head_partner(): return lax.ppermute(x, 'head', [(i, i ^ 1) for i in range(HEAD_AXIS)])  6.4 us
  transfers between devices with their start and end apart: 21, of which 11 were waited for; matrix products, arithmetic and copies ran while one was open for 1% of the time, Pallas kernels for 8%

profile of v1, /device:TPU:6, one launch (start us, length us, event | category | flops | bytes accessed | tf_op | source)
XLA Modules:
  0.0 145.0 jit_solution(17860754542733445099)
XLA Ops:
  0.7 2.3 %prep.1 = (bf16[400,384]{1,0:T(8,128)(2,1)S(1)}, f32[1,384]{1,0:T(1,128)S(1)}, s32[8]{0:T(128)S(1)}, s32[5]{0:T(128)S(1)}) custom-call(s32[1]{0:T(128)} %bitcast.frame_ref, s32[1]{0:T(128)} %bitcast.1.head_ref, s32[1]{0:T(128)S(6)} %copy.13.shift_ref, s32[32]{0:T(128)} %ids_ref.1, s32[3]{0:T(128)} %lengths_ref.1, bf16[3,128,384]{2,1,0:T(8,128)(2,1)} %video_ref.1, ...), custom_call_target="tpu_custom_call" | custom-call | tf_op jit(solution)/shard_map/prep/pallas_call | solution.py:95
  3.0 3.3 %collective-permute-start = (bf16[400,384]{1,0:T(8,128)(2,1)S(1)}, bf16[400,384]{1,0:T(8,128)(2,1)S(1)}, u32[]{:S(2)}, u32[]{:S(2)}) collective-permute-start(bf16[400,384]{1,0:T(8,128)(2,1)S(1)} %get-tuple-element.27.refs_0_), channel_id=1, source_target_pairs={{0,1},{1,0},{2,3},{3,2},{4,5},{5,4},{6,7},{7,6},{8,9},{9,8},{10,11... | collective-permute-start | bytes 921608 | tf_op jit(solution)/shard_map/ppermute | solution.py:531
  6.3 1.4 collective-permute-start.5
  7.7 3.2 %collective-permute-start.2 = (bf16[400,384]{1,0:T(8,128)(2,1)S(1)}, bf16[400,384]{1,0:T(8,128)(2,1)S(1)}, u32[]{:S(2)}, u32[]{:S(2)}) collective-permute-start(bf16[400,384]{1,0:T(8,128)(2,1)S(1)} %get-tuple-element.27.refs_0_), channel_id=1, source_target_pairs={{0,2},{1,3},{2,4},{3,5},{4,6},{5,7},{6,0},{7,1},{8,10},{9,11},{10,... | collective-permute-start | bytes 921608 | tf_op jit(solution)/shard_map/ppermute | solution.py:527
  10.9 2.7 %collective-permute-done.refs_1_ = bf16[400,384]{1,0:T(8,128)(2,1)S(1)} collective-permute-done((bf16[400,384]{1,0:T(8,128)(2,1)S(1)}, bf16[400,384]{1,0:T(8,128)(2,1)S(1)}, u32[]{:S(2)}, u32[]{:S(2)}) %collective-permute-start) | collective-permute-done | bytes 307232 | tf_op jit(solution)/shard_map/ppermute | solution.py:531
  13.6 0.8 collective-permute-start.3
  14.4 2.4 %collective-permute-start.4 = (bf16[400,384]{1,0:T(8,128)(2,1)S(1)}, bf16[400,384]{1,0:T(8,128)(2,1)S(1)}, u32[]{:S(2)}, u32[]{:S(2)}) collective-permute-start(bf16[400,384]{1,0:T(8,128)(2,1)S(1)} %collective-permute-done.refs_1_), channel_id=1, source_target_pairs={{0,2},{1,3},{2,4},{3,5},{4,6},{5,7},{6,0},{7,1},{8,10},{9,11},{10,... | collective-permute-start | bytes 921608 | tf_op jit(solution)/shard_map/ppermute | solution.py:527
  16.8 1.2 collective-permute-done.5.refs_6_
  18.0 2.0 %collective-permute-start.6 = (bf16[400,384]{1,0:T(8,128)(2,1)S(1)}, bf16[400,384]{1,0:T(8,128)(2,1)S(1)}, u32[]{:S(2)}, u32[]{:S(2)}) collective-permute-start(bf16[400,384]{1,0:T(8,128)(2,1)S(1)} %collective-permute-done.5.refs_6_), channel_id=1, source_target_pairs={{0,1},{1,0},{2,3},{3,2},{4,5},{5,4},{6,7},{7,6},{8,9},{9,8},{10,11... | collective-permute-start | bytes 921608 | tf_op jit(solution)/shard_map/ppermute | solution.py:531
  20.0 1.0 sine_multiply_fusion
  21.1 2.1 %collective-permute-done.1.refs_2_ = bf16[400,384]{1,0:T(8,128)(2,1)S(1)} collective-permute-done((bf16[400,384]{1,0:T(8,128)(2,1)S(1)}, bf16[400,384]{1,0:T(8,128)(2,1)S(1)}, u32[]{:S(2)}, u32[]{:S(2)}) %collective-permute-start.1) | collective-permute-done | bytes 307232 | tf_op jit(solution)/shard_map/ppermute | solution.py:527
  23.2 6.5 %collective-permute-done.3.refs_4_ = bf16[400,384]{1,0:T(8,128)(2,1)S(1)} collective-permute-done((bf16[400,384]{1,0:T(8,128)(2,1)S(1)}, bf16[400,384]{1,0:T(8,128)(2,1)S(1)}, u32[]{:S(2)}, u32[]{:S(2)}) %collective-permute-start.3) | collective-permute-done | bytes 307232 | tf_op jit(solution)/shard_map/ppermute | solution.py:527
  29.7 8.6 %project.1 = (bf16[8,512,128]{2,1,0:T(8,128)(2,1)}, bf16[256,128]{1,0:T(8,128)(2,1)S(1)}) custom-call(s32[8]{0:T(128)S(1)} %get-tuple-element.26.place_ref, bf16[400,384]{1,0:T(8,128)(2,1)S(1)} %get-tuple-element.27.refs_0_, bf16[400,384]{1,0:T(8,128)(2,1)S(1)} %collective-permute-done.refs_1_, bf16[400,384]{1,0:T(8,128)(2,1)S(1)} %collective-permute-done.1.refs_2_, ...), custom_call_target="tpu_custom_call" | custom-call | flops 2717908992 | bytes 12000000 | tf_op jit(solution)/shard_map/project/pallas_call | solution.py:190
  38.3 8.5 %all-to-all-start = ((bf16[8,512,128]{2,1,0:T(8,128)(2,1)}), bf16[8,512,128]{2,1,0:T(8,128)(2,1)S(1)}, u32[]{:S(2)}, u32[]{:S(2)}) async-start(bf16[8,512,128]{2,1,0:T(8,128)(2,1)} %get-tuple-element.28), calls=%async_computation | async-start | bytes 2097152 | tf_op jit(solution)/shard_map/all_to_all | solution.py:593
  47.8 1.1 collective-permute-start.9
  48.9 26.8 %all-to-all-done.q_ref = bf16[8,512,128]{2,1,0:T(8,128)(2,1)S(1)} async-done(((bf16[8,512,128]{2,1,0:T(8,128)(2,1)}), bf16[8,512,128]{2,1,0:T(8,128)(2,1)S(1)}, u32[]{:S(2)}, u32[]{:S(2)}) %all-to-all-start) | async-done | bytes 1048608 | tf_op jit(solution)/shard_map/all_to_all | solution.py:593
  75.8 0.9 collective-permute-start.7
  76.8 1.4 lay_last.1
  78.2 3.0 %attend_last.1.last_ref = bf16[8,144,128]{2,1,0:T(8,128)(2,1)S(1)} custom-call(s32[5]{0:T(128)S(1)} %get-tuple-element.29.where_ref, bf16[8,512,128]{2,1,0:T(8,128)(2,1)S(1)} %all-to-all-done.q_ref, bf16[640,128]{1,0:T(8,128)(2,1)S(1)} %get-tuple-element.32.keys_ref, bf16[640,256]{1,0:T(8,128)(2,1)S(1)} %get-tuple-element.33.value_ref), custom_call_target="tpu_custom_call" | custom-call | flops 335544320 | bytes 1000000 | tf_op jit(solution)/shard_map/attend_last/pallas_call | solution.py:399
  81.2 7.1 %attend_near.1 = (f32[1024,256]{1,0:T(8,128)S(1)}, f32[1024,128]{1,0:T(8,128)S(1)}, bf16[384,3072]{1,0:T(8,128)(2,1)S(1)}) custom-call(s32[5]{0:T(128)S(1)} %get-tuple-element.29.where_ref, bf16[8,512,128]{2,1,0:T(8,128)(2,1)S(1)} %all-to-all-done.q_ref, bf16[8,256,128]{2,1,0:T(8,128)(2,1)S(1)} %slice.4.own_ref, ...), custom_call_target="tpu_custom_call" | custom-call | flops 1207959552 | bytes 3000000 | tf_op jit(solution)/shard_map/attend_near/pallas_call | solution.py:310
  88.3 1.8 %collective-permute-done.7.y_ref = bf16[8,256,128]{2,1,0:T(8,128)(2,1)S(1)} collective-permute-done((bf16[8,256,128]{2,1,0:T(8,128)(2,1)S(1)}, bf16[8,256,128]{2,1,0:T(8,128)(2,1)S(1)}, u32[]{:S(2)}, u32[]{:S(2)}) %collective-permute-start.7) | collective-permute-done | bytes 524320 | tf_op jit(solution)/shard_map/ppermute | solution.py:535
  90.2 1.9 %collective-permute-done.12.diagonal_ref = bf16[8,256,128]{2,1,0:T(8,128)(2,1)S(1)} collective-permute-done((bf16[8,256,128]{2,1,0:T(8,128)(2,1)S(1)}, bf16[8,256,128]{2,1,0:T(8,128)(2,1)S(1)}, u32[]{:S(2)}, u32[]{:S(2)}) %collective-permute-start.12) | collective-permute-done | bytes 524320 | tf_op jit(solution)/shard_map/ppermute | solution.py:535
  92.1 5.8 %attend_far.1 = bf16[8,272,128]{2,1,0:T(8,128)(2,1)S(1)} custom-call(bf16[8,512,128]{2,1,0:T(8,128)(2,1)S(1)} %all-to-all-done.q_ref, bf16[8,256,128]{2,1,0:T(8,128)(2,1)S(1)} %collective-permute-done.7.y_ref, bf16[8,256,128]{2,1,0:T(8,128)(2,1)S(1)} %collective-permute-done.12.diagonal_ref, bf16[8,144,128]{2,1,0:T(8,128)(2,1)S(1)} %attend_last.1.last_ref, ...), custom_call_target="tpu_custom_call" | custom-call | flops 1073741824 | bytes 4000000 | tf_op jit(solution)/shard_map/attend_far/pallas_call | solution.py:450
  97.8 21.2 %all_to_all.10.back_ref = bf16[8,272,128]{2,1,0:T(8,128)(2,1)S(1)} all-to-all(bf16[8,272,128]{2,1,0:T(8,128)(2,1)S(1)} %attend_far.1), channel_id=1, replica_groups={{0,16,32,48,64,80,96,112},{8,24,40,56,72,88,104,120},{128,144,160,176,1..., dimensions={0} | all-to-all | bytes 1114112 | tf_op jit(solution)/shard_map/all_to_all | solution.py:593
  119.0 2.3 %output.1 = (bf16[384,384]{1,0:T(8,128)(2,1)S(1)}, bf16[384,384]{1,0:T(8,128)(2,1)S(1)}, bf16[384,384]{1,0:T(8,128)(2,1)S(1)}, bf16[384,384]{1,0:T(8,128)(2,1)S(...) custom-call(s32[8]{0:T(128)S(1)} %get-tuple-element.26.place_ref, ...), custom_call_target="tpu_custom_call" | custom-call | flops 905969664 | bytes 5000000 | tf_op jit(solution)/shard_map/output/pallas_call | solution.py:503
  121.8 1.6 %collective-permute-start.16 = (bf16[384,384]{1,0:T(8,128)(2,1)S(1)}, bf16[384,384]{1,0:T(8,128)(2,1)S(1)}, u32[]{:S(2)}, u32[]{:S(2)}) collective-permute-start(bf16[384,384]{1,0:T(8,128)(2,1)S(1)} %get-tuple-element.42), channel_id=1, source_target_pairs={{0,6},{1,7},{2,0},{3,1},{4,2},{5,3},{6,4},{7,5},{8,14},{9,15},{10,... | collective-permute-start | bytes 884744 | tf_op jit(solution)/shard_map/ppermute | solution.py:527
  124.2 1.6 %collective-permute-start.13 = (bf16[384,384]{1,0:T(8,128)(2,1)S(1)}, bf16[384,384]{1,0:T(8,128)(2,1)S(1)}, u32[]{:S(2)}, u32[]{:S(2)}) collective-permute-start(bf16[384,384]{1,0:T(8,128)(2,1)S(1)} %get-tuple-element.38), channel_id=1, source_target_pairs={{0,2},{1,3},{2,4},{3,5},{4,6},{5,7},{6,0},{7,1},{8,10},{9,11},{10,... | collective-permute-start | bytes 884744 | tf_op jit(solution)/shard_map/ppermute | solution.py:527
  126.3 5.1 %collective-permute-done.15 = bf16[384,384]{1,0:T(8,128)(2,1)S(1)} collective-permute-done((bf16[384,384]{1,0:T(8,128)(2,1)S(1)}, bf16[384,384]{1,0:T(8,128)(2,1)S(1)}, u32[]{:S(2)}, u32[]{:S(2)}) %collective-permute-start.15) | collective-permute-done | bytes 294944 | tf_op jit(solution)/shard_map/ppermute | solution.py:527
  131.4 1.6 %collective-permute-done.16 = bf16[384,384]{1,0:T(8,128)(2,1)S(1)} collective-permute-done((bf16[384,384]{1,0:T(8,128)(2,1)S(1)}, bf16[384,384]{1,0:T(8,128)(2,1)S(1)}, u32[]{:S(2)}, u32[]{:S(2)}) %collective-permute-start.16) | collective-permute-done | bytes 294944 | tf_op jit(solution)/shard_map/ppermute | solution.py:527
  133.5 1.9 %collective-permute-start.19 = (bf16[384,384]{1,0:T(8,128)(2,1)S(1)}, bf16[384,384]{1,0:T(8,128)(2,1)S(1)}, u32[]{:S(2)}, u32[]{:S(2)}) collective-permute-start(bf16[384,384]{1,0:T(8,128)(2,1)S(1)} %add_convert_fusion.1), channel_id=1, source_target_pairs={{0,4},{1,5},{2,6},{3,7},{4,0},{5,1},{6,2},{7,3},{8,12},{9,13},{10,... | collective-permute-start | bytes 884744 | tf_op jit(solution)/shard_map/ppermute | solution.py:527
  135.4 2.2 %collective-permute-done.13 = bf16[384,384]{1,0:T(8,128)(2,1)S(1)} collective-permute-done((bf16[384,384]{1,0:T(8,128)(2,1)S(1)}, bf16[384,384]{1,0:T(8,128)(2,1)S(1)}, u32[]{:S(2)}, u32[]{:S(2)}) %collective-permute-start.13) | collective-permute-done | bytes 294944 | tf_op jit(solution)/shard_map/ppermute | solution.py:527
  137.7 6.3 %collective-permute-done.14 = bf16[384,384]{1,0:T(8,128)(2,1)S(1)} collective-permute-done((bf16[384,384]{1,0:T(8,128)(2,1)S(1)}, bf16[384,384]{1,0:T(8,128)(2,1)S(1)}, u32[]{:S(2)}, u32[]{:S(2)}) %collective-permute-start.14) | collective-permute-done | bytes 294944 | tf_op jit(solution)/shard_map/ppermute | solution.py:527
  (28 shorter events, 4.4 us)
Async XLA Ops:
  3.0 10.6 %collective-permute-start = (bf16[400,384]{1,0:T(8,128)(2,1)S(1)}, bf16[400,384]{1,0:T(8,128)(2,1)S(1)}, u32[]{:S(2)}, u32[]{:S(2)}) collective-permute-start(bf16[400,384]{1,0:T(8,128)(2,1)S(1)} %get-tuple-element.27.refs_0_), channel_id=1, source_target_pairs={{0,1},{1,0},{2,3},{3,2},{4,5},{5,4},{6,7},{7,6},{8,9},{9,8},{10,11... | collective-permute-start | bytes 921608 | tf_op jit(solution)/shard_map/ppermute | solution.py:531
  6.3 11.7 %collective-permute-start.5 = (bf16[400,384]{1,0:T(8,128)(2,1)S(1)}, bf16[400,384]{1,0:T(8,128)(2,1)S(1)}, u32[]{:S(2)}, u32[]{:S(2)}) collective-permute-start(bf16[400,384]{1,0:T(8,128)(2,1)S(1)} %get-tuple-element.27.refs_0_), channel_id=1, source_target_pairs={{0,4},{1,5},{2,6},{3,7},{4,0},{5,1},{6,2},{7,3},{8,12},{9,13},{10,... | collective-permute-start | bytes 921608 | tf_op jit(solution)/shard_map/ppermute | solution.py:527
  7.7 15.5 %collective-permute-start.1 = (bf16[400,384]{1,0:T(8,128)(2,1)S(1)}, bf16[400,384]{1,0:T(8,128)(2,1)S(1)}, u32[]{:S(2)}, u32[]{:S(2)}) collective-permute-start(bf16[400,384]{1,0:T(8,128)(2,1)S(1)} %get-tuple-element.27.refs_0_), channel_id=1, source_target_pairs={{0,6},{1,7},{2,0},{3,1},{4,2},{5,3},{6,4},{7,5},{8,14},{9,15},{10,... | collective-permute-start | bytes 921608 | tf_op jit(solution)/shard_map/ppermute | solution.py:527
  7.7 15.5 %collective-permute-start.2 = (bf16[400,384]{1,0:T(8,128)(2,1)S(1)}, bf16[400,384]{1,0:T(8,128)(2,1)S(1)}, u32[]{:S(2)}, u32[]{:S(2)}) collective-permute-start(bf16[400,384]{1,0:T(8,128)(2,1)S(1)} %get-tuple-element.27.refs_0_), channel_id=1, source_target_pairs={{0,2},{1,3},{2,4},{3,5},{4,6},{5,7},{6,0},{7,1},{8,10},{9,11},{10,... | collective-permute-start | bytes 921608 | tf_op jit(solution)/shard_map/ppermute | solution.py:527
  13.6 16.1 %collective-permute-start.3 = (bf16[400,384]{1,0:T(8,128)(2,1)S(1)}, bf16[400,384]{1,0:T(8,128)(2,1)S(1)}, u32[]{:S(2)}, u32[]{:S(2)}) collective-permute-start(bf16[400,384]{1,0:T(8,128)(2,1)S(1)} %collective-permute-done.refs_1_), channel_id=1, source_target_pairs={{0,6},{1,7},{2,0},{3,1},{4,2},{5,3},{6,4},{7,5},{8,14},{9,15},{10,... | collective-permute-start | bytes 921608 | tf_op jit(solution)/shard_map/ppermute | solution.py:527
  14.4 15.3 %collective-permute-start.4 = (bf16[400,384]{1,0:T(8,128)(2,1)S(1)}, bf16[400,384]{1,0:T(8,128)(2,1)S(1)}, u32[]{:S(2)}, u32[]{:S(2)}) collective-permute-start(bf16[400,384]{1,0:T(8,128)(2,1)S(1)} %collective-permute-done.refs_1_), channel_id=1, source_target_pairs={{0,2},{1,3},{2,4},{3,5},{4,6},{5,7},{6,0},{7,1},{8,10},{9,11},{10,... | collective-permute-start | bytes 921608 | tf_op jit(solution)/shard_map/ppermute | solution.py:527
  18.0 11.7 %collective-permute-start.6 = (bf16[400,384]{1,0:T(8,128)(2,1)S(1)}, bf16[400,384]{1,0:T(8,128)(2,1)S(1)}, u32[]{:S(2)}, u32[]{:S(2)}) collective-permute-start(bf16[400,384]{1,0:T(8,128)(2,1)S(1)} %collective-permute-done.5.refs_6_), channel_id=1, source_target_pairs={{0,1},{1,0},{2,3},{3,2},{4,5},{5,4},{6,7},{7,6},{8,9},{9,8},{10,11... | collective-permute-start | bytes 921608 | tf_op jit(solution)/shard_map/ppermute | solution.py:531
  38.3 37.4 %all-to-all-start = ((bf16[8,512,128]{2,1,0:T(8,128)(2,1)}), bf16[8,512,128]{2,1,0:T(8,128)(2,1)S(1)}, u32[]{:S(2)}, u32[]{:S(2)}) async-start(bf16[8,512,128]{2,1,0:T(8,128)(2,1)} %get-tuple-element.28), calls=%async_computation | async-start | bytes 2097152 | tf_op jit(solution)/shard_map/all_to_all | solution.py:593
  46.7 30.0 %collective-permute-start.10 = (bf16[256,128]{1,0:T(8,128)(2,1)S(1)}, bf16[256,128]{1,0:T(8,128)(2,1)S(1)}, u32[]{:S(2)}, u32[]{:S(2)}) collective-permute-start(bf16[256,128]{1,0:T(8,128)(2,1)S(1)} %get-tuple-element.31.refs_0_), channel_id=1, source_target_pairs={{0,128},{8,136},{16,144},{24,152},{32,160},{40,168},{48,176},{56,1... | collective-permute-start | bytes 196616 | tf_op jit(solution)/shard_map/ppermute | solution.py:535
  47.4 29.4 %collective-permute-start.11 = (bf16[256,128]{1,0:T(8,128)(2,1)S(1)}, bf16[256,128]{1,0:T(8,128)(2,1)S(1)}, u32[]{:S(2)}, u32[]{:S(2)}) collective-permute-start(bf16[256,128]{1,0:T(8,128)(2,1)S(1)} %get-tuple-element.31.refs_0_), channel_id=1, source_target_pairs={{0,136},{8,128},{16,152},{24,144},{32,168},{40,160},{48,184},{56,1... | collective-permute-start | bytes 196616 | tf_op jit(solution)/shard_map/ppermute | solution.py:535
  47.8 29.0 %collective-permute-start.9 = (bf16[256,128]{1,0:T(8,128)(2,1)S(1)}, bf16[256,128]{1,0:T(8,128)(2,1)S(1)}, u32[]{:S(2)}, u32[]{:S(2)}) collective-permute-start(bf16[256,128]{1,0:T(8,128)(2,1)S(1)} %get-tuple-element.31.refs_0_), channel_id=1, source_target_pairs={{0,8},{8,0},{16,24},{24,16},{32,40},{40,32},{48,56},{56,48},{64,72... | collective-permute-start | bytes 196616 | tf_op jit(solution)/shard_map/ppermute | solution.py:535
  75.7 5.5 %collective-permute-start.8 = (bf16[8,256,128]{2,1,0:T(8,128)(2,1)S(1)}, bf16[8,256,128]{2,1,0:T(8,128)(2,1)S(1)}, u32[]{:S(2)}, u32[]{:S(2)}) collective-permute-start(bf16[8,256,128]{2,1,0:T(8,128)(2,1)S(1)} %slice.4.own_ref), channel_id=1, source_target_pairs={{0,8},{8,0},{16,24},{24,16},{32,40},{40,32},{48,56},{56,48},{64,72... | collective-permute-start | bytes 1572872 | tf_op jit(solution)/shard_map/ppermute | solution.py:535
  75.8 14.3 %collective-permute-start.7 = (bf16[8,256,128]{2,1,0:T(8,128)(2,1)S(1)}, bf16[8,256,128]{2,1,0:T(8,128)(2,1)S(1)}, u32[]{:S(2)}, u32[]{:S(2)}) collective-permute-start(bf16[8,256,128]{2,1,0:T(8,128)(2,1)S(1)} %slice.4.own_ref), channel_id=1, source_target_pairs={{0,128},{8,136},{16,144},{24,152},{32,160},{40,168},{48,176},{56,1... | collective-permute-start | bytes 1572872 | tf_op jit(solution)/shard_map/ppermute | solution.py:535
  90.2 1.9 %collective-permute-start.12 = (bf16[8,256,128]{2,1,0:T(8,128)(2,1)S(1)}, bf16[8,256,128]{2,1,0:T(8,128)(2,1)S(1)}, u32[]{:S(2)}, u32[]{:S(2)}) collective-permute-start(bf16[8,256,128]{2,1,0:T(8,128)(2,1)S(1)} %collective-permute-done.7.y_ref), channel_id=1, source_target_pairs={{0,8},{8,0},{16,24},{24,16},{32,40},{40,32},{48,56},{56,48},{64,72... | collective-permute-start | bytes 1572872 | tf_op jit(solution)/shard_map/ppermute | solution.py:535
  121.3 22.8 %copy-start = (bf16[3,128,384]{2,1,0:T(8,128)(2,1)S(1)}, bf16[3,128,384]{2,1,0:T(8,128)(2,1)}, u32[]{:S(2)}) copy-start(bf16[3,128,384]{2,1,0:T(8,128)(2,1)} %video_ref.1) | copy-start | bytes 884740
  121.4 10.0 %collective-permute-start.15 = (bf16[384,384]{1,0:T(8,128)(2,1)S(1)}, bf16[384,384]{1,0:T(8,128)(2,1)S(1)}, u32[]{:S(2)}, u32[]{:S(2)}) collective-permute-start(bf16[384,384]{1,0:T(8,128)(2,1)S(1)} %get-tuple-element.41), channel_id=1, source_target_pairs={{0,2},{1,3},{2,4},{3,5},{4,6},{5,7},{6,0},{7,1},{8,10},{9,11},{10,... | collective-permute-start | bytes 884744 | tf_op jit(solution)/shard_map/ppermute | solution.py:527
  121.8 11.2 %collective-permute-start.16 = (bf16[384,384]{1,0:T(8,128)(2,1)S(1)}, bf16[384,384]{1,0:T(8,128)(2,1)S(1)}, u32[]{:S(2)}, u32[]{:S(2)}) collective-permute-start(bf16[384,384]{1,0:T(8,128)(2,1)S(1)} %get-tuple-element.42), channel_id=1, source_target_pairs={{0,6},{1,7},{2,0},{3,1},{4,2},{5,3},{6,4},{7,5},{8,14},{9,15},{10,... | collective-permute-start | bytes 884744 | tf_op jit(solution)/shard_map/ppermute | solution.py:527
  123.5 10.0 %collective-permute-start.18 = (bf16[384,384]{1,0:T(8,128)(2,1)S(1)}, bf16[384,384]{1,0:T(8,128)(2,1)S(1)}, u32[]{:S(2)}, u32[]{:S(2)}) collective-permute-start(bf16[384,384]{1,0:T(8,128)(2,1)S(1)} %get-tuple-element.44), channel_id=1, source_target_pairs={{0,1},{1,0},{2,3},{3,2},{4,5},{5,4},{6,7},{7,6},{8,9},{9,8},{10,11... | collective-permute-start | bytes 884744 | tf_op jit(solution)/shard_map/ppermute | solution.py:531
  124.2 13.4 %collective-permute-start.13 = (bf16[384,384]{1,0:T(8,128)(2,1)S(1)}, bf16[384,384]{1,0:T(8,128)(2,1)S(1)}, u32[]{:S(2)}, u32[]{:S(2)}) collective-permute-start(bf16[384,384]{1,0:T(8,128)(2,1)S(1)} %get-tuple-element.38), channel_id=1, source_target_pairs={{0,2},{1,3},{2,4},{3,5},{4,6},{5,7},{6,0},{7,1},{8,10},{9,11},{10,... | collective-permute-start | bytes 884744 | tf_op jit(solution)/shard_map/ppermute | solution.py:527
  125.9 18.1 %collective-permute-start.14 = (bf16[384,384]{1,0:T(8,128)(2,1)S(1)}, bf16[384,384]{1,0:T(8,128)(2,1)S(1)}, u32[]{:S(2)}, u32[]{:S(2)}) collective-permute-start(bf16[384,384]{1,0:T(8,128)(2,1)S(1)} %get-tuple-element.39), channel_id=1, source_target_pairs={{0,6},{1,7},{2,0},{3,1},{4,2},{5,3},{6,4},{7,5},{8,14},{9,15},{10,... | collective-permute-start | bytes 884744 | tf_op jit(solution)/shard_map/ppermute | solution.py:527
  133.1 10.9 %collective-permute-start.17 = (bf16[384,384]{1,0:T(8,128)(2,1)S(1)}, bf16[384,384]{1,0:T(8,128)(2,1)S(1)}, u32[]{:S(2)}, u32[]{:S(2)}) collective-permute-start(bf16[384,384]{1,0:T(8,128)(2,1)S(1)} %add_convert_fusion.2), channel_id=1, source_target_pairs={{0,1},{1,0},{2,3},{3,2},{4,5},{5,4},{6,7},{7,6},{8,9},{9,8},{10,11... | collective-permute-start | bytes 884744 | tf_op jit(solution)/shard_map/ppermute | solution.py:531
  133.5 10.4 %collective-permute-start.19 = (bf16[384,384]{1,0:T(8,128)(2,1)S(1)}, bf16[384,384]{1,0:T(8,128)(2,1)S(1)}, u32[]{:S(2)}, u32[]{:S(2)}) collective-permute-start(bf16[384,384]{1,0:T(8,128)(2,1)S(1)} %add_convert_fusion.1), channel_id=1, source_target_pairs={{0,4},{1,5},{2,6},{3,7},{4,0},{5,1},{6,2},{7,3},{8,12},{9,13},{10,... | collective-permute-start | bytes 884744 | tf_op jit(solution)/shard_map/ppermute | solution.py:527

commit v2 on v1

--- a/solution.py
+++ b/solution.py
@@ -119,7 +119,7 @@
 def project_kernel(place_ref, *refs):
     blocks = refs[:HEAD_AXIS]
     (
-        w_hbm, gain_ref, cos_ref, sin_ref, out_ref, last_ref, mod_ref, acc_ref, w_ref, sems,
+        w_hbm, gain_ref, cos_ref, sin_ref, kv_ref, q_ref, last_ref, mod_ref, acc_ref, w_ref, sems,
     ) = refs[HEAD_AXIS:]
     copies = [
         pltpu.make_async_copy(w_hbm.at[n], w_ref.at[:, pl.ds(n * DSH, DSH)], sems.at[n])
@@ -177,20 +177,21 @@
                 result = turned(part, p)
             if part == 0 and p == LAST:
                 for n in range(RING):
-                    out_ref[n, 3 * TOK : 4 * TOK, :] = result
+                    q_ref[n, TOK : 2 * TOK, :] = result
             elif part == 0:
-                out_ref[p, 2 * TOK : 3 * TOK, :] = result
+                q_ref[p, 0:TOK, :] = result
             elif p == LAST:
                 last_ref[(part - 1) * TOK : part * TOK, :] = result
             else:
-                out_ref[p, (part - 1) * TOK : part * TOK, :] = result
+                kv_ref[p, (part - 1) * TOK : part * TOK, :] = result
 
 
 def project(places, blocks, w, gains, cosine, sine):
     return pl.pallas_call(
         project_kernel,
         out_shape=(
-            jax.ShapeDtypeStruct((RING, 4 * TOK, HD), jnp.bfloat16),
+            jax.ShapeDtypeStruct((RING, 2 * TOK, HD), jnp.bfloat16),
+            jax.ShapeDtypeStruct((RING, 2 * TOK, HD), jnp.bfloat16),
             jax.ShapeDtypeStruct((2 * TOK, HD), jnp.bfloat16),
         ),
         grid_spec=pltpu.PrefetchScalarGridSpec(
@@ -203,7 +204,11 @@
                 whole((TOK, HD)),
                 whole((TOK, HD)),
             ],
-            out_specs=(whole((RING, 4 * TOK, HD)), whole((2 * TOK, HD))),
+            out_specs=(
+                whole((RING, 2 * TOK, HD)),
+                whole((RING, 2 * TOK, HD)),
+                whole((2 * TOK, HD)),
+            ),
             scratch_shapes=[
                 pltpu.VMEM((ROWS, HEAD_AXIS * DSH), jnp.bfloat16),
                 pltpu.VMEM((ROWS, WIDE), jnp.float32),
@@ -222,34 +227,58 @@
 QUAD = 4
 TILE = QUAD * TOK
 SET = RING * TOK
+KEYS = QUAD * SET + TXT
+CHUNK = 1024
 DIMS = (((1,), (1,)), ((), ()))
 
 
-def score_keys(q, keys, score_ref, column, top):
-    scores = lax.dot_general(q, keys, DIMS, preferred_element_type=jnp.float32)
-    score_ref[:, column : column + scores.shape[1]] = scores
-    for lane in range(0, scores.shape[1], 128):
-        top = jnp.maximum(top, scores[:, lane : lane + 128])
-    return top
-
-
-def score_text(q, keys, valid, score_ref, column, top):
-    scores = lax.dot_general(q, keys, DIMS, preferred_element_type=jnp.float32)
-    index = lax.broadcasted_iota(jnp.int32, scores.shape, 1)
-    scores = jnp.where(index < valid, scores, -jnp.inf)
-    score_ref[:, column : column + scores.shape[1]] = scores
-    for lane in range(0, scores.shape[1], 128):
-        top = jnp.maximum(top, scores[:, lane : lane + 128])
-    return top
-
-
-def mix(score_ref, value_ref, top, count):
-    mixed = jnp.zeros((TILE, 2 * HD), jnp.float32)
-    for first in range(0, count, SET):
-        stop = min(first + SET, count)
-        weights = jnp.exp2(score_ref[:, first:stop] * EXP_SCALE - top).astype(jnp.bfloat16)
-        mixed += jnp.dot(weights, value_ref[first:stop, :], preferred_element_type=jnp.float32)
-    return mixed
+def attend_rows(flag_ref, q, keys_ref, value_ref, valid, score_ref, top_ref, mixed_ref):
+    count = keys_ref.shape[0]
+    text = TXT if count == KEYS else TXT // 2
+
+    def scores_of(first, stop):
+        scores = lax.dot_general(
+            q, keys_ref[first:stop, :], DIMS, preferred_element_type=jnp.float32
+        )
+        if first == count - text:
+            index = lax.broadcasted_iota(jnp.int32, scores.shape, 1)
+            scores = jnp.where(index < valid, scores, -jnp.inf)
+        return scores
+
+    cuts = list(range(0, count - text, CHUNK)) + [count - text, count]
+    pieces = list(zip(cuts[:-1], cuts[1:]))
+
+    @pl.when(flag_ref[0] == 1)
+    def _():
+        mixed = jnp.zeros((TILE, 2 * HD), jnp.float32)
+        for first, stop in pieces:
+            weights = jnp.exp2(scores_of(first, stop) * EXP_SCALE).astype(jnp.bfloat16)
+            mixed += jnp.dot(weights, value_ref[first:stop, :], preferred_element_type=jnp.float32)
+        mixed_ref[...] = mixed
+        top_ref[...] = jnp.zeros((TILE, 128), jnp.float32)
+
+    @pl.when(flag_ref[0] != 1)
+    def _():
+        top = jnp.full((TILE, 128), -jnp.inf, jnp.float32)
+        for first, stop in pieces:
+            scores = scores_of(first, stop)
+            score_ref[:, first:stop] = scores
+            for lane in range(0, stop - first, 128):
+                top = jnp.maximum(top, scores[:, lane : lane + 128])
+        top = jnp.max(top, axis=1, keepdims=True) * EXP_SCALE
+        top_ref[...] = jnp.broadcast_to(top, (TILE, 128))
+        mixed_ref[...] = jnp.zeros((TILE, 2 * HD), jnp.float32)
+        width = 128
+
+        def step(n, carry):
+            here = pl.ds(pl.multiple_of(n * width, width), width)
+            weights = jnp.exp2(score_ref[:, here] * EXP_SCALE - top).astype(jnp.bfloat16)
+            mixed_ref[...] += jnp.dot(
+                weights, value_ref[here, :], preferred_element_type=jnp.float32
+            )
+            return carry
+
+        lax.fori_loop(0, count // width, step, 0)
 
 
 def lay_values(value_ref, pieces):
@@ -261,85 +290,77 @@
         row += piece.shape[0]
 
 
-def set_keys(ref):
-    return ref[:, 0:TOK, :].reshape(SET, HD)
-
-
-def set_values(ref):
-    return ref[:, TOK : 2 * TOK, :].reshape(SET, HD)
-
-
-def first_step():
-    return pl.program_id(0) == 0
-
-
-def tile_rows():
-    return pl.ds(pl.multiple_of(pl.program_id(0) * TILE, TILE), TILE)
-
-
 IN_VMEM = pl.BlockSpec(memory_space=pltpu.VMEM)
 
 
-def attend_near_kernel(
-    where_ref, q_ref, own_ref, core_ref, text_ref, w_hbm,
-    mixed_ref, top_ref, w_ref, score_ref, value_ref, sem,
-):
+def in_vmem(x):
+    return pltpu.with_memory_space_constraint(x, pltpu.VMEM)
+
+
+def in_hbm(x):
+    return pltpu.with_memory_space_constraint(x, pltpu.HBM)
+
+
+def lay_kernel(where_ref, *refs):
+    set_refs = refs[:QUAD]
+    text_ref, last_text_ref, gain_ref, w_hbm, keys_ref, value_ref, w_ref, flag_ref, sem = refs[QUAD:]
     copy = pltpu.make_async_copy(w_hbm, w_ref, sem)
-
-    @pl.when(first_step())
-    def _():
-        copy.start()
-        lay_values(value_ref, [set_values(own_ref), set_values(core_ref), text_ref[1, 0]])
-
-    q = q_ref[...].reshape(TILE, HD)
-    top = jnp.full((TILE, 128), -jnp.inf, jnp.float32)
-    for n, ref in enumerate((own_ref, core_ref)):
-        top = score_keys(q, set_keys(ref), score_ref, n * SET, top)
-    top = score_text(q, text_ref[0, 0], where_ref[2], score_ref, 2 * SET, top)
-    top = jnp.max(top, axis=1, keepdims=True) * EXP_SCALE
-    here = tile_rows()
-    mixed_ref[here, :] = mix(score_ref, value_ref, top, 2 * SET + TXT)
-    top_ref[here, :] = jnp.broadcast_to(top, (TILE, 128))
-
-    @pl.when(pl.program_id(0) == SET // TILE - 1)
-    def _():
-        copy.wait()
-
-
-def attend_near(where, received, own, core, text_kv, w_out):
+    copy.start()
+    for n, ref in enumerate(set_refs):
+        keys_ref[n * SET : (n + 1) * SET, :] = ref[:, 0:TOK, :].reshape(SET, HD)
+    keys_ref[QUAD * SET :, :] = text_ref[0, 0]
+    lay_values(
+        value_ref,
+        [ref[:, TOK : 2 * TOK, :].reshape(SET, HD) for ref in set_refs] + [text_ref[1, 0]],
+    )
+    slack = 1.03 * HD
+    gains = gain_ref[...] * gain_ref[...]
+    query_norm = slack * jnp.max(gains[0:1])
+    key_norm = slack * jnp.max(gains[1:2])
+    for ref in (text_ref, last_text_ref):
+        text = ref[0, 0].astype(jnp.float32)
+        key_norm = jnp.maximum(key_norm, jnp.max(jnp.sum(text * text, axis=1)))
+    bound = EXP_SCALE * EXP_SCALE * query_norm * key_norm
+    flag_ref[0] = jnp.where(bound < MOST_LOG2 * MOST_LOG2, 1, 0)
+    copy.wait()
+
+
+MOST_LOG2 = 90.0
+
+
+def lay(where, sets, text_kv, gains, w_out):
     return pl.pallas_call(
-        attend_near_kernel,
+        lay_kernel,
         out_shape=(
-            pltpu.VMEM((SET, 2 * HD), jnp.float32),
-            pltpu.VMEM((SET, 128), jnp.float32),
+            pltpu.VMEM((KEYS, HD), jnp.bfloat16),
+            pltpu.VMEM((KEYS, 2 * HD), jnp.bfloat16),
             pltpu.VMEM(w_out.shape, w_out.dtype),
+            jax.ShapeDtypeStruct((1,), jnp.int32),
         ),
         grid_spec=pltpu.PrefetchScalarGridSpec(
             num_scalar_prefetch=1,
-            grid=(SET // TILE,),
-            in_specs=[
-                pl.BlockSpec((QUAD, TOK, HD), lambda i, w: (i, 2, 0)),
-                whole((RING, 2 * TOK, HD)),
-                whole((RING, 2 * TOK, HD)),
+            grid=(1,),
+            in_specs=[whole((RING, 2 * TOK, HD)) for _ in sets]
+            + [
                 pl.BlockSpec((2, 1, TXT, HD), lambda i, w: (0, w[0], 0, w[1])),
+                pl.BlockSpec(
+                    (1, 1, TXT, HD), lambda i, w: (0, BRANCH - 1, 0, HEADS_HERE - 1)
+                ),
+                whole((2, HD)),
                 pl.BlockSpec(memory_space=pltpu.HBM),
             ],
-            out_specs=(IN_VMEM, IN_VMEM, IN_VMEM),
-            scratch_shapes=[
-                pltpu.VMEM((TILE, 2 * SET + TXT), jnp.float32),
-                pltpu.VMEM((2 * SET + TXT, 2 * HD), jnp.bfloat16),
-                pltpu.SemaphoreType.DMA(()),
-            ],
-        ),
-        compiler_params=pltpu.CompilerParams(vmem_limit_bytes=18 * MIB),
+            out_specs=(IN_VMEM, IN_VMEM, IN_VMEM, pl.BlockSpec(memory_space=pltpu.SMEM)),
+            scratch_shapes=[pltpu.SemaphoreType.DMA(())],
+        ),
+        compiler_params=pltpu.CompilerParams(vmem_limit_bytes=16 * MIB),
         cost_estimate=pl.CostEstimate(
-            flops=4 * SET * 2304 * HD, bytes_accessed=3_000_000, transcendentals=SET * 2304
-        ),
-        name="attend_near",
-    )(where, received, own, core, text_kv, w_out)
-
-
-LAST_KEYS = QUAD * TOK + 128
+            flops=5_000_000_000, bytes_accessed=10_000_000, transcendentals=0
+        ),
+        name="lay",
+    )(where, *sets, text_kv, text_kv, gains, in_hbm(w_out))
+
+
+LAST_KEYS = QUAD * TOK + TXT // 2
 
 
 def lay_last_kernel(where_ref, *refs):
@@ -355,8 +376,8 @@
     return pl.pallas_call(
         lay_last_kernel,
         out_shape=(
-            jax.ShapeDtypeStruct((LAST_KEYS, HD), jnp.bfloat16),
-            jax.ShapeDtypeStruct((LAST_KEYS, 2 * HD), jnp.bfloat16),
+            pltpu.VMEM((LAST_KEYS, HD), jnp.bfloat16),
+            pltpu.VMEM((LAST_KEYS, 2 * HD), jnp.bfloat16),
         ),
         grid_spec=pltpu.PrefetchScalarGridSpec(
             num_scalar_prefetch=1,
@@ -364,10 +385,10 @@
             in_specs=[whole((2 * TOK, HD)) for _ in lasts]
             + [
                 pl.BlockSpec(
-                    (2, 1, 128, HD), lambda i, w: (0, BRANCH - 1, w[4], HEADS_HERE - 1)
+                    (2, 1, TXT // 2, HD), lambda i, w: (0, BRANCH - 1, w[4], HEADS_HERE - 1)
                 )
             ],
-            out_specs=(whole((LAST_KEYS, HD)), whole((LAST_KEYS, 2 * HD))),
+            out_specs=(IN_VMEM, IN_VMEM),
         ),
         compiler_params=pltpu.CompilerParams(vmem_limit_bytes=16 * MIB),
         cost_estimate=pl.CostEstimate(
@@ -377,99 +398,52 @@
     )(where, *lasts, text_kv)
 
 
-def attend_last_kernel(where_ref, q_ref, keys_ref, value_ref, out_ref, score_ref):
-    video_keys = QUAD * TOK
-    q = q_ref[...].reshape(TILE, HD)
-    top = jnp.full((TILE, 128), -jnp.inf, jnp.float32)
-    top = score_keys(q, keys_ref[0:video_keys, :], score_ref, 0, top)
-    top = score_text(q, keys_ref[video_keys:, :], where_ref[3], score_ref, video_keys, top)
-    top = jnp.max(top, axis=1, keepdims=True) * EXP_SCALE
-    mixed = mix(score_ref, value_ref, top, LAST_KEYS)
-    total = mixed[:, HD : HD + 1]
-    result = mixed[:, :HD] / total
+def attend_kernel(
+    where_ref, flag_ref, q_ref, keys_ref, value_ref, last_keys_ref, last_value_ref,
+    out_ref, score_ref, top_ref, mixed_ref,
+):
+    q = q_ref[:, 0:TOK, :].reshape(TILE, HD)
+    attend_rows(
+        flag_ref, q, keys_ref, value_ref, where_ref[2], score_ref, top_ref, mixed_ref
+    )
+    result = mixed_ref[:, :HD] / mixed_ref[:, HD : HD + 1]
     out_ref[:, 0:TOK, :] = result.astype(jnp.bfloat16).reshape(QUAD, TOK, HD)
-    level = jnp.broadcast_to(top + jnp.log(total) * LOG2E, (TILE, HD))
+    q = q_ref[:, TOK : 2 * TOK, :].reshape(TILE, HD)
+    attend_rows(
+        flag_ref, q, last_keys_ref, last_value_ref, where_ref[3], score_ref, top_ref, mixed_ref
+    )
+    total = mixed_ref[:, HD : HD + 1]
+    result = mixed_ref[:, :HD] / total
+    out_ref[:, TOK : 2 * TOK, :] = result.astype(jnp.bfloat16).reshape(QUAD, TOK, HD)
+    level = top_ref[...] + jnp.log(total) * LOG2E
     for f in range(QUAD):
         row = jnp.transpose(level[f * TOK : (f + 1) * TOK])[0:1]
         stats = limbs_of(row) + [jnp.zeros((STAT_ROWS - 3, HD), jnp.float32)]
-        out_ref[f, TOK:LAST_ROWS, :] = jnp.concatenate(stats, axis=0).astype(jnp.bfloat16)
-
-
-def attend_last(where, received, keys, values):
+        out_ref[f, 2 * TOK : RETURN, :] = jnp.concatenate(stats, axis=0).astype(jnp.bfloat16)
+
+
+def attend(where, flag, queries, keys, values, last_keys, last_values):
     return pl.pallas_call(
-        attend_last_kernel,
-        out_shape=jax.ShapeDtypeStruct((RING, LAST_ROWS, HD), jnp.bfloat16),
+        attend_kernel,
+        out_shape=jax.ShapeDtypeStruct((RING, RETURN, HD), jnp.bfloat16),
         grid_spec=pltpu.PrefetchScalarGridSpec(
-            num_scalar_prefetch=1,
+            num_scalar_prefetch=2,
             grid=(SET // TILE,),
-            in_specs=[
-                pl.BlockSpec((QUAD, TOK, HD), lambda i, w: (i, 3, 0)),
-                whole((LAST_KEYS, HD)),
-                whole((LAST_KEYS, 2 * HD)),
+            in_specs=[pl.BlockSpec((QUAD, 2 * TOK, HD), lambda i, w, f: (i, 0, 0))]
+            + [IN_VMEM] * 4,
+            out_specs=pl.BlockSpec((QUAD, RETURN, HD), lambda i, w, f: (i, 0, 0)),
+            scratch_shapes=[
+                pltpu.VMEM((TILE, KEYS), jnp.float32),
+                pltpu.VMEM((TILE, 128), jnp.float32),
+                pltpu.VMEM((TILE, 2 * HD), jnp.float32),
             ],
-            out_specs=pl.BlockSpec((QUAD, LAST_ROWS, HD), lambda i, w: (i, 0, 0)),
-            scratch_shapes=[pltpu.VMEM((TILE, LAST_KEYS), jnp.float32)],
-        ),
-        compiler_params=pltpu.CompilerParams(vmem_limit_bytes=16 * MIB),
+        ),
+        compiler_params=pltpu.CompilerParams(vmem_limit_bytes=24 * MIB),
         cost_estimate=pl.CostEstimate(
-            flops=4 * SET * 640 * HD, bytes_accessed=1_000_000, transcendentals=SET * 640
-        ),
-        name="attend_last",
-    )(where, received, keys, values)
-
-
-def attend_far_kernel(
-    q_ref, y_ref, diagonal_ref, last_ref, mixed_ref, top_ref, out_ref, score_ref, value_ref
-):
-    @pl.when(first_step())
-    def _():
-        lay_values(value_ref, [set_values(y_ref), set_values(diagonal_ref)])
-
-    q = q_ref[...].reshape(TILE, HD)
-    top = jnp.full((TILE, 128), -jnp.inf, jnp.float32)
-    for n, ref in enumerate((y_ref, diagonal_ref)):
-        top = score_keys(q, set_keys(ref), score_ref, n * SET, top)
-    here = tile_rows()
-    before = top_ref[here, 0:1]
-    top = jnp.maximum(jnp.max(top, axis=1, keepdims=True) * EXP_SCALE, before)
-    mixed = mix(score_ref, value_ref, top, 2 * SET) + mixed_ref[here, :] * jnp.exp2(before - top)
-    result = mixed[:, :HD] / mixed[:, HD : HD + 1]
-    out_ref[:, 0:TOK, :] = result.astype(jnp.bfloat16).reshape(QUAD, TOK, HD)
-    out_ref[:, TOK:RETURN, :] = last_ref[...]
-
-
-def in_vmem(x):
-    return pltpu.with_memory_space_constraint(x, pltpu.VMEM)
-
-
-def in_hbm(x):
-    return pltpu.with_memory_space_constraint(x, pltpu.HBM)
-
-
-def attend_far(received, over_y, diagonal, last, mixed, top):
-    return pl.pallas_call(
-        attend_far_kernel,
-        out_shape=jax.ShapeDtypeStruct((RING, RETURN, HD), jnp.bfloat16),
-        grid=(SET // TILE,),
-        in_specs=[
-            pl.BlockSpec((QUAD, TOK, HD), lambda i: (i, 2, 0)),
-            whole((RING, 2 * TOK, HD)),
-            whole((RING, 2 * TOK, HD)),
-            pl.BlockSpec((QUAD, LAST_ROWS, HD), lambda i: (i, 0, 0)),
-            IN_VMEM,
-            IN_VMEM,
-        ],
-        out_specs=pl.BlockSpec((QUAD, RETURN, HD), lambda i: (i, 0, 0)),
-        scratch_shapes=[
-            pltpu.VMEM((TILE, 2 * SET), jnp.float32),
-            pltpu.VMEM((2 * SET, 2 * HD), jnp.bfloat16),
-        ],
-        compiler_params=pltpu.CompilerParams(vmem_limit_bytes=18 * MIB),
-        cost_estimate=pl.CostEstimate(
-            flops=4 * SET * 2048 * HD, bytes_accessed=4_000_000, transcendentals=SET * 2048
-        ),
-        name="attend_far",
-    )(received, over_y, diagonal, last, in_vmem(mixed), in_vmem(top))
+            flops=4 * SET * 4992 * HD, bytes_accessed=4_000_000, transcendentals=SET * 4992
+        ),
+        name="attend",
+    )(where, flag, queries, *(in_vmem(x) for x in (keys, values, last_keys, last_values)))
 
 
 def output_kernel(place_ref, back_ref, w_ref, *refs):
@@ -586,24 +560,22 @@
     cosine, sine = rope_tables(frame)
     blocks = gather_head(own)
     weights = in_hbm(w_qkv.transpose(1, 0, 2))
-    send, last = project(places, blocks, weights, in_hbm(norm_gains), cosine, sine)
+    gains = in_hbm(norm_gains)
+    send_keys, send_queries, last = project(places, blocks, weights, gains, cosine, sine)
     rings = [[(y * RING + z) * 2 + core for z in range(RING)] for y in range(2) for core in range(2)]
 
     def over_rings(x):
         return lax.all_to_all(x, "frame", 0, 0, axis_index_groups=rings, tiled=True)
 
-    received = over_rings(send)
-    flips = (1, FRAMES // 2, FRAMES // 2 + 1)
-    lasts = [last] + [frame_move(last, flip) for flip in flips]
+    near = over_rings(send_keys)
+    lasts = [last] + [frame_move(last, flip) for flip in (1, FRAMES // 2, FRAMES // 2 + 1)]
     last_keys, last_values = lay_last(where, lasts, text_kv)
-    near = received[:, : 2 * TOK]
+    send_queries, near = lax.optimization_barrier((send_queries, near))
     over_y = frame_move(near, FRAMES // 2)
-    over_core = frame_move(near, 1)
-    ninth = attend_last(where, received, last_keys, last_values)
-    mixed, top, w_held = attend_near(where, received, near, over_core, text_kv, in_hbm(w_out))
-    over_y, _, _ = lax.optimization_barrier((over_y, mixed, ninth))
-    diagonal = frame_move(over_y, 1)
-    returned = attend_far(received, over_y, diagonal, ninth, mixed, top)
+    sets = [near, over_y, frame_move(near, 1), frame_move(over_y, 1)]
+    queries = over_rings(send_queries)
+    keys, values, w_held, flag = lay(where, sets, text_kv, gains, w_out)
+    returned = attend(where, flag, queries, keys, values, last_keys, last_values)
     partial = output(places, over_rings(returned), w_held)
     proj = scatter_head(partial).reshape(video.shape)
     return (video.astype(jnp.float32) + gate * proj).astype(jnp.bfloat16)

time: 146 us -> 165 us (1.13)
  blocking collectives: 21.2 us -> 47 us
  waiting for transfers between devices: 58.3 us -> 33.6 us
  Pallas kernels: 30.5 us -> 41 us
  local copies, waits for them, and re-layouts: 0.04 us -> 6.81 us
    all_to_all x1, waiting for transfers between devices: 26.8 us -> 0.79 us  [over_rings(): return lax.all_to_all(x, 'frame', 0, 0, axis_index_groups=rings, tiled=True)]
    all_to_all x1 -> x2, blocking collectives: 21.2 us -> 47 us  [over_rings(): return lax.all_to_all(x, 'frame', 0, 0, axis_index_groups=rings, tiled=True)]
    pallas_call x5 -> x4, Pallas kernels: 25.9 us -> 36.3 us  [the longest x1 23.3 us: attend(): pl.pallas_call(attend_kernel, out_shape=jax.ShapeDtypeStruct((RING, RETUR...]
    unnamed x2 -> x18, local copies, waits for them, and re-layouts: 0.01 us -> 6.81 us
    all_to_all x1, starting transfers between devices: 8.48 us -> 3.49 us  [over_rings(): return lax.all_to_all(x, 'frame', 0, 0, axis_index_groups=rings, tiled=True)]
    ppermute x10, waiting for transfers between devices: 25.1 us -> 20.2 us  [head_move(): lax.ppermute(x, 'head', [(i, (i + step) % HEAD_AXIS) for i in range(HEAD_...]
    ppermute x6, waiting for transfers between devices: 3.73 us -> 8 us  [frame_move(): return lax.ppermute(x, 'frame', [(i, i ^ flip) for i in range(FRAMES)])]
    ppermute x4, starting transfers between devices: 6.4 us -> 9 us  [head_partner(): return lax.ppermute(x, 'head', [(i, i ^ 1) for i in range(HEAD_AXIS)])]
  transfers between devices with their start and end apart: 21 -> 21, of which waited for: 11 -> 10; matrix products, arithmetic and copies ran while one was open for 1% -> 1% of each run, Pallas kernels for 8% -> 3%
where the time goes in v2:
time: 165 us; the launch traced here: 163 us
  blocking collectives  47 us (28%)
  Pallas kernels  41 us (25%)
  waiting for transfers between devices  33.6 us (20%)
  starting transfers between devices  31.2 us (19%)
  local copies, waits for them, and re-layouts  6.81 us (4%)
  other arithmetic  2.23 us (1%)
    all_to_all x2, blocking collectives, over_rings(): return lax.all_to_all(x, 'frame', 0, 0, axis_index_groups=rings, tiled=True)  47 us
    pallas_call x1, Pallas kernels, attend(): pl.pallas_call(attend_kernel, out_shape=jax.ShapeDtypeStruct((RING, RETUR...  23.3 us
    ppermute x10, waiting for transfers between devices, head_move(): lax.ppermute(x, 'head', [(i, (i + step) % HEAD_AXIS) for i in range(HEAD_...  20.2 us
    ppermute x10, starting transfers between devices, head_move(): lax.ppermute(x, 'head', [(i, (i + step) % HEAD_AXIS) for i in range(HEAD_...  15.8 us
    ppermute x4, starting transfers between devices, head_partner(): return lax.ppermute(x, 'head', [(i, i ^ 1) for i in range(HEAD_AXIS)])  9 us
    ppermute x6, waiting for transfers between devices, frame_move(): return lax.ppermute(x, 'frame', [(i, i ^ flip) for i in range(FRAMES)])  8 us
    pallas_call x1, Pallas kernels, project(): pl.pallas_call(project_kernel, out_shape=(jax.ShapeDtypeStruct((RING, 2 *...  7.92 us
    unnamed x18, local copies, waits for them, and re-layouts  6.81 us
  transfers between devices with their start and end apart: 21, of which 10 were waited for; matrix products, arithmetic and copies ran while one was open for 1% of the time, Pallas kernels for 3%

profile of v2, /device:TPU:6, one launch (start us, length us, event | category | flops | bytes accessed | tf_op | source)
XLA Modules:
  0.0 162.5 jit_solution(11604481696012637487)
XLA Ops:
  0.7 2.3 %prep.1 = (bf16[400,384]{1,0:T(8,128)(2,1)S(1)}, f32[1,384]{1,0:T(1,128)S(1)}, s32[8]{0:T(128)S(1)}, s32[5]{0:T(128)S(1)}) custom-call(s32[1]{0:T(128)} %bitcast.frame_ref, s32[1]{0:T(128)} %bitcast.1.head_ref, s32[1]{0:T(128)S(6)} %copy.13.shift_ref, s32[32]{0:T(128)} %ids_ref.1, s32[3]{0:T(128)} %lengths_ref.1, bf16[3,128,384]{2,1,0:T(8,128)(2,1)} %video_ref.1, ...), custom_call_target="tpu_custom_call" | custom-call | tf_op jit(solution)/shard_map/prep/pallas_call | solution.py:95
  3.0 3.3 %collective-permute-start = (bf16[400,384]{1,0:T(8,128)(2,1)S(1)}, bf16[400,384]{1,0:T(8,128)(2,1)S(1)}, u32[]{:S(2)}, u32[]{:S(2)}) collective-permute-start(bf16[400,384]{1,0:T(8,128)(2,1)S(1)} %get-tuple-element.31.refs_0_), channel_id=1, source_target_pairs={{0,1},{1,0},{2,3},{3,2},{4,5},{5,4},{6,7},{7,6},{8,9},{9,8},{10,11... | collective-permute-start | bytes 921608 | tf_op jit(solution)/shard_map/ppermute | solution.py:505
  6.3 1.4 collective-permute-start.5
  7.7 3.2 %collective-permute-start.2 = (bf16[400,384]{1,0:T(8,128)(2,1)S(1)}, bf16[400,384]{1,0:T(8,128)(2,1)S(1)}, u32[]{:S(2)}, u32[]{:S(2)}) collective-permute-start(bf16[400,384]{1,0:T(8,128)(2,1)S(1)} %get-tuple-element.31.refs_0_), channel_id=1, source_target_pairs={{0,2},{1,3},{2,4},{3,5},{4,6},{5,7},{6,0},{7,1},{8,10},{9,11},{10,... | collective-permute-start | bytes 921608 | tf_op jit(solution)/shard_map/ppermute | solution.py:501
  10.9 2.7 %collective-permute-done.refs_1_ = bf16[400,384]{1,0:T(8,128)(2,1)S(1)} collective-permute-done((bf16[400,384]{1,0:T(8,128)(2,1)S(1)}, bf16[400,384]{1,0:T(8,128)(2,1)S(1)}, u32[]{:S(2)}, u32[]{:S(2)}) %collective-permute-start) | collective-permute-done | bytes 307232 | tf_op jit(solution)/shard_map/ppermute | solution.py:505
  14.4 2.4 %collective-permute-start.4 = (bf16[400,384]{1,0:T(8,128)(2,1)S(1)}, bf16[400,384]{1,0:T(8,128)(2,1)S(1)}, u32[]{:S(2)}, u32[]{:S(2)}) collective-permute-start(bf16[400,384]{1,0:T(8,128)(2,1)S(1)} %collective-permute-done.refs_1_), channel_id=1, source_target_pairs={{0,2},{1,3},{2,4},{3,5},{4,6},{5,7},{6,0},{7,1},{8,10},{9,11},{10,... | collective-permute-start | bytes 921608 | tf_op jit(solution)/shard_map/ppermute | solution.py:501
  16.8 1.2 collective-permute-done.5.refs_6_
  18.0 2.0 %collective-permute-start.6 = (bf16[400,384]{1,0:T(8,128)(2,1)S(1)}, bf16[400,384]{1,0:T(8,128)(2,1)S(1)}, u32[]{:S(2)}, u32[]{:S(2)}) collective-permute-start(bf16[400,384]{1,0:T(8,128)(2,1)S(1)} %collective-permute-done.5.refs_6_), channel_id=1, source_target_pairs={{0,1},{1,0},{2,3},{3,2},{4,5},{5,4},{6,7},{7,6},{8,9},{9,8},{10,11... | collective-permute-start | bytes 921608 | tf_op jit(solution)/shard_map/ppermute | solution.py:505
  20.0 1.0 sine_multiply_fusion
  21.1 2.1 %collective-permute-done.1.refs_2_ = bf16[400,384]{1,0:T(8,128)(2,1)S(1)} collective-permute-done((bf16[400,384]{1,0:T(8,128)(2,1)S(1)}, bf16[400,384]{1,0:T(8,128)(2,1)S(1)}, u32[]{:S(2)}, u32[]{:S(2)}) %collective-permute-start.1) | collective-permute-done | bytes 307232 | tf_op jit(solution)/shard_map/ppermute | solution.py:501
  23.2 6.5 %collective-permute-done.3.refs_4_ = bf16[400,384]{1,0:T(8,128)(2,1)S(1)} collective-permute-done((bf16[400,384]{1,0:T(8,128)(2,1)S(1)}, bf16[400,384]{1,0:T(8,128)(2,1)S(1)}, u32[]{:S(2)}, u32[]{:S(2)}) %collective-permute-start.3) | collective-permute-done | bytes 307232 | tf_op jit(solution)/shard_map/ppermute | solution.py:501
  29.7 7.9 %project.1 = (bf16[8,256,128]{2,1,0:T(8,128)(2,1)S(1)}, bf16[8,256,128]{2,1,0:T(8,128)(2,1)}, bf16[256,128]{1,0:T(8,128)(2,1)S(1)}) custom-call(s32[8]{0:T(128)S(1)} %get-tuple-element.29.place_ref, bf16[400,384]{1,0:T(8,128)(2,1)S(1)} %get-tuple-element.31.refs_0_, bf16[400,384]{1,0:T(8,128)(2,1)S(1)} %collective-permute-done.refs_1_, ...), custom_call_target="tpu_custom_call" | custom-call | flops 2717908992 | bytes 12000000 | tf_op jit(solution)/shard_map/project/pallas_call | solution.py:190
  37.6 25.9 %all_to_all.15.refs_0_ = bf16[8,256,128]{2,1,0:T(8,128)(2,1)S(1)} all-to-all(bf16[8,256,128]{2,1,0:T(8,128)(2,1)S(1)} %get-tuple-element.33), channel_id=1, replica_groups={{0,16,32,48,64,80,96,112},{8,24,40,56,72,88,104,120},{128,144,160,176,1..., dimensions={0} | all-to-all | bytes 1048576 | tf_op jit(solution)/shard_map/all_to_all | solution.py:568
  64.2 1.3 collective-permute-start.11
  66.4 3.5 %all-to-all-start.1 = ((bf16[8,256,128]{2,1,0:T(8,128)(2,1)}), bf16[8,256,128]{2,1,0:T(8,128)(2,1)S(1)}, u32[]{:S(2)}, u32[]{:S(2)}) async-start(bf16[8,256,128]{2,1,0:T(8,128)(2,1)} %get-tuple-element.36), calls=%async_computation.1 | async-start | bytes 1048576 | tf_op jit(solution)/shard_map/all_to_all | solution.py:568
  69.9 7.3 %collective-permute-done.7.refs_1_ = bf16[8,256,128]{2,1,0:T(8,128)(2,1)S(1)} collective-permute-done((bf16[8,256,128]{2,1,0:T(8,128)(2,1)S(1)}, bf16[8,256,128]{2,1,0:T(8,128)(2,1)S(1)}, u32[]{:S(2)}, u32[]{:S(2)}) %collective-permute-start.7) | collective-permute-done | bytes 524320 | tf_op jit(solution)/shard_map/ppermute | solution.py:509
  77.9 1.4 lay_last.1
  80.7 3.7 %lay.1 = (bf16[4352,128]{1,0:T(8,128)(2,1)S(1)}, bf16[4352,256]{1,0:T(8,128)(2,1)S(1)}, bf16[384,3072]{1,0:T(8,128)(2,1)S(1)}, s32[1]{0:T(128)}) custom-call(s32[5]{0:T(128)S(1)} %get-tuple-element.30.where_ref, bf16[8,256,128]{2,1,0:T(8,128)(2,1)S(1)} %all_to_all.15.refs_0_, bf16[8,256,128]{2,1,0:T(8,128)(2,1)S(1)} %collective-permute-done.7.refs_1_, ...), custom_call_target="tpu_custom_call" | custom-call | flops 5000000000 | bytes 10000000 | tf_op jit(solution)/shard_map/lay/pallas_call | solution.py:332
  84.4 1.4 copy-done
  85.8 1.4 copy-done.2
  88.0 1.6 %copy-done.3 = bf16[4352,256]{1,0:T(8,128)(2,1)S(1)} copy-done((bf16[4352,256]{1,0:T(8,128)(2,1)S(1)}, bf16[4352,256]{1,0:T(8,128)(2,1)}, u32[]{:S(2)}) %copy-start.3) | copy-done | bytes 2228248
  90.6 23.3 %attend.1 = bf16[8,272,128]{2,1,0:T(8,128)(2,1)S(1)} custom-call(s32[5]{0:T(128)S(1)} %get-tuple-element.30.where_ref, s32[1]{0:T(128)} %get-tuple-element.35.flag_ref, bf16[8,256,128]{2,1,0:T(8,128)(2,1)S(1)} %all-to-all-done.1.q_ref, bf16[4352,128]{1,0:T(8,128)(2,1)S(1)} %get-tuple-element.37.keys_ref, bf16[4352,256]{1,0:T(8,128)(2,1)S(1)} %copy-done.3, ...), custom_call_target="tpu_custom_call" | custom-call | flops 2617245696 | bytes 4000000 | tf_op jit(solution)/shard_map/attend/pallas_call | solution.py:426
  113.9 21.1 %all_to_all.16.back_ref = bf16[8,272,128]{2,1,0:T(8,128)(2,1)S(1)} all-to-all(bf16[8,272,128]{2,1,0:T(8,128)(2,1)S(1)} %attend.1), channel_id=1, replica_groups={{0,16,32,48,64,80,96,112},{8,24,40,56,72,88,104,120},{128,144,160,176,1..., dimensions={0} | all-to-all | bytes 1114112 | tf_op jit(solution)/shard_map/all_to_all | solution.py:568
  134.9 2.3 %output.1 = (bf16[384,384]{1,0:T(8,128)(2,1)S(1)}, bf16[384,384]{1,0:T(8,128)(2,1)S(1)}, bf16[384,384]{1,0:T(8,128)(2,1)S(1)}, bf16[384,384]{1,0:T(8,128)(2,1)S(...) custom-call(s32[8]{0:T(128)S(1)} %get-tuple-element.29.place_ref, ...), custom_call_target="tpu_custom_call" | custom-call | flops 905969664 | bytes 5000000 | tf_op jit(solution)/shard_map/output/pallas_call | solution.py:477
  137.3 1.9 %collective-permute-start.18 = (bf16[384,384]{1,0:T(8,128)(2,1)S(1)}, bf16[384,384]{1,0:T(8,128)(2,1)S(1)}, u32[]{:S(2)}, u32[]{:S(2)}) collective-permute-start(bf16[384,384]{1,0:T(8,128)(2,1)S(1)} %get-tuple-element.50), channel_id=1, source_target_pairs={{0,1},{1,0},{2,3},{3,2},{4,5},{5,4},{6,7},{7,6},{8,9},{9,8},{10,11... | collective-permute-start | bytes 884744 | tf_op jit(solution)/shard_map/ppermute | solution.py:505
  140.0 2.4 %collective-permute-start.15 = (bf16[384,384]{1,0:T(8,128)(2,1)S(1)}, bf16[384,384]{1,0:T(8,128)(2,1)S(1)}, u32[]{:S(2)}, u32[]{:S(2)}) collective-permute-start(bf16[384,384]{1,0:T(8,128)(2,1)S(1)} %get-tuple-element.47), channel_id=1, source_target_pairs={{0,2},{1,3},{2,4},{3,5},{4,6},{5,7},{6,0},{7,1},{8,10},{9,11},{10,... | collective-permute-start | bytes 884744 | tf_op jit(solution)/shard_map/ppermute | solution.py:501
  142.5 3.2 %collective-permute-start.13 = (bf16[384,384]{1,0:T(8,128)(2,1)S(1)}, bf16[384,384]{1,0:T(8,128)(2,1)S(1)}, u32[]{:S(2)}, u32[]{:S(2)}) collective-permute-start(bf16[384,384]{1,0:T(8,128)(2,1)S(1)} %get-tuple-element.44), channel_id=1, source_target_pairs={{0,2},{1,3},{2,4},{3,5},{4,6},{5,7},{6,0},{7,1},{8,10},{9,11},{10,... | collective-permute-start | bytes 884744 | tf_op jit(solution)/shard_map/ppermute | solution.py:501
  145.7 1.9 %collective-permute-done.18 = bf16[384,384]{1,0:T(8,128)(2,1)S(1)} collective-permute-done((bf16[384,384]{1,0:T(8,128)(2,1)S(1)}, bf16[384,384]{1,0:T(8,128)(2,1)S(1)}, u32[]{:S(2)}, u32[]{:S(2)}) %collective-permute-start.18) | collective-permute-done | bytes 294944 | tf_op jit(solution)/shard_map/ppermute | solution.py:505
  147.7 1.5 collective-permute-start.19
  149.2 1.2 collective-permute-done.16
  150.5 1.8 %collective-permute-start.17 = (bf16[384,384]{1,0:T(8,128)(2,1)S(1)}, bf16[384,384]{1,0:T(8,128)(2,1)S(1)}, u32[]{:S(2)}, u32[]{:S(2)}) collective-permute-start(bf16[384,384]{1,0:T(8,128)(2,1)S(1)} %add_convert_fusion.2), channel_id=1, source_target_pairs={{0,1},{1,0},{2,3},{3,2},{4,5},{5,4},{6,7},{7,6},{8,9},{9,8},{10,11... | collective-permute-start | bytes 884744 | tf_op jit(solution)/shard_map/ppermute | solution.py:505
  152.3 9.2 %collective-permute-done.14 = bf16[384,384]{1,0:T(8,128)(2,1)S(1)} collective-permute-done((bf16[384,384]{1,0:T(8,128)(2,1)S(1)}, bf16[384,384]{1,0:T(8,128)(2,1)S(1)}, u32[]{:S(2)}, u32[]{:S(2)}) %collective-permute-start.14) | collective-permute-done | bytes 294944 | tf_op jit(solution)/shard_map/ppermute | solution.py:501
  (43 shorter events, 8.2 us)
Async XLA Ops:
  3.0 10.6 %collective-permute-start = (bf16[400,384]{1,0:T(8,128)(2,1)S(1)}, bf16[400,384]{1,0:T(8,128)(2,1)S(1)}, u32[]{:S(2)}, u32[]{:S(2)}) collective-permute-start(bf16[400,384]{1,0:T(8,128)(2,1)S(1)} %get-tuple-element.31.refs_0_), channel_id=1, source_target_pairs={{0,1},{1,0},{2,3},{3,2},{4,5},{5,4},{6,7},{7,6},{8,9},{9,8},{10,11... | collective-permute-start | bytes 921608 | tf_op jit(solution)/shard_map/ppermute | solution.py:505
  6.3 11.7 %collective-permute-start.5 = (bf16[400,384]{1,0:T(8,128)(2,1)S(1)}, bf16[400,384]{1,0:T(8,128)(2,1)S(1)}, u32[]{:S(2)}, u32[]{:S(2)}) collective-permute-start(bf16[400,384]{1,0:T(8,128)(2,1)S(1)} %get-tuple-element.31.refs_0_), channel_id=1, source_target_pairs={{0,4},{1,5},{2,6},{3,7},{4,0},{5,1},{6,2},{7,3},{8,12},{9,13},{10,... | collective-permute-start | bytes 921608 | tf_op jit(solution)/shard_map/ppermute | solution.py:501
  7.7 15.5 %collective-permute-start.1 = (bf16[400,384]{1,0:T(8,128)(2,1)S(1)}, bf16[400,384]{1,0:T(8,128)(2,1)S(1)}, u32[]{:S(2)}, u32[]{:S(2)}) collective-permute-start(bf16[400,384]{1,0:T(8,128)(2,1)S(1)} %get-tuple-element.31.refs_0_), channel_id=1, source_target_pairs={{0,6},{1,7},{2,0},{3,1},{4,2},{5,3},{6,4},{7,5},{8,14},{9,15},{10,... | collective-permute-start | bytes 921608 | tf_op jit(solution)/shard_map/ppermute | solution.py:501
  7.7 15.5 %collective-permute-start.2 = (bf16[400,384]{1,0:T(8,128)(2,1)S(1)}, bf16[400,384]{1,0:T(8,128)(2,1)S(1)}, u32[]{:S(2)}, u32[]{:S(2)}) collective-permute-start(bf16[400,384]{1,0:T(8,128)(2,1)S(1)} %get-tuple-element.31.refs_0_), channel_id=1, source_target_pairs={{0,2},{1,3},{2,4},{3,5},{4,6},{5,7},{6,0},{7,1},{8,10},{9,11},{10,... | collective-permute-start | bytes 921608 | tf_op jit(solution)/shard_map/ppermute | solution.py:501
  13.6 16.1 %collective-permute-start.3 = (bf16[400,384]{1,0:T(8,128)(2,1)S(1)}, bf16[400,384]{1,0:T(8,128)(2,1)S(1)}, u32[]{:S(2)}, u32[]{:S(2)}) collective-permute-start(bf16[400,384]{1,0:T(8,128)(2,1)S(1)} %collective-permute-done.refs_1_), channel_id=1, source_target_pairs={{0,6},{1,7},{2,0},{3,1},{4,2},{5,3},{6,4},{7,5},{8,14},{9,15},{10,... | collective-permute-start | bytes 921608 | tf_op jit(solution)/shard_map/ppermute | solution.py:501
  14.4 15.3 %collective-permute-start.4 = (bf16[400,384]{1,0:T(8,128)(2,1)S(1)}, bf16[400,384]{1,0:T(8,128)(2,1)S(1)}, u32[]{:S(2)}, u32[]{:S(2)}) collective-permute-start(bf16[400,384]{1,0:T(8,128)(2,1)S(1)} %collective-permute-done.refs_1_), channel_id=1, source_target_pairs={{0,2},{1,3},{2,4},{3,5},{4,6},{5,7},{6,0},{7,1},{8,10},{9,11},{10,... | collective-permute-start | bytes 921608 | tf_op jit(solution)/shard_map/ppermute | solution.py:501
  18.0 11.7 %collective-permute-start.6 = (bf16[400,384]{1,0:T(8,128)(2,1)S(1)}, bf16[400,384]{1,0:T(8,128)(2,1)S(1)}, u32[]{:S(2)}, u32[]{:S(2)}) collective-permute-start(bf16[400,384]{1,0:T(8,128)(2,1)S(1)} %collective-permute-done.5.refs_6_), channel_id=1, source_target_pairs={{0,1},{1,0},{2,3},{3,2},{4,5},{5,4},{6,7},{7,6},{8,9},{9,8},{10,11... | collective-permute-start | bytes 921608 | tf_op jit(solution)/shard_map/ppermute | solution.py:505
  63.5 13.6 %collective-permute-start.7 = (bf16[8,256,128]{2,1,0:T(8,128)(2,1)S(1)}, bf16[8,256,128]{2,1,0:T(8,128)(2,1)S(1)}, u32[]{:S(2)}, u32[]{:S(2)}) collective-permute-start(bf16[8,256,128]{2,1,0:T(8,128)(2,1)S(1)} %all_to_all.15.refs_0_), channel_id=1, source_target_pairs={{0,128},{8,136},{16,144},{24,152},{32,160},{40,168},{48,176},{56,1... | collective-permute-start | bytes 1572872 | tf_op jit(solution)/shard_map/ppermute | solution.py:509
  64.2 13.0 %collective-permute-start.10 = (bf16[256,128]{1,0:T(8,128)(2,1)S(1)}, bf16[256,128]{1,0:T(8,128)(2,1)S(1)}, u32[]{:S(2)}, u32[]{:S(2)}) collective-permute-start(bf16[256,128]{1,0:T(8,128)(2,1)S(1)} %get-tuple-element.39.refs_0_), channel_id=1, source_target_pairs={{0,8},{8,0},{16,24},{24,16},{32,40},{40,32},{48,56},{56,48},{64,72... | collective-permute-start | bytes 196616 | tf_op jit(solution)/shard_map/ppermute | solution.py:509
  64.2 13.6 %collective-permute-start.11 = (bf16[256,128]{1,0:T(8,128)(2,1)S(1)}, bf16[256,128]{1,0:T(8,128)(2,1)S(1)}, u32[]{:S(2)}, u32[]{:S(2)}) collective-permute-start(bf16[256,128]{1,0:T(8,128)(2,1)S(1)} %get-tuple-element.39.refs_0_), channel_id=1, source_target_pairs={{0,128},{8,136},{16,144},{24,152},{32,160},{40,168},{48,176},{56,1... | collective-permute-start | bytes 196616 | tf_op jit(solution)/shard_map/ppermute | solution.py:509
  65.6 12.3 %collective-permute-start.12 = (bf16[256,128]{1,0:T(8,128)(2,1)S(1)}, bf16[256,128]{1,0:T(8,128)(2,1)S(1)}, u32[]{:S(2)}, u32[]{:S(2)}) collective-permute-start(bf16[256,128]{1,0:T(8,128)(2,1)S(1)} %get-tuple-element.39.refs_0_), channel_id=1, source_target_pairs={{0,136},{8,128},{16,152},{24,144},{32,168},{40,160},{48,184},{56,1... | collective-permute-start | bytes 196616 | tf_op jit(solution)/shard_map/ppermute | solution.py:509
  66.1 14.6 %collective-permute-start.8 = (bf16[8,256,128]{2,1,0:T(8,128)(2,1)S(1)}, bf16[8,256,128]{2,1,0:T(8,128)(2,1)S(1)}, u32[]{:S(2)}, u32[]{:S(2)}) collective-permute-start(bf16[8,256,128]{2,1,0:T(8,128)(2,1)S(1)} %all_to_all.15.refs_0_), channel_id=1, source_target_pairs={{0,8},{8,0},{16,24},{24,16},{32,40},{40,32},{48,56},{56,48},{64,72... | collective-permute-start | bytes 1572872 | tf_op jit(solution)/shard_map/ppermute | solution.py:509
  66.4 21.6 %all-to-all-start.1 = ((bf16[8,256,128]{2,1,0:T(8,128)(2,1)}), bf16[8,256,128]{2,1,0:T(8,128)(2,1)S(1)}, u32[]{:S(2)}, u32[]{:S(2)}) async-start(bf16[8,256,128]{2,1,0:T(8,128)(2,1)} %get-tuple-element.36), calls=%async_computation.1 | async-start | bytes 1048576 | tf_op jit(solution)/shard_map/all_to_all | solution.py:568
  77.2 3.6 %collective-permute-start.9 = (bf16[8,256,128]{2,1,0:T(8,128)(2,1)S(1)}, bf16[8,256,128]{2,1,0:T(8,128)(2,1)S(1)}, u32[]{:S(2)}, u32[]{:S(2)}) collective-permute-start(bf16[8,256,128]{2,1,0:T(8,128)(2,1)S(1)} %collective-permute-done.7.refs_1_), channel_id=1, source_target_pairs={{0,8},{8,0},{16,24},{24,16},{32,40},{40,32},{48,56},{56,48},{64,72... | collective-permute-start | bytes 1572872 | tf_op jit(solution)/shard_map/ppermute | solution.py:509
  79.3 0.7 copy-start.4
  80.0 0.7 copy-start.6
  80.7 7.3 %copy-start.7 = (bf16[640,128]{1,0:T(8,128)(2,1)S(1)}, bf16[640,128]{1,0:T(8,128)(2,1)}, u32[]{:S(2)}) copy-start(bf16[640,128]{1,0:T(8,128)(2,1)} %copy-done.6) | copy-start | bytes 491524
  84.4 1.4 copy-start
  85.8 1.4 copy-start.2
  88.0 1.6 %copy-start.3 = (bf16[4352,256]{1,0:T(8,128)(2,1)S(1)}, bf16[4352,256]{1,0:T(8,128)(2,1)}, u32[]{:S(2)}) copy-start(bf16[4352,256]{1,0:T(8,128)(2,1)} %copy-done.2) | copy-start | bytes 6684676
  89.6 1.0 copy-start.5
  90.6 44.4 %copy-start.1 = (bf16[384,3072]{1,0:T(8,128)(2,1)S(1)}, bf16[384,3072]{1,0:T(8,128)(2,1)}, u32[]{:S(2)}) copy-start(bf16[384,3072]{1,0:T(8,128)(2,1)} %copy-done) | copy-start | bytes 7077892
  137.3 24.4 %copy-start.8 = (bf16[3,128,384]{2,1,0:T(8,128)(2,1)S(1)}, bf16[3,128,384]{2,1,0:T(8,128)(2,1)}, u32[]{:S(2)}) copy-start(bf16[3,128,384]{2,1,0:T(8,128)(2,1)} %video_ref.1) | copy-start | bytes 884740
  137.3 10.3 %collective-permute-start.18 = (bf16[384,384]{1,0:T(8,128)(2,1)S(1)}, bf16[384,384]{1,0:T(8,128)(2,1)S(1)}, u32[]{:S(2)}, u32[]{:S(2)}) collective-permute-start(bf16[384,384]{1,0:T(8,128)(2,1)S(1)} %get-tuple-element.50), channel_id=1, source_target_pairs={{0,1},{1,0},{2,3},{3,2},{4,5},{5,4},{6,7},{7,6},{8,9},{9,8},{10,11... | collective-permute-start | bytes 884744 | tf_op jit(solution)/shard_map/ppermute | solution.py:505
  139.2 11.1 %collective-permute-start.16 = (bf16[384,384]{1,0:T(8,128)(2,1)S(1)}, bf16[384,384]{1,0:T(8,128)(2,1)S(1)}, u32[]{:S(2)}, u32[]{:S(2)}) collective-permute-start(bf16[384,384]{1,0:T(8,128)(2,1)S(1)} %get-tuple-element.48), channel_id=1, source_target_pairs={{0,6},{1,7},{2,0},{3,1},{4,2},{5,3},{6,4},{7,5},{8,14},{9,15},{10,... | collective-permute-start | bytes 884744 | tf_op jit(solution)/shard_map/ppermute | solution.py:501
  140.0 10.3 %collective-permute-start.15 = (bf16[384,384]{1,0:T(8,128)(2,1)S(1)}, bf16[384,384]{1,0:T(8,128)(2,1)S(1)}, u32[]{:S(2)}, u32[]{:S(2)}) collective-permute-start(bf16[384,384]{1,0:T(8,128)(2,1)S(1)} %get-tuple-element.47), channel_id=1, source_target_pairs={{0,2},{1,3},{2,4},{3,5},{4,6},{5,7},{6,0},{7,1},{8,10},{9,11},{10,... | collective-permute-start | bytes 884744 | tf_op jit(solution)/shard_map/ppermute | solution.py:501
  142.5 19.0 %collective-permute-start.14 = (bf16[384,384]{1,0:T(8,128)(2,1)S(1)}, bf16[384,384]{1,0:T(8,128)(2,1)S(1)}, u32[]{:S(2)}, u32[]{:S(2)}) collective-permute-start(bf16[384,384]{1,0:T(8,128)(2,1)S(1)} %get-tuple-element.45), channel_id=1, source_target_pairs={{0,6},{1,7},{2,0},{3,1},{4,2},{5,3},{6,4},{7,5},{8,14},{9,15},{10,... | collective-permute-start | bytes 884744 | tf_op jit(solution)/shard_map/ppermute | solution.py:501
  142.5 19.0 %collective-permute-start.13 = (bf16[384,384]{1,0:T(8,128)(2,1)S(1)}, bf16[384,384]{1,0:T(8,128)(2,1)S(1)}, u32[]{:S(2)}, u32[]{:S(2)}) collective-permute-start(bf16[384,384]{1,0:T(8,128)(2,1)S(1)} %get-tuple-element.44), channel_id=1, source_target_pairs={{0,2},{1,3},{2,4},{3,5},{4,6},{5,7},{6,0},{7,1},{8,10},{9,11},{10,... | collective-permute-start | bytes 884744 | tf_op jit(solution)/shard_map/ppermute | solution.py:501
  147.7 13.8 %collective-permute-start.19 = (bf16[384,384]{1,0:T(8,128)(2,1)S(1)}, bf16[384,384]{1,0:T(8,128)(2,1)S(1)}, u32[]{:S(2)}, u32[]{:S(2)}) collective-permute-start(bf16[384,384]{1,0:T(8,128)(2,1)S(1)} %add_convert_fusion.1), channel_id=1, source_target_pairs={{0,4},{1,5},{2,6},{3,7},{4,0},{5,1},{6,2},{7,3},{8,12},{9,13},{10,... | collective-permute-start | bytes 884744 | tf_op jit(solution)/shard_map/ppermute | solution.py:501
  150.5 11.0 %collective-permute-start.17 = (bf16[384,384]{1,0:T(8,128)(2,1)S(1)}, bf16[384,384]{1,0:T(8,128)(2,1)S(1)}, u32[]{:S(2)}, u32[]{:S(2)}) collective-permute-start(bf16[384,384]{1,0:T(8,128)(2,1)S(1)} %add_convert_fusion.2), channel_id=1, source_target_pairs={{0,1},{1,0},{2,3},{3,2},{4,5},{5,4},{6,7},{7,6},{8,9},{9,8},{10,11... | collective-permute-start | bytes 884744 | tf_op jit(solution)/shard_map/ppermute | solution.py:505

commit v3 on v2

--- a/solution.py
+++ b/solution.py
@@ -164,7 +164,7 @@
         t = t * gain_ref[part : part + 1, :]
         even = lax.broadcasted_iota(jnp.int32, t.shape, 1) % 2 == 0
         other = jnp.where(even, pltpu.roll(t, HD - 1, 1), pltpu.roll(t, 1, 1))
-        return (t * cos_ref[...] + other * sin_ref[...]).astype(jnp.bfloat16)
+        return t * cos_ref[...] + other * sin_ref[...]
 
     for copy in copies:
         copy.wait()
@@ -172,9 +172,12 @@
     for part in range(3):
         for p in range(PAIRS):
             if part == 2:
-                result = piece(part, p).astype(jnp.bfloat16)
+                result = piece(part, p)
             else:
                 result = turned(part, p)
+            if part == 1:
+                result = jnp.transpose(result)
+            result = result.astype(jnp.bfloat16)
             if part == 0 and p == LAST:
                 for n in range(RING):
                     q_ref[n, TOK : 2 * TOK, :] = result
@@ -216,7 +219,7 @@
                 pltpu.SemaphoreType.DMA((3,)),
             ],
         ),
-        compiler_params=pltpu.CompilerParams(vmem_limit_bytes=28 * MIB),
+        compiler_params=pltpu.CompilerParams(vmem_limit_bytes=22 * MIB),
         cost_estimate=pl.CostEstimate(
             flops=2 * ROWS * HEAD_AXIS * DSH * 3 * DSH, bytes_accessed=12_000_000, transcendentals=0
         ),
@@ -229,17 +232,14 @@
 SET = RING * TOK
 KEYS = QUAD * SET + TXT
 CHUNK = 1024
-DIMS = (((1,), (1,)), ((), ()))
 
 
 def attend_rows(flag_ref, q, keys_ref, value_ref, valid, score_ref, top_ref, mixed_ref):
-    count = keys_ref.shape[0]
+    count = keys_ref.shape[1]
     text = TXT if count == KEYS else TXT // 2
 
     def scores_of(first, stop):
-        scores = lax.dot_general(
-            q, keys_ref[first:stop, :], DIMS, preferred_element_type=jnp.float32
-        )
+        scores = jnp.dot(q, keys_ref[:, first:stop], preferred_element_type=jnp.float32)
         if first == count - text:
             index = lax.broadcasted_iota(jnp.int32, scores.shape, 1)
             scores = jnp.where(index < valid, scores, -jnp.inf)
@@ -301,14 +301,19 @@
     return pltpu.with_memory_space_constraint(x, pltpu.HBM)
 
 
+def turned_text(text_ref):
+    return jnp.transpose(text_ref[0, 0].astype(jnp.float32)).astype(jnp.bfloat16)
+
+
 def lay_kernel(where_ref, *refs):
     set_refs = refs[:QUAD]
     text_ref, last_text_ref, gain_ref, w_hbm, keys_ref, value_ref, w_ref, flag_ref, sem = refs[QUAD:]
     copy = pltpu.make_async_copy(w_hbm, w_ref, sem)
     copy.start()
     for n, ref in enumerate(set_refs):
-        keys_ref[n * SET : (n + 1) * SET, :] = ref[:, 0:TOK, :].reshape(SET, HD)
-    keys_ref[QUAD * SET :, :] = text_ref[0, 0]
+        for f in range(RING):
+            keys_ref[:, n * SET + f * TOK : n * SET + (f + 1) * TOK] = ref[f, 0:TOK, :]
+    keys_ref[:, QUAD * SET :] = turned_text(text_ref)
     lay_values(
         value_ref,
         [ref[:, TOK : 2 * TOK, :].reshape(SET, HD) for ref in set_refs] + [text_ref[1, 0]],
@@ -332,7 +337,7 @@
     return pl.pallas_call(
         lay_kernel,
         out_shape=(
-            pltpu.VMEM((KEYS, HD), jnp.bfloat16),
+            pltpu.VMEM((HD, KEYS), jnp.bfloat16),
             pltpu.VMEM((KEYS, 2 * HD), jnp.bfloat16),
             pltpu.VMEM(w_out.shape, w_out.dtype),
             jax.ShapeDtypeStruct((1,), jnp.int32),
@@ -352,7 +357,7 @@
             out_specs=(IN_VMEM, IN_VMEM, IN_VMEM, pl.BlockSpec(memory_space=pltpu.SMEM)),
             scratch_shapes=[pltpu.SemaphoreType.DMA(())],
         ),
-        compiler_params=pltpu.CompilerParams(vmem_limit_bytes=16 * MIB),
+        compiler_params=pltpu.CompilerParams(vmem_limit_bytes=8 * MIB),
         cost_estimate=pl.CostEstimate(
             flops=5_000_000_000, bytes_accessed=10_000_000, transcendentals=0
         ),
@@ -367,8 +372,8 @@
     last_refs = refs[:QUAD]
     text_ref, keys_ref, value_ref = refs[QUAD:]
     for n, ref in enumerate(last_refs):
-        keys_ref[n * TOK : (n + 1) * TOK, :] = ref[0:TOK, :]
-    keys_ref[QUAD * TOK :, :] = text_ref[0, 0]
+        keys_ref[:, n * TOK : (n + 1) * TOK] = ref[0:TOK, :]
+    keys_ref[:, QUAD * TOK :] = turned_text(text_ref)
     lay_values(value_ref, [ref[TOK : 2 * TOK, :] for ref in last_refs] + [text_ref[1, 0]])
 
 
@@ -376,7 +381,7 @@
     return pl.pallas_call(
         lay_last_kernel,
         out_shape=(
-            pltpu.VMEM((LAST_KEYS, HD), jnp.bfloat16),
+            pltpu.VMEM((HD, LAST_KEYS), jnp.bfloat16),
             pltpu.VMEM((LAST_KEYS, 2 * HD), jnp.bfloat16),
         ),
         grid_spec=pltpu.PrefetchScalarGridSpec(
@@ -390,7 +395,7 @@
             ],
             out_specs=(IN_VMEM, IN_VMEM),
         ),
-        compiler_params=pltpu.CompilerParams(vmem_limit_bytes=16 * MIB),
+        compiler_params=pltpu.CompilerParams(vmem_limit_bytes=4 * MIB),
         cost_estimate=pl.CostEstimate(
             flops=10_000_000_000, bytes_accessed=10_000_000, transcendentals=0
         ),
@@ -438,7 +443,7 @@
                 pltpu.VMEM((TILE, 2 * HD), jnp.float32),
             ],
         ),
-        compiler_params=pltpu.CompilerParams(vmem_limit_bytes=24 * MIB),
+        compiler_params=pltpu.CompilerParams(vmem_limit_bytes=18 * MIB),
         cost_estimate=pl.CostEstimate(
             flops=4 * SET * 4992 * HD, bytes_accessed=4_000_000, transcendentals=SET * 4992
         ),
@@ -569,8 +574,8 @@
 
     near = over_rings(send_keys)
     lasts = [last] + [frame_move(last, flip) for flip in (1, FRAMES // 2, FRAMES // 2 + 1)]
+    send_queries, near, *lasts = lax.optimization_barrier((send_queries, near, *lasts))
     last_keys, last_values = lay_last(where, lasts, text_kv)
-    send_queries, near = lax.optimization_barrier((send_queries, near))
     over_y = frame_move(near, FRAMES // 2)
     sets = [near, over_y, frame_move(near, 1), frame_move(over_y, 1)]
     queries = over_rings(send_queries)

time: 165 us -> 164 us (level)
  blocking collectives: 47 us -> 21.5 us
  waiting for transfers between devices: 33.6 us -> 49.1 us
  starting transfers between devices: 31.2 us -> 39.4 us
    all_to_all x2 -> x1, blocking collectives: 47 us -> 21.5 us  [over_rings(): return lax.all_to_all(x, 'frame', 0, 0, axis_index_groups=rings, tiled=True)]
    all_to_all x1 -> x2, waiting for transfers between devices: 0.79 us -> 12.2 us  [over_rings(): return lax.all_to_all(x, 'frame', 0, 0, axis_index_groups=rings, tiled=True)]
    all_to_all x1 -> x2, starting transfers between devices: 3.49 us -> 12 us  [over_rings(): return lax.all_to_all(x, 'frame', 0, 0, axis_index_groups=rings, tiled=True)]
    ppermute x6, waiting for transfers between devices: 8 us -> 13.2 us  [frame_move(): return lax.ppermute(x, 'frame', [(i, i ^ flip) for i in range(FRAMES)])]
    ppermute x10, waiting for transfers between devices: 20.2 us -> 18.1 us  [head_move(): lax.ppermute(x, 'head', [(i, (i + step) % HEAD_AXIS) for i in range(HEAD_...]
  transfers between devices with their start and end apart: 21 -> 22, of which waited for: 10 -> 11; matrix products, arithmetic and copies ran while one was open for 1% -> 1% of each run, Pallas kernels for 3% -> 3%
where the time goes in v3:
time: 164 us; the launch traced here: 162 us
  waiting for transfers between devices  49.1 us (30%)
  Pallas kernels  41.8 us (25%)
  starting transfers between devices  39.4 us (24%)
  blocking collectives  21.5 us (13%)
  local copies, waits for them, and re-layouts  6.81 us (4%)
  other arithmetic  2.23 us (1%)
    pallas_call x1, Pallas kernels, attend(): pl.pallas_call(attend_kernel, out_shape=jax.ShapeDtypeStruct((RING, RETUR...  23.2 us
    all_to_all x1, blocking collectives, over_rings(): return lax.all_to_all(x, 'frame', 0, 0, axis_index_groups=rings, tiled=True)  21.5 us
    ppermute x10, waiting for transfers between devices, head_move(): lax.ppermute(x, 'head', [(i, (i + step) % HEAD_AXIS) for i in range(HEAD_...  18.1 us
    ppermute x10, starting transfers between devices, head_move(): lax.ppermute(x, 'head', [(i, (i + step) % HEAD_AXIS) for i in range(HEAD_...  15.9 us
    ppermute x6, waiting for transfers between devices, frame_move(): return lax.ppermute(x, 'frame', [(i, i ^ flip) for i in range(FRAMES)])  13.2 us
    all_to_all x2, waiting for transfers between devices, over_rings(): return lax.all_to_all(x, 'frame', 0, 0, axis_index_groups=rings, tiled=True)  12.2 us
    all_to_all x2, starting transfers between devices, over_rings(): return lax.all_to_all(x, 'frame', 0, 0, axis_index_groups=rings, tiled=True)  12 us
    ppermute x4, starting transfers between devices, head_partner(): return lax.ppermute(x, 'head', [(i, i ^ 1) for i in range(HEAD_AXIS)])  9 us
  transfers between devices with their start and end apart: 22, of which 11 were waited for; matrix products, arithmetic and copies ran while one was open for 1% of the time, Pallas kernels for 3%

profile of v3, /device:TPU:6, one launch (start us, length us, event | category | flops | bytes accessed | tf_op | source)
XLA Modules:
  0.0 161.7 jit_solution(5075989364599393746)
XLA Ops:
  0.7 2.3 %prep.1 = (bf16[400,384]{1,0:T(8,128)(2,1)S(1)}, f32[1,384]{1,0:T(1,128)S(1)}, s32[8]{0:T(128)S(1)}, s32[5]{0:T(128)S(1)}) custom-call(s32[1]{0:T(128)} %bitcast.frame_ref, s32[1]{0:T(128)} %bitcast.1.head_ref, s32[1]{0:T(128)S(6)} %copy.13.shift_ref, s32[32]{0:T(128)} %ids_ref.1, s32[3]{0:T(128)} %lengths_ref.1, bf16[3,128,384]{2,1,0:T(8,128)(2,1)} %video_ref.1, ...), custom_call_target="tpu_custom_call" | custom-call | tf_op jit(solution)/shard_map/prep/pallas_call | solution.py:95
  3.0 3.3 %collective-permute-start = (bf16[400,384]{1,0:T(8,128)(2,1)S(1)}, bf16[400,384]{1,0:T(8,128)(2,1)S(1)}, u32[]{:S(2)}, u32[]{:S(2)}) collective-permute-start(bf16[400,384]{1,0:T(8,128)(2,1)S(1)} %get-tuple-element.35.refs_0_), channel_id=1, source_target_pairs={{0,1},{1,0},{2,3},{3,2},{4,5},{5,4},{6,7},{7,6},{8,9},{9,8},{10,11... | collective-permute-start | bytes 921608 | tf_op jit(solution)/shard_map/ppermute | solution.py:510
  6.3 1.4 collective-permute-start.5
  7.7 3.2 %collective-permute-start.2 = (bf16[400,384]{1,0:T(8,128)(2,1)S(1)}, bf16[400,384]{1,0:T(8,128)(2,1)S(1)}, u32[]{:S(2)}, u32[]{:S(2)}) collective-permute-start(bf16[400,384]{1,0:T(8,128)(2,1)S(1)} %get-tuple-element.35.refs_0_), channel_id=1, source_target_pairs={{0,2},{1,3},{2,4},{3,5},{4,6},{5,7},{6,0},{7,1},{8,10},{9,11},{10,... | collective-permute-start | bytes 921608 | tf_op jit(solution)/shard_map/ppermute | solution.py:506
  10.9 2.7 %collective-permute-done.refs_1_ = bf16[400,384]{1,0:T(8,128)(2,1)S(1)} collective-permute-done((bf16[400,384]{1,0:T(8,128)(2,1)S(1)}, bf16[400,384]{1,0:T(8,128)(2,1)S(1)}, u32[]{:S(2)}, u32[]{:S(2)}) %collective-permute-start) | collective-permute-done | bytes 307232 | tf_op jit(solution)/shard_map/ppermute | solution.py:510
  14.4 2.4 %collective-permute-start.4 = (bf16[400,384]{1,0:T(8,128)(2,1)S(1)}, bf16[400,384]{1,0:T(8,128)(2,1)S(1)}, u32[]{:S(2)}, u32[]{:S(2)}) collective-permute-start(bf16[400,384]{1,0:T(8,128)(2,1)S(1)} %collective-permute-done.refs_1_), channel_id=1, source_target_pairs={{0,2},{1,3},{2,4},{3,5},{4,6},{5,7},{6,0},{7,1},{8,10},{9,11},{10,... | collective-permute-start | bytes 921608 | tf_op jit(solution)/shard_map/ppermute | solution.py:506
  16.8 1.2 collective-permute-done.5.refs_6_
  18.0 2.0 %collective-permute-start.6 = (bf16[400,384]{1,0:T(8,128)(2,1)S(1)}, bf16[400,384]{1,0:T(8,128)(2,1)S(1)}, u32[]{:S(2)}, u32[]{:S(2)}) collective-permute-start(bf16[400,384]{1,0:T(8,128)(2,1)S(1)} %collective-permute-done.5.refs_6_), channel_id=1, source_target_pairs={{0,1},{1,0},{2,3},{3,2},{4,5},{5,4},{6,7},{7,6},{8,9},{9,8},{10,11... | collective-permute-start | bytes 921608 | tf_op jit(solution)/shard_map/ppermute | solution.py:510
  20.0 1.0 sine_multiply_fusion
  21.1 2.1 %collective-permute-done.1.refs_2_ = bf16[400,384]{1,0:T(8,128)(2,1)S(1)} collective-permute-done((bf16[400,384]{1,0:T(8,128)(2,1)S(1)}, bf16[400,384]{1,0:T(8,128)(2,1)S(1)}, u32[]{:S(2)}, u32[]{:S(2)}) %collective-permute-start.1) | collective-permute-done | bytes 307232 | tf_op jit(solution)/shard_map/ppermute | solution.py:506
  23.2 6.5 %collective-permute-done.3.refs_4_ = bf16[400,384]{1,0:T(8,128)(2,1)S(1)} collective-permute-done((bf16[400,384]{1,0:T(8,128)(2,1)S(1)}, bf16[400,384]{1,0:T(8,128)(2,1)S(1)}, u32[]{:S(2)}, u32[]{:S(2)}) %collective-permute-start.3) | collective-permute-done | bytes 307232 | tf_op jit(solution)/shard_map/ppermute | solution.py:506
  29.7 8.5 %project.1 = (bf16[8,256,128]{2,1,0:T(8,128)(2,1)}, bf16[8,256,128]{2,1,0:T(8,128)(2,1)}, bf16[256,128]{1,0:T(8,128)(2,1)S(1)}) custom-call(s32[8]{0:T(128)S(1)} %get-tuple-element.33.place_ref, bf16[400,384]{1,0:T(8,128)(2,1)S(1)} %get-tuple-element.35.refs_0_, bf16[400,384]{1,0:T(8,128)(2,1)S(1)} %collective-permute-done.refs_1_, ...), custom_call_target="tpu_custom_call" | custom-call | flops 2717908992 | bytes 12000000 | tf_op jit(solution)/shard_map/project/pallas_call | solution.py:193
  38.1 8.5 %all-to-all-start = ((bf16[8,256,128]{2,1,0:T(8,128)(2,1)}), bf16[8,256,128]{2,1,0:T(8,128)(2,1)S(1)}, u32[]{:S(2)}, u32[]{:S(2)}) async-start(bf16[8,256,128]{2,1,0:T(8,128)(2,1)} %get-tuple-element.37), calls=%async_computation | async-start | bytes 1048576 | tf_op jit(solution)/shard_map/all_to_all | solution.py:573
  47.4 1.1 collective-permute-start.9
  48.5 3.1 %collective-permute-done.8.refs_2_ = bf16[256,128]{1,0:T(8,128)(2,1)S(1)} collective-permute-done((bf16[256,128]{1,0:T(8,128)(2,1)S(1)}, bf16[256,128]{1,0:T(8,128)(2,1)S(1)}, u32[]{:S(2)}, u32[]{:S(2)}) %collective-permute-start.8) | collective-permute-done | bytes 65568 | tf_op jit(solution)/shard_map/ppermute | solution.py:514
  52.1 12.2 %all-to-all-done.refs_0_ = bf16[8,256,128]{2,1,0:T(8,128)(2,1)S(1)} async-done(((bf16[8,256,128]{2,1,0:T(8,128)(2,1)}), bf16[8,256,128]{2,1,0:T(8,128)(2,1)S(1)}, u32[]{:S(2)}, u32[]{:S(2)}) %all-to-all-start) | async-done | bytes 524320 | tf_op jit(solution)/shard_map/all_to_all | solution.py:573
  65.0 3.5 %all-to-all-start.1 = ((bf16[8,256,128]{2,1,0:T(8,128)(2,1)}), bf16[8,256,128]{2,1,0:T(8,128)(2,1)S(1)}, u32[]{:S(2)}, u32[]{:S(2)}) async-start(bf16[8,256,128]{2,1,0:T(8,128)(2,1)} %get-tuple-element.41), calls=%async_computation.1 | async-start | bytes 1048576 | tf_op jit(solution)/shard_map/all_to_all | solution.py:573
  68.5 9.7 %collective-permute-done.10.refs_1_ = bf16[8,256,128]{2,1,0:T(8,128)(2,1)S(1)} collective-permute-done((bf16[8,256,128]{2,1,0:T(8,128)(2,1)S(1)}, bf16[8,256,128]{2,1,0:T(8,128)(2,1)S(1)}, u32[]{:S(2)}, u32[]{:S(2)}) %collective-permute-start.10) | collective-permute-done | bytes 524320 | tf_op jit(solution)/shard_map/ppermute | solution.py:514
  78.1 1.5 lay_last.1
  81.1 4.0 %lay.1 = (bf16[128,4352]{1,0:T(8,128)(2,1)S(1)}, bf16[4352,256]{1,0:T(8,128)(2,1)S(1)}, bf16[384,3072]{1,0:T(8,128)(2,1)S(1)}, s32[1]{0:T(128)}) custom-call(s32[5]{0:T(128)S(1)} %get-tuple-element.34.where_ref, bf16[8,256,128]{2,1,0:T(8,128)(2,1)S(1)} %all-to-all-done.refs_0_, bf16[8,256,128]{2,1,0:T(8,128)(2,1)S(1)} %collective-permute-done.10.refs_1_, ...), custom_call_target="tpu_custom_call" | custom-call | flops 5000000000 | bytes 10000000 | tf_op jit(solution)/shard_map/lay/pallas_call | solution.py:337
  85.1 1.4 copy-done
  86.6 1.4 copy-done.2
  88.0 1.6 %copy-done.3 = bf16[4352,256]{1,0:T(8,128)(2,1)S(1)} copy-done((bf16[4352,256]{1,0:T(8,128)(2,1)S(1)}, bf16[4352,256]{1,0:T(8,128)(2,1)}, u32[]{:S(2)}) %copy-start.3) | copy-done | bytes 2228248
  90.6 23.2 %attend.1 = bf16[8,272,128]{2,1,0:T(8,128)(2,1)S(1)} custom-call(s32[5]{0:T(128)S(1)} %get-tuple-element.34.where_ref, s32[1]{0:T(128)} %get-tuple-element.40.flag_ref, bf16[8,256,128]{2,1,0:T(8,128)(2,1)S(1)} %all-to-all-done.1.q_ref, bf16[128,4352]{1,0:T(8,128)(2,1)S(1)} %get-tuple-element.42.keys_ref, bf16[4352,256]{1,0:T(8,128)(2,1)S(1)} %copy-done.3, ...), custom_call_target="tpu_custom_call" | custom-call | flops 2617245696 | bytes 4000000 | tf_op jit(solution)/shard_map/attend/pallas_call | solution.py:431
  113.7 21.5 %all_to_all.15.back_ref = bf16[8,272,128]{2,1,0:T(8,128)(2,1)S(1)} all-to-all(bf16[8,272,128]{2,1,0:T(8,128)(2,1)S(1)} %attend.1), channel_id=1, replica_groups={{0,16,32,48,64,80,96,112},{8,24,40,56,72,88,104,120},{128,144,160,176,1..., dimensions={0} | all-to-all | bytes 1114112 | tf_op jit(solution)/shard_map/all_to_all | solution.py:573
  135.3 2.3 %output.1 = (bf16[384,384]{1,0:T(8,128)(2,1)S(1)}, bf16[384,384]{1,0:T(8,128)(2,1)S(1)}, bf16[384,384]{1,0:T(8,128)(2,1)S(1)}, bf16[384,384]{1,0:T(8,128)(2,1)S(...) custom-call(s32[8]{0:T(128)S(1)} %get-tuple-element.33.place_ref, ...), custom_call_target="tpu_custom_call" | custom-call | flops 905969664 | bytes 5000000 | tf_op jit(solution)/shard_map/output/pallas_call | solution.py:482
  139.3 2.4 %collective-permute-start.15 = (bf16[384,384]{1,0:T(8,128)(2,1)S(1)}, bf16[384,384]{1,0:T(8,128)(2,1)S(1)}, u32[]{:S(2)}, u32[]{:S(2)}) collective-permute-start(bf16[384,384]{1,0:T(8,128)(2,1)S(1)} %get-tuple-element.55), channel_id=1, source_target_pairs={{0,2},{1,3},{2,4},{3,5},{4,6},{5,7},{6,0},{7,1},{8,10},{9,11},{10,... | collective-permute-start | bytes 884744 | tf_op jit(solution)/shard_map/ppermute | solution.py:506
  141.7 3.2 %collective-permute-start.13 = (bf16[384,384]{1,0:T(8,128)(2,1)S(1)}, bf16[384,384]{1,0:T(8,128)(2,1)S(1)}, u32[]{:S(2)}, u32[]{:S(2)}) collective-permute-start(bf16[384,384]{1,0:T(8,128)(2,1)S(1)} %get-tuple-element.52), channel_id=1, source_target_pairs={{0,2},{1,3},{2,4},{3,5},{4,6},{5,7},{6,0},{7,1},{8,10},{9,11},{10,... | collective-permute-start | bytes 884744 | tf_op jit(solution)/shard_map/ppermute | solution.py:506
  145.0 2.8 %collective-permute-done.18 = bf16[384,384]{1,0:T(8,128)(2,1)S(1)} collective-permute-done((bf16[384,384]{1,0:T(8,128)(2,1)S(1)}, bf16[384,384]{1,0:T(8,128)(2,1)S(1)}, u32[]{:S(2)}, u32[]{:S(2)}) %collective-permute-start.18) | collective-permute-done | bytes 294944 | tf_op jit(solution)/shard_map/ppermute | solution.py:510
  147.9 1.5 collective-permute-start.19
  149.8 2.8 %collective-permute-start.17 = (bf16[384,384]{1,0:T(8,128)(2,1)S(1)}, bf16[384,384]{1,0:T(8,128)(2,1)S(1)}, u32[]{:S(2)}, u32[]{:S(2)}) collective-permute-start(bf16[384,384]{1,0:T(8,128)(2,1)S(1)} %add_convert_fusion.2), channel_id=1, source_target_pairs={{0,1},{1,0},{2,3},{3,2},{4,5},{5,4},{6,7},{7,6},{8,9},{9,8},{10,11... | collective-permute-start | bytes 884744 | tf_op jit(solution)/shard_map/ppermute | solution.py:510
  152.6 8.1 %collective-permute-done.14 = bf16[384,384]{1,0:T(8,128)(2,1)S(1)} collective-permute-done((bf16[384,384]{1,0:T(8,128)(2,1)S(1)}, bf16[384,384]{1,0:T(8,128)(2,1)S(1)}, u32[]{:S(2)}, u32[]{:S(2)}) %collective-permute-start.14) | collective-permute-done | bytes 294944 | tf_op jit(solution)/shard_map/ppermute | solution.py:506
  (44 shorter events, 8.3 us)
Async XLA Ops:
  3.0 10.6 %collective-permute-start = (bf16[400,384]{1,0:T(8,128)(2,1)S(1)}, bf16[400,384]{1,0:T(8,128)(2,1)S(1)}, u32[]{:S(2)}, u32[]{:S(2)}) collective-permute-start(bf16[400,384]{1,0:T(8,128)(2,1)S(1)} %get-tuple-element.35.refs_0_), channel_id=1, source_target_pairs={{0,1},{1,0},{2,3},{3,2},{4,5},{5,4},{6,7},{7,6},{8,9},{9,8},{10,11... | collective-permute-start | bytes 921608 | tf_op jit(solution)/shard_map/ppermute | solution.py:510
  6.3 11.7 %collective-permute-start.5 = (bf16[400,384]{1,0:T(8,128)(2,1)S(1)}, bf16[400,384]{1,0:T(8,128)(2,1)S(1)}, u32[]{:S(2)}, u32[]{:S(2)}) collective-permute-start(bf16[400,384]{1,0:T(8,128)(2,1)S(1)} %get-tuple-element.35.refs_0_), channel_id=1, source_target_pairs={{0,4},{1,5},{2,6},{3,7},{4,0},{5,1},{6,2},{7,3},{8,12},{9,13},{10,... | collective-permute-start | bytes 921608 | tf_op jit(solution)/shard_map/ppermute | solution.py:506
  7.7 15.5 %collective-permute-start.1 = (bf16[400,384]{1,0:T(8,128)(2,1)S(1)}, bf16[400,384]{1,0:T(8,128)(2,1)S(1)}, u32[]{:S(2)}, u32[]{:S(2)}) collective-permute-start(bf16[400,384]{1,0:T(8,128)(2,1)S(1)} %get-tuple-element.35.refs_0_), channel_id=1, source_target_pairs={{0,6},{1,7},{2,0},{3,1},{4,2},{5,3},{6,4},{7,5},{8,14},{9,15},{10,... | collective-permute-start | bytes 921608 | tf_op jit(solution)/shard_map/ppermute | solution.py:506
  7.7 15.5 %collective-permute-start.2 = (bf16[400,384]{1,0:T(8,128)(2,1)S(1)}, bf16[400,384]{1,0:T(8,128)(2,1)S(1)}, u32[]{:S(2)}, u32[]{:S(2)}) collective-permute-start(bf16[400,384]{1,0:T(8,128)(2,1)S(1)} %get-tuple-element.35.refs_0_), channel_id=1, source_target_pairs={{0,2},{1,3},{2,4},{3,5},{4,6},{5,7},{6,0},{7,1},{8,10},{9,11},{10,... | collective-permute-start | bytes 921608 | tf_op jit(solution)/shard_map/ppermute | solution.py:506
  13.6 16.1 %collective-permute-start.3 = (bf16[400,384]{1,0:T(8,128)(2,1)S(1)}, bf16[400,384]{1,0:T(8,128)(2,1)S(1)}, u32[]{:S(2)}, u32[]{:S(2)}) collective-permute-start(bf16[400,384]{1,0:T(8,128)(2,1)S(1)} %collective-permute-done.refs_1_), channel_id=1, source_target_pairs={{0,6},{1,7},{2,0},{3,1},{4,2},{5,3},{6,4},{7,5},{8,14},{9,15},{10,... | collective-permute-start | bytes 921608 | tf_op jit(solution)/shard_map/ppermute | solution.py:506
  14.4 15.3 %collective-permute-start.4 = (bf16[400,384]{1,0:T(8,128)(2,1)S(1)}, bf16[400,384]{1,0:T(8,128)(2,1)S(1)}, u32[]{:S(2)}, u32[]{:S(2)}) collective-permute-start(bf16[400,384]{1,0:T(8,128)(2,1)S(1)} %collective-permute-done.refs_1_), channel_id=1, source_target_pairs={{0,2},{1,3},{2,4},{3,5},{4,6},{5,7},{6,0},{7,1},{8,10},{9,11},{10,... | collective-permute-start | bytes 921608 | tf_op jit(solution)/shard_map/ppermute | solution.py:506
  18.0 11.7 %collective-permute-start.6 = (bf16[400,384]{1,0:T(8,128)(2,1)S(1)}, bf16[400,384]{1,0:T(8,128)(2,1)S(1)}, u32[]{:S(2)}, u32[]{:S(2)}) collective-permute-start(bf16[400,384]{1,0:T(8,128)(2,1)S(1)} %collective-permute-done.5.refs_6_), channel_id=1, source_target_pairs={{0,1},{1,0},{2,3},{3,2},{4,5},{5,4},{6,7},{7,6},{8,9},{9,8},{10,11... | collective-permute-start | bytes 921608 | tf_op jit(solution)/shard_map/ppermute | solution.py:510
  38.1 26.2 %all-to-all-start = ((bf16[8,256,128]{2,1,0:T(8,128)(2,1)}), bf16[8,256,128]{2,1,0:T(8,128)(2,1)S(1)}, u32[]{:S(2)}, u32[]{:S(2)}) async-start(bf16[8,256,128]{2,1,0:T(8,128)(2,1)} %get-tuple-element.37), calls=%async_computation | async-start | bytes 1048576 | tf_op jit(solution)/shard_map/all_to_all | solution.py:573
  46.6 1.9 %collective-permute-start.7 = (bf16[256,128]{1,0:T(8,128)(2,1)S(1)}, bf16[256,128]{1,0:T(8,128)(2,1)S(1)}, u32[]{:S(2)}, u32[]{:S(2)}) collective-permute-start(bf16[256,128]{1,0:T(8,128)(2,1)S(1)} %get-tuple-element.44.refs_0_), channel_id=1, source_target_pairs={{0,8},{8,0},{16,24},{24,16},{32,40},{40,32},{48,56},{56,48},{64,72... | collective-permute-start | bytes 196616 | tf_op jit(solution)/shard_map/ppermute | solution.py:514
  46.6 5.0 %collective-permute-start.8 = (bf16[256,128]{1,0:T(8,128)(2,1)S(1)}, bf16[256,128]{1,0:T(8,128)(2,1)S(1)}, u32[]{:S(2)}, u32[]{:S(2)}) collective-permute-start(bf16[256,128]{1,0:T(8,128)(2,1)S(1)} %get-tuple-element.44.refs_0_), channel_id=1, source_target_pairs={{0,128},{8,136},{16,144},{24,152},{32,160},{40,168},{48,176},{56,1... | collective-permute-start | bytes 196616 | tf_op jit(solution)/shard_map/ppermute | solution.py:514
  47.4 4.7 %collective-permute-start.9 = (bf16[256,128]{1,0:T(8,128)(2,1)S(1)}, bf16[256,128]{1,0:T(8,128)(2,1)S(1)}, u32[]{:S(2)}, u32[]{:S(2)}) collective-permute-start(bf16[256,128]{1,0:T(8,128)(2,1)S(1)} %get-tuple-element.44.refs_0_), channel_id=1, source_target_pairs={{0,136},{8,128},{16,152},{24,144},{32,168},{40,160},{48,184},{56,1... | collective-permute-start | bytes 196616 | tf_op jit(solution)/shard_map/ppermute | solution.py:514
  64.3 13.8 %collective-permute-start.10 = (bf16[8,256,128]{2,1,0:T(8,128)(2,1)S(1)}, bf16[8,256,128]{2,1,0:T(8,128)(2,1)S(1)}, u32[]{:S(2)}, u32[]{:S(2)}) collective-permute-start(bf16[8,256,128]{2,1,0:T(8,128)(2,1)S(1)} %all-to-all-done.refs_0_), channel_id=1, source_target_pairs={{0,128},{8,136},{16,144},{24,152},{32,160},{40,168},{48,176},{56,1... | collective-permute-start | bytes 1572872 | tf_op jit(solution)/shard_map/ppermute | solution.py:514
  65.0 16.1 %collective-permute-start.11 = (bf16[8,256,128]{2,1,0:T(8,128)(2,1)S(1)}, bf16[8,256,128]{2,1,0:T(8,128)(2,1)S(1)}, u32[]{:S(2)}, u32[]{:S(2)}) collective-permute-start(bf16[8,256,128]{2,1,0:T(8,128)(2,1)S(1)} %all-to-all-done.refs_0_), channel_id=1, source_target_pairs={{0,8},{8,0},{16,24},{24,16},{32,40},{40,32},{48,56},{56,48},{64,72... | collective-permute-start | bytes 1572872 | tf_op jit(solution)/shard_map/ppermute | solution.py:514
  65.0 23.0 %all-to-all-start.1 = ((bf16[8,256,128]{2,1,0:T(8,128)(2,1)}), bf16[8,256,128]{2,1,0:T(8,128)(2,1)S(1)}, u32[]{:S(2)}, u32[]{:S(2)}) async-start(bf16[8,256,128]{2,1,0:T(8,128)(2,1)} %get-tuple-element.41), calls=%async_computation.1 | async-start | bytes 1048576 | tf_op jit(solution)/shard_map/all_to_all | solution.py:573
  78.1 3.0 %collective-permute-start.12 = (bf16[8,256,128]{2,1,0:T(8,128)(2,1)S(1)}, bf16[8,256,128]{2,1,0:T(8,128)(2,1)S(1)}, u32[]{:S(2)}, u32[]{:S(2)}) collective-permute-start(bf16[8,256,128]{2,1,0:T(8,128)(2,1)S(1)} %collective-permute-done.10.refs_1_), channel_id=1, source_target_pairs={{0,8},{8,0},{16,24},{24,16},{32,40},{40,32},{48,56},{56,48},{64,72... | collective-permute-start | bytes 1572872 | tf_op jit(solution)/shard_map/ppermute | solution.py:514
  79.7 0.7 copy-start.4
  80.4 0.7 copy-start.6
  81.1 6.9 %copy-start.7 = (bf16[128,640]{1,0:T(8,128)(2,1)S(1)}, bf16[128,640]{1,0:T(8,128)(2,1)}, u32[]{:S(2)}) copy-start(bf16[128,640]{1,0:T(8,128)(2,1)} %copy-done.6) | copy-start | bytes 491524
  85.1 1.4 copy-start
  86.5 1.4 copy-start.2
  88.0 1.6 %copy-start.3 = (bf16[4352,256]{1,0:T(8,128)(2,1)S(1)}, bf16[4352,256]{1,0:T(8,128)(2,1)}, u32[]{:S(2)}) copy-start(bf16[4352,256]{1,0:T(8,128)(2,1)} %copy-done.2) | copy-start | bytes 6684676
  89.6 1.0 copy-start.5
  90.6 44.7 %copy-start.1 = (bf16[384,3072]{1,0:T(8,128)(2,1)S(1)}, bf16[384,3072]{1,0:T(8,128)(2,1)}, u32[]{:S(2)}) copy-start(bf16[384,3072]{1,0:T(8,128)(2,1)} %copy-done) | copy-start | bytes 7077892
  137.6 23.3 %copy-start.8 = (bf16[3,128,384]{2,1,0:T(8,128)(2,1)S(1)}, bf16[3,128,384]{2,1,0:T(8,128)(2,1)}, u32[]{:S(2)}) copy-start(bf16[3,128,384]{2,1,0:T(8,128)(2,1)} %video_ref.1) | copy-start | bytes 884740
  137.6 10.2 %collective-permute-start.18 = (bf16[384,384]{1,0:T(8,128)(2,1)S(1)}, bf16[384,384]{1,0:T(8,128)(2,1)S(1)}, u32[]{:S(2)}, u32[]{:S(2)}) collective-permute-start(bf16[384,384]{1,0:T(8,128)(2,1)S(1)} %get-tuple-element.58), channel_id=1, source_target_pairs={{0,1},{1,0},{2,3},{3,2},{4,5},{5,4},{6,7},{7,6},{8,9},{9,8},{10,11... | collective-permute-start | bytes 884744 | tf_op jit(solution)/shard_map/ppermute | solution.py:510
  138.5 11.2 %collective-permute-start.16 = (bf16[384,384]{1,0:T(8,128)(2,1)S(1)}, bf16[384,384]{1,0:T(8,128)(2,1)S(1)}, u32[]{:S(2)}, u32[]{:S(2)}) collective-permute-start(bf16[384,384]{1,0:T(8,128)(2,1)S(1)} %get-tuple-element.56), channel_id=1, source_target_pairs={{0,6},{1,7},{2,0},{3,1},{4,2},{5,3},{6,4},{7,5},{8,14},{9,15},{10,... | collective-permute-start | bytes 884744 | tf_op jit(solution)/shard_map/ppermute | solution.py:506
  139.3 10.4 %collective-permute-start.15 = (bf16[384,384]{1,0:T(8,128)(2,1)S(1)}, bf16[384,384]{1,0:T(8,128)(2,1)S(1)}, u32[]{:S(2)}, u32[]{:S(2)}) collective-permute-start(bf16[384,384]{1,0:T(8,128)(2,1)S(1)} %get-tuple-element.55), channel_id=1, source_target_pairs={{0,2},{1,3},{2,4},{3,5},{4,6},{5,7},{6,0},{7,1},{8,10},{9,11},{10,... | collective-permute-start | bytes 884744 | tf_op jit(solution)/shard_map/ppermute | solution.py:506
  141.7 18.9 %collective-permute-start.14 = (bf16[384,384]{1,0:T(8,128)(2,1)S(1)}, bf16[384,384]{1,0:T(8,128)(2,1)S(1)}, u32[]{:S(2)}, u32[]{:S(2)}) collective-permute-start(bf16[384,384]{1,0:T(8,128)(2,1)S(1)} %get-tuple-element.53), channel_id=1, source_target_pairs={{0,6},{1,7},{2,0},{3,1},{4,2},{5,3},{6,4},{7,5},{8,14},{9,15},{10,... | collective-permute-start | bytes 884744 | tf_op jit(solution)/shard_map/ppermute | solution.py:506
  141.7 18.9 %collective-permute-start.13 = (bf16[384,384]{1,0:T(8,128)(2,1)S(1)}, bf16[384,384]{1,0:T(8,128)(2,1)S(1)}, u32[]{:S(2)}, u32[]{:S(2)}) collective-permute-start(bf16[384,384]{1,0:T(8,128)(2,1)S(1)} %get-tuple-element.52), channel_id=1, source_target_pairs={{0,2},{1,3},{2,4},{3,5},{4,6},{5,7},{6,0},{7,1},{8,10},{9,11},{10,... | collective-permute-start | bytes 884744 | tf_op jit(solution)/shard_map/ppermute | solution.py:506
  147.9 12.8 %collective-permute-start.19 = (bf16[384,384]{1,0:T(8,128)(2,1)S(1)}, bf16[384,384]{1,0:T(8,128)(2,1)S(1)}, u32[]{:S(2)}, u32[]{:S(2)}) collective-permute-start(bf16[384,384]{1,0:T(8,128)(2,1)S(1)} %add_convert_fusion.1), channel_id=1, source_target_pairs={{0,4},{1,5},{2,6},{3,7},{4,0},{5,1},{6,2},{7,3},{8,12},{9,13},{10,... | collective-permute-start | bytes 884744 | tf_op jit(solution)/shard_map/ppermute | solution.py:506
  149.8 10.9 %collective-permute-start.17 = (bf16[384,384]{1,0:T(8,128)(2,1)S(1)}, bf16[384,384]{1,0:T(8,128)(2,1)S(1)}, u32[]{:S(2)}, u32[]{:S(2)}) collective-permute-start(bf16[384,384]{1,0:T(8,128)(2,1)S(1)} %add_convert_fusion.2), channel_id=1, source_target_pairs={{0,1},{1,0},{2,3},{3,2},{4,5},{5,4},{6,7},{7,6},{8,9},{9,8},{10,11... | collective-permute-start | bytes 884744 | tf_op jit(solution)/shard_map/ppermute | solution.py:510

commit v4 on v1

--- a/solution.py
+++ b/solution.py
@@ -36,6 +36,17 @@
     return pl.BlockSpec(shape, lambda *_: (0,) * len(shape))
 
 
+IN_VMEM = pl.BlockSpec(memory_space=pltpu.VMEM)
+
+
+def in_vmem(x):
+    return pltpu.with_memory_space_constraint(x, pltpu.VMEM)
+
+
+def in_hbm(x):
+    return pltpu.with_memory_space_constraint(x, pltpu.HBM)
+
+
 def limbs_of(value):
     limbs = []
     for _ in range(3):
@@ -66,8 +77,8 @@
 
 
 def prep_kernel(
-    frame_ref, head_ref, shift_ref, ids_ref, lengths_ref, video_ref, table_ref,
-    own_ref, gate_ref, place_ref, where_ref,
+    frame_ref, head_ref, shift_ref, ids_ref, lengths_ref, video_ref, table_ref, gain_ref,
+    own_ref, gate_ref, gain_out_ref, place_ref, where_ref,
 ):
     head = head_ref[0]
     for s, step in enumerate((0, 0, 2, -2, 2, -2, 4, 4)):
@@ -84,6 +95,7 @@
     level = ids_ref[lax.rem(frame_ref[0] + shift_ref[0], FRAMES)]
     looked = [table_ref[part, pl.ds(level, 1), :] for part in range(3)]
     gate_ref[...] = looked[2]
+    gain_out_ref[...] = gain_ref[...]
     limbs = limbs_of(looked[0]) + limbs_of(looked[1])
     limbs.append(jnp.zeros((MOD_ROWS - 6, DSH), jnp.float32))
     for b in range(BRANCH):
@@ -91,29 +103,31 @@
     own_ref[ROWS:SENT, :] = jnp.concatenate(limbs, axis=0).astype(jnp.bfloat16)
 
 
-def prep(frame, head, queue_shift, timestep_ids, lengths, video, table):
+def prep(frame, head, queue_shift, timestep_ids, lengths, video, table, gains):
     return pl.pallas_call(
         prep_kernel,
         out_shape=(
-            jax.ShapeDtypeStruct((SENT, DSH), jnp.bfloat16),
+            pltpu.VMEM((SENT, DSH), jnp.bfloat16),
             jax.ShapeDtypeStruct((1, DSH), jnp.float32),
+            pltpu.VMEM((2, HD), jnp.float32),
             jax.ShapeDtypeStruct((HEAD_AXIS,), jnp.int32),
             jax.ShapeDtypeStruct((5,), jnp.int32),
         ),
         grid_spec=pltpu.PrefetchScalarGridSpec(
             num_scalar_prefetch=5,
             grid=(1,),
-            in_specs=[whole((BRANCH, TOK, DSH)), whole((3, FRAMES, DSH))],
+            in_specs=[whole((BRANCH, TOK, DSH)), whole((3, FRAMES, DSH)), whole((2, HD))],
             out_specs=(
-                whole((SENT, DSH)),
+                IN_VMEM,
                 whole((1, DSH)),
+                IN_VMEM,
                 pl.BlockSpec(memory_space=pltpu.SMEM),
                 pl.BlockSpec(memory_space=pltpu.SMEM),
             ),
         ),
         compiler_params=pltpu.CompilerParams(vmem_limit_bytes=16 * MIB),
         name="prep",
-    )(frame, head, queue_shift, timestep_ids, lengths, video, table)
+    )(frame, head, queue_shift, timestep_ids, lengths, video, table, gains)
 
 
 def project_kernel(place_ref, *refs):
@@ -190,20 +204,15 @@
     return pl.pallas_call(
         project_kernel,
         out_shape=(
-            jax.ShapeDtypeStruct((RING, 4 * TOK, HD), jnp.bfloat16),
-            jax.ShapeDtypeStruct((2 * TOK, HD), jnp.bfloat16),
+            pltpu.VMEM((RING, 4 * TOK, HD), jnp.bfloat16),
+            pltpu.VMEM((2 * TOK, HD), jnp.bfloat16),
         ),
         grid_spec=pltpu.PrefetchScalarGridSpec(
             num_scalar_prefetch=1,
             grid=(1,),
-            in_specs=[whole((SENT, DSH)) for _ in blocks]
-            + [
-                pl.BlockSpec(memory_space=pltpu.HBM),
-                whole((2, HD)),
-                whole((TOK, HD)),
-                whole((TOK, HD)),
-            ],
-            out_specs=(whole((RING, 4 * TOK, HD)), whole((2 * TOK, HD))),
+            in_specs=[IN_VMEM] * HEAD_AXIS
+            + [pl.BlockSpec(memory_space=pltpu.HBM), IN_VMEM, IN_VMEM, IN_VMEM],
+            out_specs=(IN_VMEM, IN_VMEM),
             scratch_shapes=[
                 pltpu.VMEM((ROWS, HEAD_AXIS * DSH), jnp.bfloat16),
                 pltpu.VMEM((ROWS, WIDE), jnp.float32),
@@ -216,7 +225,7 @@
             flops=2 * ROWS * HEAD_AXIS * DSH * 3 * DSH, bytes_accessed=12_000_000, transcendentals=0
         ),
         name="project",
-    )(places, *blocks, w, gains, cosine, sine)
+    )(places, *map(in_vmem, blocks), w, *map(in_vmem, (gains, cosine, sine)))
 
 
 QUAD = 4
@@ -277,12 +286,9 @@
     return pl.ds(pl.multiple_of(pl.program_id(0) * TILE, TILE), TILE)
 
 
-IN_VMEM = pl.BlockSpec(memory_space=pltpu.VMEM)
-
-
 def attend_near_kernel(
     where_ref, q_ref, own_ref, core_ref, text_ref, w_hbm,
-    mixed_ref, top_ref, w_ref, score_ref, value_ref, sem,
+    mixed_ref, top_ref, q_out_ref, w_ref, score_ref, value_ref, sem,
 ):
     copy = pltpu.make_async_copy(w_hbm, w_ref, sem)
 
@@ -300,6 +306,7 @@
     here = tile_rows()
     mixed_ref[here, :] = mix(score_ref, value_ref, top, 2 * SET + TXT)
     top_ref[here, :] = jnp.broadcast_to(top, (TILE, 128))
+    q_out_ref[here, :] = q
 
     @pl.when(pl.program_id(0) == SET // TILE - 1)
     def _():
@@ -312,6 +319,7 @@
         out_shape=(
             pltpu.VMEM((SET, 2 * HD), jnp.float32),
             pltpu.VMEM((SET, 128), jnp.float32),
+            pltpu.VMEM((SET, HD), jnp.bfloat16),
             pltpu.VMEM(w_out.shape, w_out.dtype),
         ),
         grid_spec=pltpu.PrefetchScalarGridSpec(
@@ -324,7 +332,7 @@
                 pl.BlockSpec((2, 1, TXT, HD), lambda i, w: (0, w[0], 0, w[1])),
                 pl.BlockSpec(memory_space=pltpu.HBM),
             ],
-            out_specs=(IN_VMEM, IN_VMEM, IN_VMEM),
+            out_specs=(IN_VMEM,) * 4,
             scratch_shapes=[
                 pltpu.VMEM((TILE, 2 * SET + TXT), jnp.float32),
                 pltpu.VMEM((2 * SET + TXT, 2 * HD), jnp.bfloat16),
@@ -387,18 +395,19 @@
     mixed = mix(score_ref, value_ref, top, LAST_KEYS)
     total = mixed[:, HD : HD + 1]
     result = mixed[:, :HD] / total
-    out_ref[:, 0:TOK, :] = result.astype(jnp.bfloat16).reshape(QUAD, TOK, HD)
+    first = pl.program_id(0) * QUAD
+    out_ref[pl.ds(first, QUAD), 0:TOK, :] = result.astype(jnp.bfloat16).reshape(QUAD, TOK, HD)
     level = jnp.broadcast_to(top + jnp.log(total) * LOG2E, (TILE, HD))
     for f in range(QUAD):
         row = jnp.transpose(level[f * TOK : (f + 1) * TOK])[0:1]
         stats = limbs_of(row) + [jnp.zeros((STAT_ROWS - 3, HD), jnp.float32)]
-        out_ref[f, TOK:LAST_ROWS, :] = jnp.concatenate(stats, axis=0).astype(jnp.bfloat16)
+        out_ref[first + f, TOK:LAST_ROWS, :] = jnp.concatenate(stats, axis=0).astype(jnp.bfloat16)
 
 
 def attend_last(where, received, keys, values):
     return pl.pallas_call(
         attend_last_kernel,
-        out_shape=jax.ShapeDtypeStruct((RING, LAST_ROWS, HD), jnp.bfloat16),
+        out_shape=pltpu.VMEM((RING, LAST_ROWS, HD), jnp.bfloat16),
         grid_spec=pltpu.PrefetchScalarGridSpec(
             num_scalar_prefetch=1,
             grid=(SET // TILE,),
@@ -407,7 +416,7 @@
                 whole((LAST_KEYS, HD)),
                 whole((LAST_KEYS, 2 * HD)),
             ],
-            out_specs=pl.BlockSpec((QUAD, LAST_ROWS, HD), lambda i, w: (i, 0, 0)),
+            out_specs=IN_VMEM,
             scratch_shapes=[pltpu.VMEM((TILE, LAST_KEYS), jnp.float32)],
         ),
         compiler_params=pltpu.CompilerParams(vmem_limit_bytes=16 * MIB),
@@ -425,41 +434,27 @@
     def _():
         lay_values(value_ref, [set_values(y_ref), set_values(diagonal_ref)])
 
-    q = q_ref[...].reshape(TILE, HD)
+    here = tile_rows()
+    q = q_ref[here, :]
     top = jnp.full((TILE, 128), -jnp.inf, jnp.float32)
     for n, ref in enumerate((y_ref, diagonal_ref)):
         top = score_keys(q, set_keys(ref), score_ref, n * SET, top)
-    here = tile_rows()
     before = top_ref[here, 0:1]
     top = jnp.maximum(jnp.max(top, axis=1, keepdims=True) * EXP_SCALE, before)
     mixed = mix(score_ref, value_ref, top, 2 * SET) + mixed_ref[here, :] * jnp.exp2(before - top)
     result = mixed[:, :HD] / mixed[:, HD : HD + 1]
-    out_ref[:, 0:TOK, :] = result.astype(jnp.bfloat16).reshape(QUAD, TOK, HD)
-    out_ref[:, TOK:RETURN, :] = last_ref[...]
-
-
-def in_vmem(x):
-    return pltpu.with_memory_space_constraint(x, pltpu.VMEM)
-
-
-def in_hbm(x):
-    return pltpu.with_memory_space_constraint(x, pltpu.HBM)
-
-
-def attend_far(received, over_y, diagonal, last, mixed, top):
+    frames = pl.ds(pl.program_id(0) * QUAD, QUAD)
+    out_ref[frames, 0:TOK, :] = result.astype(jnp.bfloat16).reshape(QUAD, TOK, HD)
+    out_ref[frames, TOK:RETURN, :] = last_ref[frames]
+
+
+def attend_far(queries, over_y, diagonal, last, mixed, top):
     return pl.pallas_call(
         attend_far_kernel,
-        out_shape=jax.ShapeDtypeStruct((RING, RETURN, HD), jnp.bfloat16),
+        out_shape=pltpu.VMEM((RING, RETURN, HD), jnp.bfloat16),
         grid=(SET // TILE,),
-        in_specs=[
-            pl.BlockSpec((QUAD, TOK, HD), lambda i: (i, 2, 0)),
-            whole((RING, 2 * TOK, HD)),
-            whole((RING, 2 * TOK, HD)),
-            pl.BlockSpec((QUAD, LAST_ROWS, HD), lambda i: (i, 0, 0)),
-            IN_VMEM,
-            IN_VMEM,
-        ],
-        out_specs=pl.BlockSpec((QUAD, RETURN, HD), lambda i: (i, 0, 0)),
+        in_specs=[IN_VMEM] * 6,
+        out_specs=IN_VMEM,
         scratch_shapes=[
             pltpu.VMEM((TILE, 2 * SET), jnp.float32),
             pltpu.VMEM((2 * SET, 2 * HD), jnp.bfloat16),
@@ -469,7 +464,7 @@
             flops=4 * SET * 2048 * HD, bytes_accessed=4_000_000, transcendentals=SET * 2048
         ),
         name="attend_far",
-    )(received, over_y, diagonal, last, in_vmem(mixed), in_vmem(top))
+    )(*map(in_vmem, (queries, over_y, diagonal, last, mixed, top)))
 
 
 def output_kernel(place_ref, back_ref, w_ref, *refs):
@@ -503,16 +498,16 @@
     return pl.pallas_call(
         output_kernel,
         out_shape=tuple(
-            jax.ShapeDtypeStruct((ROWS, DSH), jnp.bfloat16) for _ in range(HEAD_AXIS)
+            pltpu.VMEM((ROWS, DSH), jnp.bfloat16) for _ in range(HEAD_AXIS)
         ),
         grid_spec=pltpu.PrefetchScalarGridSpec(
             num_scalar_prefetch=1,
             grid=(1,),
             in_specs=[
-                whole((RING, RETURN, HD)),
+                IN_VMEM,
                 IN_VMEM,
             ],
-            out_specs=tuple(whole((ROWS, DSH)) for _ in range(HEAD_AXIS)),
+            out_specs=(IN_VMEM,) * HEAD_AXIS,
             scratch_shapes=[pltpu.VMEM((ROWS, DSH), jnp.bfloat16)],
         ),
         compiler_params=pltpu.CompilerParams(vmem_limit_bytes=24 * MIB),
@@ -520,7 +515,7 @@
             flops=2 * ROWS * DSH * DSH * HEAD_AXIS, bytes_accessed=5_000_000, transcendentals=0
         ),
         name="output",
-    )(places, back, in_vmem(w_out))
+    )(places, in_vmem(back), in_vmem(w_out))
 
 
 def head_move(x, step):
@@ -574,7 +569,7 @@
     text_kv = in_hbm(text_kv)
     frame = lax.axis_index("frame").astype(jnp.int32)
     head = lax.axis_index("head").astype(jnp.int32)
-    own, gate, places, where = prep(
+    own, gate, gains, places, where = prep(
         frame.reshape(1),
         head.reshape(1),
         queue_shift,
@@ -582,11 +577,12 @@
         in_hbm(text_lengths),
         in_hbm(video),
         in_hbm(mod_table.transpose(1, 0, 2)),
+        in_hbm(norm_gains),
     )
     cosine, sine = rope_tables(frame)
     blocks = gather_head(own)
     weights = in_hbm(w_qkv.transpose(1, 0, 2))
-    send, last = project(places, blocks, weights, in_hbm(norm_gains), cosine, sine)
+    send, last = project(places, blocks, weights, gains, cosine, sine)
     rings = [[(y * RING + z) * 2 + core for z in range(RING)] for y in range(2) for core in range(2)]
 
     def over_rings(x):
@@ -600,10 +596,10 @@
     over_y = frame_move(near, FRAMES // 2)
     over_core = frame_move(near, 1)
     ninth = attend_last(where, received, last_keys, last_values)
-    mixed, top, w_held = attend_near(where, received, near, over_core, text_kv, in_hbm(w_out))
+    mixed, top, queries, w_held = attend_near(where, received, near, over_core, text_kv, in_hbm(w_out))
     over_y, _, _ = lax.optimization_barrier((over_y, mixed, ninth))
     diagonal = frame_move(over_y, 1)
-    returned = attend_far(received, over_y, diagonal, ninth, mixed, top)
+    returned = attend_far(queries, over_y, diagonal, ninth, mixed, top)
     partial = output(places, over_rings(returned), w_held)
     proj = scatter_head(partial).reshape(video.shape)
     return (video.astype(jnp.float32) + gate * proj).astype(jnp.bfloat16)

time: 146 us -> 147 us (level)
  starting transfers between devices: 32 us -> 36.2 us
  waiting for transfers between devices: 58.3 us -> 54.2 us
    ppermute x10, waiting for transfers between devices: 25.1 us -> 18.1 us  [head_move(): lax.ppermute(x, 'head', [(i, (i + step) % HEAD_AXIS) for i in range(HEAD_...]
    ppermute x4, waiting for transfers between devices: 2.69 us -> 5.51 us  [head_partner(): return lax.ppermute(x, 'head', [(i, i ^ 1) for i in range(HEAD_AXIS)])]
    ppermute x4, starting transfers between devices: 6.4 us -> 9 us  [head_partner(): return lax.ppermute(x, 'head', [(i, i ^ 1) for i in range(HEAD_AXIS)])]
    ppermute x10, starting transfers between devices: 13.9 us -> 15.8 us  [head_move(): lax.ppermute(x, 'head', [(i, (i + step) % HEAD_AXIS) for i in range(HEAD_...]
  transfers between devices with their start and end apart: 21 -> 21, of which waited for: 11 -> 10; matrix products, arithmetic and copies ran while one was open for 1% -> 1% of each run, Pallas kernels for 8% -> 8%
where the time goes in v4:
time: 147 us; the launch traced here: 145 us
  waiting for transfers between devices  54.2 us (37%)
  starting transfers between devices  36.2 us (25%)
  Pallas kernels  30.1 us (20%)
  blocking collectives  21.1 us (14%)
  other arithmetic  2.23 us (2%)
    all_to_all x1, waiting for transfers between devices, over_rings(): return lax.all_to_all(x, 'frame', 0, 0, axis_index_groups=rings, tiled=True)  27.1 us
    all_to_all x1, blocking collectives, over_rings(): return lax.all_to_all(x, 'frame', 0, 0, axis_index_groups=rings, tiled=True)  21.1 us
    ppermute x10, waiting for transfers between devices, head_move(): lax.ppermute(x, 'head', [(i, (i + step) % HEAD_AXIS) for i in range(HEAD_...  18.1 us
    ppermute x10, starting transfers between devices, head_move(): lax.ppermute(x, 'head', [(i, (i + step) % HEAD_AXIS) for i in range(HEAD_...  15.8 us
    ppermute x4, starting transfers between devices, head_partner(): return lax.ppermute(x, 'head', [(i, i ^ 1) for i in range(HEAD_AXIS)])  9 us
    all_to_all x1, starting transfers between devices, over_rings(): return lax.all_to_all(x, 'frame', 0, 0, axis_index_groups=rings, tiled=True)  8.48 us
    pallas_call x1, Pallas kernels, project(): pl.pallas_call(project_kernel, out_shape=(pltpu.VMEM((RING, 4 * TOK, HD),...  7.91 us
    pallas_call x1, Pallas kernels, attend_near(): pl.pallas_call(attend_near_kernel, out_shape=(pltpu.VMEM((SET, 2 * HD), j...  7.26 us
  transfers between devices with their start and end apart: 21, of which 10 were waited for; matrix products, arithmetic and copies ran while one was open for 1% of the time, Pallas kernels for 8%

profile of v4, /device:TPU:6, one launch (start us, length us, event | category | flops | bytes accessed | tf_op | source)
XLA Modules:
  0.0 144.7 jit_solution(7194167581474789450)
XLA Ops:
  0.7 2.4 %prep.1 = (bf16[400,384]{1,0:T(8,128)(2,1)S(1)}, f32[1,384]{1,0:T(1,128)S(1)}, f32[2,128]{1,0:T(2,128)S(1)}, s32[8]{0:T(128)S(1)}, s32[5]{0:T(128)S(1)}) custom-call(s32[1]{0:T(128)} %bitcast.frame_ref, s32[1]{0:T(128)} %bitcast.1.head_ref, s32[1]{0:T(128)S(6)} %copy.13.shift_ref, s32[32]{0:T(128)} %ids_ref.1, s32[3]{0:T(128)} %lengths_ref.1, ...), custom_call_target="tpu_custom_call" | custom-call | tf_op jit(solution)/shard_map/prep/pallas_call | solution.py:107
  3.0 3.3 %collective-permute-start = (bf16[400,384]{1,0:T(8,128)(2,1)S(1)}, bf16[400,384]{1,0:T(8,128)(2,1)S(1)}, u32[]{:S(2)}, u32[]{:S(2)}) collective-permute-start(bf16[400,384]{1,0:T(8,128)(2,1)S(1)} %get-tuple-element.30.refs_0_), channel_id=1, source_target_pairs={{0,1},{1,0},{2,3},{3,2},{4,5},{5,4},{6,7},{7,6},{8,9},{9,8},{10,11... | collective-permute-start | bytes 921608 | tf_op jit(solution)/shard_map/ppermute | solution.py:526
  6.3 1.4 collective-permute-start.5
  7.7 3.2 %collective-permute-start.2 = (bf16[400,384]{1,0:T(8,128)(2,1)S(1)}, bf16[400,384]{1,0:T(8,128)(2,1)S(1)}, u32[]{:S(2)}, u32[]{:S(2)}) collective-permute-start(bf16[400,384]{1,0:T(8,128)(2,1)S(1)} %get-tuple-element.30.refs_0_), channel_id=1, source_target_pairs={{0,2},{1,3},{2,4},{3,5},{4,6},{5,7},{6,0},{7,1},{8,10},{9,11},{10,... | collective-permute-start | bytes 921608 | tf_op jit(solution)/shard_map/ppermute | solution.py:522
  10.9 2.7 %collective-permute-done.refs_1_ = bf16[400,384]{1,0:T(8,128)(2,1)S(1)} collective-permute-done((bf16[400,384]{1,0:T(8,128)(2,1)S(1)}, bf16[400,384]{1,0:T(8,128)(2,1)S(1)}, u32[]{:S(2)}, u32[]{:S(2)}) %collective-permute-start) | collective-permute-done | bytes 307232 | tf_op jit(solution)/shard_map/ppermute | solution.py:526
  13.6 0.8 collective-permute-start.3
  14.5 2.4 %collective-permute-start.4 = (bf16[400,384]{1,0:T(8,128)(2,1)S(1)}, bf16[400,384]{1,0:T(8,128)(2,1)S(1)}, u32[]{:S(2)}, u32[]{:S(2)}) collective-permute-start(bf16[400,384]{1,0:T(8,128)(2,1)S(1)} %collective-permute-done.refs_1_), channel_id=1, source_target_pairs={{0,2},{1,3},{2,4},{3,5},{4,6},{5,7},{6,0},{7,1},{8,10},{9,11},{10,... | collective-permute-start | bytes 921608 | tf_op jit(solution)/shard_map/ppermute | solution.py:522
  16.9 1.2 collective-permute-done.5.refs_6_
  18.0 2.0 %collective-permute-start.6 = (bf16[400,384]{1,0:T(8,128)(2,1)S(1)}, bf16[400,384]{1,0:T(8,128)(2,1)S(1)}, u32[]{:S(2)}, u32[]{:S(2)}) collective-permute-start(bf16[400,384]{1,0:T(8,128)(2,1)S(1)} %collective-permute-done.5.refs_6_), channel_id=1, source_target_pairs={{0,1},{1,0},{2,3},{3,2},{4,5},{5,4},{6,7},{7,6},{8,9},{9,8},{10,11... | collective-permute-start | bytes 921608 | tf_op jit(solution)/shard_map/ppermute | solution.py:526
  20.1 1.0 sine_multiply_fusion
  21.1 2.1 %collective-permute-done.1.refs_2_ = bf16[400,384]{1,0:T(8,128)(2,1)S(1)} collective-permute-done((bf16[400,384]{1,0:T(8,128)(2,1)S(1)}, bf16[400,384]{1,0:T(8,128)(2,1)S(1)}, u32[]{:S(2)}, u32[]{:S(2)}) %collective-permute-start.1) | collective-permute-done | bytes 307232 | tf_op jit(solution)/shard_map/ppermute | solution.py:522
  23.2 6.5 %collective-permute-done.3.refs_4_ = bf16[400,384]{1,0:T(8,128)(2,1)S(1)} collective-permute-done((bf16[400,384]{1,0:T(8,128)(2,1)S(1)}, bf16[400,384]{1,0:T(8,128)(2,1)S(1)}, u32[]{:S(2)}, u32[]{:S(2)}) %collective-permute-start.3) | collective-permute-done | bytes 307232 | tf_op jit(solution)/shard_map/ppermute | solution.py:522
  29.7 7.9 %project.1 = (bf16[8,512,128]{2,1,0:T(8,128)(2,1)}, bf16[256,128]{1,0:T(8,128)(2,1)S(1)}) custom-call(s32[8]{0:T(128)S(1)} %get-tuple-element.28.place_ref, bf16[400,384]{1,0:T(8,128)(2,1)S(1)} %get-tuple-element.30.refs_0_, bf16[400,384]{1,0:T(8,128)(2,1)S(1)} %collective-permute-done.refs_1_, bf16[400,384]{1,0:T(8,128)(2,1)S(1)} %collective-permute-done.1.refs_2_, ...), custom_call_target="tpu_custom_call" | custom-call | flops 2717908992 | bytes 12000000 | tf_op jit(solution)/shard_map/project/pallas_call | solution.py:204
  37.6 8.5 %all-to-all-start = ((bf16[8,512,128]{2,1,0:T(8,128)(2,1)}), bf16[8,512,128]{2,1,0:T(8,128)(2,1)S(1)}, u32[]{:S(2)}, u32[]{:S(2)}) async-start(bf16[8,512,128]{2,1,0:T(8,128)(2,1)} %get-tuple-element.32), calls=%async_computation | async-start | bytes 2097152 | tf_op jit(solution)/shard_map/all_to_all | solution.py:589
  46.9 1.1 collective-permute-start.11
  48.0 27.1 %all-to-all-done.q_ref = bf16[8,512,128]{2,1,0:T(8,128)(2,1)S(1)} async-done(((bf16[8,512,128]{2,1,0:T(8,128)(2,1)}), bf16[8,512,128]{2,1,0:T(8,128)(2,1)S(1)}, u32[]{:S(2)}, u32[]{:S(2)}) %all-to-all-start) | async-done | bytes 1048608 | tf_op jit(solution)/shard_map/all_to_all | solution.py:589
  75.2 0.9 collective-permute-start.8
  76.2 1.4 lay_last.1
  77.6 3.0 %attend_last.1.last_ref = bf16[8,144,128]{2,1,0:T(8,128)(2,1)S(1)} custom-call(s32[5]{0:T(128)S(1)} %get-tuple-element.29.where_ref, bf16[8,512,128]{2,1,0:T(8,128)(2,1)S(1)} %all-to-all-done.q_ref, bf16[640,128]{1,0:T(8,128)(2,1)S(1)} %get-tuple-element.36.keys_ref, bf16[640,256]{1,0:T(8,128)(2,1)S(1)} %get-tuple-element.37.value_ref), custom_call_target="tpu_custom_call" | custom-call | flops 335544320 | bytes 1000000 | tf_op jit(solution)/shard_map/attend_last/pallas_call | solution.py:408
  80.7 7.3 %attend_near.1 = (f32[1024,256]{1,0:T(8,128)S(1)}, f32[1024,128]{1,0:T(8,128)S(1)}, bf16[1024,128]{1,0:T(8,128)(2,1)S(1)}, bf16[384,3072]{1,0:T(8,128)(2,1)S(1)}) custom-call(s32[5]{0:T(128)S(1)} %get-tuple-element.29.where_ref, bf16[8,512,128]{2,1,0:T(8,128)(2,1)S(1)} %all-to-all-done.q_ref, bf16[8,256,128]{2,1,0:T(8,128)(2,1)S(1)} %slice.4.own_ref, ...), custom_call_target="tpu_custom_call" | custom-call | flops 1207959552 | bytes 3000000 | tf_op jit(solution)/shard_map/attend_near/pallas_call | solution.py:317
  87.9 1.6 %collective-permute-done.8.y_ref = bf16[8,256,128]{2,1,0:T(8,128)(2,1)S(1)} collective-permute-done((bf16[8,256,128]{2,1,0:T(8,128)(2,1)S(1)}, bf16[8,256,128]{2,1,0:T(8,128)(2,1)S(1)}, u32[]{:S(2)}, u32[]{:S(2)}) %collective-permute-start.8) | collective-permute-done | bytes 524320 | tf_op jit(solution)/shard_map/ppermute | solution.py:530
  89.5 1.9 %collective-permute-done.12.diagonal_ref = bf16[8,256,128]{2,1,0:T(8,128)(2,1)S(1)} collective-permute-done((bf16[8,256,128]{2,1,0:T(8,128)(2,1)S(1)}, bf16[8,256,128]{2,1,0:T(8,128)(2,1)S(1)}, u32[]{:S(2)}, u32[]{:S(2)}) %collective-permute-start.12) | collective-permute-done | bytes 524320 | tf_op jit(solution)/shard_map/ppermute | solution.py:530
  91.4 5.7 %attend_far.1 = bf16[8,272,128]{2,1,0:T(8,128)(2,1)S(1)} custom-call(bf16[1024,128]{1,0:T(8,128)(2,1)S(1)} %get-tuple-element.33.q_ref, bf16[8,256,128]{2,1,0:T(8,128)(2,1)S(1)} %collective-permute-done.8.y_ref, bf16[8,256,128]{2,1,0:T(8,128)(2,1)S(1)} %collective-permute-done.12.diagonal_ref, bf16[8,144,128]{2,1,0:T(8,128)(2,1)S(1)} %attend_last.1.last_ref, ...), custom_call_target="tpu_custom_call" | custom-call | flops 1073741824 | bytes 4000000 | tf_op jit(solution)/shard_map/attend_far/pallas_call | solution.py:452
  97.2 21.1 %all_to_all.10.back_ref = bf16[8,272,128]{2,1,0:T(8,128)(2,1)S(1)} all-to-all(bf16[8,272,128]{2,1,0:T(8,128)(2,1)S(1)} %attend_far.1), channel_id=1, replica_groups={{0,16,32,48,64,80,96,112},{8,24,40,56,72,88,104,120},{128,144,160,176,1..., dimensions={0} | all-to-all | bytes 1114112 | tf_op jit(solution)/shard_map/all_to_all | solution.py:589
  118.3 2.3 %output.1 = (bf16[384,384]{1,0:T(8,128)(2,1)S(1)}, bf16[384,384]{1,0:T(8,128)(2,1)S(1)}, bf16[384,384]{1,0:T(8,128)(2,1)S(1)}, bf16[384,384]{1,0:T(8,128)(2,1)S(...) custom-call(s32[8]{0:T(128)S(1)} %get-tuple-element.28.place_ref, ...), custom_call_target="tpu_custom_call" | custom-call | flops 905969664 | bytes 5000000 | tf_op jit(solution)/shard_map/output/pallas_call | solution.py:498
  120.7 0.9 collective-permute-start.18
  122.4 2.4 %collective-permute-start.15 = (bf16[384,384]{1,0:T(8,128)(2,1)S(1)}, bf16[384,384]{1,0:T(8,128)(2,1)S(1)}, u32[]{:S(2)}, u32[]{:S(2)}) collective-permute-start(bf16[384,384]{1,0:T(8,128)(2,1)S(1)} %get-tuple-element.45), channel_id=1, source_target_pairs={{0,2},{1,3},{2,4},{3,5},{4,6},{5,7},{6,0},{7,1},{8,10},{9,11},{10,... | collective-permute-start | bytes 884744 | tf_op jit(solution)/shard_map/ppermute | solution.py:522
  124.8 3.2 %collective-permute-start.13 = (bf16[384,384]{1,0:T(8,128)(2,1)S(1)}, bf16[384,384]{1,0:T(8,128)(2,1)S(1)}, u32[]{:S(2)}, u32[]{:S(2)}) collective-permute-start(bf16[384,384]{1,0:T(8,128)(2,1)S(1)} %get-tuple-element.42), channel_id=1, source_target_pairs={{0,2},{1,3},{2,4},{3,5},{4,6},{5,7},{6,0},{7,1},{8,10},{9,11},{10,... | collective-permute-start | bytes 884744 | tf_op jit(solution)/shard_map/ppermute | solution.py:522
  128.0 2.8 %collective-permute-done.18 = bf16[384,384]{1,0:T(8,128)(2,1)S(1)} collective-permute-done((bf16[384,384]{1,0:T(8,128)(2,1)S(1)}, bf16[384,384]{1,0:T(8,128)(2,1)S(1)}, u32[]{:S(2)}, u32[]{:S(2)}) %collective-permute-start.18) | collective-permute-done | bytes 294944 | tf_op jit(solution)/shard_map/ppermute | solution.py:526
  130.9 1.5 %collective-permute-start.19 = (bf16[384,384]{1,0:T(8,128)(2,1)S(1)}, bf16[384,384]{1,0:T(8,128)(2,1)S(1)}, u32[]{:S(2)}, u32[]{:S(2)}) collective-permute-start(bf16[384,384]{1,0:T(8,128)(2,1)S(1)} %add_convert_fusion.1), channel_id=1, source_target_pairs={{0,4},{1,5},{2,6},{3,7},{4,0},{5,1},{6,2},{7,3},{8,12},{9,13},{10,... | collective-permute-start | bytes 884744 | tf_op jit(solution)/shard_map/ppermute | solution.py:522
  132.8 2.9 %collective-permute-start.17 = (bf16[384,384]{1,0:T(8,128)(2,1)S(1)}, bf16[384,384]{1,0:T(8,128)(2,1)S(1)}, u32[]{:S(2)}, u32[]{:S(2)}) collective-permute-start(bf16[384,384]{1,0:T(8,128)(2,1)S(1)} %add_convert_fusion.2), channel_id=1, source_target_pairs={{0,1},{1,0},{2,3},{3,2},{4,5},{5,4},{6,7},{7,6},{8,9},{9,8},{10,11... | collective-permute-start | bytes 884744 | tf_op jit(solution)/shard_map/ppermute | solution.py:526
  135.7 8.0 %collective-permute-done.14 = bf16[384,384]{1,0:T(8,128)(2,1)S(1)} collective-permute-done((bf16[384,384]{1,0:T(8,128)(2,1)S(1)}, bf16[384,384]{1,0:T(8,128)(2,1)S(1)}, u32[]{:S(2)}, u32[]{:S(2)}) %collective-permute-start.14) | collective-permute-done | bytes 294944 | tf_op jit(solution)/shard_map/ppermute | solution.py:522
  (28 shorter events, 3.2 us)
Async XLA Ops:
  3.0 10.6 %collective-permute-start = (bf16[400,384]{1,0:T(8,128)(2,1)S(1)}, bf16[400,384]{1,0:T(8,128)(2,1)S(1)}, u32[]{:S(2)}, u32[]{:S(2)}) collective-permute-start(bf16[400,384]{1,0:T(8,128)(2,1)S(1)} %get-tuple-element.30.refs_0_), channel_id=1, source_target_pairs={{0,1},{1,0},{2,3},{3,2},{4,5},{5,4},{6,7},{7,6},{8,9},{9,8},{10,11... | collective-permute-start | bytes 921608 | tf_op jit(solution)/shard_map/ppermute | solution.py:526
  6.3 11.7 %collective-permute-start.5 = (bf16[400,384]{1,0:T(8,128)(2,1)S(1)}, bf16[400,384]{1,0:T(8,128)(2,1)S(1)}, u32[]{:S(2)}, u32[]{:S(2)}) collective-permute-start(bf16[400,384]{1,0:T(8,128)(2,1)S(1)} %get-tuple-element.30.refs_0_), channel_id=1, source_target_pairs={{0,4},{1,5},{2,6},{3,7},{4,0},{5,1},{6,2},{7,3},{8,12},{9,13},{10,... | collective-permute-start | bytes 921608 | tf_op jit(solution)/shard_map/ppermute | solution.py:522
  7.7 15.5 %collective-permute-start.1 = (bf16[400,384]{1,0:T(8,128)(2,1)S(1)}, bf16[400,384]{1,0:T(8,128)(2,1)S(1)}, u32[]{:S(2)}, u32[]{:S(2)}) collective-permute-start(bf16[400,384]{1,0:T(8,128)(2,1)S(1)} %get-tuple-element.30.refs_0_), channel_id=1, source_target_pairs={{0,6},{1,7},{2,0},{3,1},{4,2},{5,3},{6,4},{7,5},{8,14},{9,15},{10,... | collective-permute-start | bytes 921608 | tf_op jit(solution)/shard_map/ppermute | solution.py:522
  7.7 15.5 %collective-permute-start.2 = (bf16[400,384]{1,0:T(8,128)(2,1)S(1)}, bf16[400,384]{1,0:T(8,128)(2,1)S(1)}, u32[]{:S(2)}, u32[]{:S(2)}) collective-permute-start(bf16[400,384]{1,0:T(8,128)(2,1)S(1)} %get-tuple-element.30.refs_0_), channel_id=1, source_target_pairs={{0,2},{1,3},{2,4},{3,5},{4,6},{5,7},{6,0},{7,1},{8,10},{9,11},{10,... | collective-permute-start | bytes 921608 | tf_op jit(solution)/shard_map/ppermute | solution.py:522
  13.6 16.1 %collective-permute-start.3 = (bf16[400,384]{1,0:T(8,128)(2,1)S(1)}, bf16[400,384]{1,0:T(8,128)(2,1)S(1)}, u32[]{:S(2)}, u32[]{:S(2)}) collective-permute-start(bf16[400,384]{1,0:T(8,128)(2,1)S(1)} %collective-permute-done.refs_1_), channel_id=1, source_target_pairs={{0,6},{1,7},{2,0},{3,1},{4,2},{5,3},{6,4},{7,5},{8,14},{9,15},{10,... | collective-permute-start | bytes 921608 | tf_op jit(solution)/shard_map/ppermute | solution.py:522
  14.5 15.3 %collective-permute-start.4 = (bf16[400,384]{1,0:T(8,128)(2,1)S(1)}, bf16[400,384]{1,0:T(8,128)(2,1)S(1)}, u32[]{:S(2)}, u32[]{:S(2)}) collective-permute-start(bf16[400,384]{1,0:T(8,128)(2,1)S(1)} %collective-permute-done.refs_1_), channel_id=1, source_target_pairs={{0,2},{1,3},{2,4},{3,5},{4,6},{5,7},{6,0},{7,1},{8,10},{9,11},{10,... | collective-permute-start | bytes 921608 | tf_op jit(solution)/shard_map/ppermute | solution.py:522
  18.0 11.7 %collective-permute-start.6 = (bf16[400,384]{1,0:T(8,128)(2,1)S(1)}, bf16[400,384]{1,0:T(8,128)(2,1)S(1)}, u32[]{:S(2)}, u32[]{:S(2)}) collective-permute-start(bf16[400,384]{1,0:T(8,128)(2,1)S(1)} %collective-permute-done.5.refs_6_), channel_id=1, source_target_pairs={{0,1},{1,0},{2,3},{3,2},{4,5},{5,4},{6,7},{7,6},{8,9},{9,8},{10,11... | collective-permute-start | bytes 921608 | tf_op jit(solution)/shard_map/ppermute | solution.py:526
  37.6 37.4 %all-to-all-start = ((bf16[8,512,128]{2,1,0:T(8,128)(2,1)}), bf16[8,512,128]{2,1,0:T(8,128)(2,1)S(1)}, u32[]{:S(2)}, u32[]{:S(2)}) async-start(bf16[8,512,128]{2,1,0:T(8,128)(2,1)} %get-tuple-element.32), calls=%async_computation | async-start | bytes 2097152 | tf_op jit(solution)/shard_map/all_to_all | solution.py:589
  46.1 30.0 %collective-permute-start.9 = (bf16[256,128]{1,0:T(8,128)(2,1)S(1)}, bf16[256,128]{1,0:T(8,128)(2,1)S(1)}, u32[]{:S(2)}, u32[]{:S(2)}) collective-permute-start(bf16[256,128]{1,0:T(8,128)(2,1)S(1)} %get-tuple-element.35.refs_0_), channel_id=1, source_target_pairs={{0,8},{8,0},{16,24},{24,16},{32,40},{40,32},{48,56},{56,48},{64,72... | collective-permute-start | bytes 196616 | tf_op jit(solution)/shard_map/ppermute | solution.py:530
  46.1 30.0 %collective-permute-start.10 = (bf16[256,128]{1,0:T(8,128)(2,1)S(1)}, bf16[256,128]{1,0:T(8,128)(2,1)S(1)}, u32[]{:S(2)}, u32[]{:S(2)}) collective-permute-start(bf16[256,128]{1,0:T(8,128)(2,1)S(1)} %get-tuple-element.35.refs_0_), channel_id=1, source_target_pairs={{0,128},{8,136},{16,144},{24,152},{32,160},{40,168},{48,176},{56,1... | collective-permute-start | bytes 196616 | tf_op jit(solution)/shard_map/ppermute | solution.py:530
  46.9 29.3 %collective-permute-start.11 = (bf16[256,128]{1,0:T(8,128)(2,1)S(1)}, bf16[256,128]{1,0:T(8,128)(2,1)S(1)}, u32[]{:S(2)}, u32[]{:S(2)}) collective-permute-start(bf16[256,128]{1,0:T(8,128)(2,1)S(1)} %get-tuple-element.35.refs_0_), channel_id=1, source_target_pairs={{0,136},{8,128},{16,152},{24,144},{32,168},{40,160},{48,184},{56,1... | collective-permute-start | bytes 196616 | tf_op jit(solution)/shard_map/ppermute | solution.py:530
  75.1 5.5 %collective-permute-start.7 = (bf16[8,256,128]{2,1,0:T(8,128)(2,1)S(1)}, bf16[8,256,128]{2,1,0:T(8,128)(2,1)S(1)}, u32[]{:S(2)}, u32[]{:S(2)}) collective-permute-start(bf16[8,256,128]{2,1,0:T(8,128)(2,1)S(1)} %slice.4.own_ref), channel_id=1, source_target_pairs={{0,8},{8,0},{16,24},{24,16},{32,40},{40,32},{48,56},{56,48},{64,72... | collective-permute-start | bytes 1572872 | tf_op jit(solution)/shard_map/ppermute | solution.py:530
  75.2 14.3 %collective-permute-start.8 = (bf16[8,256,128]{2,1,0:T(8,128)(2,1)S(1)}, bf16[8,256,128]{2,1,0:T(8,128)(2,1)S(1)}, u32[]{:S(2)}, u32[]{:S(2)}) collective-permute-start(bf16[8,256,128]{2,1,0:T(8,128)(2,1)S(1)} %slice.4.own_ref), channel_id=1, source_target_pairs={{0,128},{8,136},{16,144},{24,152},{32,160},{40,168},{48,176},{56,1... | collective-permute-start | bytes 1572872 | tf_op jit(solution)/shard_map/ppermute | solution.py:530
  89.5 1.9 %collective-permute-start.12 = (bf16[8,256,128]{2,1,0:T(8,128)(2,1)S(1)}, bf16[8,256,128]{2,1,0:T(8,128)(2,1)S(1)}, u32[]{:S(2)}, u32[]{:S(2)}) collective-permute-start(bf16[8,256,128]{2,1,0:T(8,128)(2,1)S(1)} %collective-permute-done.8.y_ref), channel_id=1, source_target_pairs={{0,8},{8,0},{16,24},{24,16},{32,40},{40,32},{48,56},{56,48},{64,72... | collective-permute-start | bytes 1572872 | tf_op jit(solution)/shard_map/ppermute | solution.py:530
  120.7 23.2 %copy-start = (bf16[3,128,384]{2,1,0:T(8,128)(2,1)S(1)}, bf16[3,128,384]{2,1,0:T(8,128)(2,1)}, u32[]{:S(2)}) copy-start(bf16[3,128,384]{2,1,0:T(8,128)(2,1)} %video_ref.1) | copy-start | bytes 884740
  120.7 10.2 %collective-permute-start.18 = (bf16[384,384]{1,0:T(8,128)(2,1)S(1)}, bf16[384,384]{1,0:T(8,128)(2,1)S(1)}, u32[]{:S(2)}, u32[]{:S(2)}) collective-permute-start(bf16[384,384]{1,0:T(8,128)(2,1)S(1)} %get-tuple-element.48), channel_id=1, source_target_pairs={{0,1},{1,0},{2,3},{3,2},{4,5},{5,4},{6,7},{7,6},{8,9},{9,8},{10,11... | collective-permute-start | bytes 884744 | tf_op jit(solution)/shard_map/ppermute | solution.py:526
  121.5 11.2 %collective-permute-start.16 = (bf16[384,384]{1,0:T(8,128)(2,1)S(1)}, bf16[384,384]{1,0:T(8,128)(2,1)S(1)}, u32[]{:S(2)}, u32[]{:S(2)}) collective-permute-start(bf16[384,384]{1,0:T(8,128)(2,1)S(1)} %get-tuple-element.46), channel_id=1, source_target_pairs={{0,6},{1,7},{2,0},{3,1},{4,2},{5,3},{6,4},{7,5},{8,14},{9,15},{10,... | collective-permute-start | bytes 884744 | tf_op jit(solution)/shard_map/ppermute | solution.py:522
  122.4 10.3 %collective-permute-start.15 = (bf16[384,384]{1,0:T(8,128)(2,1)S(1)}, bf16[384,384]{1,0:T(8,128)(2,1)S(1)}, u32[]{:S(2)}, u32[]{:S(2)}) collective-permute-start(bf16[384,384]{1,0:T(8,128)(2,1)S(1)} %get-tuple-element.45), channel_id=1, source_target_pairs={{0,2},{1,3},{2,4},{3,5},{4,6},{5,7},{6,0},{7,1},{8,10},{9,11},{10,... | collective-permute-start | bytes 884744 | tf_op jit(solution)/shard_map/ppermute | solution.py:522
  124.8 18.9 %collective-permute-start.14 = (bf16[384,384]{1,0:T(8,128)(2,1)S(1)}, bf16[384,384]{1,0:T(8,128)(2,1)S(1)}, u32[]{:S(2)}, u32[]{:S(2)}) collective-permute-start(bf16[384,384]{1,0:T(8,128)(2,1)S(1)} %get-tuple-element.43), channel_id=1, source_target_pairs={{0,6},{1,7},{2,0},{3,1},{4,2},{5,3},{6,4},{7,5},{8,14},{9,15},{10,... | collective-permute-start | bytes 884744 | tf_op jit(solution)/shard_map/ppermute | solution.py:522
  124.8 18.9 %collective-permute-start.13 = (bf16[384,384]{1,0:T(8,128)(2,1)S(1)}, bf16[384,384]{1,0:T(8,128)(2,1)S(1)}, u32[]{:S(2)}, u32[]{:S(2)}) collective-permute-start(bf16[384,384]{1,0:T(8,128)(2,1)S(1)} %get-tuple-element.42), channel_id=1, source_target_pairs={{0,2},{1,3},{2,4},{3,5},{4,6},{5,7},{6,0},{7,1},{8,10},{9,11},{10,... | collective-permute-start | bytes 884744 | tf_op jit(solution)/shard_map/ppermute | solution.py:522
  130.9 12.8 %collective-permute-start.19 = (bf16[384,384]{1,0:T(8,128)(2,1)S(1)}, bf16[384,384]{1,0:T(8,128)(2,1)S(1)}, u32[]{:S(2)}, u32[]{:S(2)}) collective-permute-start(bf16[384,384]{1,0:T(8,128)(2,1)S(1)} %add_convert_fusion.1), channel_id=1, source_target_pairs={{0,4},{1,5},{2,6},{3,7},{4,0},{5,1},{6,2},{7,3},{8,12},{9,13},{10,... | collective-permute-start | bytes 884744 | tf_op jit(solution)/shard_map/ppermute | solution.py:522
  132.8 10.9 %collective-permute-start.17 = (bf16[384,384]{1,0:T(8,128)(2,1)S(1)}, bf16[384,384]{1,0:T(8,128)(2,1)S(1)}, u32[]{:S(2)}, u32[]{:S(2)}) collective-permute-start(bf16[384,384]{1,0:T(8,128)(2,1)S(1)} %add_convert_fusion.2), channel_id=1, source_target_pairs={{0,1},{1,0},{2,3},{3,2},{4,5},{5,4},{6,7},{7,6},{8,9},{9,8},{10,11... | collective-permute-start | bytes 884744 | tf_op jit(solution)/shard_map/ppermute | solution.py:526

commit v5 on v4

--- a/solution.py
+++ b/solution.py
@@ -1,3 +1,5 @@
+import functools
+
 import jax
 import jax.numpy as jnp
 import numpy as np
@@ -286,25 +288,53 @@
     return pl.ds(pl.multiple_of(pl.program_id(0) * TILE, TILE), TILE)
 
 
+def gather_rows(q, pieces, score_ref, before):
+    top = jnp.full((TILE, 128), -jnp.inf, jnp.float32)
+    column = 0
+    for keys, _, valid in pieces:
+        if valid is None:
+            top = score_keys(q, keys, score_ref, column, top)
+        else:
+            top = score_text(q, keys, valid, score_ref, column, top)
+        column += keys.shape[0]
+    top = jnp.max(top, axis=1, keepdims=True) * EXP_SCALE
+    if before is not None:
+        top = jnp.maximum(top, before)
+    total = jnp.zeros((TILE, 128), jnp.float32)
+    mixed = jnp.zeros((TILE, HD), jnp.float32)
+    column = 0
+    for _, values, _ in pieces:
+        stop = column + values.shape[0]
+        weights = jnp.exp2(score_ref[:, column:stop] * EXP_SCALE - top)
+        for lane in range(0, stop - column, 128):
+            total += weights[:, lane : lane + 128]
+        mixed += jnp.dot(weights.astype(jnp.bfloat16), values, preferred_element_type=jnp.float32)
+        column = stop
+    return top, total, mixed
+
+
+def set_piece(ref):
+    return set_keys(ref), set_values(ref), None
+
+
 def attend_near_kernel(
     where_ref, q_ref, own_ref, core_ref, text_ref, w_hbm,
-    mixed_ref, top_ref, q_out_ref, w_ref, score_ref, value_ref, sem,
+    mixed_ref, total_ref, top_ref, q_out_ref, w_ref, score_ref, sem,
 ):
     copy = pltpu.make_async_copy(w_hbm, w_ref, sem)
 
     @pl.when(first_step())
     def _():
         copy.start()
-        lay_values(value_ref, [set_values(own_ref), set_values(core_ref), text_ref[1, 0]])
 
     q = q_ref[...].reshape(TILE, HD)
-    top = jnp.full((TILE, 128), -jnp.inf, jnp.float32)
-    for n, ref in enumerate((own_ref, core_ref)):
-        top = score_keys(q, set_keys(ref), score_ref, n * SET, top)
-    top = score_text(q, text_ref[0, 0], where_ref[2], score_ref, 2 * SET, top)
-    top = jnp.max(top, axis=1, keepdims=True) * EXP_SCALE
+    text = (text_ref[0, 0], text_ref[1, 0], where_ref[2])
+    top, total, mixed = gather_rows(
+        q, [set_piece(own_ref), set_piece(core_ref), text], score_ref, None
+    )
     here = tile_rows()
-    mixed_ref[here, :] = mix(score_ref, value_ref, top, 2 * SET + TXT)
+    mixed_ref[here, :] = mixed
+    total_ref[here, :] = total
     top_ref[here, :] = jnp.broadcast_to(top, (TILE, 128))
     q_out_ref[here, :] = q
 
@@ -313,15 +343,13 @@
         copy.wait()
 
 
+STATE = (pltpu.VMEM((SET, HD), jnp.float32),) * 3
+
+
 def attend_near(where, received, own, core, text_kv, w_out):
     return pl.pallas_call(
         attend_near_kernel,
-        out_shape=(
-            pltpu.VMEM((SET, 2 * HD), jnp.float32),
-            pltpu.VMEM((SET, 128), jnp.float32),
-            pltpu.VMEM((SET, HD), jnp.bfloat16),
-            pltpu.VMEM(w_out.shape, w_out.dtype),
-        ),
+        out_shape=STATE + (pltpu.VMEM((SET, HD), jnp.bfloat16), pltpu.VMEM(w_out.shape, w_out.dtype)),
         grid_spec=pltpu.PrefetchScalarGridSpec(
             num_scalar_prefetch=1,
             grid=(SET // TILE,),
@@ -332,10 +360,9 @@
                 pl.BlockSpec((2, 1, TXT, HD), lambda i, w: (0, w[0], 0, w[1])),
                 pl.BlockSpec(memory_space=pltpu.HBM),
             ],
-            out_specs=(IN_VMEM,) * 4,
+            out_specs=(IN_VMEM,) * 5,
             scratch_shapes=[
                 pltpu.VMEM((TILE, 2 * SET + TXT), jnp.float32),
-                pltpu.VMEM((2 * SET + TXT, 2 * HD), jnp.bfloat16),
                 pltpu.SemaphoreType.DMA(()),
             ],
         ),
@@ -427,48 +454,48 @@
     )(where, received, keys, values)
 
 
-def attend_far_kernel(
-    q_ref, y_ref, diagonal_ref, last_ref, mixed_ref, top_ref, out_ref, score_ref, value_ref
-):
-    @pl.when(first_step())
-    def _():
-        lay_values(value_ref, [set_values(y_ref), set_values(diagonal_ref)])
-
+def attend_far_kernel(finish, q_ref, set_ref, *refs):
+    mixed_in, total_in, top_in, *refs = refs
     here = tile_rows()
-    q = q_ref[here, :]
-    top = jnp.full((TILE, 128), -jnp.inf, jnp.float32)
-    for n, ref in enumerate((y_ref, diagonal_ref)):
-        top = score_keys(q, set_keys(ref), score_ref, n * SET, top)
-    before = top_ref[here, 0:1]
-    top = jnp.maximum(jnp.max(top, axis=1, keepdims=True) * EXP_SCALE, before)
-    mixed = mix(score_ref, value_ref, top, 2 * SET) + mixed_ref[here, :] * jnp.exp2(before - top)
-    result = mixed[:, :HD] / mixed[:, HD : HD + 1]
-    frames = pl.ds(pl.program_id(0) * QUAD, QUAD)
-    out_ref[frames, 0:TOK, :] = result.astype(jnp.bfloat16).reshape(QUAD, TOK, HD)
-    out_ref[frames, TOK:RETURN, :] = last_ref[frames]
-
-
-def attend_far(queries, over_y, diagonal, last, mixed, top):
+    before = top_in[here, 0:1]
+    score_ref = refs[-1]
+    top, total, mixed = gather_rows(q_ref[here, :], [set_piece(set_ref)], score_ref, before)
+    decay = jnp.exp2(before - top)
+    total += total_in[here, :] * decay
+    mixed += mixed_in[here, :] * decay
+    if finish:
+        last_ref, out_ref = refs[:2]
+        result = (mixed / jnp.sum(total, axis=1, keepdims=True)).astype(jnp.bfloat16)
+        frames = pl.ds(pl.program_id(0) * QUAD, QUAD)
+        out_ref[frames, 0:TOK, :] = result.reshape(QUAD, TOK, HD)
+        out_ref[frames, TOK:RETURN, :] = last_ref[frames]
+    else:
+        mixed_ref, total_ref, top_ref = refs[:3]
+        mixed_ref[here, :] = mixed
+        total_ref[here, :] = total
+        top_ref[here, :] = jnp.broadcast_to(top, (TILE, 128))
+
+
+def attend_far(queries, keys, state, last=None):
+    finish = last is not None
+    operands = [queries, keys, *state] + ([last] if finish else [])
     return pl.pallas_call(
-        attend_far_kernel,
-        out_shape=pltpu.VMEM((RING, RETURN, HD), jnp.bfloat16),
+        functools.partial(attend_far_kernel, finish),
+        out_shape=pltpu.VMEM((RING, RETURN, HD), jnp.bfloat16) if finish else STATE,
         grid=(SET // TILE,),
-        in_specs=[IN_VMEM] * 6,
-        out_specs=IN_VMEM,
-        scratch_shapes=[
-            pltpu.VMEM((TILE, 2 * SET), jnp.float32),
-            pltpu.VMEM((2 * SET, 2 * HD), jnp.bfloat16),
-        ],
-        compiler_params=pltpu.CompilerParams(vmem_limit_bytes=18 * MIB),
+        in_specs=[IN_VMEM] * len(operands),
+        out_specs=IN_VMEM if finish else (IN_VMEM,) * 3,
+        scratch_shapes=[pltpu.VMEM((TILE, SET), jnp.float32)],
+        compiler_params=pltpu.CompilerParams(vmem_limit_bytes=16 * MIB),
         cost_estimate=pl.CostEstimate(
-            flops=4 * SET * 2048 * HD, bytes_accessed=4_000_000, transcendentals=SET * 2048
+            flops=4 * SET * SET * HD, bytes_accessed=3_000_000, transcendentals=SET * SET
         ),
         name="attend_far",
-    )(*map(in_vmem, (queries, over_y, diagonal, last, mixed, top)))
+    )(*map(in_vmem, operands))
 
 
 def output_kernel(place_ref, back_ref, w_ref, *refs):
-    out_refs, attn_ref = refs[:HEAD_AXIS], refs[HEAD_AXIS]
+    out_refs, attn_ref = refs[:-1], refs[-1]
     for p in range(RING):
         b, hd = divmod(p, HEADS_HERE)
         attn_ref[b * TOK : (b + 1) * TOK, hd * HD : (hd + 1) * HD] = back_ref[p, 0:TOK, :]
@@ -487,18 +514,22 @@
         total += weight
         mixed += weight * back_ref[p, TOK : 2 * TOK, :].astype(jnp.float32)
     attn_ref[(BRANCH - 1) * TOK :, (HEADS_HERE - 1) * HD :] = (mixed / total).astype(jnp.bfloat16)
-    for s in range(HEAD_AXIS):
+    targets = [(0, 0), (1, 0), (2, 0), (3, 0), (2, 1), (3, 1), (4, 0), (5, 0)]
+    for s, (n, half) in enumerate(targets):
         start = pl.multiple_of(place_ref[s] * DSH, DSH)
-        out_refs[s][...] = jnp.dot(
+        out_refs[n][half * ROWS : (half + 1) * ROWS, :] = jnp.dot(
             attn_ref[...], w_ref[:, pl.ds(start, DSH)], preferred_element_type=jnp.float32
         ).astype(jnp.bfloat16)
+
+
+PART_ROWS = (ROWS, ROWS, 2 * ROWS, 2 * ROWS, ROWS, ROWS)
 
 
 def output(places, back, w_out):
     return pl.pallas_call(
         output_kernel,
         out_shape=tuple(
-            pltpu.VMEM((ROWS, DSH), jnp.bfloat16) for _ in range(HEAD_AXIS)
+            pltpu.VMEM((rows, DSH), jnp.bfloat16) for rows in PART_ROWS
         ),
         grid_spec=pltpu.PrefetchScalarGridSpec(
             num_scalar_prefetch=1,
@@ -507,7 +538,7 @@
                 IN_VMEM,
                 IN_VMEM,
             ],
-            out_specs=(IN_VMEM,) * HEAD_AXIS,
+            out_specs=(IN_VMEM,) * len(PART_ROWS),
             scratch_shapes=[pltpu.VMEM((ROWS, DSH), jnp.bfloat16)],
         ),
         compiler_params=pltpu.CompilerParams(vmem_limit_bytes=24 * MIB),
@@ -555,12 +586,13 @@
 
 
 def scatter_head(parts):
-    for_opposite = head_partner(parts[7])
-    for_partner = [head_move(parts[4], 2), head_move(parts[5], -2)]
-    direct = [head_move(parts[2], 2), head_move(parts[3], -2)]
-    over_y = head_partner(add(parts[1], *for_partner).astype(jnp.bfloat16))
-    across = head_move(add(parts[6], for_opposite).astype(jnp.bfloat16), 4)
-    return add(parts[0], *direct, over_y, across)
+    own, partner, ahead, behind, opposite, over = parts
+    for_opposite = head_partner(over)
+    near = [head_move(ahead, 2), head_move(behind, -2)]
+    across = head_move(add(opposite, for_opposite).astype(jnp.bfloat16), 4)
+    for_partner = [x[ROWS:] for x in near]
+    over_y = head_partner(add(partner, *for_partner).astype(jnp.bfloat16))
+    return add(own, *(x[:ROWS] for x in near), over_y, across)
 
 
 def body(
@@ -594,12 +626,14 @@
     last_keys, last_values = lay_last(where, lasts, text_kv)
     near = received[:, : 2 * TOK]
     over_y = frame_move(near, FRAMES // 2)
-    over_core = frame_move(near, 1)
+    near_later, last_keys = lax.optimization_barrier((near, last_keys))
+    over_core = frame_move(near_later, 1)
     ninth = attend_last(where, received, last_keys, last_values)
-    mixed, top, queries, w_held = attend_near(where, received, near, over_core, text_kv, in_hbm(w_out))
-    over_y, _, _ = lax.optimization_barrier((over_y, mixed, ninth))
+    *state, queries, w_held = attend_near(where, received, near, over_core, text_kv, in_hbm(w_out))
+    over_y, _, _ = lax.optimization_barrier((over_y, state[0], ninth))
     diagonal = frame_move(over_y, 1)
-    returned = attend_far(queries, over_y, diagonal, ninth, mixed, top)
+    state = attend_far(queries, over_y, state)
+    returned = attend_far(queries, diagonal, state, ninth)
     partial = output(places, over_rings(returned), w_held)
     proj = scatter_head(partial).reshape(video.shape)
     return (video.astype(jnp.float32) + gate * proj).astype(jnp.bfloat16)

time: 147 us -> 153 us (1.041); the launches traced: 145 us -> 152 us
  waiting for transfers between devices: 54.2 us -> 66.7 us
  starting transfers between devices: 36.2 us -> 29.8 us
    ppermute x4, waiting for transfers between devices: 5.51 us -> 18.9 us  [head_partner(): return lax.ppermute(x, 'head', [(i, i ^ 1) for i in range(HEAD_AXIS)])]
    all_to_all x1, waiting for transfers between devices: 27.1 us -> 22.1 us  [over_rings(): return lax.all_to_all(x, 'frame', 0, 0, axis_index_groups=rings, tiled=True)]
    ppermute x10 -> x8, starting transfers between devices: 15.8 us -> 11.5 us  [head_move(): lax.ppermute(x, 'head', [(i, (i + step) % HEAD_AXIS) for i in range(HEAD_...]
    ppermute x6, waiting for transfers between devices: 3.52 us -> 6.57 us  [frame_move(): return lax.ppermute(x, 'frame', [(i, i ^ flip) for i in range(FRAMES)])]
    ppermute x4, starting transfers between devices: 9 us -> 6.93 us  [head_partner(): return lax.ppermute(x, 'head', [(i, i ^ 1) for i in range(HEAD_AXIS)])]
    ppermute x10 -> x8, waiting for transfers between devices: 18.1 us -> 19.2 us  [head_move(): lax.ppermute(x, 'head', [(i, (i + step) % HEAD_AXIS) for i in range(HEAD_...]
    pallas_call x3 -> x4, Pallas kernels: 15.3 us -> 16.4 us  [the longest x1 7.36 us: attend_near(): pl.pallas_call(attend_near_kernel, out_shape=STATE + (pltpu.VMEM((SET, HD...]
  transfers between devices with their start and end apart: 21 -> 19, of which waited for: 10 -> 12; matrix products, arithmetic and copies ran while one was open for 1% -> 1% of each run, Pallas kernels for 8% -> 10%
where the time goes in v5:
time: 153 us; the launch traced here: 152 us
  waiting for transfers between devices  66.7 us (44%)
  Pallas kernels  31.2 us (20%)
  starting transfers between devices  29.8 us (19%)
  blocking collectives  21.5 us (14%)
  other arithmetic  2.21 us (1%)
    all_to_all x1, waiting for transfers between devices, over_rings(): return lax.all_to_all(x, 'frame', 0, 0, axis_index_groups=rings, tiled=True)  22.1 us
    all_to_all x1, blocking collectives, over_rings(): return lax.all_to_all(x, 'frame', 0, 0, axis_index_groups=rings, tiled=True)  21.5 us
    ppermute x8, waiting for transfers between devices, head_move(): lax.ppermute(x, 'head', [(i, (i + step) % HEAD_AXIS) for i in range(HEAD_...  19.2 us
    ppermute x4, waiting for transfers between devices, head_partner(): return lax.ppermute(x, 'head', [(i, i ^ 1) for i in range(HEAD_AXIS)])  18.9 us
    ppermute x8, starting transfers between devices, head_move(): lax.ppermute(x, 'head', [(i, (i + step) % HEAD_AXIS) for i in range(HEAD_...  11.5 us
    all_to_all x1, starting transfers between devices, over_rings(): return lax.all_to_all(x, 'frame', 0, 0, axis_index_groups=rings, tiled=True)  8.48 us
    pallas_call x1, Pallas kernels, project(): pl.pallas_call(project_kernel, out_shape=(pltpu.VMEM((RING, 4 * TOK, HD),...  7.91 us
    pallas_call x1, Pallas kernels, attend_near(): pl.pallas_call(attend_near_kernel, out_shape=STATE + (pltpu.VMEM((SET, HD...  7.36 us
  transfers between devices with their start and end apart: 19, of which 12 were waited for; matrix products, arithmetic and copies ran while one was open for 1% of the time, Pallas kernels for 10%

profile of v5, /device:TPU:6, one launch (start us, length us, event | category | flops | bytes accessed | tf_op | source)
XLA Modules:
  0.0 152.2 jit_solution(16545564090335326499)
XLA Ops:
  0.7 2.4 %prep.1 = (bf16[400,384]{1,0:T(8,128)(2,1)S(1)}, f32[1,384]{1,0:T(1,128)S(1)}, f32[2,128]{1,0:T(2,128)S(1)}, s32[8]{0:T(128)S(1)}, s32[5]{0:T(128)S(1)}) custom-call(s32[1]{0:T(128)} %bitcast.frame_ref, s32[1]{0:T(128)} %bitcast.1.head_ref, s32[1]{0:T(128)S(6)} %copy.13.shift_ref, s32[32]{0:T(128)} %ids_ref.1, s32[3]{0:T(128)} %lengths_ref.1, ...), custom_call_target="tpu_custom_call" | custom-call | tf_op jit(solution)/shard_map/prep/pallas_call | solution.py:109
  3.0 3.3 %collective-permute-start = (bf16[400,384]{1,0:T(8,128)(2,1)S(1)}, bf16[400,384]{1,0:T(8,128)(2,1)S(1)}, u32[]{:S(2)}, u32[]{:S(2)}) collective-permute-start(bf16[400,384]{1,0:T(8,128)(2,1)S(1)} %get-tuple-element.34.refs_0_), channel_id=1, source_target_pairs={{0,1},{1,0},{2,3},{3,2},{4,5},{5,4},{6,7},{7,6},{8,9},{9,8},{10,11... | collective-permute-start | bytes 921608 | tf_op jit(solution)/shard_map/ppermute | solution.py:557
  6.3 1.4 collective-permute-start.5
  7.7 3.2 %collective-permute-start.2 = (bf16[400,384]{1,0:T(8,128)(2,1)S(1)}, bf16[400,384]{1,0:T(8,128)(2,1)S(1)}, u32[]{:S(2)}, u32[]{:S(2)}) collective-permute-start(bf16[400,384]{1,0:T(8,128)(2,1)S(1)} %get-tuple-element.34.refs_0_), channel_id=1, source_target_pairs={{0,2},{1,3},{2,4},{3,5},{4,6},{5,7},{6,0},{7,1},{8,10},{9,11},{10,... | collective-permute-start | bytes 921608 | tf_op jit(solution)/shard_map/ppermute | solution.py:553
  10.9 2.7 %collective-permute-done.refs_1_ = bf16[400,384]{1,0:T(8,128)(2,1)S(1)} collective-permute-done((bf16[400,384]{1,0:T(8,128)(2,1)S(1)}, bf16[400,384]{1,0:T(8,128)(2,1)S(1)}, u32[]{:S(2)}, u32[]{:S(2)}) %collective-permute-start) | collective-permute-done | bytes 307232 | tf_op jit(solution)/shard_map/ppermute | solution.py:557
  14.5 2.4 %collective-permute-start.4 = (bf16[400,384]{1,0:T(8,128)(2,1)S(1)}, bf16[400,384]{1,0:T(8,128)(2,1)S(1)}, u32[]{:S(2)}, u32[]{:S(2)}) collective-permute-start(bf16[400,384]{1,0:T(8,128)(2,1)S(1)} %collective-permute-done.refs_1_), channel_id=1, source_target_pairs={{0,2},{1,3},{2,4},{3,5},{4,6},{5,7},{6,0},{7,1},{8,10},{9,11},{10,... | collective-permute-start | bytes 921608 | tf_op jit(solution)/shard_map/ppermute | solution.py:553
  16.9 1.2 collective-permute-done.5.refs_6_
  18.0 2.0 %collective-permute-start.6 = (bf16[400,384]{1,0:T(8,128)(2,1)S(1)}, bf16[400,384]{1,0:T(8,128)(2,1)S(1)}, u32[]{:S(2)}, u32[]{:S(2)}) collective-permute-start(bf16[400,384]{1,0:T(8,128)(2,1)S(1)} %collective-permute-done.5.refs_6_), channel_id=1, source_target_pairs={{0,1},{1,0},{2,3},{3,2},{4,5},{5,4},{6,7},{7,6},{8,9},{9,8},{10,11... | collective-permute-start | bytes 921608 | tf_op jit(solution)/shard_map/ppermute | solution.py:557
  20.1 1.0 sine_multiply_fusion
  21.1 2.1 %collective-permute-done.1.refs_2_ = bf16[400,384]{1,0:T(8,128)(2,1)S(1)} collective-permute-done((bf16[400,384]{1,0:T(8,128)(2,1)S(1)}, bf16[400,384]{1,0:T(8,128)(2,1)S(1)}, u32[]{:S(2)}, u32[]{:S(2)}) %collective-permute-start.1) | collective-permute-done | bytes 307232 | tf_op jit(solution)/shard_map/ppermute | solution.py:553
  23.2 6.5 %collective-permute-done.3.refs_4_ = bf16[400,384]{1,0:T(8,128)(2,1)S(1)} collective-permute-done((bf16[400,384]{1,0:T(8,128)(2,1)S(1)}, bf16[400,384]{1,0:T(8,128)(2,1)S(1)}, u32[]{:S(2)}, u32[]{:S(2)}) %collective-permute-start.3) | collective-permute-done | bytes 307232 | tf_op jit(solution)/shard_map/ppermute | solution.py:553
  29.7 7.9 %project.1 = (bf16[8,512,128]{2,1,0:T(8,128)(2,1)}, bf16[256,128]{1,0:T(8,128)(2,1)S(1)}) custom-call(s32[8]{0:T(128)S(1)} %get-tuple-element.32.place_ref, bf16[400,384]{1,0:T(8,128)(2,1)S(1)} %get-tuple-element.34.refs_0_, bf16[400,384]{1,0:T(8,128)(2,1)S(1)} %collective-permute-done.refs_1_, bf16[400,384]{1,0:T(8,128)(2,1)S(1)} %collective-permute-done.1.refs_2_, ...), custom_call_target="tpu_custom_call" | custom-call | flops 2717908992 | bytes 12000000 | tf_op jit(solution)/shard_map/project/pallas_call | solution.py:206
  37.6 8.5 %all-to-all-start = ((bf16[8,512,128]{2,1,0:T(8,128)(2,1)}), bf16[8,512,128]{2,1,0:T(8,128)(2,1)S(1)}, u32[]{:S(2)}, u32[]{:S(2)}) async-start(bf16[8,512,128]{2,1,0:T(8,128)(2,1)} %get-tuple-element.36), calls=%async_computation | async-start | bytes 2097152 | tf_op jit(solution)/shard_map/all_to_all | solution.py:621
  46.9 1.1 collective-permute-start.9
  48.0 3.1 %collective-permute-done.8.refs_2_ = bf16[256,128]{1,0:T(8,128)(2,1)S(1)} collective-permute-done((bf16[256,128]{1,0:T(8,128)(2,1)S(1)}, bf16[256,128]{1,0:T(8,128)(2,1)S(1)}, u32[]{:S(2)}, u32[]{:S(2)}) %collective-permute-start.8) | collective-permute-done | bytes 65568 | tf_op jit(solution)/shard_map/ppermute | solution.py:561
  51.6 1.4 lay_last.1
  53.0 22.1 %all-to-all-done.q_ref = bf16[8,512,128]{2,1,0:T(8,128)(2,1)S(1)} async-done(((bf16[8,512,128]{2,1,0:T(8,128)(2,1)}), bf16[8,512,128]{2,1,0:T(8,128)(2,1)S(1)}, u32[]{:S(2)}, u32[]{:S(2)}) %all-to-all-start) | async-done | bytes 1048608 | tf_op jit(solution)/shard_map/all_to_all | solution.py:621
  75.2 0.9 collective-permute-start.11
  76.2 3.0 %attend_last.1.refs_3_ = bf16[8,144,128]{2,1,0:T(8,128)(2,1)S(1)} custom-call(s32[5]{0:T(128)S(1)} %get-tuple-element.33.where_ref, bf16[8,512,128]{2,1,0:T(8,128)(2,1)S(1)} %all-to-all-done.q_ref, bf16[640,128]{1,0:T(8,128)(2,1)S(1)} %get-tuple-element.42.keys_ref, bf16[640,256]{1,0:T(8,128)(2,1)S(1)} %get-tuple-element.43.value_ref), custom_call_target="tpu_custom_call" | custom-call | flops 335544320 | bytes 1000000 | tf_op jit(solution)/shard_map/attend_last/pallas_call | solution.py:435
  79.2 7.4 %attend_near.1 = (f32[1024,128]{1,0:T(8,128)S(1)}, f32[1024,128]{1,0:T(8,128)S(1)}, f32[1024,128]{1,0:T(8,128)S(1)}, bf16[1024,128]{1,0:T(8,128)(2,1)S(1)}, bf16[384,3072]{1,0:T(8,128)(2,1)S(1)}) custom-call(s32[5]{0:T(128)S(1)} %get-tuple-element.33.where_ref, bf16[8,512,128]{2,1,0:T(8,128)(2,1)S(1)} %all-to-all-done.q_ref, ...), custom_call_target="tpu_custom_call" | custom-call | flops 1207959552 | bytes 3000000 | tf_op jit(solution)/shard_map/attend_near/pallas_call | solution.py:350
  86.5 3.0 %collective-permute-done.11.set_ref = bf16[8,256,128]{2,1,0:T(8,128)(2,1)S(1)} collective-permute-done((bf16[8,256,128]{2,1,0:T(8,128)(2,1)S(1)}, bf16[8,256,128]{2,1,0:T(8,128)(2,1)S(1)}, u32[]{:S(2)}, u32[]{:S(2)}) %collective-permute-start.11) | collective-permute-done | bytes 524320 | tf_op jit(solution)/shard_map/ppermute | solution.py:561
  89.5 3.4 %attend_far.2 = (f32[1024,128]{1,0:T(8,128)S(1)}, f32[1024,128]{1,0:T(8,128)S(1)}, f32[1024,128]{1,0:T(8,128)S(1)}) custom-call(bf16[1024,128]{1,0:T(8,128)(2,1)S(1)} %get-tuple-element.40.q_ref, bf16[8,256,128]{2,1,0:T(8,128)(2,1)S(1)} %collective-permute-done.11.set_ref, f32[1024,128]{1,0:T(8,128)S(1)} %get-tuple-element.41.refs_0_, ...), custom_call_target="tpu_custom_call" | custom-call | flops 536870912 | bytes 3000000 | tf_op jit(solution)/shard_map/attend_far/pallas_call | solution.py:482
  93.0 3.3 %attend_far.3 = bf16[8,272,128]{2,1,0:T(8,128)(2,1)S(1)} custom-call(bf16[1024,128]{1,0:T(8,128)(2,1)S(1)} %get-tuple-element.40.q_ref, bf16[8,256,128]{2,1,0:T(8,128)(2,1)S(1)} %collective-permute-done.12.set_ref, f32[1024,128]{1,0:T(8,128)S(1)} %get-tuple-element.47.refs_0_, f32[1024,128]{1,0:T(8,128)S(1)} %get-tuple-element.48.refs_1_, ...), custom_call_target="tpu_custom_call" | custom-call | flops 536870912 | bytes 3000000 | tf_op jit(solution)/shard_map/attend_far/pallas_call | solution.py:482
  96.3 21.5 %all_to_all.10.back_ref = bf16[8,272,128]{2,1,0:T(8,128)(2,1)S(1)} all-to-all(bf16[8,272,128]{2,1,0:T(8,128)(2,1)S(1)} %attend_far.3), channel_id=1, replica_groups={{0,16,32,48,64,80,96,112},{8,24,40,56,72,88,104,120},{128,144,160,176,1..., dimensions={0} | all-to-all | bytes 1114112 | tf_op jit(solution)/shard_map/all_to_all | solution.py:621
  117.8 2.3 %output.1 = (bf16[384,384]{1,0:T(8,128)(2,1)S(1)}, bf16[384,384]{1,0:T(8,128)(2,1)S(1)}, bf16[768,384]{1,0:T(8,128)(2,1)S(1)}, bf16[768,384]{1,0:T(8,128)(2,1)S(...) custom-call(s32[8]{0:T(128)S(1)} %get-tuple-element.32.place_ref, ...), custom_call_target="tpu_custom_call" | custom-call | flops 905969664 | bytes 5000000 | tf_op jit(solution)/shard_map/output/pallas_call | solution.py:529
  120.7 1.6 %collective-permute-start.14 = (bf16[768,384]{1,0:T(8,128)(2,1)S(1)}, bf16[768,384]{1,0:T(8,128)(2,1)S(1)}, u32[]{:S(2)}, u32[]{:S(2)}) collective-permute-start(bf16[768,384]{1,0:T(8,128)(2,1)S(1)} %get-tuple-element.53), channel_id=1, source_target_pairs={{0,6},{1,7},{2,0},{3,1},{4,2},{5,3},{6,4},{7,5},{8,14},{9,15},{10,... | collective-permute-start | bytes 1769480 | tf_op jit(solution)/shard_map/ppermute | solution.py:553
  123.0 8.8 %collective-permute-done.16 = bf16[384,384]{1,0:T(8,128)(2,1)S(1)} collective-permute-done((bf16[384,384]{1,0:T(8,128)(2,1)S(1)}, bf16[384,384]{1,0:T(8,128)(2,1)S(1)}, u32[]{:S(2)}, u32[]{:S(2)}) %collective-permute-start.16) | collective-permute-done | bytes 294944 | tf_op jit(solution)/shard_map/ppermute | solution.py:557
  131.9 1.5 collective-permute-start.17
  133.4 3.1 %collective-permute-done.13 = bf16[768,384]{1,0:T(8,128)(2,1)S(1)} collective-permute-done((bf16[768,384]{1,0:T(8,128)(2,1)S(1)}, bf16[768,384]{1,0:T(8,128)(2,1)S(1)}, u32[]{:S(2)}, u32[]{:S(2)}) %collective-permute-start.13) | collective-permute-done | bytes 589856 | tf_op jit(solution)/shard_map/ppermute | solution.py:553
  136.5 6.3 %collective-permute-done.14 = bf16[768,384]{1,0:T(8,128)(2,1)S(1)} collective-permute-done((bf16[768,384]{1,0:T(8,128)(2,1)S(1)}, bf16[768,384]{1,0:T(8,128)(2,1)S(1)}, u32[]{:S(2)}, u32[]{:S(2)}) %collective-permute-start.14) | collective-permute-done | bytes 589856 | tf_op jit(solution)/shard_map/ppermute | solution.py:553
  143.0 0.9 collective-permute-start.15
  143.9 7.4 %collective-permute-done.15 = bf16[384,384]{1,0:T(8,128)(2,1)S(1)} collective-permute-done((bf16[384,384]{1,0:T(8,128)(2,1)S(1)}, bf16[384,384]{1,0:T(8,128)(2,1)S(1)}, u32[]{:S(2)}, u32[]{:S(2)}) %collective-permute-start.15) | collective-permute-done | bytes 294944 | tf_op jit(solution)/shard_map/ppermute | solution.py:557
  (25 shorter events, 4.6 us)
Async XLA Ops:
  3.0 10.6 %collective-permute-start = (bf16[400,384]{1,0:T(8,128)(2,1)S(1)}, bf16[400,384]{1,0:T(8,128)(2,1)S(1)}, u32[]{:S(2)}, u32[]{:S(2)}) collective-permute-start(bf16[400,384]{1,0:T(8,128)(2,1)S(1)} %get-tuple-element.34.refs_0_), channel_id=1, source_target_pairs={{0,1},{1,0},{2,3},{3,2},{4,5},{5,4},{6,7},{7,6},{8,9},{9,8},{10,11... | collective-permute-start | bytes 921608 | tf_op jit(solution)/shard_map/ppermute | solution.py:557
  6.3 11.7 %collective-permute-start.5 = (bf16[400,384]{1,0:T(8,128)(2,1)S(1)}, bf16[400,384]{1,0:T(8,128)(2,1)S(1)}, u32[]{:S(2)}, u32[]{:S(2)}) collective-permute-start(bf16[400,384]{1,0:T(8,128)(2,1)S(1)} %get-tuple-element.34.refs_0_), channel_id=1, source_target_pairs={{0,4},{1,5},{2,6},{3,7},{4,0},{5,1},{6,2},{7,3},{8,12},{9,13},{10,... | collective-permute-start | bytes 921608 | tf_op jit(solution)/shard_map/ppermute | solution.py:553
  7.7 15.5 %collective-permute-start.1 = (bf16[400,384]{1,0:T(8,128)(2,1)S(1)}, bf16[400,384]{1,0:T(8,128)(2,1)S(1)}, u32[]{:S(2)}, u32[]{:S(2)}) collective-permute-start(bf16[400,384]{1,0:T(8,128)(2,1)S(1)} %get-tuple-element.34.refs_0_), channel_id=1, source_target_pairs={{0,6},{1,7},{2,0},{3,1},{4,2},{5,3},{6,4},{7,5},{8,14},{9,15},{10,... | collective-permute-start | bytes 921608 | tf_op jit(solution)/shard_map/ppermute | solution.py:553
  7.7 15.5 %collective-permute-start.2 = (bf16[400,384]{1,0:T(8,128)(2,1)S(1)}, bf16[400,384]{1,0:T(8,128)(2,1)S(1)}, u32[]{:S(2)}, u32[]{:S(2)}) collective-permute-start(bf16[400,384]{1,0:T(8,128)(2,1)S(1)} %get-tuple-element.34.refs_0_), channel_id=1, source_target_pairs={{0,2},{1,3},{2,4},{3,5},{4,6},{5,7},{6,0},{7,1},{8,10},{9,11},{10,... | collective-permute-start | bytes 921608 | tf_op jit(solution)/shard_map/ppermute | solution.py:553
  13.6 16.1 %collective-permute-start.3 = (bf16[400,384]{1,0:T(8,128)(2,1)S(1)}, bf16[400,384]{1,0:T(8,128)(2,1)S(1)}, u32[]{:S(2)}, u32[]{:S(2)}) collective-permute-start(bf16[400,384]{1,0:T(8,128)(2,1)S(1)} %collective-permute-done.refs_1_), channel_id=1, source_target_pairs={{0,6},{1,7},{2,0},{3,1},{4,2},{5,3},{6,4},{7,5},{8,14},{9,15},{10,... | collective-permute-start | bytes 921608 | tf_op jit(solution)/shard_map/ppermute | solution.py:553
  14.5 15.3 %collective-permute-start.4 = (bf16[400,384]{1,0:T(8,128)(2,1)S(1)}, bf16[400,384]{1,0:T(8,128)(2,1)S(1)}, u32[]{:S(2)}, u32[]{:S(2)}) collective-permute-start(bf16[400,384]{1,0:T(8,128)(2,1)S(1)} %collective-permute-done.refs_1_), channel_id=1, source_target_pairs={{0,2},{1,3},{2,4},{3,5},{4,6},{5,7},{6,0},{7,1},{8,10},{9,11},{10,... | collective-permute-start | bytes 921608 | tf_op jit(solution)/shard_map/ppermute | solution.py:553
  18.0 11.7 %collective-permute-start.6 = (bf16[400,384]{1,0:T(8,128)(2,1)S(1)}, bf16[400,384]{1,0:T(8,128)(2,1)S(1)}, u32[]{:S(2)}, u32[]{:S(2)}) collective-permute-start(bf16[400,384]{1,0:T(8,128)(2,1)S(1)} %collective-permute-done.5.refs_6_), channel_id=1, source_target_pairs={{0,1},{1,0},{2,3},{3,2},{4,5},{5,4},{6,7},{7,6},{8,9},{9,8},{10,11... | collective-permute-start | bytes 921608 | tf_op jit(solution)/shard_map/ppermute | solution.py:557
  37.6 37.4 %all-to-all-start = ((bf16[8,512,128]{2,1,0:T(8,128)(2,1)}), bf16[8,512,128]{2,1,0:T(8,128)(2,1)S(1)}, u32[]{:S(2)}, u32[]{:S(2)}) async-start(bf16[8,512,128]{2,1,0:T(8,128)(2,1)} %get-tuple-element.36), calls=%async_computation | async-start | bytes 2097152 | tf_op jit(solution)/shard_map/all_to_all | solution.py:621
  46.1 1.9 %collective-permute-start.7 = (bf16[256,128]{1,0:T(8,128)(2,1)S(1)}, bf16[256,128]{1,0:T(8,128)(2,1)S(1)}, u32[]{:S(2)}, u32[]{:S(2)}) collective-permute-start(bf16[256,128]{1,0:T(8,128)(2,1)S(1)} %get-tuple-element.37.refs_0_), channel_id=1, source_target_pairs={{0,8},{8,0},{16,24},{24,16},{32,40},{40,32},{48,56},{56,48},{64,72... | collective-permute-start | bytes 196616 | tf_op jit(solution)/shard_map/ppermute | solution.py:561
  46.1 5.0 %collective-permute-start.8 = (bf16[256,128]{1,0:T(8,128)(2,1)S(1)}, bf16[256,128]{1,0:T(8,128)(2,1)S(1)}, u32[]{:S(2)}, u32[]{:S(2)}) collective-permute-start(bf16[256,128]{1,0:T(8,128)(2,1)S(1)} %get-tuple-element.37.refs_0_), channel_id=1, source_target_pairs={{0,128},{8,136},{16,144},{24,152},{32,160},{40,168},{48,176},{56,1... | collective-permute-start | bytes 196616 | tf_op jit(solution)/shard_map/ppermute | solution.py:561
  46.9 4.7 %collective-permute-start.9 = (bf16[256,128]{1,0:T(8,128)(2,1)S(1)}, bf16[256,128]{1,0:T(8,128)(2,1)S(1)}, u32[]{:S(2)}, u32[]{:S(2)}) collective-permute-start(bf16[256,128]{1,0:T(8,128)(2,1)S(1)} %get-tuple-element.37.refs_0_), channel_id=1, source_target_pairs={{0,136},{8,128},{16,152},{24,144},{32,168},{40,160},{48,184},{56,1... | collective-permute-start | bytes 196616 | tf_op jit(solution)/shard_map/ppermute | solution.py:561
  75.1 4.1 %collective-permute-start.10 = (bf16[8,256,128]{2,1,0:T(8,128)(2,1)S(1)}, bf16[8,256,128]{2,1,0:T(8,128)(2,1)S(1)}, u32[]{:S(2)}, u32[]{:S(2)}) collective-permute-start(bf16[8,256,128]{2,1,0:T(8,128)(2,1)S(1)} %slice.20.own_ref), channel_id=1, source_target_pairs={{0,8},{8,0},{16,24},{24,16},{32,40},{40,32},{48,56},{56,48},{64,72... | collective-permute-start | bytes 1572872 | tf_op jit(solution)/shard_map/ppermute | solution.py:561
  75.2 14.3 %collective-permute-start.11 = (bf16[8,256,128]{2,1,0:T(8,128)(2,1)S(1)}, bf16[8,256,128]{2,1,0:T(8,128)(2,1)S(1)}, u32[]{:S(2)}, u32[]{:S(2)}) collective-permute-start(bf16[8,256,128]{2,1,0:T(8,128)(2,1)S(1)} %slice.20.own_ref), channel_id=1, source_target_pairs={{0,128},{8,136},{16,144},{24,152},{32,160},{40,168},{48,176},{56,1... | collective-permute-start | bytes 1572872 | tf_op jit(solution)/shard_map/ppermute | solution.py:561
  89.5 3.4 %collective-permute-start.12 = (bf16[8,256,128]{2,1,0:T(8,128)(2,1)S(1)}, bf16[8,256,128]{2,1,0:T(8,128)(2,1)S(1)}, u32[]{:S(2)}, u32[]{:S(2)}) collective-permute-start(bf16[8,256,128]{2,1,0:T(8,128)(2,1)S(1)} %collective-permute-done.11.set_ref), channel_id=1, source_target_pairs={{0,8},{8,0},{16,24},{24,16},{32,40},{40,32},{48,56},{56,48},{64,72... | collective-permute-start | bytes 1572872 | tf_op jit(solution)/shard_map/ppermute | solution.py:561
  120.2 31.3 %copy-start = (bf16[3,128,384]{2,1,0:T(8,128)(2,1)S(1)}, bf16[3,128,384]{2,1,0:T(8,128)(2,1)}, u32[]{:S(2)}) copy-start(bf16[3,128,384]{2,1,0:T(8,128)(2,1)} %video_ref.1) | copy-start | bytes 884740
  120.2 16.3 %collective-permute-start.13 = (bf16[768,384]{1,0:T(8,128)(2,1)S(1)}, bf16[768,384]{1,0:T(8,128)(2,1)S(1)}, u32[]{:S(2)}, u32[]{:S(2)}) collective-permute-start(bf16[768,384]{1,0:T(8,128)(2,1)S(1)} %get-tuple-element.52), channel_id=1, source_target_pairs={{0,2},{1,3},{2,4},{3,5},{4,6},{5,7},{6,0},{7,1},{8,10},{9,11},{10,... | collective-permute-start | bytes 1769480 | tf_op jit(solution)/shard_map/ppermute | solution.py:553
  120.7 22.2 %collective-permute-start.14 = (bf16[768,384]{1,0:T(8,128)(2,1)S(1)}, bf16[768,384]{1,0:T(8,128)(2,1)S(1)}, u32[]{:S(2)}, u32[]{:S(2)}) collective-permute-start(bf16[768,384]{1,0:T(8,128)(2,1)S(1)} %get-tuple-element.53), channel_id=1, source_target_pairs={{0,6},{1,7},{2,0},{3,1},{4,2},{5,3},{6,4},{7,5},{8,14},{9,15},{10,... | collective-permute-start | bytes 1769480 | tf_op jit(solution)/shard_map/ppermute | solution.py:553
  122.3 9.5 %collective-permute-start.16 = (bf16[384,384]{1,0:T(8,128)(2,1)S(1)}, bf16[384,384]{1,0:T(8,128)(2,1)S(1)}, u32[]{:S(2)}, u32[]{:S(2)}) collective-permute-start(bf16[384,384]{1,0:T(8,128)(2,1)S(1)} %get-tuple-element.56), channel_id=1, source_target_pairs={{0,1},{1,0},{2,3},{3,2},{4,5},{5,4},{6,7},{7,6},{8,9},{9,8},{10,11... | collective-permute-start | bytes 884744 | tf_op jit(solution)/shard_map/ppermute | solution.py:557
  131.9 11.9 %collective-permute-start.17 = (bf16[384,384]{1,0:T(8,128)(2,1)S(1)}, bf16[384,384]{1,0:T(8,128)(2,1)S(1)}, u32[]{:S(2)}, u32[]{:S(2)}) collective-permute-start(bf16[384,384]{1,0:T(8,128)(2,1)S(1)} %add_convert_fusion.1), channel_id=1, source_target_pairs={{0,4},{1,5},{2,6},{3,7},{4,0},{5,1},{6,2},{7,3},{8,12},{9,13},{10,... | collective-permute-start | bytes 884744 | tf_op jit(solution)/shard_map/ppermute | solution.py:553
  143.0 8.3 %collective-permute-start.15 = (bf16[384,384]{1,0:T(8,128)(2,1)S(1)}, bf16[384,384]{1,0:T(8,128)(2,1)S(1)}, u32[]{:S(2)}, u32[]{:S(2)}) collective-permute-start(bf16[384,384]{1,0:T(8,128)(2,1)S(1)} %add_convert_fusion.2), channel_id=1, source_target_pairs={{0,1},{1,0},{2,3},{3,2},{4,5},{5,4},{6,7},{7,6},{8,9},{9,8},{10,11... | collective-permute-start | bytes 884744 | tf_op jit(solution)/shard_map/ppermute | solution.py:557

commit v6 on v5

--- a/solution.py
+++ b/solution.py
@@ -514,39 +514,41 @@
         total += weight
         mixed += weight * back_ref[p, TOK : 2 * TOK, :].astype(jnp.float32)
     attn_ref[(BRANCH - 1) * TOK :, (HEADS_HERE - 1) * HD :] = (mixed / total).astype(jnp.bfloat16)
-    targets = [(0, 0), (1, 0), (2, 0), (3, 0), (2, 1), (3, 1), (4, 0), (5, 0)]
-    for s, (n, half) in enumerate(targets):
+    multiply(place_ref, EARLY, attn_ref, w_ref, out_refs)
+
+
+EARLY = (4, 5)
+LATE = (7, 2, 3, 0, 1, 6)
+
+
+def multiply(place_ref, places, attn_ref, w_ref, out_refs):
+    for s, out_ref in zip(places, out_refs):
         start = pl.multiple_of(place_ref[s] * DSH, DSH)
-        out_refs[n][half * ROWS : (half + 1) * ROWS, :] = jnp.dot(
+        out_ref[...] = jnp.dot(
             attn_ref[...], w_ref[:, pl.ds(start, DSH)], preferred_element_type=jnp.float32
         ).astype(jnp.bfloat16)
 
 
-PART_ROWS = (ROWS, ROWS, 2 * ROWS, 2 * ROWS, ROWS, ROWS)
-
-
-def output(places, back, w_out):
+def late_kernel(place_ref, attn_ref, w_ref, *out_refs):
+    multiply(place_ref, LATE, attn_ref, w_ref, out_refs)
+
+
+def output(kernel, places, rows, w_out, count):
     return pl.pallas_call(
-        output_kernel,
-        out_shape=tuple(
-            pltpu.VMEM((rows, DSH), jnp.bfloat16) for rows in PART_ROWS
-        ),
+        kernel,
+        out_shape=(pltpu.VMEM((ROWS, DSH), jnp.bfloat16),) * count,
         grid_spec=pltpu.PrefetchScalarGridSpec(
             num_scalar_prefetch=1,
             grid=(1,),
-            in_specs=[
-                IN_VMEM,
-                IN_VMEM,
-            ],
-            out_specs=(IN_VMEM,) * len(PART_ROWS),
-            scratch_shapes=[pltpu.VMEM((ROWS, DSH), jnp.bfloat16)],
-        ),
-        compiler_params=pltpu.CompilerParams(vmem_limit_bytes=24 * MIB),
+            in_specs=[IN_VMEM, IN_VMEM],
+            out_specs=(IN_VMEM,) * count,
+        ),
+        compiler_params=pltpu.CompilerParams(vmem_limit_bytes=16 * MIB),
         cost_estimate=pl.CostEstimate(
-            flops=2 * ROWS * DSH * DSH * HEAD_AXIS, bytes_accessed=5_000_000, transcendentals=0
+            flops=2 * ROWS * DSH * DSH * count, bytes_accessed=3_000_000, transcendentals=0
         ),
         name="output",
-    )(places, in_vmem(back), in_vmem(w_out))
+    )(places, in_vmem(rows), in_vmem(w_out))
 
 
 def head_move(x, step):
@@ -585,14 +587,17 @@
     return total
 
 
-def scatter_head(parts):
-    own, partner, ahead, behind, opposite, over = parts
+def scatter_head(places, back, w_out):
+    ahead, behind, attention = output(output_kernel, places, back, w_out, 3)
+    for_partner = [head_move(ahead, 2), head_move(behind, -2)]
+    over, ahead, behind, own, partner, opposite = output(
+        late_kernel, places, attention, w_out, len(LATE)
+    )
     for_opposite = head_partner(over)
-    near = [head_move(ahead, 2), head_move(behind, -2)]
+    direct = [head_move(ahead, 2), head_move(behind, -2)]
+    over_y = head_partner(add(partner, *for_partner).astype(jnp.bfloat16))
     across = head_move(add(opposite, for_opposite).astype(jnp.bfloat16), 4)
-    for_partner = [x[ROWS:] for x in near]
-    over_y = head_partner(add(partner, *for_partner).astype(jnp.bfloat16))
-    return add(own, *(x[:ROWS] for x in near), over_y, across)
+    return add(own, *direct, over_y, across)
 
 
 def body(
@@ -626,16 +631,16 @@
     last_keys, last_values = lay_last(where, lasts, text_kv)
     near = received[:, : 2 * TOK]
     over_y = frame_move(near, FRAMES // 2)
-    near_later, last_keys = lax.optimization_barrier((near, last_keys))
+    ninth = attend_last(where, received, last_keys, last_values)
+    near_later, _ = lax.optimization_barrier((near, ninth))
     over_core = frame_move(near_later, 1)
-    ninth = attend_last(where, received, last_keys, last_values)
     *state, queries, w_held = attend_near(where, received, near, over_core, text_kv, in_hbm(w_out))
     over_y, _, _ = lax.optimization_barrier((over_y, state[0], ninth))
     diagonal = frame_move(over_y, 1)
     state = attend_far(queries, over_y, state)
     returned = attend_far(queries, diagonal, state, ninth)
-    partial = output(places, over_rings(returned), w_held)
-    proj = scatter_head(partial).reshape(video.shape)
+    back = over_rings(returned)
+    proj = scatter_head(places, back, w_held).reshape(video.shape)
     return (video.astype(jnp.float32) + gate * proj).astype(jnp.bfloat16)
 
 

time: 153 us -> 147 us (0.961)
  waiting for transfers between devices: 66.7 us -> 58.1 us
    ppermute x4, waiting for transfers between devices: 18.9 us -> 5.47 us  [head_partner(): return lax.ppermute(x, 'head', [(i, i ^ 1) for i in range(HEAD_AXIS)])]
    ppermute x6, waiting for transfers between devices: 6.57 us -> 9.6 us  [frame_move(): return lax.ppermute(x, 'frame', [(i, i ^ flip) for i in range(FRAMES)])]
    ppermute x8 -> x10, starting transfers between devices: 11.5 us -> 13.6 us  [head_move(): lax.ppermute(x, 'head', [(i, (i + step) % HEAD_AXIS) for i in range(HEAD_...]
    ppermute x8 -> x10, waiting for transfers between devices: 19.2 us -> 20.9 us  [head_move(): lax.ppermute(x, 'head', [(i, (i + step) % HEAD_AXIS) for i in range(HEAD_...]
  transfers between devices with their start and end apart: 19 -> 21, of which waited for: 12 -> 13; matrix products, arithmetic and copies ran while one was open for 1% -> 1% of each run, Pallas kernels for 10% -> 10%
where the time goes in v6:
time: 147 us; the launch traced here: 146 us
  waiting for transfers between devices  58.1 us (40%)
  Pallas kernels  31.8 us (22%)
  starting transfers between devices  31.3 us (21%)
  blocking collectives  21.5 us (15%)
  other arithmetic  2.21 us (2%)
    all_to_all x1, waiting for transfers between devices, over_rings(): return lax.all_to_all(x, 'frame', 0, 0, axis_index_groups=rings, tiled=True)  22.1 us
    all_to_all x1, blocking collectives, over_rings(): return lax.all_to_all(x, 'frame', 0, 0, axis_index_groups=rings, tiled=True)  21.5 us
    ppermute x10, waiting for transfers between devices, head_move(): lax.ppermute(x, 'head', [(i, (i + step) % HEAD_AXIS) for i in range(HEAD_...  20.9 us
    ppermute x10, starting transfers between devices, head_move(): lax.ppermute(x, 'head', [(i, (i + step) % HEAD_AXIS) for i in range(HEAD_...  13.6 us
    ppermute x6, waiting for transfers between devices, frame_move(): return lax.ppermute(x, 'frame', [(i, i ^ flip) for i in range(FRAMES)])  9.6 us
    all_to_all x1, starting transfers between devices, over_rings(): return lax.all_to_all(x, 'frame', 0, 0, axis_index_groups=rings, tiled=True)  8.48 us
    pallas_call x1, Pallas kernels, project(): pl.pallas_call(project_kernel, out_shape=(pltpu.VMEM((RING, 4 * TOK, HD),...  7.88 us
    pallas_call x1, Pallas kernels, attend_near(): pl.pallas_call(attend_near_kernel, out_shape=STATE + (pltpu.VMEM((SET, HD...  7.35 us
  transfers between devices with their start and end apart: 21, of which 13 were waited for; matrix products, arithmetic and copies ran while one was open for 1% of the time, Pallas kernels for 10%

profile of v6, /device:TPU:6, one launch (start us, length us, event | category | flops | bytes accessed | tf_op | source)
XLA Modules:
  0.0 145.7 jit_solution(8073398973222707367)
XLA Ops:
  0.7 2.4 %prep.1 = (bf16[400,384]{1,0:T(8,128)(2,1)S(1)}, f32[1,384]{1,0:T(1,128)S(1)}, f32[2,128]{1,0:T(2,128)S(1)}, s32[8]{0:T(128)S(1)}, s32[5]{0:T(128)S(1)}) custom-call(s32[1]{0:T(128)} %bitcast.frame_ref, s32[1]{0:T(128)} %bitcast.1.head_ref, s32[1]{0:T(128)S(6)} %copy.13.shift_ref, s32[32]{0:T(128)} %ids_ref.1, s32[3]{0:T(128)} %lengths_ref.1, ...), custom_call_target="tpu_custom_call" | custom-call | tf_op jit(solution)/shard_map/prep/pallas_call | solution.py:109
  3.0 3.3 %collective-permute-start = (bf16[400,384]{1,0:T(8,128)(2,1)S(1)}, bf16[400,384]{1,0:T(8,128)(2,1)S(1)}, u32[]{:S(2)}, u32[]{:S(2)}) collective-permute-start(bf16[400,384]{1,0:T(8,128)(2,1)S(1)} %get-tuple-element.36.refs_0_), channel_id=1, source_target_pairs={{0,1},{1,0},{2,3},{3,2},{4,5},{5,4},{6,7},{7,6},{8,9},{9,8},{10,11... | collective-permute-start | bytes 921608 | tf_op jit(solution)/shard_map/ppermute | solution.py:559
  6.3 1.4 collective-permute-start.5
  7.7 3.2 %collective-permute-start.2 = (bf16[400,384]{1,0:T(8,128)(2,1)S(1)}, bf16[400,384]{1,0:T(8,128)(2,1)S(1)}, u32[]{:S(2)}, u32[]{:S(2)}) collective-permute-start(bf16[400,384]{1,0:T(8,128)(2,1)S(1)} %get-tuple-element.36.refs_0_), channel_id=1, source_target_pairs={{0,2},{1,3},{2,4},{3,5},{4,6},{5,7},{6,0},{7,1},{8,10},{9,11},{10,... | collective-permute-start | bytes 921608 | tf_op jit(solution)/shard_map/ppermute | solution.py:555
  10.9 2.7 %collective-permute-done.refs_1_ = bf16[400,384]{1,0:T(8,128)(2,1)S(1)} collective-permute-done((bf16[400,384]{1,0:T(8,128)(2,1)S(1)}, bf16[400,384]{1,0:T(8,128)(2,1)S(1)}, u32[]{:S(2)}, u32[]{:S(2)}) %collective-permute-start) | collective-permute-done | bytes 307232 | tf_op jit(solution)/shard_map/ppermute | solution.py:559
  14.5 2.4 %collective-permute-start.4 = (bf16[400,384]{1,0:T(8,128)(2,1)S(1)}, bf16[400,384]{1,0:T(8,128)(2,1)S(1)}, u32[]{:S(2)}, u32[]{:S(2)}) collective-permute-start(bf16[400,384]{1,0:T(8,128)(2,1)S(1)} %collective-permute-done.refs_1_), channel_id=1, source_target_pairs={{0,2},{1,3},{2,4},{3,5},{4,6},{5,7},{6,0},{7,1},{8,10},{9,11},{10,... | collective-permute-start | bytes 921608 | tf_op jit(solution)/shard_map/ppermute | solution.py:555
  16.9 1.2 collective-permute-done.5.refs_6_
  18.0 2.0 %collective-permute-start.6 = (bf16[400,384]{1,0:T(8,128)(2,1)S(1)}, bf16[400,384]{1,0:T(8,128)(2,1)S(1)}, u32[]{:S(2)}, u32[]{:S(2)}) collective-permute-start(bf16[400,384]{1,0:T(8,128)(2,1)S(1)} %collective-permute-done.5.refs_6_), channel_id=1, source_target_pairs={{0,1},{1,0},{2,3},{3,2},{4,5},{5,4},{6,7},{7,6},{8,9},{9,8},{10,11... | collective-permute-start | bytes 921608 | tf_op jit(solution)/shard_map/ppermute | solution.py:559
  20.1 1.0 sine_multiply_fusion
  21.1 2.1 %collective-permute-done.1.refs_2_ = bf16[400,384]{1,0:T(8,128)(2,1)S(1)} collective-permute-done((bf16[400,384]{1,0:T(8,128)(2,1)S(1)}, bf16[400,384]{1,0:T(8,128)(2,1)S(1)}, u32[]{:S(2)}, u32[]{:S(2)}) %collective-permute-start.1) | collective-permute-done | bytes 307232 | tf_op jit(solution)/shard_map/ppermute | solution.py:555
  23.2 6.5 %collective-permute-done.3.refs_4_ = bf16[400,384]{1,0:T(8,128)(2,1)S(1)} collective-permute-done((bf16[400,384]{1,0:T(8,128)(2,1)S(1)}, bf16[400,384]{1,0:T(8,128)(2,1)S(1)}, u32[]{:S(2)}, u32[]{:S(2)}) %collective-permute-start.3) | collective-permute-done | bytes 307232 | tf_op jit(solution)/shard_map/ppermute | solution.py:555
  29.7 7.9 %project.1 = (bf16[8,512,128]{2,1,0:T(8,128)(2,1)}, bf16[256,128]{1,0:T(8,128)(2,1)S(1)}) custom-call(s32[8]{0:T(128)S(1)} %get-tuple-element.34.place_ref, bf16[400,384]{1,0:T(8,128)(2,1)S(1)} %get-tuple-element.36.refs_0_, bf16[400,384]{1,0:T(8,128)(2,1)S(1)} %collective-permute-done.refs_1_, bf16[400,384]{1,0:T(8,128)(2,1)S(1)} %collective-permute-done.1.refs_2_, ...), custom_call_target="tpu_custom_call" | custom-call | flops 2717908992 | bytes 12000000 | tf_op jit(solution)/shard_map/project/pallas_call | solution.py:206
  37.6 8.5 %all-to-all-start = ((bf16[8,512,128]{2,1,0:T(8,128)(2,1)}), bf16[8,512,128]{2,1,0:T(8,128)(2,1)S(1)}, u32[]{:S(2)}, u32[]{:S(2)}) async-start(bf16[8,512,128]{2,1,0:T(8,128)(2,1)} %get-tuple-element.38), calls=%async_computation | async-start | bytes 2097152 | tf_op jit(solution)/shard_map/all_to_all | solution.py:626
  46.9 1.1 collective-permute-start.9
  48.0 3.1 %collective-permute-done.8.refs_2_ = bf16[256,128]{1,0:T(8,128)(2,1)S(1)} collective-permute-done((bf16[256,128]{1,0:T(8,128)(2,1)S(1)}, bf16[256,128]{1,0:T(8,128)(2,1)S(1)}, u32[]{:S(2)}, u32[]{:S(2)}) %collective-permute-start.8) | collective-permute-done | bytes 65568 | tf_op jit(solution)/shard_map/ppermute | solution.py:563
  51.5 1.4 lay_last.1
  53.0 22.1 %all-to-all-done.q_ref = bf16[8,512,128]{2,1,0:T(8,128)(2,1)S(1)} async-done(((bf16[8,512,128]{2,1,0:T(8,128)(2,1)}), bf16[8,512,128]{2,1,0:T(8,128)(2,1)S(1)}, u32[]{:S(2)}, u32[]{:S(2)}) %all-to-all-start) | async-done | bytes 1048608 | tf_op jit(solution)/shard_map/all_to_all | solution.py:626
  75.1 3.0 %attend_last.1.refs_3_ = bf16[8,144,128]{2,1,0:T(8,128)(2,1)S(1)} custom-call(s32[5]{0:T(128)S(1)} %get-tuple-element.35.where_ref, bf16[8,512,128]{2,1,0:T(8,128)(2,1)S(1)} %all-to-all-done.q_ref, bf16[640,128]{1,0:T(8,128)(2,1)S(1)} %get-tuple-element.40.keys_ref, bf16[640,256]{1,0:T(8,128)(2,1)S(1)} %get-tuple-element.41.value_ref), custom_call_target="tpu_custom_call" | custom-call | flops 335544320 | bytes 1000000 | tf_op jit(solution)/shard_map/attend_last/pallas_call | solution.py:435
  80.1 7.4 %attend_near.1 = (f32[1024,128]{1,0:T(8,128)S(1)}, f32[1024,128]{1,0:T(8,128)S(1)}, f32[1024,128]{1,0:T(8,128)S(1)}, bf16[1024,128]{1,0:T(8,128)(2,1)S(1)}, bf16[384,3072]{1,0:T(8,128)(2,1)S(1)}) custom-call(s32[5]{0:T(128)S(1)} %get-tuple-element.35.where_ref, bf16[8,512,128]{2,1,0:T(8,128)(2,1)S(1)} %all-to-all-done.q_ref, ...), custom_call_target="tpu_custom_call" | custom-call | flops 1207959552 | bytes 3000000 | tf_op jit(solution)/shard_map/attend_near/pallas_call | solution.py:350
  87.4 5.1 %collective-permute-done.11.set_ref = bf16[8,256,128]{2,1,0:T(8,128)(2,1)S(1)} collective-permute-done((bf16[8,256,128]{2,1,0:T(8,128)(2,1)S(1)}, bf16[8,256,128]{2,1,0:T(8,128)(2,1)S(1)}, u32[]{:S(2)}, u32[]{:S(2)}) %collective-permute-start.11) | collective-permute-done | bytes 524320 | tf_op jit(solution)/shard_map/ppermute | solution.py:563
  92.5 3.4 %attend_far.2 = (f32[1024,128]{1,0:T(8,128)S(1)}, f32[1024,128]{1,0:T(8,128)S(1)}, f32[1024,128]{1,0:T(8,128)S(1)}) custom-call(bf16[1024,128]{1,0:T(8,128)(2,1)S(1)} %get-tuple-element.43.q_ref, bf16[8,256,128]{2,1,0:T(8,128)(2,1)S(1)} %collective-permute-done.11.set_ref, f32[1024,128]{1,0:T(8,128)S(1)} %get-tuple-element.44.refs_0_, ...), custom_call_target="tpu_custom_call" | custom-call | flops 536870912 | bytes 3000000 | tf_op jit(solution)/shard_map/attend_far/pallas_call | solution.py:482
  96.0 3.3 %attend_far.3 = bf16[8,272,128]{2,1,0:T(8,128)(2,1)S(1)} custom-call(bf16[1024,128]{1,0:T(8,128)(2,1)S(1)} %get-tuple-element.43.q_ref, bf16[8,256,128]{2,1,0:T(8,128)(2,1)S(1)} %collective-permute-done.12.set_ref, f32[1024,128]{1,0:T(8,128)S(1)} %get-tuple-element.48.refs_0_, f32[1024,128]{1,0:T(8,128)S(1)} %get-tuple-element.49.refs_1_, ...), custom_call_target="tpu_custom_call" | custom-call | flops 536870912 | bytes 3000000 | tf_op jit(solution)/shard_map/attend_far/pallas_call | solution.py:482
  99.3 21.5 %all_to_all.10.back_ref = bf16[8,272,128]{2,1,0:T(8,128)(2,1)S(1)} all-to-all(bf16[8,272,128]{2,1,0:T(8,128)(2,1)S(1)} %attend_far.3), channel_id=1, replica_groups={{0,16,32,48,64,80,96,112},{8,24,40,56,72,88,104,120},{128,144,160,176,1..., dimensions={0} | all-to-all | bytes 1114112 | tf_op jit(solution)/shard_map/all_to_all | solution.py:626
  120.8 1.3 output.2
  122.6 1.6 %collective-permute-start.16 = (bf16[384,384]{1,0:T(8,128)(2,1)S(1)}, bf16[384,384]{1,0:T(8,128)(2,1)S(1)}, u32[]{:S(2)}, u32[]{:S(2)}) collective-permute-start(bf16[384,384]{1,0:T(8,128)(2,1)S(1)} %get-tuple-element.58), channel_id=1, source_target_pairs={{0,6},{1,7},{2,0},{3,1},{4,2},{5,3},{6,4},{7,5},{8,14},{9,15},{10,... | collective-permute-start | bytes 884744 | tf_op jit(solution)/shard_map/ppermute | solution.py:555
  124.2 1.8 %output.3 = (bf16[384,384]{1,0:T(8,128)(2,1)S(1)}, bf16[384,384]{1,0:T(8,128)(2,1)S(1)}, bf16[384,384]{1,0:T(8,128)(2,1)S(1)}, bf16[384,384]{1,0:T(8,128)(2,1)S(...) custom-call(s32[8]{0:T(128)S(1)} %get-tuple-element.34.place_ref, ...), custom_call_target="tpu_custom_call" | custom-call | flops 679477248 | bytes 3000000 | tf_op jit(solution)/shard_map/output/pallas_call | solution.py:537
  126.8 1.6 %collective-permute-start.13 = (bf16[384,384]{1,0:T(8,128)(2,1)S(1)}, bf16[384,384]{1,0:T(8,128)(2,1)S(1)}, u32[]{:S(2)}, u32[]{:S(2)}) collective-permute-start(bf16[384,384]{1,0:T(8,128)(2,1)S(1)} %get-tuple-element.54), channel_id=1, source_target_pairs={{0,2},{1,3},{2,4},{3,5},{4,6},{5,7},{6,0},{7,1},{8,10},{9,11},{10,... | collective-permute-start | bytes 884744 | tf_op jit(solution)/shard_map/ppermute | solution.py:555
  128.9 3.2 %collective-permute-done.15 = bf16[384,384]{1,0:T(8,128)(2,1)S(1)} collective-permute-done((bf16[384,384]{1,0:T(8,128)(2,1)S(1)}, bf16[384,384]{1,0:T(8,128)(2,1)S(1)}, u32[]{:S(2)}, u32[]{:S(2)}) %collective-permute-start.15) | collective-permute-done | bytes 294944 | tf_op jit(solution)/shard_map/ppermute | solution.py:555
  132.1 1.2 collective-permute-done.16
  133.5 2.8 %collective-permute-done.18 = bf16[384,384]{1,0:T(8,128)(2,1)S(1)} collective-permute-done((bf16[384,384]{1,0:T(8,128)(2,1)S(1)}, bf16[384,384]{1,0:T(8,128)(2,1)S(1)}, u32[]{:S(2)}, u32[]{:S(2)}) %collective-permute-start.18) | collective-permute-done | bytes 294944 | tf_op jit(solution)/shard_map/ppermute | solution.py:559
  136.4 1.6 %collective-permute-start.19 = (bf16[384,384]{1,0:T(8,128)(2,1)S(1)}, bf16[384,384]{1,0:T(8,128)(2,1)S(1)}, u32[]{:S(2)}, u32[]{:S(2)}) collective-permute-start(bf16[384,384]{1,0:T(8,128)(2,1)S(1)} %add_convert_fusion.1), channel_id=1, source_target_pairs={{0,4},{1,5},{2,6},{3,7},{4,0},{5,1},{6,2},{7,3},{8,12},{9,13},{10,... | collective-permute-start | bytes 884744 | tf_op jit(solution)/shard_map/ppermute | solution.py:555
  138.0 6.7 %collective-permute-done.14 = bf16[384,384]{1,0:T(8,128)(2,1)S(1)} collective-permute-done((bf16[384,384]{1,0:T(8,128)(2,1)S(1)}, bf16[384,384]{1,0:T(8,128)(2,1)S(1)}, u32[]{:S(2)}, u32[]{:S(2)}) %collective-permute-start.14) | collective-permute-done | bytes 294944 | tf_op jit(solution)/shard_map/ppermute | solution.py:555
  (30 shorter events, 7.1 us)
Async XLA Ops:
  3.0 10.6 %collective-permute-start = (bf16[400,384]{1,0:T(8,128)(2,1)S(1)}, bf16[400,384]{1,0:T(8,128)(2,1)S(1)}, u32[]{:S(2)}, u32[]{:S(2)}) collective-permute-start(bf16[400,384]{1,0:T(8,128)(2,1)S(1)} %get-tuple-element.36.refs_0_), channel_id=1, source_target_pairs={{0,1},{1,0},{2,3},{3,2},{4,5},{5,4},{6,7},{7,6},{8,9},{9,8},{10,11... | collective-permute-start | bytes 921608 | tf_op jit(solution)/shard_map/ppermute | solution.py:559
  6.3 11.7 %collective-permute-start.5 = (bf16[400,384]{1,0:T(8,128)(2,1)S(1)}, bf16[400,384]{1,0:T(8,128)(2,1)S(1)}, u32[]{:S(2)}, u32[]{:S(2)}) collective-permute-start(bf16[400,384]{1,0:T(8,128)(2,1)S(1)} %get-tuple-element.36.refs_0_), channel_id=1, source_target_pairs={{0,4},{1,5},{2,6},{3,7},{4,0},{5,1},{6,2},{7,3},{8,12},{9,13},{10,... | collective-permute-start | bytes 921608 | tf_op jit(solution)/shard_map/ppermute | solution.py:555
  7.7 15.5 %collective-permute-start.1 = (bf16[400,384]{1,0:T(8,128)(2,1)S(1)}, bf16[400,384]{1,0:T(8,128)(2,1)S(1)}, u32[]{:S(2)}, u32[]{:S(2)}) collective-permute-start(bf16[400,384]{1,0:T(8,128)(2,1)S(1)} %get-tuple-element.36.refs_0_), channel_id=1, source_target_pairs={{0,6},{1,7},{2,0},{3,1},{4,2},{5,3},{6,4},{7,5},{8,14},{9,15},{10,... | collective-permute-start | bytes 921608 | tf_op jit(solution)/shard_map/ppermute | solution.py:555
  7.7 15.5 %collective-permute-start.2 = (bf16[400,384]{1,0:T(8,128)(2,1)S(1)}, bf16[400,384]{1,0:T(8,128)(2,1)S(1)}, u32[]{:S(2)}, u32[]{:S(2)}) collective-permute-start(bf16[400,384]{1,0:T(8,128)(2,1)S(1)} %get-tuple-element.36.refs_0_), channel_id=1, source_target_pairs={{0,2},{1,3},{2,4},{3,5},{4,6},{5,7},{6,0},{7,1},{8,10},{9,11},{10,... | collective-permute-start | bytes 921608 | tf_op jit(solution)/shard_map/ppermute | solution.py:555
  13.6 16.1 %collective-permute-start.3 = (bf16[400,384]{1,0:T(8,128)(2,1)S(1)}, bf16[400,384]{1,0:T(8,128)(2,1)S(1)}, u32[]{:S(2)}, u32[]{:S(2)}) collective-permute-start(bf16[400,384]{1,0:T(8,128)(2,1)S(1)} %collective-permute-done.refs_1_), channel_id=1, source_target_pairs={{0,6},{1,7},{2,0},{3,1},{4,2},{5,3},{6,4},{7,5},{8,14},{9,15},{10,... | collective-permute-start | bytes 921608 | tf_op jit(solution)/shard_map/ppermute | solution.py:555
  14.5 15.3 %collective-permute-start.4 = (bf16[400,384]{1,0:T(8,128)(2,1)S(1)}, bf16[400,384]{1,0:T(8,128)(2,1)S(1)}, u32[]{:S(2)}, u32[]{:S(2)}) collective-permute-start(bf16[400,384]{1,0:T(8,128)(2,1)S(1)} %collective-permute-done.refs_1_), channel_id=1, source_target_pairs={{0,2},{1,3},{2,4},{3,5},{4,6},{5,7},{6,0},{7,1},{8,10},{9,11},{10,... | collective-permute-start | bytes 921608 | tf_op jit(solution)/shard_map/ppermute | solution.py:555
  18.0 11.7 %collective-permute-start.6 = (bf16[400,384]{1,0:T(8,128)(2,1)S(1)}, bf16[400,384]{1,0:T(8,128)(2,1)S(1)}, u32[]{:S(2)}, u32[]{:S(2)}) collective-permute-start(bf16[400,384]{1,0:T(8,128)(2,1)S(1)} %collective-permute-done.5.refs_6_), channel_id=1, source_target_pairs={{0,1},{1,0},{2,3},{3,2},{4,5},{5,4},{6,7},{7,6},{8,9},{9,8},{10,11... | collective-permute-start | bytes 921608 | tf_op jit(solution)/shard_map/ppermute | solution.py:559
  37.6 37.4 %all-to-all-start = ((bf16[8,512,128]{2,1,0:T(8,128)(2,1)}), bf16[8,512,128]{2,1,0:T(8,128)(2,1)S(1)}, u32[]{:S(2)}, u32[]{:S(2)}) async-start(bf16[8,512,128]{2,1,0:T(8,128)(2,1)} %get-tuple-element.38), calls=%async_computation | async-start | bytes 2097152 | tf_op jit(solution)/shard_map/all_to_all | solution.py:626
  46.1 1.9 %collective-permute-start.7 = (bf16[256,128]{1,0:T(8,128)(2,1)S(1)}, bf16[256,128]{1,0:T(8,128)(2,1)S(1)}, u32[]{:S(2)}, u32[]{:S(2)}) collective-permute-start(bf16[256,128]{1,0:T(8,128)(2,1)S(1)} %get-tuple-element.39.refs_0_), channel_id=1, source_target_pairs={{0,8},{8,0},{16,24},{24,16},{32,40},{40,32},{48,56},{56,48},{64,72... | collective-permute-start | bytes 196616 | tf_op jit(solution)/shard_map/ppermute | solution.py:563
  46.1 5.0 %collective-permute-start.8 = (bf16[256,128]{1,0:T(8,128)(2,1)S(1)}, bf16[256,128]{1,0:T(8,128)(2,1)S(1)}, u32[]{:S(2)}, u32[]{:S(2)}) collective-permute-start(bf16[256,128]{1,0:T(8,128)(2,1)S(1)} %get-tuple-element.39.refs_0_), channel_id=1, source_target_pairs={{0,128},{8,136},{16,144},{24,152},{32,160},{40,168},{48,176},{56,1... | collective-permute-start | bytes 196616 | tf_op jit(solution)/shard_map/ppermute | solution.py:563
  46.9 4.7 %collective-permute-start.9 = (bf16[256,128]{1,0:T(8,128)(2,1)S(1)}, bf16[256,128]{1,0:T(8,128)(2,1)S(1)}, u32[]{:S(2)}, u32[]{:S(2)}) collective-permute-start(bf16[256,128]{1,0:T(8,128)(2,1)S(1)} %get-tuple-element.39.refs_0_), channel_id=1, source_target_pairs={{0,136},{8,128},{16,152},{24,144},{32,168},{40,160},{48,184},{56,1... | collective-permute-start | bytes 196616 | tf_op jit(solution)/shard_map/ppermute | solution.py:563
  78.1 2.0 %collective-permute-start.10 = (bf16[8,256,128]{2,1,0:T(8,128)(2,1)S(1)}, bf16[8,256,128]{2,1,0:T(8,128)(2,1)S(1)}, u32[]{:S(2)}, u32[]{:S(2)}) collective-permute-start(bf16[8,256,128]{2,1,0:T(8,128)(2,1)S(1)} %slice.4.own_ref), channel_id=1, source_target_pairs={{0,8},{8,0},{16,24},{24,16},{32,40},{40,32},{48,56},{56,48},{64,72... | collective-permute-start | bytes 1572872 | tf_op jit(solution)/shard_map/ppermute | solution.py:563
  78.2 14.3 %collective-permute-start.11 = (bf16[8,256,128]{2,1,0:T(8,128)(2,1)S(1)}, bf16[8,256,128]{2,1,0:T(8,128)(2,1)S(1)}, u32[]{:S(2)}, u32[]{:S(2)}) collective-permute-start(bf16[8,256,128]{2,1,0:T(8,128)(2,1)S(1)} %slice.4.own_ref), channel_id=1, source_target_pairs={{0,128},{8,136},{16,144},{24,152},{32,160},{40,168},{48,176},{56,1... | collective-permute-start | bytes 1572872 | tf_op jit(solution)/shard_map/ppermute | solution.py:563
  92.5 3.4 %collective-permute-start.12 = (bf16[8,256,128]{2,1,0:T(8,128)(2,1)S(1)}, bf16[8,256,128]{2,1,0:T(8,128)(2,1)S(1)}, u32[]{:S(2)}, u32[]{:S(2)}) collective-permute-start(bf16[8,256,128]{2,1,0:T(8,128)(2,1)S(1)} %collective-permute-done.11.set_ref), channel_id=1, source_target_pairs={{0,8},{8,0},{16,24},{24,16},{32,40},{40,32},{48,56},{56,48},{64,72... | collective-permute-start | bytes 1572872 | tf_op jit(solution)/shard_map/ppermute | solution.py:563
  122.1 10.0 %collective-permute-start.15 = (bf16[384,384]{1,0:T(8,128)(2,1)S(1)}, bf16[384,384]{1,0:T(8,128)(2,1)S(1)}, u32[]{:S(2)}, u32[]{:S(2)}) collective-permute-start(bf16[384,384]{1,0:T(8,128)(2,1)S(1)} %get-tuple-element.57), channel_id=1, source_target_pairs={{0,2},{1,3},{2,4},{3,5},{4,6},{5,7},{6,0},{7,1},{8,10},{9,11},{10,... | collective-permute-start | bytes 884744 | tf_op jit(solution)/shard_map/ppermute | solution.py:555
  122.6 10.7 %collective-permute-start.16 = (bf16[384,384]{1,0:T(8,128)(2,1)S(1)}, bf16[384,384]{1,0:T(8,128)(2,1)S(1)}, u32[]{:S(2)}, u32[]{:S(2)}) collective-permute-start(bf16[384,384]{1,0:T(8,128)(2,1)S(1)} %get-tuple-element.58), channel_id=1, source_target_pairs={{0,6},{1,7},{2,0},{3,1},{4,2},{5,3},{6,4},{7,5},{8,14},{9,15},{10,... | collective-permute-start | bytes 884744 | tf_op jit(solution)/shard_map/ppermute | solution.py:555
  126.0 19.0 %copy-start = (bf16[3,128,384]{2,1,0:T(8,128)(2,1)S(1)}, bf16[3,128,384]{2,1,0:T(8,128)(2,1)}, u32[]{:S(2)}) copy-start(bf16[3,128,384]{2,1,0:T(8,128)(2,1)} %video_ref.1) | copy-start | bytes 884740
  126.0 10.3 %collective-permute-start.18 = (bf16[384,384]{1,0:T(8,128)(2,1)S(1)}, bf16[384,384]{1,0:T(8,128)(2,1)S(1)}, u32[]{:S(2)}, u32[]{:S(2)}) collective-permute-start(bf16[384,384]{1,0:T(8,128)(2,1)S(1)} %get-tuple-element.60), channel_id=1, source_target_pairs={{0,1},{1,0},{2,3},{3,2},{4,5},{5,4},{6,7},{7,6},{8,9},{9,8},{10,11... | collective-permute-start | bytes 884744 | tf_op jit(solution)/shard_map/ppermute | solution.py:559
  126.8 11.2 %collective-permute-start.13 = (bf16[384,384]{1,0:T(8,128)(2,1)S(1)}, bf16[384,384]{1,0:T(8,128)(2,1)S(1)}, u32[]{:S(2)}, u32[]{:S(2)}) collective-permute-start(bf16[384,384]{1,0:T(8,128)(2,1)S(1)} %get-tuple-element.54), channel_id=1, source_target_pairs={{0,2},{1,3},{2,4},{3,5},{4,6},{5,7},{6,0},{7,1},{8,10},{9,11},{10,... | collective-permute-start | bytes 884744 | tf_op jit(solution)/shard_map/ppermute | solution.py:555
  128.5 16.3 %collective-permute-start.14 = (bf16[384,384]{1,0:T(8,128)(2,1)S(1)}, bf16[384,384]{1,0:T(8,128)(2,1)S(1)}, u32[]{:S(2)}, u32[]{:S(2)}) collective-permute-start(bf16[384,384]{1,0:T(8,128)(2,1)S(1)} %get-tuple-element.55), channel_id=1, source_target_pairs={{0,6},{1,7},{2,0},{3,1},{4,2},{5,3},{6,4},{7,5},{8,14},{9,15},{10,... | collective-permute-start | bytes 884744 | tf_op jit(solution)/shard_map/ppermute | solution.py:555
  133.4 11.3 %collective-permute-start.17 = (bf16[384,384]{1,0:T(8,128)(2,1)S(1)}, bf16[384,384]{1,0:T(8,128)(2,1)S(1)}, u32[]{:S(2)}, u32[]{:S(2)}) collective-permute-start(bf16[384,384]{1,0:T(8,128)(2,1)S(1)} %add_convert_fusion.2), channel_id=1, source_target_pairs={{0,1},{1,0},{2,3},{3,2},{4,5},{5,4},{6,7},{7,6},{8,9},{9,8},{10,11... | collective-permute-start | bytes 884744 | tf_op jit(solution)/shard_map/ppermute | solution.py:559
  136.4 8.4 %collective-permute-start.19 = (bf16[384,384]{1,0:T(8,128)(2,1)S(1)}, bf16[384,384]{1,0:T(8,128)(2,1)S(1)}, u32[]{:S(2)}, u32[]{:S(2)}) collective-permute-start(bf16[384,384]{1,0:T(8,128)(2,1)S(1)} %add_convert_fusion.1), channel_id=1, source_target_pairs={{0,4},{1,5},{2,6},{3,7},{4,0},{5,1},{6,2},{7,3},{8,12},{9,13},{10,... | collective-permute-start | bytes 884744 | tf_op jit(solution)/shard_map/ppermute | solution.py:555

commit v7 on v6

--- a/solution.py
+++ b/solution.py
@@ -288,29 +288,51 @@
     return pl.ds(pl.multiple_of(pl.program_id(0) * TILE, TILE), TILE)
 
 
-def gather_rows(q, pieces, score_ref, before):
-    top = jnp.full((TILE, 128), -jnp.inf, jnp.float32)
-    column = 0
-    for keys, _, valid in pieces:
-        if valid is None:
-            top = score_keys(q, keys, score_ref, column, top)
-        else:
-            top = score_text(q, keys, valid, score_ref, column, top)
-        column += keys.shape[0]
-    top = jnp.max(top, axis=1, keepdims=True) * EXP_SCALE
-    if before is not None:
-        top = jnp.maximum(top, before)
-    total = jnp.zeros((TILE, 128), jnp.float32)
-    mixed = jnp.zeros((TILE, HD), jnp.float32)
-    column = 0
-    for _, values, _ in pieces:
-        stop = column + values.shape[0]
-        weights = jnp.exp2(score_ref[:, column:stop] * EXP_SCALE - top)
-        for lane in range(0, stop - column, 128):
+def gather_rows(flag_ref, q, pieces, before, score_ref, top_ref, total_ref, mixed_ref):
+    def add_up(weights, values, total, mixed):
+        for lane in range(0, weights.shape[1], 128):
             total += weights[:, lane : lane + 128]
         mixed += jnp.dot(weights.astype(jnp.bfloat16), values, preferred_element_type=jnp.float32)
-        column = stop
-    return top, total, mixed
+        return total, mixed
+
+    zeros = jnp.zeros((TILE, 128), jnp.float32)
+
+    @pl.when(flag_ref[0] == 1)
+    def _():
+        total, mixed = zeros, zeros
+        for keys, values, valid in pieces:
+            scores = lax.dot_general(q, keys, DIMS, preferred_element_type=jnp.float32)
+            if valid is not None:
+                index = lax.broadcasted_iota(jnp.int32, scores.shape, 1)
+                scores = jnp.where(index < valid, scores, -jnp.inf)
+            total, mixed = add_up(jnp.exp2(scores * EXP_SCALE), values, total, mixed)
+        top_ref[...] = zeros
+        total_ref[...] = total
+        mixed_ref[...] = mixed
+
+    @pl.when(flag_ref[0] != 1)
+    def _():
+        top = jnp.full((TILE, 128), -jnp.inf, jnp.float32)
+        column = 0
+        for keys, _, valid in pieces:
+            if valid is None:
+                top = score_keys(q, keys, score_ref, column, top)
+            else:
+                top = score_text(q, keys, valid, score_ref, column, top)
+            column += keys.shape[0]
+        top = jnp.max(top, axis=1, keepdims=True) * EXP_SCALE
+        if before is not None:
+            top = jnp.maximum(top, before)
+        total, mixed = zeros, zeros
+        column = 0
+        for _, values, _ in pieces:
+            stop = column + values.shape[0]
+            weights = jnp.exp2(score_ref[:, column:stop] * EXP_SCALE - top)
+            total, mixed = add_up(weights, values, total, mixed)
+            column = stop
+        top_ref[...] = jnp.broadcast_to(top, (TILE, 128))
+        total_ref[...] = total
+        mixed_ref[...] = mixed
 
 
 def set_piece(ref):
@@ -318,7 +340,7 @@
 
 
 def attend_near_kernel(
-    where_ref, q_ref, own_ref, core_ref, text_ref, w_hbm,
+    where_ref, flag_ref, q_ref, own_ref, core_ref, text_ref, w_hbm,
     mixed_ref, total_ref, top_ref, q_out_ref, w_ref, score_ref, sem,
 ):
     copy = pltpu.make_async_copy(w_hbm, w_ref, sem)
@@ -329,13 +351,11 @@
 
     q = q_ref[...].reshape(TILE, HD)
     text = (text_ref[0, 0], text_ref[1, 0], where_ref[2])
-    top, total, mixed = gather_rows(
-        q, [set_piece(own_ref), set_piece(core_ref), text], score_ref, None
+    here = tile_rows()
+    gather_rows(
+        flag_ref, q, [set_piece(own_ref), set_piece(core_ref), text], None, score_ref,
+        top_ref.at[here], total_ref.at[here], mixed_ref.at[here],
     )
-    here = tile_rows()
-    mixed_ref[here, :] = mixed
-    total_ref[here, :] = total
-    top_ref[here, :] = jnp.broadcast_to(top, (TILE, 128))
     q_out_ref[here, :] = q
 
     @pl.when(pl.program_id(0) == SET // TILE - 1)
@@ -346,18 +366,18 @@
 STATE = (pltpu.VMEM((SET, HD), jnp.float32),) * 3
 
 
-def attend_near(where, received, own, core, text_kv, w_out):
+def attend_near(where, flag, received, own, core, text_kv, w_out):
     return pl.pallas_call(
         attend_near_kernel,
         out_shape=STATE + (pltpu.VMEM((SET, HD), jnp.bfloat16), pltpu.VMEM(w_out.shape, w_out.dtype)),
         grid_spec=pltpu.PrefetchScalarGridSpec(
-            num_scalar_prefetch=1,
+            num_scalar_prefetch=2,
             grid=(SET // TILE,),
             in_specs=[
-                pl.BlockSpec((QUAD, TOK, HD), lambda i, w: (i, 2, 0)),
+                pl.BlockSpec((QUAD, TOK, HD), lambda i, w, f: (i, 2, 0)),
                 whole((RING, 2 * TOK, HD)),
                 whole((RING, 2 * TOK, HD)),
-                pl.BlockSpec((2, 1, TXT, HD), lambda i, w: (0, w[0], 0, w[1])),
+                pl.BlockSpec((2, 1, TXT, HD), lambda i, w, f: (0, w[0], 0, w[1])),
                 pl.BlockSpec(memory_space=pltpu.HBM),
             ],
             out_specs=(IN_VMEM,) * 5,
@@ -371,7 +391,7 @@
             flops=4 * SET * 2304 * HD, bytes_accessed=3_000_000, transcendentals=SET * 2304
         ),
         name="attend_near",
-    )(where, received, own, core, text_kv, w_out)
+    )(where, flag, received, own, core, text_kv, w_out)
 
 
 LAST_KEYS = QUAD * TOK + 128
@@ -379,19 +399,31 @@
 
 def lay_last_kernel(where_ref, *refs):
     last_refs = refs[:QUAD]
-    text_ref, keys_ref, value_ref = refs[QUAD:]
+    text_ref, own_text_ref, gain_ref, keys_ref, value_ref, flag_ref = refs[QUAD:]
     for n, ref in enumerate(last_refs):
         keys_ref[n * TOK : (n + 1) * TOK, :] = ref[0:TOK, :]
     keys_ref[QUAD * TOK :, :] = text_ref[0, 0]
     lay_values(value_ref, [ref[TOK : 2 * TOK, :] for ref in last_refs] + [text_ref[1, 0]])
-
-
-def lay_last(where, lasts, text_kv):
+    room = 1.03 * HD
+    gains = gain_ref[...] * gain_ref[...]
+    text = own_text_ref[0, 0].astype(jnp.float32)
+    key_norm = jnp.maximum(
+        room * jnp.max(gains[1:2]), jnp.max(jnp.sum(text * text, axis=1, keepdims=True))
+    )
+    bound = EXP_SCALE * EXP_SCALE * room * jnp.max(gains[0:1]) * key_norm
+    flag_ref[0] = jnp.where(bound < MOST_LOG2 * MOST_LOG2, 1, 0)
+
+
+MOST_LOG2 = 90.0
+
+
+def lay_last(where, lasts, text_kv, gains):
     return pl.pallas_call(
         lay_last_kernel,
         out_shape=(
             jax.ShapeDtypeStruct((LAST_KEYS, HD), jnp.bfloat16),
             jax.ShapeDtypeStruct((LAST_KEYS, 2 * HD), jnp.bfloat16),
+            jax.ShapeDtypeStruct((1,), jnp.int32),
         ),
         grid_spec=pltpu.PrefetchScalarGridSpec(
             num_scalar_prefetch=1,
@@ -400,16 +432,22 @@
             + [
                 pl.BlockSpec(
                     (2, 1, 128, HD), lambda i, w: (0, BRANCH - 1, w[4], HEADS_HERE - 1)
-                )
+                ),
+                pl.BlockSpec((1, 1, TXT, HD), lambda i, w: (0, w[0], 0, w[1])),
+                whole((2, HD)),
             ],
-            out_specs=(whole((LAST_KEYS, HD)), whole((LAST_KEYS, 2 * HD))),
+            out_specs=(
+                whole((LAST_KEYS, HD)),
+                whole((LAST_KEYS, 2 * HD)),
+                pl.BlockSpec(memory_space=pltpu.SMEM),
+            ),
         ),
         compiler_params=pltpu.CompilerParams(vmem_limit_bytes=16 * MIB),
         cost_estimate=pl.CostEstimate(
             flops=10_000_000_000, bytes_accessed=10_000_000, transcendentals=0
         ),
         name="lay_last",
-    )(where, *lasts, text_kv)
+    )(where, *lasts, text_kv, text_kv, gains)
 
 
 def attend_last_kernel(where_ref, q_ref, keys_ref, value_ref, out_ref, score_ref):
@@ -454,15 +492,18 @@
     )(where, received, keys, values)
 
 
-def attend_far_kernel(finish, q_ref, set_ref, *refs):
+def attend_far_kernel(finish, flag_ref, q_ref, set_ref, *refs):
     mixed_in, total_in, top_in, *refs = refs
+    score_ref, top_ref, total_ref, mixed_ref = refs[-4:]
     here = tile_rows()
     before = top_in[here, 0:1]
-    score_ref = refs[-1]
-    top, total, mixed = gather_rows(q_ref[here, :], [set_piece(set_ref)], score_ref, before)
-    decay = jnp.exp2(before - top)
-    total += total_in[here, :] * decay
-    mixed += mixed_in[here, :] * decay
+    gather_rows(
+        flag_ref, q_ref[here, :], [set_piece(set_ref)], before, score_ref,
+        top_ref, total_ref, mixed_ref,
+    )
+    decay = jnp.exp2(before - top_ref[:, 0:1])
+    total = total_ref[...] + total_in[here, :] * decay
+    mixed = mixed_ref[...] + mixed_in[here, :] * decay
     if finish:
         last_ref, out_ref = refs[:2]
         result = (mixed / jnp.sum(total, axis=1, keepdims=True)).astype(jnp.bfloat16)
@@ -470,28 +511,32 @@
         out_ref[frames, 0:TOK, :] = result.reshape(QUAD, TOK, HD)
         out_ref[frames, TOK:RETURN, :] = last_ref[frames]
     else:
-        mixed_ref, total_ref, top_ref = refs[:3]
-        mixed_ref[here, :] = mixed
-        total_ref[here, :] = total
-        top_ref[here, :] = jnp.broadcast_to(top, (TILE, 128))
-
-
-def attend_far(queries, keys, state, last=None):
+        mixed_out, total_out, top_out = refs[:3]
+        mixed_out[here, :] = mixed
+        total_out[here, :] = total
+        top_out[here, :] = top_ref[...]
+
+
+def attend_far(flag, queries, keys, state, last=None):
     finish = last is not None
     operands = [queries, keys, *state] + ([last] if finish else [])
     return pl.pallas_call(
         functools.partial(attend_far_kernel, finish),
         out_shape=pltpu.VMEM((RING, RETURN, HD), jnp.bfloat16) if finish else STATE,
-        grid=(SET // TILE,),
-        in_specs=[IN_VMEM] * len(operands),
-        out_specs=IN_VMEM if finish else (IN_VMEM,) * 3,
-        scratch_shapes=[pltpu.VMEM((TILE, SET), jnp.float32)],
+        grid_spec=pltpu.PrefetchScalarGridSpec(
+            num_scalar_prefetch=1,
+            grid=(SET // TILE,),
+            in_specs=[IN_VMEM] * len(operands),
+            out_specs=IN_VMEM if finish else (IN_VMEM,) * 3,
+            scratch_shapes=[pltpu.VMEM((TILE, SET), jnp.float32)]
+            + [pltpu.VMEM((TILE, 128), jnp.float32)] * 3,
+        ),
         compiler_params=pltpu.CompilerParams(vmem_limit_bytes=16 * MIB),
         cost_estimate=pl.CostEstimate(
             flops=4 * SET * SET * HD, bytes_accessed=3_000_000, transcendentals=SET * SET
         ),
         name="attend_far",
-    )(*map(in_vmem, operands))
+    )(flag, *map(in_vmem, operands))
 
 
 def output_kernel(place_ref, back_ref, w_ref, *refs):
@@ -628,17 +673,19 @@
     received = over_rings(send)
     flips = (1, FRAMES // 2, FRAMES // 2 + 1)
     lasts = [last] + [frame_move(last, flip) for flip in flips]
-    last_keys, last_values = lay_last(where, lasts, text_kv)
+    last_keys, last_values, flag = lay_last(where, lasts, text_kv, gains)
     near = received[:, : 2 * TOK]
     over_y = frame_move(near, FRAMES // 2)
+    near_later, last_keys = lax.optimization_barrier((near, last_keys))
+    over_core = frame_move(near_later, 1)
     ninth = attend_last(where, received, last_keys, last_values)
-    near_later, _ = lax.optimization_barrier((near, ninth))
-    over_core = frame_move(near_later, 1)
-    *state, queries, w_held = attend_near(where, received, near, over_core, text_kv, in_hbm(w_out))
+    *state, queries, w_held = attend_near(
+        where, flag, received, near, over_core, text_kv, in_hbm(w_out)
+    )
     over_y, _, _ = lax.optimization_barrier((over_y, state[0], ninth))
     diagonal = frame_move(over_y, 1)
-    state = attend_far(queries, over_y, state)
-    returned = attend_far(queries, diagonal, state, ninth)
+    state = attend_far(flag, queries, over_y, state)
+    returned = attend_far(flag, queries, diagonal, state, ninth)
     back = over_rings(returned)
     proj = scatter_head(places, back, w_held).reshape(video.shape)
     return (video.astype(jnp.float32) + gate * proj).astype(jnp.bfloat16)

time: 147 us -> 147 us (level)
  waiting for transfers between devices: 58.1 us -> 53.1 us
  Pallas kernels: 31.8 us -> 36 us
    ppermute x6, waiting for transfers between devices: 9.6 us -> 5.55 us  [frame_move(): return lax.ppermute(x, 'frame', [(i, i ^ flip) for i in range(FRAMES)])]
    pallas_call x2, Pallas kernels: 6.74 us -> 9.15 us  [attend_far(): pl.pallas_call(functools.partial(attend_far_kernel, finish), out_shape=pl...]
  transfers between devices with their start and end apart: 21 -> 21, of which waited for: 13 -> 12; matrix products, arithmetic and copies ran while one was open for 1% -> 1% of each run, Pallas kernels for 10% -> 14%
where the time goes in v7:
time: 147 us; the launch traced here: 145 us
  waiting for transfers between devices  53.1 us (36%)
  Pallas kernels  36 us (24%)
  starting transfers between devices  31.7 us (22%)
  blocking collectives  21.5 us (15%)
  other arithmetic  2.21 us (2%)
    all_to_all x1, blocking collectives, over_rings(): return lax.all_to_all(x, 'frame', 0, 0, axis_index_groups=rings, tiled=True)  21.5 us
    all_to_all x1, waiting for transfers between devices, over_rings(): return lax.all_to_all(x, 'frame', 0, 0, axis_index_groups=rings, tiled=True)  21.4 us
    ppermute x10, waiting for transfers between devices, head_move(): lax.ppermute(x, 'head', [(i, (i + step) % HEAD_AXIS) for i in range(HEAD_...  21.2 us
    ppermute x10, starting transfers between devices, head_move(): lax.ppermute(x, 'head', [(i, (i + step) % HEAD_AXIS) for i in range(HEAD_...  14 us
    pallas_call x2, Pallas kernels, attend_far(): pl.pallas_call(functools.partial(attend_far_kernel, finish), out_shape=pl...  9.15 us
    all_to_all x1, starting transfers between devices, over_rings(): return lax.all_to_all(x, 'frame', 0, 0, axis_index_groups=rings, tiled=True)  8.48 us
    pallas_call x1, Pallas kernels, attend_near(): pl.pallas_call(attend_near_kernel, out_shape=STATE + (pltpu.VMEM((SET, HD...  8.37 us
    pallas_call x1, Pallas kernels, project(): pl.pallas_call(project_kernel, out_shape=(pltpu.VMEM((RING, 4 * TOK, HD),...  7.88 us
  transfers between devices with their start and end apart: 21, of which 12 were waited for; matrix products, arithmetic and copies ran while one was open for 1% of the time, Pallas kernels for 14%

profile of v7, /device:TPU:6, one launch (start us, length us, event | category | flops | bytes accessed | tf_op | source)
XLA Modules:
  0.0 145.3 jit_solution(11130886655890427062)
XLA Ops:
  0.7 2.4 %prep.1 = (bf16[400,384]{1,0:T(8,128)(2,1)S(1)}, f32[1,384]{1,0:T(1,128)S(1)}, f32[2,128]{1,0:T(2,128)S(1)}, s32[8]{0:T(128)S(1)}, s32[5]{0:T(128)S(1)}) custom-call(s32[1]{0:T(128)} %bitcast.frame_ref, s32[1]{0:T(128)} %bitcast.1.head_ref, s32[1]{0:T(128)S(6)} %copy.13.shift_ref, s32[32]{0:T(128)} %ids_ref.1, s32[3]{0:T(128)} %lengths_ref.1, ...), custom_call_target="tpu_custom_call" | custom-call | tf_op jit(solution)/shard_map/prep/pallas_call | solution.py:109
  3.0 3.3 %collective-permute-start = (bf16[400,384]{1,0:T(8,128)(2,1)S(1)}, bf16[400,384]{1,0:T(8,128)(2,1)S(1)}, u32[]{:S(2)}, u32[]{:S(2)}) collective-permute-start(bf16[400,384]{1,0:T(8,128)(2,1)S(1)} %get-tuple-element.38.refs_0_), channel_id=1, source_target_pairs={{0,1},{1,0},{2,3},{3,2},{4,5},{5,4},{6,7},{7,6},{8,9},{9,8},{10,11... | collective-permute-start | bytes 921608 | tf_op jit(solution)/shard_map/ppermute | solution.py:604
  6.3 1.4 collective-permute-start.5
  7.7 3.2 %collective-permute-start.2 = (bf16[400,384]{1,0:T(8,128)(2,1)S(1)}, bf16[400,384]{1,0:T(8,128)(2,1)S(1)}, u32[]{:S(2)}, u32[]{:S(2)}) collective-permute-start(bf16[400,384]{1,0:T(8,128)(2,1)S(1)} %get-tuple-element.38.refs_0_), channel_id=1, source_target_pairs={{0,2},{1,3},{2,4},{3,5},{4,6},{5,7},{6,0},{7,1},{8,10},{9,11},{10,... | collective-permute-start | bytes 921608 | tf_op jit(solution)/shard_map/ppermute | solution.py:600
  10.9 2.7 %collective-permute-done.refs_1_ = bf16[400,384]{1,0:T(8,128)(2,1)S(1)} collective-permute-done((bf16[400,384]{1,0:T(8,128)(2,1)S(1)}, bf16[400,384]{1,0:T(8,128)(2,1)S(1)}, u32[]{:S(2)}, u32[]{:S(2)}) %collective-permute-start) | collective-permute-done | bytes 307232 | tf_op jit(solution)/shard_map/ppermute | solution.py:604
  14.5 2.4 %collective-permute-start.4 = (bf16[400,384]{1,0:T(8,128)(2,1)S(1)}, bf16[400,384]{1,0:T(8,128)(2,1)S(1)}, u32[]{:S(2)}, u32[]{:S(2)}) collective-permute-start(bf16[400,384]{1,0:T(8,128)(2,1)S(1)} %collective-permute-done.refs_1_), channel_id=1, source_target_pairs={{0,2},{1,3},{2,4},{3,5},{4,6},{5,7},{6,0},{7,1},{8,10},{9,11},{10,... | collective-permute-start | bytes 921608 | tf_op jit(solution)/shard_map/ppermute | solution.py:600
  16.9 1.2 collective-permute-done.5.refs_6_
  18.0 2.0 %collective-permute-start.6 = (bf16[400,384]{1,0:T(8,128)(2,1)S(1)}, bf16[400,384]{1,0:T(8,128)(2,1)S(1)}, u32[]{:S(2)}, u32[]{:S(2)}) collective-permute-start(bf16[400,384]{1,0:T(8,128)(2,1)S(1)} %collective-permute-done.5.refs_6_), channel_id=1, source_target_pairs={{0,1},{1,0},{2,3},{3,2},{4,5},{5,4},{6,7},{7,6},{8,9},{9,8},{10,11... | collective-permute-start | bytes 921608 | tf_op jit(solution)/shard_map/ppermute | solution.py:604
  20.1 1.0 sine_multiply_fusion
  21.1 2.1 %collective-permute-done.1.refs_2_ = bf16[400,384]{1,0:T(8,128)(2,1)S(1)} collective-permute-done((bf16[400,384]{1,0:T(8,128)(2,1)S(1)}, bf16[400,384]{1,0:T(8,128)(2,1)S(1)}, u32[]{:S(2)}, u32[]{:S(2)}) %collective-permute-start.1) | collective-permute-done | bytes 307232 | tf_op jit(solution)/shard_map/ppermute | solution.py:600
  23.2 6.5 %collective-permute-done.3.refs_4_ = bf16[400,384]{1,0:T(8,128)(2,1)S(1)} collective-permute-done((bf16[400,384]{1,0:T(8,128)(2,1)S(1)}, bf16[400,384]{1,0:T(8,128)(2,1)S(1)}, u32[]{:S(2)}, u32[]{:S(2)}) %collective-permute-start.3) | collective-permute-done | bytes 307232 | tf_op jit(solution)/shard_map/ppermute | solution.py:600
  29.7 7.9 %project.1 = (bf16[8,512,128]{2,1,0:T(8,128)(2,1)}, bf16[256,128]{1,0:T(8,128)(2,1)S(1)}) custom-call(s32[8]{0:T(128)S(1)} %get-tuple-element.36.place_ref, bf16[400,384]{1,0:T(8,128)(2,1)S(1)} %get-tuple-element.38.refs_0_, bf16[400,384]{1,0:T(8,128)(2,1)S(1)} %collective-permute-done.refs_1_, bf16[400,384]{1,0:T(8,128)(2,1)S(1)} %collective-permute-done.1.refs_2_, ...), custom_call_target="tpu_custom_call" | custom-call | flops 2717908992 | bytes 12000000 | tf_op jit(solution)/shard_map/project/pallas_call | solution.py:206
  37.6 8.5 %all-to-all-start = ((bf16[8,512,128]{2,1,0:T(8,128)(2,1)}), bf16[8,512,128]{2,1,0:T(8,128)(2,1)S(1)}, u32[]{:S(2)}, u32[]{:S(2)}) async-start(bf16[8,512,128]{2,1,0:T(8,128)(2,1)} %get-tuple-element.42), calls=%async_computation | async-start | bytes 2097152 | tf_op jit(solution)/shard_map/all_to_all | solution.py:671
  46.9 1.1 collective-permute-start.9
  48.0 3.1 %collective-permute-done.8.refs_2_ = bf16[256,128]{1,0:T(8,128)(2,1)S(1)} collective-permute-done((bf16[256,128]{1,0:T(8,128)(2,1)S(1)}, bf16[256,128]{1,0:T(8,128)(2,1)S(1)}, u32[]{:S(2)}, u32[]{:S(2)}) %collective-permute-start.8) | collective-permute-done | bytes 65568 | tf_op jit(solution)/shard_map/ppermute | solution.py:608
  51.5 2.1 %lay_last.1 = (bf16[640,128]{1,0:T(8,128)(2,1)S(1)}, bf16[640,256]{1,0:T(8,128)(2,1)S(1)}, s32[1]{0:T(128)}) custom-call(s32[5]{0:T(128)S(1)} %get-tuple-element.37.where_ref, bf16[256,128]{1,0:T(8,128)(2,1)S(1)} %get-tuple-element.40.refs_0_, bf16[256,128]{1,0:T(8,128)(2,1)S(1)} %collective-permute-done.7.refs_1_, ...), custom_call_target="tpu_custom_call" | custom-call | flops 10000000000 | bytes 10000000 | tf_op jit(solution)/shard_map/lay_last/pallas_call | solution.py:421
  53.7 21.4 %all-to-all-done.q_ref = bf16[8,512,128]{2,1,0:T(8,128)(2,1)S(1)} async-done(((bf16[8,512,128]{2,1,0:T(8,128)(2,1)}), bf16[8,512,128]{2,1,0:T(8,128)(2,1)S(1)}, u32[]{:S(2)}, u32[]{:S(2)}) %all-to-all-start) | async-done | bytes 1048608 | tf_op jit(solution)/shard_map/all_to_all | solution.py:671
  76.1 3.0 %attend_last.1.refs_3_ = bf16[8,144,128]{2,1,0:T(8,128)(2,1)S(1)} custom-call(s32[5]{0:T(128)S(1)} %get-tuple-element.37.where_ref, bf16[8,512,128]{2,1,0:T(8,128)(2,1)S(1)} %all-to-all-done.q_ref, bf16[640,128]{1,0:T(8,128)(2,1)S(1)} %get-tuple-element.47.keys_ref, bf16[640,256]{1,0:T(8,128)(2,1)S(1)} %get-tuple-element.48.value_ref), custom_call_target="tpu_custom_call" | custom-call | flops 335544320 | bytes 1000000 | tf_op jit(solution)/shard_map/attend_last/pallas_call | solution.py:473
  79.1 8.4 %attend_near.1 = (f32[1024,128]{1,0:T(8,128)S(1)}, f32[1024,128]{1,0:T(8,128)S(1)}, f32[1024,128]{1,0:T(8,128)S(1)}, bf16[1024,128]{1,0:T(8,128)(2,1)S(1)}, bf16[384,3072]{1,0:T(8,128)(2,1)S(1)}) custom-call(s32[5]{0:T(128)S(1)} %get-tuple-element.37.where_ref, s32[1]{0:T(128)} %get-tuple-element.41.flag_ref, bf16[8,512,128]{2,1,0:T(8,128)(2,1)S(1)} %all-to-all-done.q_ref, ...), custom_call_target="tpu_custom_call" | custom-call | flops 1207959552 | bytes 3000000 | tf_op jit(solution)/shard_map/attend_near/pallas_call | solution.py:370
  87.5 2.0 %collective-permute-done.11.set_ref = bf16[8,256,128]{2,1,0:T(8,128)(2,1)S(1)} collective-permute-done((bf16[8,256,128]{2,1,0:T(8,128)(2,1)S(1)}, bf16[8,256,128]{2,1,0:T(8,128)(2,1)S(1)}, u32[]{:S(2)}, u32[]{:S(2)}) %collective-permute-start.11) | collective-permute-done | bytes 524320 | tf_op jit(solution)/shard_map/ppermute | solution.py:608
  89.5 4.5 %attend_far.2 = (f32[1024,128]{1,0:T(8,128)S(1)}, f32[1024,128]{1,0:T(8,128)S(1)}, f32[1024,128]{1,0:T(8,128)S(1)}) custom-call(s32[1]{0:T(128)} %get-tuple-element.41.flag_ref, bf16[1024,128]{1,0:T(8,128)(2,1)S(1)} %get-tuple-element.45.q_ref, bf16[8,256,128]{2,1,0:T(8,128)(2,1)S(1)} %collective-permute-done.11.set_ref, ...), custom_call_target="tpu_custom_call" | custom-call | flops 536870912 | bytes 3000000 | tf_op jit(solution)/shard_map/attend_far/pallas_call | solution.py:523
  94.0 4.7 %attend_far.3 = bf16[8,272,128]{2,1,0:T(8,128)(2,1)S(1)} custom-call(s32[1]{0:T(128)} %get-tuple-element.41.flag_ref, bf16[1024,128]{1,0:T(8,128)(2,1)S(1)} %get-tuple-element.45.q_ref, bf16[8,256,128]{2,1,0:T(8,128)(2,1)S(1)} %collective-permute-done.12.set_ref, f32[1024,128]{1,0:T(8,128)S(1)} %get-tuple-element.52.refs_0_, ...), custom_call_target="tpu_custom_call" | custom-call | flops 536870912 | bytes 3000000 | tf_op jit(solution)/shard_map/attend_far/pallas_call | solution.py:523
  98.7 21.5 %all_to_all.10.back_ref = bf16[8,272,128]{2,1,0:T(8,128)(2,1)S(1)} all-to-all(bf16[8,272,128]{2,1,0:T(8,128)(2,1)S(1)} %attend_far.3), channel_id=1, replica_groups={{0,16,32,48,64,80,96,112},{8,24,40,56,72,88,104,120},{128,144,160,176,1..., dimensions={0} | all-to-all | bytes 1114112 | tf_op jit(solution)/shard_map/all_to_all | solution.py:671
  120.2 1.2 output.2
  122.0 1.6 %collective-permute-start.16 = (bf16[384,384]{1,0:T(8,128)(2,1)S(1)}, bf16[384,384]{1,0:T(8,128)(2,1)S(1)}, u32[]{:S(2)}, u32[]{:S(2)}) collective-permute-start(bf16[384,384]{1,0:T(8,128)(2,1)S(1)} %get-tuple-element.62), channel_id=1, source_target_pairs={{0,6},{1,7},{2,0},{3,1},{4,2},{5,3},{6,4},{7,5},{8,14},{9,15},{10,... | collective-permute-start | bytes 884744 | tf_op jit(solution)/shard_map/ppermute | solution.py:600
  123.6 1.8 %output.3 = (bf16[384,384]{1,0:T(8,128)(2,1)S(1)}, bf16[384,384]{1,0:T(8,128)(2,1)S(1)}, bf16[384,384]{1,0:T(8,128)(2,1)S(1)}, bf16[384,384]{1,0:T(8,128)(2,1)S(...) custom-call(s32[8]{0:T(128)S(1)} %get-tuple-element.36.place_ref, ...), custom_call_target="tpu_custom_call" | custom-call | flops 679477248 | bytes 3000000 | tf_op jit(solution)/shard_map/output/pallas_call | solution.py:582
  126.2 1.6 %collective-permute-start.13 = (bf16[384,384]{1,0:T(8,128)(2,1)S(1)}, bf16[384,384]{1,0:T(8,128)(2,1)S(1)}, u32[]{:S(2)}, u32[]{:S(2)}) collective-permute-start(bf16[384,384]{1,0:T(8,128)(2,1)S(1)} %get-tuple-element.58), channel_id=1, source_target_pairs={{0,2},{1,3},{2,4},{3,5},{4,6},{5,7},{6,0},{7,1},{8,10},{9,11},{10,... | collective-permute-start | bytes 884744 | tf_op jit(solution)/shard_map/ppermute | solution.py:600
  128.3 3.2 %collective-permute-done.15 = bf16[384,384]{1,0:T(8,128)(2,1)S(1)} collective-permute-done((bf16[384,384]{1,0:T(8,128)(2,1)S(1)}, bf16[384,384]{1,0:T(8,128)(2,1)S(1)}, u32[]{:S(2)}, u32[]{:S(2)}) %collective-permute-start.15) | collective-permute-done | bytes 294944 | tf_op jit(solution)/shard_map/ppermute | solution.py:600
  131.5 1.4 collective-permute-done.16
  133.1 2.3 %collective-permute-done.18 = bf16[384,384]{1,0:T(8,128)(2,1)S(1)} collective-permute-done((bf16[384,384]{1,0:T(8,128)(2,1)S(1)}, bf16[384,384]{1,0:T(8,128)(2,1)S(1)}, u32[]{:S(2)}, u32[]{:S(2)}) %collective-permute-start.18) | collective-permute-done | bytes 294944 | tf_op jit(solution)/shard_map/ppermute | solution.py:604
  135.4 2.0 %collective-permute-start.19 = (bf16[384,384]{1,0:T(8,128)(2,1)S(1)}, bf16[384,384]{1,0:T(8,128)(2,1)S(1)}, u32[]{:S(2)}, u32[]{:S(2)}) collective-permute-start(bf16[384,384]{1,0:T(8,128)(2,1)S(1)} %add_convert_fusion.1), channel_id=1, source_target_pairs={{0,4},{1,5},{2,6},{3,7},{4,0},{5,1},{6,2},{7,3},{8,12},{9,13},{10,... | collective-permute-start | bytes 884744 | tf_op jit(solution)/shard_map/ppermute | solution.py:600
  137.4 6.9 %collective-permute-done.14 = bf16[384,384]{1,0:T(8,128)(2,1)S(1)} collective-permute-done((bf16[384,384]{1,0:T(8,128)(2,1)S(1)}, bf16[384,384]{1,0:T(8,128)(2,1)S(1)}, u32[]{:S(2)}, u32[]{:S(2)}) %collective-permute-start.14) | collective-permute-done | bytes 294944 | tf_op jit(solution)/shard_map/ppermute | solution.py:600
  (30 shorter events, 6.2 us)
Async XLA Ops:
  3.0 10.6 %collective-permute-start = (bf16[400,384]{1,0:T(8,128)(2,1)S(1)}, bf16[400,384]{1,0:T(8,128)(2,1)S(1)}, u32[]{:S(2)}, u32[]{:S(2)}) collective-permute-start(bf16[400,384]{1,0:T(8,128)(2,1)S(1)} %get-tuple-element.38.refs_0_), channel_id=1, source_target_pairs={{0,1},{1,0},{2,3},{3,2},{4,5},{5,4},{6,7},{7,6},{8,9},{9,8},{10,11... | collective-permute-start | bytes 921608 | tf_op jit(solution)/shard_map/ppermute | solution.py:604
  6.3 11.7 %collective-permute-start.5 = (bf16[400,384]{1,0:T(8,128)(2,1)S(1)}, bf16[400,384]{1,0:T(8,128)(2,1)S(1)}, u32[]{:S(2)}, u32[]{:S(2)}) collective-permute-start(bf16[400,384]{1,0:T(8,128)(2,1)S(1)} %get-tuple-element.38.refs_0_), channel_id=1, source_target_pairs={{0,4},{1,5},{2,6},{3,7},{4,0},{5,1},{6,2},{7,3},{8,12},{9,13},{10,... | collective-permute-start | bytes 921608 | tf_op jit(solution)/shard_map/ppermute | solution.py:600
  7.7 15.5 %collective-permute-start.1 = (bf16[400,384]{1,0:T(8,128)(2,1)S(1)}, bf16[400,384]{1,0:T(8,128)(2,1)S(1)}, u32[]{:S(2)}, u32[]{:S(2)}) collective-permute-start(bf16[400,384]{1,0:T(8,128)(2,1)S(1)} %get-tuple-element.38.refs_0_), channel_id=1, source_target_pairs={{0,6},{1,7},{2,0},{3,1},{4,2},{5,3},{6,4},{7,5},{8,14},{9,15},{10,... | collective-permute-start | bytes 921608 | tf_op jit(solution)/shard_map/ppermute | solution.py:600
  7.7 15.5 %collective-permute-start.2 = (bf16[400,384]{1,0:T(8,128)(2,1)S(1)}, bf16[400,384]{1,0:T(8,128)(2,1)S(1)}, u32[]{:S(2)}, u32[]{:S(2)}) collective-permute-start(bf16[400,384]{1,0:T(8,128)(2,1)S(1)} %get-tuple-element.38.refs_0_), channel_id=1, source_target_pairs={{0,2},{1,3},{2,4},{3,5},{4,6},{5,7},{6,0},{7,1},{8,10},{9,11},{10,... | collective-permute-start | bytes 921608 | tf_op jit(solution)/shard_map/ppermute | solution.py:600
  13.6 16.1 %collective-permute-start.3 = (bf16[400,384]{1,0:T(8,128)(2,1)S(1)}, bf16[400,384]{1,0:T(8,128)(2,1)S(1)}, u32[]{:S(2)}, u32[]{:S(2)}) collective-permute-start(bf16[400,384]{1,0:T(8,128)(2,1)S(1)} %collective-permute-done.refs_1_), channel_id=1, source_target_pairs={{0,6},{1,7},{2,0},{3,1},{4,2},{5,3},{6,4},{7,5},{8,14},{9,15},{10,... | collective-permute-start | bytes 921608 | tf_op jit(solution)/shard_map/ppermute | solution.py:600
  14.5 15.3 %collective-permute-start.4 = (bf16[400,384]{1,0:T(8,128)(2,1)S(1)}, bf16[400,384]{1,0:T(8,128)(2,1)S(1)}, u32[]{:S(2)}, u32[]{:S(2)}) collective-permute-start(bf16[400,384]{1,0:T(8,128)(2,1)S(1)} %collective-permute-done.refs_1_), channel_id=1, source_target_pairs={{0,2},{1,3},{2,4},{3,5},{4,6},{5,7},{6,0},{7,1},{8,10},{9,11},{10,... | collective-permute-start | bytes 921608 | tf_op jit(solution)/shard_map/ppermute | solution.py:600
  18.0 11.7 %collective-permute-start.6 = (bf16[400,384]{1,0:T(8,128)(2,1)S(1)}, bf16[400,384]{1,0:T(8,128)(2,1)S(1)}, u32[]{:S(2)}, u32[]{:S(2)}) collective-permute-start(bf16[400,384]{1,0:T(8,128)(2,1)S(1)} %collective-permute-done.5.refs_6_), channel_id=1, source_target_pairs={{0,1},{1,0},{2,3},{3,2},{4,5},{5,4},{6,7},{7,6},{8,9},{9,8},{10,11... | collective-permute-start | bytes 921608 | tf_op jit(solution)/shard_map/ppermute | solution.py:604
  37.6 37.4 %all-to-all-start = ((bf16[8,512,128]{2,1,0:T(8,128)(2,1)}), bf16[8,512,128]{2,1,0:T(8,128)(2,1)S(1)}, u32[]{:S(2)}, u32[]{:S(2)}) async-start(bf16[8,512,128]{2,1,0:T(8,128)(2,1)} %get-tuple-element.42), calls=%async_computation | async-start | bytes 2097152 | tf_op jit(solution)/shard_map/all_to_all | solution.py:671
  46.1 1.9 %collective-permute-start.7 = (bf16[256,128]{1,0:T(8,128)(2,1)S(1)}, bf16[256,128]{1,0:T(8,128)(2,1)S(1)}, u32[]{:S(2)}, u32[]{:S(2)}) collective-permute-start(bf16[256,128]{1,0:T(8,128)(2,1)S(1)} %get-tuple-element.40.refs_0_), channel_id=1, source_target_pairs={{0,8},{8,0},{16,24},{24,16},{32,40},{40,32},{48,56},{56,48},{64,72... | collective-permute-start | bytes 196616 | tf_op jit(solution)/shard_map/ppermute | solution.py:608
  46.1 5.0 %collective-permute-start.8 = (bf16[256,128]{1,0:T(8,128)(2,1)S(1)}, bf16[256,128]{1,0:T(8,128)(2,1)S(1)}, u32[]{:S(2)}, u32[]{:S(2)}) collective-permute-start(bf16[256,128]{1,0:T(8,128)(2,1)S(1)} %get-tuple-element.40.refs_0_), channel_id=1, source_target_pairs={{0,128},{8,136},{16,144},{24,152},{32,160},{40,168},{48,176},{56,1... | collective-permute-start | bytes 196616 | tf_op jit(solution)/shard_map/ppermute | solution.py:608
  46.9 4.7 %collective-permute-start.9 = (bf16[256,128]{1,0:T(8,128)(2,1)S(1)}, bf16[256,128]{1,0:T(8,128)(2,1)S(1)}, u32[]{:S(2)}, u32[]{:S(2)}) collective-permute-start(bf16[256,128]{1,0:T(8,128)(2,1)S(1)} %get-tuple-element.40.refs_0_), channel_id=1, source_target_pairs={{0,136},{8,128},{16,152},{24,144},{32,168},{40,160},{48,184},{56,1... | collective-permute-start | bytes 196616 | tf_op jit(solution)/shard_map/ppermute | solution.py:608
  75.1 4.1 %collective-permute-start.10 = (bf16[8,256,128]{2,1,0:T(8,128)(2,1)S(1)}, bf16[8,256,128]{2,1,0:T(8,128)(2,1)S(1)}, u32[]{:S(2)}, u32[]{:S(2)}) collective-permute-start(bf16[8,256,128]{2,1,0:T(8,128)(2,1)S(1)} %slice.4.own_ref), channel_id=1, source_target_pairs={{0,8},{8,0},{16,24},{24,16},{32,40},{40,32},{48,56},{56,48},{64,72... | collective-permute-start | bytes 1572872 | tf_op jit(solution)/shard_map/ppermute | solution.py:608
  75.2 14.3 %collective-permute-start.11 = (bf16[8,256,128]{2,1,0:T(8,128)(2,1)S(1)}, bf16[8,256,128]{2,1,0:T(8,128)(2,1)S(1)}, u32[]{:S(2)}, u32[]{:S(2)}) collective-permute-start(bf16[8,256,128]{2,1,0:T(8,128)(2,1)S(1)} %slice.4.own_ref), channel_id=1, source_target_pairs={{0,128},{8,136},{16,144},{24,152},{32,160},{40,168},{48,176},{56,1... | collective-permute-start | bytes 1572872 | tf_op jit(solution)/shard_map/ppermute | solution.py:608
  89.5 4.5 %collective-permute-start.12 = (bf16[8,256,128]{2,1,0:T(8,128)(2,1)S(1)}, bf16[8,256,128]{2,1,0:T(8,128)(2,1)S(1)}, u32[]{:S(2)}, u32[]{:S(2)}) collective-permute-start(bf16[8,256,128]{2,1,0:T(8,128)(2,1)S(1)} %collective-permute-done.11.set_ref), channel_id=1, source_target_pairs={{0,8},{8,0},{16,24},{24,16},{32,40},{40,32},{48,56},{56,48},{64,72... | collective-permute-start | bytes 1572872 | tf_op jit(solution)/shard_map/ppermute | solution.py:608
  121.5 10.0 %collective-permute-start.15 = (bf16[384,384]{1,0:T(8,128)(2,1)S(1)}, bf16[384,384]{1,0:T(8,128)(2,1)S(1)}, u32[]{:S(2)}, u32[]{:S(2)}) collective-permute-start(bf16[384,384]{1,0:T(8,128)(2,1)S(1)} %get-tuple-element.61), channel_id=1, source_target_pairs={{0,2},{1,3},{2,4},{3,5},{4,6},{5,7},{6,0},{7,1},{8,10},{9,11},{10,... | collective-permute-start | bytes 884744 | tf_op jit(solution)/shard_map/ppermute | solution.py:600
  122.0 10.9 %collective-permute-start.16 = (bf16[384,384]{1,0:T(8,128)(2,1)S(1)}, bf16[384,384]{1,0:T(8,128)(2,1)S(1)}, u32[]{:S(2)}, u32[]{:S(2)}) collective-permute-start(bf16[384,384]{1,0:T(8,128)(2,1)S(1)} %get-tuple-element.62), channel_id=1, source_target_pairs={{0,6},{1,7},{2,0},{3,1},{4,2},{5,3},{6,4},{7,5},{8,14},{9,15},{10,... | collective-permute-start | bytes 884744 | tf_op jit(solution)/shard_map/ppermute | solution.py:600
  125.4 19.1 %copy-start = (bf16[3,128,384]{2,1,0:T(8,128)(2,1)S(1)}, bf16[3,128,384]{2,1,0:T(8,128)(2,1)}, u32[]{:S(2)}) copy-start(bf16[3,128,384]{2,1,0:T(8,128)(2,1)} %video_ref.1) | copy-start | bytes 884740
  125.4 9.9 %collective-permute-start.18 = (bf16[384,384]{1,0:T(8,128)(2,1)S(1)}, bf16[384,384]{1,0:T(8,128)(2,1)S(1)}, u32[]{:S(2)}, u32[]{:S(2)}) collective-permute-start(bf16[384,384]{1,0:T(8,128)(2,1)S(1)} %get-tuple-element.64), channel_id=1, source_target_pairs={{0,1},{1,0},{2,3},{3,2},{4,5},{5,4},{6,7},{7,6},{8,9},{9,8},{10,11... | collective-permute-start | bytes 884744 | tf_op jit(solution)/shard_map/ppermute | solution.py:604
  126.2 11.2 %collective-permute-start.13 = (bf16[384,384]{1,0:T(8,128)(2,1)S(1)}, bf16[384,384]{1,0:T(8,128)(2,1)S(1)}, u32[]{:S(2)}, u32[]{:S(2)}) collective-permute-start(bf16[384,384]{1,0:T(8,128)(2,1)S(1)} %get-tuple-element.58), channel_id=1, source_target_pairs={{0,2},{1,3},{2,4},{3,5},{4,6},{5,7},{6,0},{7,1},{8,10},{9,11},{10,... | collective-permute-start | bytes 884744 | tf_op jit(solution)/shard_map/ppermute | solution.py:600
  127.9 16.4 %collective-permute-start.14 = (bf16[384,384]{1,0:T(8,128)(2,1)S(1)}, bf16[384,384]{1,0:T(8,128)(2,1)S(1)}, u32[]{:S(2)}, u32[]{:S(2)}) collective-permute-start(bf16[384,384]{1,0:T(8,128)(2,1)S(1)} %get-tuple-element.59), channel_id=1, source_target_pairs={{0,6},{1,7},{2,0},{3,1},{4,2},{5,3},{6,4},{7,5},{8,14},{9,15},{10,... | collective-permute-start | bytes 884744 | tf_op jit(solution)/shard_map/ppermute | solution.py:600
  133.0 11.4 %collective-permute-start.17 = (bf16[384,384]{1,0:T(8,128)(2,1)S(1)}, bf16[384,384]{1,0:T(8,128)(2,1)S(1)}, u32[]{:S(2)}, u32[]{:S(2)}) collective-permute-start(bf16[384,384]{1,0:T(8,128)(2,1)S(1)} %add_convert_fusion.2), channel_id=1, source_target_pairs={{0,1},{1,0},{2,3},{3,2},{4,5},{5,4},{6,7},{7,6},{8,9},{9,8},{10,11... | collective-permute-start | bytes 884744 | tf_op jit(solution)/shard_map/ppermute | solution.py:604
  135.4 8.9 %collective-permute-start.19 = (bf16[384,384]{1,0:T(8,128)(2,1)S(1)}, bf16[384,384]{1,0:T(8,128)(2,1)S(1)}, u32[]{:S(2)}, u32[]{:S(2)}) collective-permute-start(bf16[384,384]{1,0:T(8,128)(2,1)S(1)} %add_convert_fusion.1), channel_id=1, source_target_pairs={{0,4},{1,5},{2,6},{3,7},{4,0},{5,1},{6,2},{7,3},{8,12},{9,13},{10,... | collective-permute-start | bytes 884744 | tf_op jit(solution)/shard_map/ppermute | solution.py:600

commit v8 on v7

--- a/solution.py
+++ b/solution.py
@@ -22,6 +22,7 @@
 ROWS = BRANCH * TOK
 MOD_ROWS = 16
 SENT = ROWS + MOD_ROWS
+CUT = ROWS // 2
 LAST = PAIRS - 1
 STAT_ROWS = 16
 LAST_ROWS = TOK + STAT_ROWS
@@ -133,41 +134,50 @@
 
 
 def project_kernel(place_ref, *refs):
-    blocks = refs[:HEAD_AXIS]
+    blocks, parts = refs[:6], refs[6:10]
     (
         w_hbm, gain_ref, cos_ref, sin_ref, out_ref, last_ref, mod_ref, acc_ref, w_ref, sems,
-    ) = refs[HEAD_AXIS:]
+    ) = refs[10:]
     copies = [
         pltpu.make_async_copy(w_hbm.at[n], w_ref.at[:, pl.ds(n * DSH, DSH)], sems.at[n])
         for n in range(3)
     ]
     for copy in copies:
         copy.start()
+    limbs = [block[ROWS:SENT, :] for block in blocks]
+    limbs += [parts[n][ROWS - CUT : SENT - CUT, :] for n in (1, 3)]
+    mods = []
+    for limb in limbs:
+        limb = limb.astype(jnp.float32)
+        shift = limb[0:1] + limb[1:2] + limb[2:3]
+        mods.append((shift, 1.0 + (limb[3:4] + limb[4:5] + limb[5:6])))
     step = 64
-
-    def chunk(n, carry):
-        here = pl.ds(pl.multiple_of(n * step, step), step)
-        total = jnp.zeros((step, 128), jnp.float32)
-        square = jnp.zeros((step, 128), jnp.float32)
-        for block in blocks:
-            for lane in range(0, DSH, 128):
-                x = block[here, lane : lane + 128].astype(jnp.float32)
-                total += x
-                square += x * x
-        mean = jnp.sum(total, axis=1, keepdims=True) / (HEAD_AXIS * DSH)
-        var = jnp.sum(square, axis=1, keepdims=True) / (HEAD_AXIS * DSH) - mean * mean
-        inv = lax.rsqrt(var + norm_eps)
-        for s, block in enumerate(blocks):
-            limbs = block[ROWS:SENT, :].astype(jnp.float32)
-            shift = limbs[0:1] + limbs[1:2] + limbs[2:3]
-            scale = limbs[3:4] + limbs[4:5] + limbs[5:6]
-            x = block[here, :].astype(jnp.float32)
-            y = (x - mean) * inv * (1.0 + scale) + shift
-            start = pl.multiple_of(place_ref[s] * DSH, DSH)
-            mod_ref[here, pl.ds(start, DSH)] = y.astype(jnp.bfloat16)
-        return carry
-
-    lax.fori_loop(0, ROWS // step, chunk, 0)
+    for first in (0, CUT):
+        late = 1 if first else 0
+
+        def chunk(n, carry):
+            there = pl.ds(pl.multiple_of(n * step, step), step)
+            here = pl.ds(pl.multiple_of(first + n * step, step), step)
+            sources = [(block, here) for block in blocks]
+            sources += [(parts[late], there), (parts[2 + late], there)]
+            total = jnp.zeros((step, 128), jnp.float32)
+            square = jnp.zeros((step, 128), jnp.float32)
+            for ref, rows in sources:
+                for lane in range(0, DSH, 128):
+                    x = ref[rows, lane : lane + 128].astype(jnp.float32)
+                    total += x
+                    square += x * x
+            mean = jnp.sum(total, axis=1, keepdims=True) / (HEAD_AXIS * DSH)
+            var = jnp.sum(square, axis=1, keepdims=True) / (HEAD_AXIS * DSH) - mean * mean
+            inv = lax.rsqrt(var + norm_eps)
+            for s, (ref, rows) in enumerate(sources):
+                shift, scale = mods[s]
+                y = (ref[rows, :].astype(jnp.float32) - mean) * inv * scale + shift
+                start = pl.multiple_of(place_ref[s] * DSH, DSH)
+                mod_ref[here, pl.ds(start, DSH)] = y.astype(jnp.bfloat16)
+            return carry
+
+        lax.fori_loop(0, CUT // step, chunk, 0)
 
     def piece(part, p):
         b, hd = divmod(p, HEADS_HERE)
@@ -212,7 +222,7 @@
         grid_spec=pltpu.PrefetchScalarGridSpec(
             num_scalar_prefetch=1,
             grid=(1,),
-            in_specs=[IN_VMEM] * HEAD_AXIS
+            in_specs=[IN_VMEM] * len(blocks)
             + [pl.BlockSpec(memory_space=pltpu.HBM), IN_VMEM, IN_VMEM, IN_VMEM],
             out_specs=(IN_VMEM, IN_VMEM),
             scratch_shapes=[
@@ -562,8 +572,8 @@
     multiply(place_ref, EARLY, attn_ref, w_ref, out_refs)
 
 
-EARLY = (4, 5)
-LATE = (7, 2, 3, 0, 1, 6)
+EARLY = (4, 5, 7)
+LATE = (2, 3, 0, 1, 6)
 
 
 def multiply(place_ref, places, attn_ref, w_ref, out_refs):
@@ -610,9 +620,9 @@
 
 def gather_head(own):
     partner = head_partner(own)
-    opposite = head_move(own, 4)
     ahead = head_move(own, -2)
     behind = head_move(own, 2)
+    opposite = [head_move(behind[:CUT], 2), head_move(ahead[CUT:], -2)]
     return [
         own,
         partner,
@@ -620,8 +630,8 @@
         behind,
         head_move(partner, -2),
         head_move(partner, 2),
-        opposite,
-        head_partner(opposite),
+        *opposite,
+        *map(head_partner, opposite),
     ]
 
 
@@ -633,12 +643,12 @@
 
 
 def scatter_head(places, back, w_out):
-    ahead, behind, attention = output(output_kernel, places, back, w_out, 3)
+    ahead, behind, over, attention = output(output_kernel, places, back, w_out, 4)
     for_partner = [head_move(ahead, 2), head_move(behind, -2)]
-    over, ahead, behind, own, partner, opposite = output(
+    for_opposite = head_partner(over)
+    ahead, behind, own, partner, opposite = output(
         late_kernel, places, attention, w_out, len(LATE)
     )
-    for_opposite = head_partner(over)
     direct = [head_move(ahead, 2), head_move(behind, -2)]
     over_y = head_partner(add(partner, *for_partner).astype(jnp.bfloat16))
     across = head_move(add(opposite, for_opposite).astype(jnp.bfloat16), 4)

time: 147 us -> 145 us (0.986)
  waiting for transfers between devices: 53.1 us -> 46 us
  starting transfers between devices: 31.7 us -> 37.9 us
    ppermute x4 -> x5, starting transfers between devices: 6.25 us -> 11.5 us  [head_partner(): return lax.ppermute(x, 'head', [(i, i ^ 1) for i in range(HEAD_AXIS)])]
    ppermute x10 -> x11, waiting for transfers between devices: 21.2 us -> 16.3 us  [head_move(): lax.ppermute(x, 'head', [(i, (i + step) % HEAD_AXIS) for i in range(HEAD_...]
    all_to_all x1, waiting for transfers between devices: 21.4 us -> 18.6 us  [over_rings(): return lax.all_to_all(x, 'frame', 0, 0, axis_index_groups=rings, tiled=True)]
    ppermute x10 -> x11, starting transfers between devices: 14 us -> 15.4 us  [head_move(): lax.ppermute(x, 'head', [(i, (i + step) % HEAD_AXIS) for i in range(HEAD_...]
    ppermute x4 -> x5, waiting for transfers between devices: 4.95 us -> 5.4 us  [head_partner(): return lax.ppermute(x, 'head', [(i, i ^ 1) for i in range(HEAD_AXIS)])]
  transfers between devices with their start and end apart: 21 -> 23, of which waited for: 12 -> 12; matrix products, arithmetic and copies ran while one was open for 1% -> 1% of each run, Pallas kernels for 14% -> 14%
where the time goes in v8:
time: 145 us
  waiting for transfers between devices  46 us (32%)
  starting transfers between devices  37.9 us (26%)
  Pallas kernels  36 us (25%)
  blocking collectives  21.5 us (15%)
  other arithmetic  2.23 us (2%)
    all_to_all x1, blocking collectives, over_rings(): return lax.all_to_all(x, 'frame', 0, 0, axis_index_groups=rings, tiled=True)  21.5 us
    all_to_all x1, waiting for transfers between devices, over_rings(): return lax.all_to_all(x, 'frame', 0, 0, axis_index_groups=rings, tiled=True)  18.6 us
    ppermute x11, waiting for transfers between devices, head_move(): lax.ppermute(x, 'head', [(i, (i + step) % HEAD_AXIS) for i in range(HEAD_...  16.3 us
    ppermute x11, starting transfers between devices, head_move(): lax.ppermute(x, 'head', [(i, (i + step) % HEAD_AXIS) for i in range(HEAD_...  15.4 us
    ppermute x5, starting transfers between devices, head_partner(): return lax.ppermute(x, 'head', [(i, i ^ 1) for i in range(HEAD_AXIS)])  11.5 us
    pallas_call x2, Pallas kernels, attend_far(): pl.pallas_call(functools.partial(attend_far_kernel, finish), out_shape=pl...  9.15 us
    all_to_all x1, starting transfers between devices, over_rings(): return lax.all_to_all(x, 'frame', 0, 0, axis_index_groups=rings, tiled=True)  8.48 us
    pallas_call x1, Pallas kernels, attend_near(): pl.pallas_call(attend_near_kernel, out_shape=STATE + (pltpu.VMEM((SET, HD...  8.37 us
  transfers between devices with their start and end apart: 23, of which 12 were waited for; matrix products, arithmetic and copies ran while one was open for 1% of the time, Pallas kernels for 14%

profile of v8, /device:TPU:6, one launch (start us, length us, event | category | flops | bytes accessed | tf_op | source)
XLA Modules:
  0.0 144.6 jit_solution(16255440391991458536)
XLA Ops:
  0.7 2.4 %prep.1 = (bf16[400,384]{1,0:T(8,128)(2,1)S(1)}, f32[1,384]{1,0:T(1,128)S(1)}, f32[2,128]{1,0:T(2,128)S(1)}, s32[8]{0:T(128)S(1)}, s32[5]{0:T(128)S(1)}) custom-call(s32[1]{0:T(128)} %bitcast.frame_ref, s32[1]{0:T(128)} %bitcast.1.head_ref, s32[1]{0:T(128)S(6)} %copy.13.shift_ref, s32[32]{0:T(128)} %ids_ref.1, s32[3]{0:T(128)} %lengths_ref.1, ...), custom_call_target="tpu_custom_call" | custom-call | tf_op jit(solution)/shard_map/prep/pallas_call | solution.py:110
  3.9 2.4 %collective-permute-start.2 = (bf16[400,384]{1,0:T(8,128)(2,1)S(1)}, bf16[400,384]{1,0:T(8,128)(2,1)S(1)}, u32[]{:S(2)}, u32[]{:S(2)}) collective-permute-start(bf16[400,384]{1,0:T(8,128)(2,1)S(1)} %get-tuple-element.38.refs_0_), channel_id=1, source_target_pairs={{0,2},{1,3},{2,4},{3,5},{4,6},{5,7},{6,0},{7,1},{8,10},{9,11},{10,... | collective-permute-start | bytes 921608 | tf_op jit(solution)/shard_map/ppermute | solution.py:610
  6.3 3.2 %collective-permute-start = (bf16[400,384]{1,0:T(8,128)(2,1)S(1)}, bf16[400,384]{1,0:T(8,128)(2,1)S(1)}, u32[]{:S(2)}, u32[]{:S(2)}) collective-permute-start(bf16[400,384]{1,0:T(8,128)(2,1)S(1)} %get-tuple-element.38.refs_0_), channel_id=1, source_target_pairs={{0,1},{1,0},{2,3},{3,2},{4,5},{5,4},{6,7},{7,6},{8,9},{9,8},{10,11... | collective-permute-start | bytes 921608 | tf_op jit(solution)/shard_map/ppermute | solution.py:614
  9.5 3.8 %collective-permute-done.1.refs_2_ = bf16[400,384]{1,0:T(8,128)(2,1)S(1)} collective-permute-done((bf16[400,384]{1,0:T(8,128)(2,1)S(1)}, bf16[400,384]{1,0:T(8,128)(2,1)S(1)}, u32[]{:S(2)}, u32[]{:S(2)}) %collective-permute-start.1) | collective-permute-done | bytes 307232 | tf_op jit(solution)/shard_map/ppermute | solution.py:610
  13.5 3.3 %collective-permute-start.5 = (bf16[192,384]{1,0:T(8,128)(2,1)S(1)}, bf16[192,384]{1,0:T(8,128)(2,1)S(1)}, u32[]{:S(2)}, u32[]{:S(2)}) collective-permute-start(bf16[192,384]{1,0:T(8,128)(2,1)S(1)} %slice.12), channel_id=1, source_target_pairs={{0,2},{1,3},{2,4},{3,5},{4,6},{5,7},{6,0},{7,1},{8,10},{9,11},{10,... | collective-permute-start | bytes 442376 | tf_op jit(solution)/shard_map/ppermute | solution.py:610
  16.8 3.2 %collective-permute-start.4 = (bf16[400,384]{1,0:T(8,128)(2,1)S(1)}, bf16[400,384]{1,0:T(8,128)(2,1)S(1)}, u32[]{:S(2)}, u32[]{:S(2)}) collective-permute-start(bf16[400,384]{1,0:T(8,128)(2,1)S(1)} %collective-permute-done.refs_1_), channel_id=1, source_target_pairs={{0,2},{1,3},{2,4},{3,5},{4,6},{5,7},{6,0},{7,1},{8,10},{9,11},{10,... | collective-permute-start | bytes 921608 | tf_op jit(solution)/shard_map/ppermute | solution.py:610
  20.7 3.2 %collective-permute-start.7 = (bf16[192,384]{1,0:T(8,128)(2,1)S(1)}, bf16[192,384]{1,0:T(8,128)(2,1)S(1)}, u32[]{:S(2)}, u32[]{:S(2)}) collective-permute-start(bf16[192,384]{1,0:T(8,128)(2,1)S(1)} %collective-permute-done.5.refs_6_), channel_id=1, source_target_pairs={{0,1},{1,0},{2,3},{3,2},{4,5},{5,4},{6,7},{7,6},{8,9},{9,8},{10,11... | collective-permute-start | bytes 442376 | tf_op jit(solution)/shard_map/ppermute | solution.py:614
  24.2 1.0 sine_multiply_fusion
  25.3 2.9 %collective-permute-done.7.refs_8_ = bf16[192,384]{1,0:T(8,128)(2,1)S(1)} collective-permute-done((bf16[192,384]{1,0:T(8,128)(2,1)S(1)}, bf16[192,384]{1,0:T(8,128)(2,1)S(1)}, u32[]{:S(2)}, u32[]{:S(2)}) %collective-permute-start.7) | collective-permute-done | bytes 147488 | tf_op jit(solution)/shard_map/ppermute | solution.py:614
  28.2 2.5 %collective-permute-done.8.refs_9_ = bf16[208,384]{1,0:T(8,128)(2,1)S(1)} collective-permute-done((bf16[208,384]{1,0:T(8,128)(2,1)S(1)}, bf16[208,384]{1,0:T(8,128)(2,1)S(1)}, u32[]{:S(2)}, u32[]{:S(2)}) %collective-permute-start.8) | collective-permute-done | bytes 159776 | tf_op jit(solution)/shard_map/ppermute | solution.py:614
  30.7 7.9 %project.1 = (bf16[8,512,128]{2,1,0:T(8,128)(2,1)}, bf16[256,128]{1,0:T(8,128)(2,1)S(1)}) custom-call(s32[8]{0:T(128)S(1)} %get-tuple-element.36.place_ref, bf16[400,384]{1,0:T(8,128)(2,1)S(1)} %get-tuple-element.38.refs_0_, bf16[400,384]{1,0:T(8,128)(2,1)S(1)} %collective-permute-done.refs_1_, bf16[400,384]{1,0:T(8,128)(2,1)S(1)} %collective-permute-done.1.refs_2_, ...), custom_call_target="tpu_custom_call" | custom-call | flops 2717908992 | bytes 12000000 | tf_op jit(solution)/shard_map/project/pallas_call | solution.py:216
  38.6 8.5 %all-to-all-start = ((bf16[8,512,128]{2,1,0:T(8,128)(2,1)}), bf16[8,512,128]{2,1,0:T(8,128)(2,1)S(1)}, u32[]{:S(2)}, u32[]{:S(2)}) async-start(bf16[8,512,128]{2,1,0:T(8,128)(2,1)} %get-tuple-element.42), calls=%async_computation | async-start | bytes 2097152 | tf_op jit(solution)/shard_map/all_to_all | solution.py:681
  47.7 1.5 %collective-permute-start.9 = (bf16[256,128]{1,0:T(8,128)(2,1)S(1)}, bf16[256,128]{1,0:T(8,128)(2,1)S(1)}, u32[]{:S(2)}, u32[]{:S(2)}) collective-permute-start(bf16[256,128]{1,0:T(8,128)(2,1)S(1)} %get-tuple-element.40.refs_0_), channel_id=1, source_target_pairs={{0,8},{8,0},{16,24},{24,16},{32,40},{40,32},{48,56},{56,48},{64,72... | collective-permute-start | bytes 196616 | tf_op jit(solution)/shard_map/ppermute | solution.py:618
  49.2 2.7 %collective-permute-done.10.refs_2_ = bf16[256,128]{1,0:T(8,128)(2,1)S(1)} collective-permute-done((bf16[256,128]{1,0:T(8,128)(2,1)S(1)}, bf16[256,128]{1,0:T(8,128)(2,1)S(1)}, u32[]{:S(2)}, u32[]{:S(2)}) %collective-permute-start.10) | collective-permute-done | bytes 65568 | tf_op jit(solution)/shard_map/ppermute | solution.py:618
  52.1 2.1 %lay_last.1 = (bf16[640,128]{1,0:T(8,128)(2,1)S(1)}, bf16[640,256]{1,0:T(8,128)(2,1)S(1)}, s32[1]{0:T(128)}) custom-call(s32[5]{0:T(128)S(1)} %get-tuple-element.37.where_ref, bf16[256,128]{1,0:T(8,128)(2,1)S(1)} %get-tuple-element.40.refs_0_, bf16[256,128]{1,0:T(8,128)(2,1)S(1)} %collective-permute-done.9.refs_1_, ...), custom_call_target="tpu_custom_call" | custom-call | flops 10000000000 | bytes 10000000 | tf_op jit(solution)/shard_map/lay_last/pallas_call | solution.py:431
  54.2 18.6 %all-to-all-done.q_ref = bf16[8,512,128]{2,1,0:T(8,128)(2,1)S(1)} async-done(((bf16[8,512,128]{2,1,0:T(8,128)(2,1)}), bf16[8,512,128]{2,1,0:T(8,128)(2,1)S(1)}, u32[]{:S(2)}, u32[]{:S(2)}) %all-to-all-start) | async-done | bytes 1048608 | tf_op jit(solution)/shard_map/all_to_all | solution.py:681
  73.2 3.0 %attend_last.1.refs_3_ = bf16[8,144,128]{2,1,0:T(8,128)(2,1)S(1)} custom-call(s32[5]{0:T(128)S(1)} %get-tuple-element.37.where_ref, bf16[8,512,128]{2,1,0:T(8,128)(2,1)S(1)} %all-to-all-done.q_ref, bf16[640,128]{1,0:T(8,128)(2,1)S(1)} %get-tuple-element.47.keys_ref, bf16[640,256]{1,0:T(8,128)(2,1)S(1)} %get-tuple-element.48.value_ref), custom_call_target="tpu_custom_call" | custom-call | flops 335544320 | bytes 1000000 | tf_op jit(solution)/shard_map/attend_last/pallas_call | solution.py:483
  76.3 8.4 %attend_near.1 = (f32[1024,128]{1,0:T(8,128)S(1)}, f32[1024,128]{1,0:T(8,128)S(1)}, f32[1024,128]{1,0:T(8,128)S(1)}, bf16[1024,128]{1,0:T(8,128)(2,1)S(1)}, bf16[384,3072]{1,0:T(8,128)(2,1)S(1)}) custom-call(s32[5]{0:T(128)S(1)} %get-tuple-element.37.where_ref, s32[1]{0:T(128)} %get-tuple-element.41.flag_ref, bf16[8,512,128]{2,1,0:T(8,128)(2,1)S(1)} %all-to-all-done.q_ref, ...), custom_call_target="tpu_custom_call" | custom-call | flops 1207959552 | bytes 3000000 | tf_op jit(solution)/shard_map/attend_near/pallas_call | solution.py:380
  84.6 2.8 %collective-permute-done.13.set_ref = bf16[8,256,128]{2,1,0:T(8,128)(2,1)S(1)} collective-permute-done((bf16[8,256,128]{2,1,0:T(8,128)(2,1)S(1)}, bf16[8,256,128]{2,1,0:T(8,128)(2,1)S(1)}, u32[]{:S(2)}, u32[]{:S(2)}) %collective-permute-start.13) | collective-permute-done | bytes 524320 | tf_op jit(solution)/shard_map/ppermute | solution.py:618
  87.5 4.5 %attend_far.2 = (f32[1024,128]{1,0:T(8,128)S(1)}, f32[1024,128]{1,0:T(8,128)S(1)}, f32[1024,128]{1,0:T(8,128)S(1)}) custom-call(s32[1]{0:T(128)} %get-tuple-element.41.flag_ref, bf16[1024,128]{1,0:T(8,128)(2,1)S(1)} %get-tuple-element.45.q_ref, bf16[8,256,128]{2,1,0:T(8,128)(2,1)S(1)} %collective-permute-done.13.set_ref, ...), custom_call_target="tpu_custom_call" | custom-call | flops 536870912 | bytes 3000000 | tf_op jit(solution)/shard_map/attend_far/pallas_call | solution.py:533
  92.0 4.7 %attend_far.3 = bf16[8,272,128]{2,1,0:T(8,128)(2,1)S(1)} custom-call(s32[1]{0:T(128)} %get-tuple-element.41.flag_ref, bf16[1024,128]{1,0:T(8,128)(2,1)S(1)} %get-tuple-element.45.q_ref, bf16[8,256,128]{2,1,0:T(8,128)(2,1)S(1)} %collective-permute-done.14.set_ref, f32[1024,128]{1,0:T(8,128)S(1)} %get-tuple-element.52.refs_0_, ...), custom_call_target="tpu_custom_call" | custom-call | flops 536870912 | bytes 3000000 | tf_op jit(solution)/shard_map/attend_far/pallas_call | solution.py:533
  96.7 21.5 %all_to_all.10.back_ref = bf16[8,272,128]{2,1,0:T(8,128)(2,1)S(1)} all-to-all(bf16[8,272,128]{2,1,0:T(8,128)(2,1)S(1)} %attend_far.3), channel_id=1, replica_groups={{0,16,32,48,64,80,96,112},{8,24,40,56,72,88,104,120},{128,144,160,176,1..., dimensions={0} | all-to-all | bytes 1114112 | tf_op jit(solution)/shard_map/all_to_all | solution.py:681
  118.2 1.5 %output.2 = (bf16[384,384]{1,0:T(8,128)(2,1)S(1)}, bf16[384,384]{1,0:T(8,128)(2,1)S(1)}, bf16[384,384]{1,0:T(8,128)(2,1)S(1)}, bf16[384,384]{1,0:T(8,128)(2,1)S(1)}) custom-call(s32[8]{0:T(128)S(1)} %get-tuple-element.36.place_ref, bf16[8,272,128]{2,1,0:T(8,128)(2,1)S(1)} %all_to_all.10.back_ref, bf16[384,3072]{1,0:T(8,128)(2,1)S(1)} %get-tuple-element.55.w_ref), custom_call_target="tpu_custom_call" | custom-call | flops 452984832 | bytes 3000000 | tf_op jit(solution)/shard_map/output/pallas_call | solution.py:592
  119.7 1.7 %collective-permute-start.17 = (bf16[384,384]{1,0:T(8,128)(2,1)S(1)}, bf16[384,384]{1,0:T(8,128)(2,1)S(1)}, u32[]{:S(2)}, u32[]{:S(2)}) collective-permute-start(bf16[384,384]{1,0:T(8,128)(2,1)S(1)} %get-tuple-element.61), channel_id=1, source_target_pairs={{0,2},{1,3},{2,4},{3,5},{4,6},{5,7},{6,0},{7,1},{8,10},{9,11},{10,... | collective-permute-start | bytes 884744 | tf_op jit(solution)/shard_map/ppermute | solution.py:610
  121.8 1.8 %collective-permute-start.20 = (bf16[384,384]{1,0:T(8,128)(2,1)S(1)}, bf16[384,384]{1,0:T(8,128)(2,1)S(1)}, u32[]{:S(2)}, u32[]{:S(2)}) collective-permute-start(bf16[384,384]{1,0:T(8,128)(2,1)S(1)} %get-tuple-element.64), channel_id=1, source_target_pairs={{0,1},{1,0},{2,3},{3,2},{4,5},{5,4},{6,7},{7,6},{8,9},{9,8},{10,11... | collective-permute-start | bytes 884744 | tf_op jit(solution)/shard_map/ppermute | solution.py:614
  123.6 1.6 %output.3 = (bf16[384,384]{1,0:T(8,128)(2,1)S(1)}, bf16[384,384]{1,0:T(8,128)(2,1)S(1)}, bf16[384,384]{1,0:T(8,128)(2,1)S(1)}, bf16[384,384]{1,0:T(8,128)(2,1)S(1)}, bf16[384,384]{1,0:T(8,128)(2,1)S(1)}) custom-call(s32[8]{0:T(128)S(1)} %get-tuple-element.36.place_ref, bf16[384,384]{1,0:T(8,128)(2,1)S(1)} %get-tuple-element.56.attn_ref, ...), custom_call_target="tpu_custom_call" | custom-call | flops 566231040 | bytes 3000000 | tf_op jit(solution)/shard_map/output/pallas_call | solution.py:592
  125.2 3.3 %collective-permute-start.15 = (bf16[384,384]{1,0:T(8,128)(2,1)S(1)}, bf16[384,384]{1,0:T(8,128)(2,1)S(1)}, u32[]{:S(2)}, u32[]{:S(2)}) collective-permute-start(bf16[384,384]{1,0:T(8,128)(2,1)S(1)} %get-tuple-element.58), channel_id=1, source_target_pairs={{0,2},{1,3},{2,4},{3,5},{4,6},{5,7},{6,0},{7,1},{8,10},{9,11},{10,... | collective-permute-start | bytes 884744 | tf_op jit(solution)/shard_map/ppermute | solution.py:610
  128.5 1.2 collective-permute-done.17
  129.7 1.3 collective-permute-done.18
  131.1 3.0 %collective-permute-start.19 = (bf16[384,384]{1,0:T(8,128)(2,1)S(1)}, bf16[384,384]{1,0:T(8,128)(2,1)S(1)}, u32[]{:S(2)}, u32[]{:S(2)}) collective-permute-start(bf16[384,384]{1,0:T(8,128)(2,1)S(1)} %add_convert_fusion.2), channel_id=1, source_target_pairs={{0,1},{1,0},{2,3},{3,2},{4,5},{5,4},{6,7},{7,6},{8,9},{9,8},{10,11... | collective-permute-start | bytes 884744 | tf_op jit(solution)/shard_map/ppermute | solution.py:614
  134.3 1.0 collective-permute-done.15
  135.3 8.3 %collective-permute-done.16 = bf16[384,384]{1,0:T(8,128)(2,1)S(1)} collective-permute-done((bf16[384,384]{1,0:T(8,128)(2,1)S(1)}, bf16[384,384]{1,0:T(8,128)(2,1)S(1)}, u32[]{:S(2)}, u32[]{:S(2)}) %collective-permute-start.16) | collective-permute-done | bytes 294944 | tf_op jit(solution)/shard_map/ppermute | solution.py:610
  (36 shorter events, 5.0 us)
Async XLA Ops:
  3.0 10.3 %collective-permute-start.1 = (bf16[400,384]{1,0:T(8,128)(2,1)S(1)}, bf16[400,384]{1,0:T(8,128)(2,1)S(1)}, u32[]{:S(2)}, u32[]{:S(2)}) collective-permute-start(bf16[400,384]{1,0:T(8,128)(2,1)S(1)} %get-tuple-element.38.refs_0_), channel_id=1, source_target_pairs={{0,6},{1,7},{2,0},{3,1},{4,2},{5,3},{6,4},{7,5},{8,14},{9,15},{10,... | collective-permute-start | bytes 921608 | tf_op jit(solution)/shard_map/ppermute | solution.py:610
  3.9 9.5 %collective-permute-start.2 = (bf16[400,384]{1,0:T(8,128)(2,1)S(1)}, bf16[400,384]{1,0:T(8,128)(2,1)S(1)}, u32[]{:S(2)}, u32[]{:S(2)}) collective-permute-start(bf16[400,384]{1,0:T(8,128)(2,1)S(1)} %get-tuple-element.38.refs_0_), channel_id=1, source_target_pairs={{0,2},{1,3},{2,4},{3,5},{4,6},{5,7},{6,0},{7,1},{8,10},{9,11},{10,... | collective-permute-start | bytes 921608 | tf_op jit(solution)/shard_map/ppermute | solution.py:610
  6.3 10.4 %collective-permute-start = (bf16[400,384]{1,0:T(8,128)(2,1)S(1)}, bf16[400,384]{1,0:T(8,128)(2,1)S(1)}, u32[]{:S(2)}, u32[]{:S(2)}) collective-permute-start(bf16[400,384]{1,0:T(8,128)(2,1)S(1)} %get-tuple-element.38.refs_0_), channel_id=1, source_target_pairs={{0,1},{1,0},{2,3},{3,2},{4,5},{5,4},{6,7},{7,6},{8,9},{9,8},{10,11... | collective-permute-start | bytes 921608 | tf_op jit(solution)/shard_map/ppermute | solution.py:614
  13.3 10.5 %collective-permute-start.6 = (bf16[208,384]{1,0:T(8,128)(2,1)S(1)}, bf16[208,384]{1,0:T(8,128)(2,1)S(1)}, u32[]{:S(2)}, u32[]{:S(2)}) collective-permute-start(bf16[208,384]{1,0:T(8,128)(2,1)S(1)} %slice.13), channel_id=1, source_target_pairs={{0,6},{1,7},{2,0},{3,1},{4,2},{5,3},{6,4},{7,5},{8,14},{9,15},{10,... | collective-permute-start | bytes 479240 | tf_op jit(solution)/shard_map/ppermute | solution.py:610
  13.5 7.2 %collective-permute-start.5 = (bf16[192,384]{1,0:T(8,128)(2,1)S(1)}, bf16[192,384]{1,0:T(8,128)(2,1)S(1)}, u32[]{:S(2)}, u32[]{:S(2)}) collective-permute-start(bf16[192,384]{1,0:T(8,128)(2,1)S(1)} %slice.12), channel_id=1, source_target_pairs={{0,2},{1,3},{2,4},{3,5},{4,6},{5,7},{6,0},{7,1},{8,10},{9,11},{10,... | collective-permute-start | bytes 442376 | tf_op jit(solution)/shard_map/ppermute | solution.py:610
  16.8 11.4 %collective-permute-start.3 = (bf16[400,384]{1,0:T(8,128)(2,1)S(1)}, bf16[400,384]{1,0:T(8,128)(2,1)S(1)}, u32[]{:S(2)}, u32[]{:S(2)}) collective-permute-start(bf16[400,384]{1,0:T(8,128)(2,1)S(1)} %collective-permute-done.refs_1_), channel_id=1, source_target_pairs={{0,6},{1,7},{2,0},{3,1},{4,2},{5,3},{6,4},{7,5},{8,14},{9,15},{10,... | collective-permute-start | bytes 921608 | tf_op jit(solution)/shard_map/ppermute | solution.py:610
  16.8 11.4 %collective-permute-start.4 = (bf16[400,384]{1,0:T(8,128)(2,1)S(1)}, bf16[400,384]{1,0:T(8,128)(2,1)S(1)}, u32[]{:S(2)}, u32[]{:S(2)}) collective-permute-start(bf16[400,384]{1,0:T(8,128)(2,1)S(1)} %collective-permute-done.refs_1_), channel_id=1, source_target_pairs={{0,2},{1,3},{2,4},{3,5},{4,6},{5,7},{6,0},{7,1},{8,10},{9,11},{10,... | collective-permute-start | bytes 921608 | tf_op jit(solution)/shard_map/ppermute | solution.py:610
  20.7 7.5 %collective-permute-start.7 = (bf16[192,384]{1,0:T(8,128)(2,1)S(1)}, bf16[192,384]{1,0:T(8,128)(2,1)S(1)}, u32[]{:S(2)}, u32[]{:S(2)}) collective-permute-start(bf16[192,384]{1,0:T(8,128)(2,1)S(1)} %collective-permute-done.5.refs_6_), channel_id=1, source_target_pairs={{0,1},{1,0},{2,3},{3,2},{4,5},{5,4},{6,7},{7,6},{8,9},{9,8},{10,11... | collective-permute-start | bytes 442376 | tf_op jit(solution)/shard_map/ppermute | solution.py:614
  23.9 6.8 %collective-permute-start.8 = (bf16[208,384]{1,0:T(8,128)(2,1)S(1)}, bf16[208,384]{1,0:T(8,128)(2,1)S(1)}, u32[]{:S(2)}, u32[]{:S(2)}) collective-permute-start(bf16[208,384]{1,0:T(8,128)(2,1)S(1)} %collective-permute-done.6.refs_7_), channel_id=1, source_target_pairs={{0,1},{1,0},{2,3},{3,2},{4,5},{5,4},{6,7},{7,6},{8,9},{9,8},{10,11... | collective-permute-start | bytes 479240 | tf_op jit(solution)/shard_map/ppermute | solution.py:614
  38.6 34.3 %all-to-all-start = ((bf16[8,512,128]{2,1,0:T(8,128)(2,1)}), bf16[8,512,128]{2,1,0:T(8,128)(2,1)S(1)}, u32[]{:S(2)}, u32[]{:S(2)}) async-start(bf16[8,512,128]{2,1,0:T(8,128)(2,1)} %get-tuple-element.42), calls=%async_computation | async-start | bytes 2097152 | tf_op jit(solution)/shard_map/all_to_all | solution.py:681
  47.0 4.9 %collective-permute-start.10 = (bf16[256,128]{1,0:T(8,128)(2,1)S(1)}, bf16[256,128]{1,0:T(8,128)(2,1)S(1)}, u32[]{:S(2)}, u32[]{:S(2)}) collective-permute-start(bf16[256,128]{1,0:T(8,128)(2,1)S(1)} %get-tuple-element.40.refs_0_), channel_id=1, source_target_pairs={{0,128},{8,136},{16,144},{24,152},{32,160},{40,168},{48,176},{56,1... | collective-permute-start | bytes 196616 | tf_op jit(solution)/shard_map/ppermute | solution.py:618
  47.7 4.4 %collective-permute-start.11 = (bf16[256,128]{1,0:T(8,128)(2,1)S(1)}, bf16[256,128]{1,0:T(8,128)(2,1)S(1)}, u32[]{:S(2)}, u32[]{:S(2)}) collective-permute-start(bf16[256,128]{1,0:T(8,128)(2,1)S(1)} %get-tuple-element.40.refs_0_), channel_id=1, source_target_pairs={{0,136},{8,128},{16,152},{24,144},{32,168},{40,160},{48,184},{56,1... | collective-permute-start | bytes 196616 | tf_op jit(solution)/shard_map/ppermute | solution.py:618
  47.7 4.4 %collective-permute-start.9 = (bf16[256,128]{1,0:T(8,128)(2,1)S(1)}, bf16[256,128]{1,0:T(8,128)(2,1)S(1)}, u32[]{:S(2)}, u32[]{:S(2)}) collective-permute-start(bf16[256,128]{1,0:T(8,128)(2,1)S(1)} %get-tuple-element.40.refs_0_), channel_id=1, source_target_pairs={{0,8},{8,0},{16,24},{24,16},{32,40},{40,32},{48,56},{56,48},{64,72... | collective-permute-start | bytes 196616 | tf_op jit(solution)/shard_map/ppermute | solution.py:618
  72.9 3.4 %collective-permute-start.12 = (bf16[8,256,128]{2,1,0:T(8,128)(2,1)S(1)}, bf16[8,256,128]{2,1,0:T(8,128)(2,1)S(1)}, u32[]{:S(2)}, u32[]{:S(2)}) collective-permute-start(bf16[8,256,128]{2,1,0:T(8,128)(2,1)S(1)} %slice.14.own_ref), channel_id=1, source_target_pairs={{0,8},{8,0},{16,24},{24,16},{32,40},{40,32},{48,56},{56,48},{64,72... | collective-permute-start | bytes 1572872 | tf_op jit(solution)/shard_map/ppermute | solution.py:618
  73.1 14.3 %collective-permute-start.13 = (bf16[8,256,128]{2,1,0:T(8,128)(2,1)S(1)}, bf16[8,256,128]{2,1,0:T(8,128)(2,1)S(1)}, u32[]{:S(2)}, u32[]{:S(2)}) collective-permute-start(bf16[8,256,128]{2,1,0:T(8,128)(2,1)S(1)} %slice.14.own_ref), channel_id=1, source_target_pairs={{0,128},{8,136},{16,144},{24,152},{32,160},{40,168},{48,176},{56,1... | collective-permute-start | bytes 1572872 | tf_op jit(solution)/shard_map/ppermute | solution.py:618
  87.5 4.5 %collective-permute-start.14 = (bf16[8,256,128]{2,1,0:T(8,128)(2,1)S(1)}, bf16[8,256,128]{2,1,0:T(8,128)(2,1)S(1)}, u32[]{:S(2)}, u32[]{:S(2)}) collective-permute-start(bf16[8,256,128]{2,1,0:T(8,128)(2,1)S(1)} %collective-permute-done.13.set_ref), channel_id=1, source_target_pairs={{0,8},{8,0},{16,24},{24,16},{32,40},{40,32},{48,56},{56,48},{64,72... | collective-permute-start | bytes 1572872 | tf_op jit(solution)/shard_map/ppermute | solution.py:618
  119.7 10.0 %collective-permute-start.17 = (bf16[384,384]{1,0:T(8,128)(2,1)S(1)}, bf16[384,384]{1,0:T(8,128)(2,1)S(1)}, u32[]{:S(2)}, u32[]{:S(2)}) collective-permute-start(bf16[384,384]{1,0:T(8,128)(2,1)S(1)} %get-tuple-element.61), channel_id=1, source_target_pairs={{0,2},{1,3},{2,4},{3,5},{4,6},{5,7},{6,0},{7,1},{8,10},{9,11},{10,... | collective-permute-start | bytes 884744 | tf_op jit(solution)/shard_map/ppermute | solution.py:610
  121.5 9.5 %collective-permute-start.18 = (bf16[384,384]{1,0:T(8,128)(2,1)S(1)}, bf16[384,384]{1,0:T(8,128)(2,1)S(1)}, u32[]{:S(2)}, u32[]{:S(2)}) collective-permute-start(bf16[384,384]{1,0:T(8,128)(2,1)S(1)} %get-tuple-element.62), channel_id=1, source_target_pairs={{0,6},{1,7},{2,0},{3,1},{4,2},{5,3},{6,4},{7,5},{8,14},{9,15},{10,... | collective-permute-start | bytes 884744 | tf_op jit(solution)/shard_map/ppermute | solution.py:610
  121.8 12.3 %collective-permute-start.20 = (bf16[384,384]{1,0:T(8,128)(2,1)S(1)}, bf16[384,384]{1,0:T(8,128)(2,1)S(1)}, u32[]{:S(2)}, u32[]{:S(2)}) collective-permute-start(bf16[384,384]{1,0:T(8,128)(2,1)S(1)} %get-tuple-element.64), channel_id=1, source_target_pairs={{0,1},{1,0},{2,3},{3,2},{4,5},{5,4},{6,7},{7,6},{8,9},{9,8},{10,11... | collective-permute-start | bytes 884744 | tf_op jit(solution)/shard_map/ppermute | solution.py:614
  125.2 18.6 %copy-start = (bf16[3,128,384]{2,1,0:T(8,128)(2,1)S(1)}, bf16[3,128,384]{2,1,0:T(8,128)(2,1)}, u32[]{:S(2)}) copy-start(bf16[3,128,384]{2,1,0:T(8,128)(2,1)} %video_ref.1) | copy-start | bytes 884740
  125.2 10.1 %collective-permute-start.15 = (bf16[384,384]{1,0:T(8,128)(2,1)S(1)}, bf16[384,384]{1,0:T(8,128)(2,1)S(1)}, u32[]{:S(2)}, u32[]{:S(2)}) collective-permute-start(bf16[384,384]{1,0:T(8,128)(2,1)S(1)} %get-tuple-element.58), channel_id=1, source_target_pairs={{0,2},{1,3},{2,4},{3,5},{4,6},{5,7},{6,0},{7,1},{8,10},{9,11},{10,... | collective-permute-start | bytes 884744 | tf_op jit(solution)/shard_map/ppermute | solution.py:610
  128.5 15.1 %collective-permute-start.16 = (bf16[384,384]{1,0:T(8,128)(2,1)S(1)}, bf16[384,384]{1,0:T(8,128)(2,1)S(1)}, u32[]{:S(2)}, u32[]{:S(2)}) collective-permute-start(bf16[384,384]{1,0:T(8,128)(2,1)S(1)} %get-tuple-element.59), channel_id=1, source_target_pairs={{0,6},{1,7},{2,0},{3,1},{4,2},{5,3},{6,4},{7,5},{8,14},{9,15},{10,... | collective-permute-start | bytes 884744 | tf_op jit(solution)/shard_map/ppermute | solution.py:610
  131.1 12.5 %collective-permute-start.19 = (bf16[384,384]{1,0:T(8,128)(2,1)S(1)}, bf16[384,384]{1,0:T(8,128)(2,1)S(1)}, u32[]{:S(2)}, u32[]{:S(2)}) collective-permute-start(bf16[384,384]{1,0:T(8,128)(2,1)S(1)} %add_convert_fusion.2), channel_id=1, source_target_pairs={{0,1},{1,0},{2,3},{3,2},{4,5},{5,4},{6,7},{7,6},{8,9},{9,8},{10,11... | collective-permute-start | bytes 884744 | tf_op jit(solution)/shard_map/ppermute | solution.py:614
  134.2 9.4 %collective-permute-start.21 = (bf16[384,384]{1,0:T(8,128)(2,1)S(1)}, bf16[384,384]{1,0:T(8,128)(2,1)S(1)}, u32[]{:S(2)}, u32[]{:S(2)}) collective-permute-start(bf16[384,384]{1,0:T(8,128)(2,1)S(1)} %add_convert_fusion.1), channel_id=1, source_target_pairs={{0,4},{1,5},{2,6},{3,7},{4,0},{5,1},{6,2},{7,3},{8,12},{9,13},{10,... | collective-permute-start | bytes 884744 | tf_op jit(solution)/shard_map/ppermute | solution.py:610

commit v9 on v8

--- a/solution.py
+++ b/solution.py
@@ -28,6 +28,8 @@
 LAST_ROWS = TOK + STAT_ROWS
 RETURN = TOK + LAST_ROWS
 WIDE = 3 * DSH
+W_PARTS = 4
+W_ROWS = HEAD_AXIS * DSH // W_PARTS
 rope_base = 256.0
 norm_eps = 1e-06
 LOG2E = float(np.log2(np.e))
@@ -138,10 +140,15 @@
     (
         w_hbm, gain_ref, cos_ref, sin_ref, out_ref, last_ref, mod_ref, acc_ref, w_ref, sems,
     ) = refs[10:]
-    copies = [
-        pltpu.make_async_copy(w_hbm.at[n], w_ref.at[:, pl.ds(n * DSH, DSH)], sems.at[n])
-        for n in range(3)
-    ]
+    copies = []
+    for n in range(3):
+        for r in range(W_PARTS):
+            rows = pl.ds(r * W_ROWS, W_ROWS)
+            copies.append(
+                pltpu.make_async_copy(
+                    w_hbm.at[n, rows], w_ref.at[rows, pl.ds(n * DSH, DSH)], sems.at[n, r]
+                )
+            )
     for copy in copies:
         copy.start()
     limbs = [block[ROWS:SENT, :] for block in blocks]
@@ -229,7 +236,7 @@
                 pltpu.VMEM((ROWS, HEAD_AXIS * DSH), jnp.bfloat16),
                 pltpu.VMEM((ROWS, WIDE), jnp.float32),
                 pltpu.VMEM((HEAD_AXIS * DSH, WIDE), jnp.bfloat16),
-                pltpu.SemaphoreType.DMA((3,)),
+                pltpu.SemaphoreType.DMA((3, W_PARTS)),
             ],
         ),
         compiler_params=pltpu.CompilerParams(vmem_limit_bytes=28 * MIB),
@@ -572,8 +579,8 @@
     multiply(place_ref, EARLY, attn_ref, w_ref, out_refs)
 
 
-EARLY = (4, 5, 7)
-LATE = (2, 3, 0, 1, 6)
+EARLY = (4, 5)
+LATE = (7, 2, 3, 0, 1, 6)
 
 
 def multiply(place_ref, places, attn_ref, w_ref, out_refs):
@@ -643,12 +650,12 @@
 
 
 def scatter_head(places, back, w_out):
-    ahead, behind, over, attention = output(output_kernel, places, back, w_out, 4)
+    ahead, behind, attention = output(output_kernel, places, back, w_out, 3)
     for_partner = [head_move(ahead, 2), head_move(behind, -2)]
-    for_opposite = head_partner(over)
-    ahead, behind, own, partner, opposite = output(
+    over, ahead, behind, own, partner, opposite = output(
         late_kernel, places, attention, w_out, len(LATE)
     )
+    for_opposite = head_partner(over)
     direct = [head_move(ahead, 2), head_move(behind, -2)]
     over_y = head_partner(add(partner, *for_partner).astype(jnp.bfloat16))
     across = head_move(add(opposite, for_opposite).astype(jnp.bfloat16), 4)

time: 145 us -> 146 us (level)
  starting transfers between devices: 37.9 us -> 40.1 us
  waiting for transfers between devices: 46 us -> 44 us
    ppermute x11, starting transfers between devices: 15.4 us -> 17.8 us  [head_move(): lax.ppermute(x, 'head', [(i, (i + step) % HEAD_AXIS) for i in range(HEAD_...]
    ppermute x11, waiting for transfers between devices: 16.3 us -> 14.2 us  [head_move(): lax.ppermute(x, 'head', [(i, (i + step) % HEAD_AXIS) for i in range(HEAD_...]
  transfers between devices with their start and end apart: 23 -> 23, of which waited for: 12 -> 11; matrix products, arithmetic and copies ran while one was open for 1% -> 1% of each run, Pallas kernels for 14% -> 14%
where the time goes in v9:
time: 146 us; the launch traced here: 145 us
  waiting for transfers between devices  44 us (30%)
  starting transfers between devices  40.1 us (27%)
  Pallas kernels  35.9 us (25%)
  blocking collectives  21.5 us (15%)
  other arithmetic  2.21 us (2%)
    all_to_all x1, blocking collectives, over_rings(): return lax.all_to_all(x, 'frame', 0, 0, axis_index_groups=rings, tiled=True)  21.5 us
    all_to_all x1, waiting for transfers between devices, over_rings(): return lax.all_to_all(x, 'frame', 0, 0, axis_index_groups=rings, tiled=True)  18.6 us
    ppermute x11, starting transfers between devices, head_move(): lax.ppermute(x, 'head', [(i, (i + step) % HEAD_AXIS) for i in range(HEAD_...  17.8 us
    ppermute x11, waiting for transfers between devices, head_move(): lax.ppermute(x, 'head', [(i, (i + step) % HEAD_AXIS) for i in range(HEAD_...  14.2 us
    ppermute x5, starting transfers between devices, head_partner(): return lax.ppermute(x, 'head', [(i, i ^ 1) for i in range(HEAD_AXIS)])  11.4 us
    pallas_call x2, Pallas kernels, attend_far(): pl.pallas_call(functools.partial(attend_far_kernel, finish), out_shape=pl...  9.15 us
    all_to_all x1, starting transfers between devices, over_rings(): return lax.all_to_all(x, 'frame', 0, 0, axis_index_groups=rings, tiled=True)  8.48 us
    pallas_call x1, Pallas kernels, attend_near(): pl.pallas_call(attend_near_kernel, out_shape=STATE + (pltpu.VMEM((SET, HD...  8.37 us
  transfers between devices with their start and end apart: 23, of which 11 were waited for; matrix products, arithmetic and copies ran while one was open for 1% of the time, Pallas kernels for 14%

profile of v9, /device:TPU:6, one launch (start us, length us, event | category | flops | bytes accessed | tf_op | source)
XLA Modules:
  0.0 144.7 jit_solution(5998978390335280495)
XLA Ops:
  0.7 2.4 %prep.1 = (bf16[400,384]{1,0:T(8,128)(2,1)S(1)}, f32[1,384]{1,0:T(1,128)S(1)}, f32[2,128]{1,0:T(2,128)S(1)}, s32[8]{0:T(128)S(1)}, s32[5]{0:T(128)S(1)}) custom-call(s32[1]{0:T(128)} %bitcast.frame_ref, s32[1]{0:T(128)} %bitcast.1.head_ref, s32[1]{0:T(128)S(6)} %copy.13.shift_ref, s32[32]{0:T(128)} %ids_ref.1, s32[3]{0:T(128)} %lengths_ref.1, ...), custom_call_target="tpu_custom_call" | custom-call | tf_op jit(solution)/shard_map/prep/pallas_call | solution.py:112
  3.0 0.9 collective-permute-start.1
  3.9 2.4 %collective-permute-start.2 = (bf16[400,384]{1,0:T(8,128)(2,1)S(1)}, bf16[400,384]{1,0:T(8,128)(2,1)S(1)}, u32[]{:S(2)}, u32[]{:S(2)}) collective-permute-start(bf16[400,384]{1,0:T(8,128)(2,1)S(1)} %get-tuple-element.38.refs_0_), channel_id=1, source_target_pairs={{0,2},{1,3},{2,4},{3,5},{4,6},{5,7},{6,0},{7,1},{8,10},{9,11},{10,... | collective-permute-start | bytes 921608 | tf_op jit(solution)/shard_map/ppermute | solution.py:617
  6.3 3.2 %collective-permute-start = (bf16[400,384]{1,0:T(8,128)(2,1)S(1)}, bf16[400,384]{1,0:T(8,128)(2,1)S(1)}, u32[]{:S(2)}, u32[]{:S(2)}) collective-permute-start(bf16[400,384]{1,0:T(8,128)(2,1)S(1)} %get-tuple-element.38.refs_0_), channel_id=1, source_target_pairs={{0,1},{1,0},{2,3},{3,2},{4,5},{5,4},{6,7},{7,6},{8,9},{9,8},{10,11... | collective-permute-start | bytes 921608 | tf_op jit(solution)/shard_map/ppermute | solution.py:621
  9.5 3.8 %collective-permute-done.1.refs_2_ = bf16[400,384]{1,0:T(8,128)(2,1)S(1)} collective-permute-done((bf16[400,384]{1,0:T(8,128)(2,1)S(1)}, bf16[400,384]{1,0:T(8,128)(2,1)S(1)}, u32[]{:S(2)}, u32[]{:S(2)}) %collective-permute-start.1) | collective-permute-done | bytes 307232 | tf_op jit(solution)/shard_map/ppermute | solution.py:617
  13.5 3.3 %collective-permute-start.5 = (bf16[192,384]{1,0:T(8,128)(2,1)S(1)}, bf16[192,384]{1,0:T(8,128)(2,1)S(1)}, u32[]{:S(2)}, u32[]{:S(2)}) collective-permute-start(bf16[192,384]{1,0:T(8,128)(2,1)S(1)} %slice.12), channel_id=1, source_target_pairs={{0,2},{1,3},{2,4},{3,5},{4,6},{5,7},{6,0},{7,1},{8,10},{9,11},{10,... | collective-permute-start | bytes 442376 | tf_op jit(solution)/shard_map/ppermute | solution.py:617
  16.8 3.2 %collective-permute-start.4 = (bf16[400,384]{1,0:T(8,128)(2,1)S(1)}, bf16[400,384]{1,0:T(8,128)(2,1)S(1)}, u32[]{:S(2)}, u32[]{:S(2)}) collective-permute-start(bf16[400,384]{1,0:T(8,128)(2,1)S(1)} %collective-permute-done.refs_1_), channel_id=1, source_target_pairs={{0,2},{1,3},{2,4},{3,5},{4,6},{5,7},{6,0},{7,1},{8,10},{9,11},{10,... | collective-permute-start | bytes 921608 | tf_op jit(solution)/shard_map/ppermute | solution.py:617
  20.7 3.2 %collective-permute-start.7 = (bf16[192,384]{1,0:T(8,128)(2,1)S(1)}, bf16[192,384]{1,0:T(8,128)(2,1)S(1)}, u32[]{:S(2)}, u32[]{:S(2)}) collective-permute-start(bf16[192,384]{1,0:T(8,128)(2,1)S(1)} %collective-permute-done.5.refs_6_), channel_id=1, source_target_pairs={{0,1},{1,0},{2,3},{3,2},{4,5},{5,4},{6,7},{7,6},{8,9},{9,8},{10,11... | collective-permute-start | bytes 442376 | tf_op jit(solution)/shard_map/ppermute | solution.py:621
  24.2 1.0 sine_multiply_fusion
  25.3 2.9 %collective-permute-done.7.refs_8_ = bf16[192,384]{1,0:T(8,128)(2,1)S(1)} collective-permute-done((bf16[192,384]{1,0:T(8,128)(2,1)S(1)}, bf16[192,384]{1,0:T(8,128)(2,1)S(1)}, u32[]{:S(2)}, u32[]{:S(2)}) %collective-permute-start.7) | collective-permute-done | bytes 147488 | tf_op jit(solution)/shard_map/ppermute | solution.py:621
  28.2 2.5 %collective-permute-done.8.refs_9_ = bf16[208,384]{1,0:T(8,128)(2,1)S(1)} collective-permute-done((bf16[208,384]{1,0:T(8,128)(2,1)S(1)}, bf16[208,384]{1,0:T(8,128)(2,1)S(1)}, u32[]{:S(2)}, u32[]{:S(2)}) %collective-permute-start.8) | collective-permute-done | bytes 159776 | tf_op jit(solution)/shard_map/ppermute | solution.py:621
  30.7 7.9 %project.1 = (bf16[8,512,128]{2,1,0:T(8,128)(2,1)}, bf16[256,128]{1,0:T(8,128)(2,1)S(1)}) custom-call(s32[8]{0:T(128)S(1)} %get-tuple-element.36.place_ref, bf16[400,384]{1,0:T(8,128)(2,1)S(1)} %get-tuple-element.38.refs_0_, bf16[400,384]{1,0:T(8,128)(2,1)S(1)} %collective-permute-done.refs_1_, bf16[400,384]{1,0:T(8,128)(2,1)S(1)} %collective-permute-done.1.refs_2_, ...), custom_call_target="tpu_custom_call" | custom-call | flops 2717908992 | bytes 12000000 | tf_op jit(solution)/shard_map/project/pallas_call | solution.py:223
  38.5 8.5 %all-to-all-start = ((bf16[8,512,128]{2,1,0:T(8,128)(2,1)}), bf16[8,512,128]{2,1,0:T(8,128)(2,1)S(1)}, u32[]{:S(2)}, u32[]{:S(2)}) async-start(bf16[8,512,128]{2,1,0:T(8,128)(2,1)} %get-tuple-element.42), calls=%async_computation | async-start | bytes 2097152 | tf_op jit(solution)/shard_map/all_to_all | solution.py:688
  47.7 1.5 %collective-permute-start.9 = (bf16[256,128]{1,0:T(8,128)(2,1)S(1)}, bf16[256,128]{1,0:T(8,128)(2,1)S(1)}, u32[]{:S(2)}, u32[]{:S(2)}) collective-permute-start(bf16[256,128]{1,0:T(8,128)(2,1)S(1)} %get-tuple-element.40.refs_0_), channel_id=1, source_target_pairs={{0,8},{8,0},{16,24},{24,16},{32,40},{40,32},{48,56},{56,48},{64,72... | collective-permute-start | bytes 196616 | tf_op jit(solution)/shard_map/ppermute | solution.py:625
  49.2 2.7 %collective-permute-done.10.refs_2_ = bf16[256,128]{1,0:T(8,128)(2,1)S(1)} collective-permute-done((bf16[256,128]{1,0:T(8,128)(2,1)S(1)}, bf16[256,128]{1,0:T(8,128)(2,1)S(1)}, u32[]{:S(2)}, u32[]{:S(2)}) %collective-permute-start.10) | collective-permute-done | bytes 65568 | tf_op jit(solution)/shard_map/ppermute | solution.py:625
  52.1 2.1 %lay_last.1 = (bf16[640,128]{1,0:T(8,128)(2,1)S(1)}, bf16[640,256]{1,0:T(8,128)(2,1)S(1)}, s32[1]{0:T(128)}) custom-call(s32[5]{0:T(128)S(1)} %get-tuple-element.37.where_ref, bf16[256,128]{1,0:T(8,128)(2,1)S(1)} %get-tuple-element.40.refs_0_, bf16[256,128]{1,0:T(8,128)(2,1)S(1)} %collective-permute-done.9.refs_1_, ...), custom_call_target="tpu_custom_call" | custom-call | flops 10000000000 | bytes 10000000 | tf_op jit(solution)/shard_map/lay_last/pallas_call | solution.py:438
  54.2 18.6 %all-to-all-done.q_ref = bf16[8,512,128]{2,1,0:T(8,128)(2,1)S(1)} async-done(((bf16[8,512,128]{2,1,0:T(8,128)(2,1)}), bf16[8,512,128]{2,1,0:T(8,128)(2,1)S(1)}, u32[]{:S(2)}, u32[]{:S(2)}) %all-to-all-start) | async-done | bytes 1048608 | tf_op jit(solution)/shard_map/all_to_all | solution.py:688
  73.2 3.0 %attend_last.1.refs_3_ = bf16[8,144,128]{2,1,0:T(8,128)(2,1)S(1)} custom-call(s32[5]{0:T(128)S(1)} %get-tuple-element.37.where_ref, bf16[8,512,128]{2,1,0:T(8,128)(2,1)S(1)} %all-to-all-done.q_ref, bf16[640,128]{1,0:T(8,128)(2,1)S(1)} %get-tuple-element.47.keys_ref, bf16[640,256]{1,0:T(8,128)(2,1)S(1)} %get-tuple-element.48.value_ref), custom_call_target="tpu_custom_call" | custom-call | flops 335544320 | bytes 1000000 | tf_op jit(solution)/shard_map/attend_last/pallas_call | solution.py:490
  76.2 8.4 %attend_near.1 = (f32[1024,128]{1,0:T(8,128)S(1)}, f32[1024,128]{1,0:T(8,128)S(1)}, f32[1024,128]{1,0:T(8,128)S(1)}, bf16[1024,128]{1,0:T(8,128)(2,1)S(1)}, bf16[384,3072]{1,0:T(8,128)(2,1)S(1)}) custom-call(s32[5]{0:T(128)S(1)} %get-tuple-element.37.where_ref, s32[1]{0:T(128)} %get-tuple-element.41.flag_ref, bf16[8,512,128]{2,1,0:T(8,128)(2,1)S(1)} %all-to-all-done.q_ref, ...), custom_call_target="tpu_custom_call" | custom-call | flops 1207959552 | bytes 3000000 | tf_op jit(solution)/shard_map/attend_near/pallas_call | solution.py:387
  84.6 2.8 %collective-permute-done.13.set_ref = bf16[8,256,128]{2,1,0:T(8,128)(2,1)S(1)} collective-permute-done((bf16[8,256,128]{2,1,0:T(8,128)(2,1)S(1)}, bf16[8,256,128]{2,1,0:T(8,128)(2,1)S(1)}, u32[]{:S(2)}, u32[]{:S(2)}) %collective-permute-start.13) | collective-permute-done | bytes 524320 | tf_op jit(solution)/shard_map/ppermute | solution.py:625
  87.5 4.5 %attend_far.2 = (f32[1024,128]{1,0:T(8,128)S(1)}, f32[1024,128]{1,0:T(8,128)S(1)}, f32[1024,128]{1,0:T(8,128)S(1)}) custom-call(s32[1]{0:T(128)} %get-tuple-element.41.flag_ref, bf16[1024,128]{1,0:T(8,128)(2,1)S(1)} %get-tuple-element.45.q_ref, bf16[8,256,128]{2,1,0:T(8,128)(2,1)S(1)} %collective-permute-done.13.set_ref, ...), custom_call_target="tpu_custom_call" | custom-call | flops 536870912 | bytes 3000000 | tf_op jit(solution)/shard_map/attend_far/pallas_call | solution.py:540
  92.0 4.7 %attend_far.3 = bf16[8,272,128]{2,1,0:T(8,128)(2,1)S(1)} custom-call(s32[1]{0:T(128)} %get-tuple-element.41.flag_ref, bf16[1024,128]{1,0:T(8,128)(2,1)S(1)} %get-tuple-element.45.q_ref, bf16[8,256,128]{2,1,0:T(8,128)(2,1)S(1)} %collective-permute-done.14.set_ref, f32[1024,128]{1,0:T(8,128)S(1)} %get-tuple-element.52.refs_0_, ...), custom_call_target="tpu_custom_call" | custom-call | flops 536870912 | bytes 3000000 | tf_op jit(solution)/shard_map/attend_far/pallas_call | solution.py:540
  96.6 21.5 %all_to_all.10.back_ref = bf16[8,272,128]{2,1,0:T(8,128)(2,1)S(1)} all-to-all(bf16[8,272,128]{2,1,0:T(8,128)(2,1)S(1)} %attend_far.3), channel_id=1, replica_groups={{0,16,32,48,64,80,96,112},{8,24,40,56,72,88,104,120},{128,144,160,176,1..., dimensions={0} | all-to-all | bytes 1114112 | tf_op jit(solution)/shard_map/all_to_all | solution.py:688
  118.2 1.2 output.2
  119.4 2.0 %collective-permute-start.17 = (bf16[384,384]{1,0:T(8,128)(2,1)S(1)}, bf16[384,384]{1,0:T(8,128)(2,1)S(1)}, u32[]{:S(2)}, u32[]{:S(2)}) collective-permute-start(bf16[384,384]{1,0:T(8,128)(2,1)S(1)} %get-tuple-element.61), channel_id=1, source_target_pairs={{0,2},{1,3},{2,4},{3,5},{4,6},{5,7},{6,0},{7,1},{8,10},{9,11},{10,... | collective-permute-start | bytes 884744 | tf_op jit(solution)/shard_map/ppermute | solution.py:617
  121.7 1.8 %output.3 = (bf16[384,384]{1,0:T(8,128)(2,1)S(1)}, bf16[384,384]{1,0:T(8,128)(2,1)S(1)}, bf16[384,384]{1,0:T(8,128)(2,1)S(1)}, bf16[384,384]{1,0:T(8,128)(2,1)S(...) custom-call(s32[8]{0:T(128)S(1)} %get-tuple-element.36.place_ref, ...), custom_call_target="tpu_custom_call" | custom-call | flops 679477248 | bytes 3000000 | tf_op jit(solution)/shard_map/output/pallas_call | solution.py:599
  123.5 1.9 %collective-permute-start.20 = (bf16[384,384]{1,0:T(8,128)(2,1)S(1)}, bf16[384,384]{1,0:T(8,128)(2,1)S(1)}, u32[]{:S(2)}, u32[]{:S(2)}) collective-permute-start(bf16[384,384]{1,0:T(8,128)(2,1)S(1)} %get-tuple-element.64), channel_id=1, source_target_pairs={{0,1},{1,0},{2,3},{3,2},{4,5},{5,4},{6,7},{7,6},{8,9},{9,8},{10,11... | collective-permute-start | bytes 884744 | tf_op jit(solution)/shard_map/ppermute | solution.py:621
  125.4 3.2 %collective-permute-start.15 = (bf16[384,384]{1,0:T(8,128)(2,1)S(1)}, bf16[384,384]{1,0:T(8,128)(2,1)S(1)}, u32[]{:S(2)}, u32[]{:S(2)}) collective-permute-start(bf16[384,384]{1,0:T(8,128)(2,1)S(1)} %get-tuple-element.58), channel_id=1, source_target_pairs={{0,2},{1,3},{2,4},{3,5},{4,6},{5,7},{6,0},{7,1},{8,10},{9,11},{10,... | collective-permute-start | bytes 884744 | tf_op jit(solution)/shard_map/ppermute | solution.py:617
  129.4 1.5 %collective-permute-done.18 = bf16[384,384]{1,0:T(8,128)(2,1)S(1)} collective-permute-done((bf16[384,384]{1,0:T(8,128)(2,1)S(1)}, bf16[384,384]{1,0:T(8,128)(2,1)S(1)}, u32[]{:S(2)}, u32[]{:S(2)}) %collective-permute-start.18) | collective-permute-done | bytes 294944 | tf_op jit(solution)/shard_map/ppermute | solution.py:617
  131.1 2.8 %collective-permute-start.19 = (bf16[384,384]{1,0:T(8,128)(2,1)S(1)}, bf16[384,384]{1,0:T(8,128)(2,1)S(1)}, u32[]{:S(2)}, u32[]{:S(2)}) collective-permute-start(bf16[384,384]{1,0:T(8,128)(2,1)S(1)} %add_convert_fusion.2), channel_id=1, source_target_pairs={{0,1},{1,0},{2,3},{3,2},{4,5},{5,4},{6,7},{7,6},{8,9},{9,8},{10,11... | collective-permute-start | bytes 884744 | tf_op jit(solution)/shard_map/ppermute | solution.py:621
  133.9 2.3 %collective-permute-start.21 = (bf16[384,384]{1,0:T(8,128)(2,1)S(1)}, bf16[384,384]{1,0:T(8,128)(2,1)S(1)}, u32[]{:S(2)}, u32[]{:S(2)}) collective-permute-start(bf16[384,384]{1,0:T(8,128)(2,1)S(1)} %add_convert_fusion.1), channel_id=1, source_target_pairs={{0,4},{1,5},{2,6},{3,7},{4,0},{5,1},{6,2},{7,3},{8,12},{9,13},{10,... | collective-permute-start | bytes 884744 | tf_op jit(solution)/shard_map/ppermute | solution.py:617
  136.2 7.5 %collective-permute-done.16 = bf16[384,384]{1,0:T(8,128)(2,1)S(1)} collective-permute-done((bf16[384,384]{1,0:T(8,128)(2,1)S(1)}, bf16[384,384]{1,0:T(8,128)(2,1)S(1)}, u32[]{:S(2)}, u32[]{:S(2)}) %collective-permute-start.16) | collective-permute-done | bytes 294944 | tf_op jit(solution)/shard_map/ppermute | solution.py:617
  (36 shorter events, 4.7 us)
Async XLA Ops:
  3.0 10.3 %collective-permute-start.1 = (bf16[400,384]{1,0:T(8,128)(2,1)S(1)}, bf16[400,384]{1,0:T(8,128)(2,1)S(1)}, u32[]{:S(2)}, u32[]{:S(2)}) collective-permute-start(bf16[400,384]{1,0:T(8,128)(2,1)S(1)} %get-tuple-element.38.refs_0_), channel_id=1, source_target_pairs={{0,6},{1,7},{2,0},{3,1},{4,2},{5,3},{6,4},{7,5},{8,14},{9,15},{10,... | collective-permute-start | bytes 921608 | tf_op jit(solution)/shard_map/ppermute | solution.py:617
  3.9 9.5 %collective-permute-start.2 = (bf16[400,384]{1,0:T(8,128)(2,1)S(1)}, bf16[400,384]{1,0:T(8,128)(2,1)S(1)}, u32[]{:S(2)}, u32[]{:S(2)}) collective-permute-start(bf16[400,384]{1,0:T(8,128)(2,1)S(1)} %get-tuple-element.38.refs_0_), channel_id=1, source_target_pairs={{0,2},{1,3},{2,4},{3,5},{4,6},{5,7},{6,0},{7,1},{8,10},{9,11},{10,... | collective-permute-start | bytes 921608 | tf_op jit(solution)/shard_map/ppermute | solution.py:617
  6.3 10.4 %collective-permute-start = (bf16[400,384]{1,0:T(8,128)(2,1)S(1)}, bf16[400,384]{1,0:T(8,128)(2,1)S(1)}, u32[]{:S(2)}, u32[]{:S(2)}) collective-permute-start(bf16[400,384]{1,0:T(8,128)(2,1)S(1)} %get-tuple-element.38.refs_0_), channel_id=1, source_target_pairs={{0,1},{1,0},{2,3},{3,2},{4,5},{5,4},{6,7},{7,6},{8,9},{9,8},{10,11... | collective-permute-start | bytes 921608 | tf_op jit(solution)/shard_map/ppermute | solution.py:621
  13.3 10.6 %collective-permute-start.6 = (bf16[208,384]{1,0:T(8,128)(2,1)S(1)}, bf16[208,384]{1,0:T(8,128)(2,1)S(1)}, u32[]{:S(2)}, u32[]{:S(2)}) collective-permute-start(bf16[208,384]{1,0:T(8,128)(2,1)S(1)} %slice.13), channel_id=1, source_target_pairs={{0,6},{1,7},{2,0},{3,1},{4,2},{5,3},{6,4},{7,5},{8,14},{9,15},{10,... | collective-permute-start | bytes 479240 | tf_op jit(solution)/shard_map/ppermute | solution.py:617
  13.5 7.2 %collective-permute-start.5 = (bf16[192,384]{1,0:T(8,128)(2,1)S(1)}, bf16[192,384]{1,0:T(8,128)(2,1)S(1)}, u32[]{:S(2)}, u32[]{:S(2)}) collective-permute-start(bf16[192,384]{1,0:T(8,128)(2,1)S(1)} %slice.12), channel_id=1, source_target_pairs={{0,2},{1,3},{2,4},{3,5},{4,6},{5,7},{6,0},{7,1},{8,10},{9,11},{10,... | collective-permute-start | bytes 442376 | tf_op jit(solution)/shard_map/ppermute | solution.py:617
  16.8 11.4 %collective-permute-start.3 = (bf16[400,384]{1,0:T(8,128)(2,1)S(1)}, bf16[400,384]{1,0:T(8,128)(2,1)S(1)}, u32[]{:S(2)}, u32[]{:S(2)}) collective-permute-start(bf16[400,384]{1,0:T(8,128)(2,1)S(1)} %collective-permute-done.refs_1_), channel_id=1, source_target_pairs={{0,6},{1,7},{2,0},{3,1},{4,2},{5,3},{6,4},{7,5},{8,14},{9,15},{10,... | collective-permute-start | bytes 921608 | tf_op jit(solution)/shard_map/ppermute | solution.py:617
  16.8 11.4 %collective-permute-start.4 = (bf16[400,384]{1,0:T(8,128)(2,1)S(1)}, bf16[400,384]{1,0:T(8,128)(2,1)S(1)}, u32[]{:S(2)}, u32[]{:S(2)}) collective-permute-start(bf16[400,384]{1,0:T(8,128)(2,1)S(1)} %collective-permute-done.refs_1_), channel_id=1, source_target_pairs={{0,2},{1,3},{2,4},{3,5},{4,6},{5,7},{6,0},{7,1},{8,10},{9,11},{10,... | collective-permute-start | bytes 921608 | tf_op jit(solution)/shard_map/ppermute | solution.py:617
  20.7 7.5 %collective-permute-start.7 = (bf16[192,384]{1,0:T(8,128)(2,1)S(1)}, bf16[192,384]{1,0:T(8,128)(2,1)S(1)}, u32[]{:S(2)}, u32[]{:S(2)}) collective-permute-start(bf16[192,384]{1,0:T(8,128)(2,1)S(1)} %collective-permute-done.5.refs_6_), channel_id=1, source_target_pairs={{0,1},{1,0},{2,3},{3,2},{4,5},{5,4},{6,7},{7,6},{8,9},{9,8},{10,11... | collective-permute-start | bytes 442376 | tf_op jit(solution)/shard_map/ppermute | solution.py:621
  23.9 6.8 %collective-permute-start.8 = (bf16[208,384]{1,0:T(8,128)(2,1)S(1)}, bf16[208,384]{1,0:T(8,128)(2,1)S(1)}, u32[]{:S(2)}, u32[]{:S(2)}) collective-permute-start(bf16[208,384]{1,0:T(8,128)(2,1)S(1)} %collective-permute-done.6.refs_7_), channel_id=1, source_target_pairs={{0,1},{1,0},{2,3},{3,2},{4,5},{5,4},{6,7},{7,6},{8,9},{9,8},{10,11... | collective-permute-start | bytes 479240 | tf_op jit(solution)/shard_map/ppermute | solution.py:621
  38.5 34.2 %all-to-all-start = ((bf16[8,512,128]{2,1,0:T(8,128)(2,1)}), bf16[8,512,128]{2,1,0:T(8,128)(2,1)S(1)}, u32[]{:S(2)}, u32[]{:S(2)}) async-start(bf16[8,512,128]{2,1,0:T(8,128)(2,1)} %get-tuple-element.42), calls=%async_computation | async-start | bytes 2097152 | tf_op jit(solution)/shard_map/all_to_all | solution.py:688
  47.0 4.9 %collective-permute-start.10 = (bf16[256,128]{1,0:T(8,128)(2,1)S(1)}, bf16[256,128]{1,0:T(8,128)(2,1)S(1)}, u32[]{:S(2)}, u32[]{:S(2)}) collective-permute-start(bf16[256,128]{1,0:T(8,128)(2,1)S(1)} %get-tuple-element.40.refs_0_), channel_id=1, source_target_pairs={{0,128},{8,136},{16,144},{24,152},{32,160},{40,168},{48,176},{56,1... | collective-permute-start | bytes 196616 | tf_op jit(solution)/shard_map/ppermute | solution.py:625
  47.7 4.4 %collective-permute-start.11 = (bf16[256,128]{1,0:T(8,128)(2,1)S(1)}, bf16[256,128]{1,0:T(8,128)(2,1)S(1)}, u32[]{:S(2)}, u32[]{:S(2)}) collective-permute-start(bf16[256,128]{1,0:T(8,128)(2,1)S(1)} %get-tuple-element.40.refs_0_), channel_id=1, source_target_pairs={{0,136},{8,128},{16,152},{24,144},{32,168},{40,160},{48,184},{56,1... | collective-permute-start | bytes 196616 | tf_op jit(solution)/shard_map/ppermute | solution.py:625
  47.7 4.4 %collective-permute-start.9 = (bf16[256,128]{1,0:T(8,128)(2,1)S(1)}, bf16[256,128]{1,0:T(8,128)(2,1)S(1)}, u32[]{:S(2)}, u32[]{:S(2)}) collective-permute-start(bf16[256,128]{1,0:T(8,128)(2,1)S(1)} %get-tuple-element.40.refs_0_), channel_id=1, source_target_pairs={{0,8},{8,0},{16,24},{24,16},{32,40},{40,32},{48,56},{56,48},{64,72... | collective-permute-start | bytes 196616 | tf_op jit(solution)/shard_map/ppermute | solution.py:625
  72.8 3.4 %collective-permute-start.12 = (bf16[8,256,128]{2,1,0:T(8,128)(2,1)S(1)}, bf16[8,256,128]{2,1,0:T(8,128)(2,1)S(1)}, u32[]{:S(2)}, u32[]{:S(2)}) collective-permute-start(bf16[8,256,128]{2,1,0:T(8,128)(2,1)S(1)} %slice.14.own_ref), channel_id=1, source_target_pairs={{0,8},{8,0},{16,24},{24,16},{32,40},{40,32},{48,56},{56,48},{64,72... | collective-permute-start | bytes 1572872 | tf_op jit(solution)/shard_map/ppermute | solution.py:625
  73.1 14.3 %collective-permute-start.13 = (bf16[8,256,128]{2,1,0:T(8,128)(2,1)S(1)}, bf16[8,256,128]{2,1,0:T(8,128)(2,1)S(1)}, u32[]{:S(2)}, u32[]{:S(2)}) collective-permute-start(bf16[8,256,128]{2,1,0:T(8,128)(2,1)S(1)} %slice.14.own_ref), channel_id=1, source_target_pairs={{0,128},{8,136},{16,144},{24,152},{32,160},{40,168},{48,176},{56,1... | collective-permute-start | bytes 1572872 | tf_op jit(solution)/shard_map/ppermute | solution.py:625
  87.5 4.5 %collective-permute-start.14 = (bf16[8,256,128]{2,1,0:T(8,128)(2,1)S(1)}, bf16[8,256,128]{2,1,0:T(8,128)(2,1)S(1)}, u32[]{:S(2)}, u32[]{:S(2)}) collective-permute-start(bf16[8,256,128]{2,1,0:T(8,128)(2,1)S(1)} %collective-permute-done.13.set_ref), channel_id=1, source_target_pairs={{0,8},{8,0},{16,24},{24,16},{32,40},{40,32},{48,56},{56,48},{64,72... | collective-permute-start | bytes 1572872 | tf_op jit(solution)/shard_map/ppermute | solution.py:625
  119.4 10.0 %collective-permute-start.17 = (bf16[384,384]{1,0:T(8,128)(2,1)S(1)}, bf16[384,384]{1,0:T(8,128)(2,1)S(1)}, u32[]{:S(2)}, u32[]{:S(2)}) collective-permute-start(bf16[384,384]{1,0:T(8,128)(2,1)S(1)} %get-tuple-element.61), channel_id=1, source_target_pairs={{0,2},{1,3},{2,4},{3,5},{4,6},{5,7},{6,0},{7,1},{8,10},{9,11},{10,... | collective-permute-start | bytes 884744 | tf_op jit(solution)/shard_map/ppermute | solution.py:617
  121.4 9.5 %collective-permute-start.18 = (bf16[384,384]{1,0:T(8,128)(2,1)S(1)}, bf16[384,384]{1,0:T(8,128)(2,1)S(1)}, u32[]{:S(2)}, u32[]{:S(2)}) collective-permute-start(bf16[384,384]{1,0:T(8,128)(2,1)S(1)} %get-tuple-element.62), channel_id=1, source_target_pairs={{0,6},{1,7},{2,0},{3,1},{4,2},{5,3},{6,4},{7,5},{8,14},{9,15},{10,... | collective-permute-start | bytes 884744 | tf_op jit(solution)/shard_map/ppermute | solution.py:617
  123.5 20.3 %copy-start = (bf16[3,128,384]{2,1,0:T(8,128)(2,1)S(1)}, bf16[3,128,384]{2,1,0:T(8,128)(2,1)}, u32[]{:S(2)}) copy-start(bf16[3,128,384]{2,1,0:T(8,128)(2,1)} %video_ref.1) | copy-start | bytes 884740
  123.5 10.3 %collective-permute-start.20 = (bf16[384,384]{1,0:T(8,128)(2,1)S(1)}, bf16[384,384]{1,0:T(8,128)(2,1)S(1)}, u32[]{:S(2)}, u32[]{:S(2)}) collective-permute-start(bf16[384,384]{1,0:T(8,128)(2,1)S(1)} %get-tuple-element.64), channel_id=1, source_target_pairs={{0,1},{1,0},{2,3},{3,2},{4,5},{5,4},{6,7},{7,6},{8,9},{9,8},{10,11... | collective-permute-start | bytes 884744 | tf_op jit(solution)/shard_map/ppermute | solution.py:621
  125.4 10.8 %collective-permute-start.15 = (bf16[384,384]{1,0:T(8,128)(2,1)S(1)}, bf16[384,384]{1,0:T(8,128)(2,1)S(1)}, u32[]{:S(2)}, u32[]{:S(2)}) collective-permute-start(bf16[384,384]{1,0:T(8,128)(2,1)S(1)} %get-tuple-element.58), channel_id=1, source_target_pairs={{0,2},{1,3},{2,4},{3,5},{4,6},{5,7},{6,0},{7,1},{8,10},{9,11},{10,... | collective-permute-start | bytes 884744 | tf_op jit(solution)/shard_map/ppermute | solution.py:617
  128.7 15.0 %collective-permute-start.16 = (bf16[384,384]{1,0:T(8,128)(2,1)S(1)}, bf16[384,384]{1,0:T(8,128)(2,1)S(1)}, u32[]{:S(2)}, u32[]{:S(2)}) collective-permute-start(bf16[384,384]{1,0:T(8,128)(2,1)S(1)} %get-tuple-element.59), channel_id=1, source_target_pairs={{0,6},{1,7},{2,0},{3,1},{4,2},{5,3},{6,4},{7,5},{8,14},{9,15},{10,... | collective-permute-start | bytes 884744 | tf_op jit(solution)/shard_map/ppermute | solution.py:617
  131.1 12.6 %collective-permute-start.19 = (bf16[384,384]{1,0:T(8,128)(2,1)S(1)}, bf16[384,384]{1,0:T(8,128)(2,1)S(1)}, u32[]{:S(2)}, u32[]{:S(2)}) collective-permute-start(bf16[384,384]{1,0:T(8,128)(2,1)S(1)} %add_convert_fusion.2), channel_id=1, source_target_pairs={{0,1},{1,0},{2,3},{3,2},{4,5},{5,4},{6,7},{7,6},{8,9},{9,8},{10,11... | collective-permute-start | bytes 884744 | tf_op jit(solution)/shard_map/ppermute | solution.py:621
  133.9 9.8 %collective-permute-start.21 = (bf16[384,384]{1,0:T(8,128)(2,1)S(1)}, bf16[384,384]{1,0:T(8,128)(2,1)S(1)}, u32[]{:S(2)}, u32[]{:S(2)}) collective-permute-start(bf16[384,384]{1,0:T(8,128)(2,1)S(1)} %add_convert_fusion.1), channel_id=1, source_target_pairs={{0,4},{1,5},{2,6},{3,7},{4,0},{5,1},{6,2},{7,3},{8,12},{9,13},{10,... | collective-permute-start | bytes 884744 | tf_op jit(solution)/shard_map/ppermute | solution.py:617

commit v10 on v8

--- a/solution.py
+++ b/solution.py
@@ -136,7 +136,7 @@
 def project_kernel(place_ref, *refs):
     blocks, parts = refs[:6], refs[6:10]
     (
-        w_hbm, gain_ref, cos_ref, sin_ref, out_ref, last_ref, mod_ref, acc_ref, w_ref, sems,
+        w_hbm, gain_ref, cos_ref, sin_ref, out_ref, last_ref, early_ref, late_ref, acc_ref, w_ref, sems,
     ) = refs[10:]
     copies = [
         pltpu.make_async_copy(w_hbm.at[n], w_ref.at[:, pl.ds(n * DSH, DSH)], sems.at[n])
@@ -152,32 +152,39 @@
         shift = limb[0:1] + limb[1:2] + limb[2:3]
         mods.append((shift, 1.0 + (limb[3:4] + limb[4:5] + limb[5:6])))
     step = 64
-    for first in (0, CUT):
-        late = 1 if first else 0
-
-        def chunk(n, carry):
-            there = pl.ds(pl.multiple_of(n * step, step), step)
-            here = pl.ds(pl.multiple_of(first + n * step, step), step)
-            sources = [(block, here) for block in blocks]
-            sources += [(parts[late], there), (parts[2 + late], there)]
-            total = jnp.zeros((step, 128), jnp.float32)
-            square = jnp.zeros((step, 128), jnp.float32)
-            for ref, rows in sources:
-                for lane in range(0, DSH, 128):
-                    x = ref[rows, lane : lane + 128].astype(jnp.float32)
-                    total += x
-                    square += x * x
-            mean = jnp.sum(total, axis=1, keepdims=True) / (HEAD_AXIS * DSH)
-            var = jnp.sum(square, axis=1, keepdims=True) / (HEAD_AXIS * DSH) - mean * mean
-            inv = lax.rsqrt(var + norm_eps)
-            for s, (ref, rows) in enumerate(sources):
-                shift, scale = mods[s]
-                y = (ref[rows, :].astype(jnp.float32) - mean) * inv * scale + shift
-                start = pl.multiple_of(place_ref[s] * DSH, DSH)
-                mod_ref[here, pl.ds(start, DSH)] = y.astype(jnp.bfloat16)
-            return carry
-
-        lax.fori_loop(0, CUT // step, chunk, 0)
+
+    def normalize(late, n, mod_ref):
+        there = pl.ds(n * step if isinstance(n, int) else pl.multiple_of(n * step, step), step)
+        here = there if not late else pl.ds(CUT + n * step, step)
+        sources = [(block, here) for block in blocks]
+        sources += [(parts[late], there), (parts[2 + late], there)]
+        total = jnp.zeros((step, 128), jnp.float32)
+        square = jnp.zeros((step, 128), jnp.float32)
+        for ref, rows in sources:
+            for lane in range(0, DSH, 128):
+                x = ref[rows, lane : lane + 128].astype(jnp.float32)
+                total += x
+                square += x * x
+        mean = jnp.sum(total, axis=1, keepdims=True) / (HEAD_AXIS * DSH)
+        var = jnp.sum(square, axis=1, keepdims=True) / (HEAD_AXIS * DSH) - mean * mean
+        inv = lax.rsqrt(var + norm_eps)
+        for s, (ref, rows) in enumerate(sources):
+            shift, scale = mods[s]
+            y = (ref[rows, :].astype(jnp.float32) - mean) * inv * scale + shift
+            start = pl.multiple_of(place_ref[s] * DSH, DSH)
+            mod_ref[there, pl.ds(start, DSH)] = y.astype(jnp.bfloat16)
+
+    def early_step(n, carry):
+        normalize(0, n, early_ref)
+        return carry
+
+    lax.fori_loop(0, CUT // step, early_step, 0)
+    for copy in copies:
+        copy.wait()
+    acc_ref[0:CUT, :] = jnp.dot(early_ref[...], w_ref[...], preferred_element_type=jnp.float32)
+    for n in range(CUT // step):
+        normalize(1, n, late_ref)
+    acc_ref[CUT:, :] = jnp.dot(late_ref[...], w_ref[...], preferred_element_type=jnp.float32)
 
     def piece(part, p):
         b, hd = divmod(p, HEADS_HERE)
@@ -192,9 +199,6 @@
         other = jnp.where(even, pltpu.roll(t, HD - 1, 1), pltpu.roll(t, 1, 1))
         return (t * cos_ref[...] + other * sin_ref[...]).astype(jnp.bfloat16)
 
-    for copy in copies:
-        copy.wait()
-    acc_ref[...] = jnp.dot(mod_ref[...], w_ref[...], preferred_element_type=jnp.float32)
     for part in range(3):
         for p in range(PAIRS):
             if part == 2:
@@ -226,7 +230,8 @@
             + [pl.BlockSpec(memory_space=pltpu.HBM), IN_VMEM, IN_VMEM, IN_VMEM],
             out_specs=(IN_VMEM, IN_VMEM),
             scratch_shapes=[
-                pltpu.VMEM((ROWS, HEAD_AXIS * DSH), jnp.bfloat16),
+                pltpu.VMEM((CUT, HEAD_AXIS * DSH), jnp.bfloat16),
+                pltpu.VMEM((CUT, HEAD_AXIS * DSH), jnp.bfloat16),
                 pltpu.VMEM((ROWS, WIDE), jnp.float32),
                 pltpu.VMEM((HEAD_AXIS * DSH, WIDE), jnp.bfloat16),
                 pltpu.SemaphoreType.DMA((3,)),

time: 145 us -> 145 us (level)
  no operation moved by 1% of the time
where the time goes in v10:
time: 145 us
  waiting for transfers between devices  46 us (32%)
  starting transfers between devices  37.8 us (26%)
  Pallas kernels  36.6 us (25%)
  blocking collectives  21.5 us (15%)
  other arithmetic  2.23 us (2%)
    all_to_all x1, blocking collectives, over_rings(): return lax.all_to_all(x, 'frame', 0, 0, axis_index_groups=rings, tiled=True)  21.5 us
    all_to_all x1, waiting for transfers between devices, over_rings(): return lax.all_to_all(x, 'frame', 0, 0, axis_index_groups=rings, tiled=True)  18.6 us
    ppermute x11, waiting for transfers between devices, head_move(): lax.ppermute(x, 'head', [(i, (i + step) % HEAD_AXIS) for i in range(HEAD_...  16.2 us
    ppermute x11, starting transfers between devices, head_move(): lax.ppermute(x, 'head', [(i, (i + step) % HEAD_AXIS) for i in range(HEAD_...  15.4 us
    ppermute x5, starting transfers between devices, head_partner(): return lax.ppermute(x, 'head', [(i, i ^ 1) for i in range(HEAD_AXIS)])  11.5 us
    pallas_call x2, Pallas kernels, attend_far(): pl.pallas_call(functools.partial(attend_far_kernel, finish), out_shape=pl...  9.15 us
    all_to_all x1, starting transfers between devices, over_rings(): return lax.all_to_all(x, 'frame', 0, 0, axis_index_groups=rings, tiled=True)  8.48 us
    pallas_call x1, Pallas kernels, project(): pl.pallas_call(project_kernel, out_shape=(pltpu.VMEM((RING, 4 * TOK, HD),...  8.47 us
  transfers between devices with their start and end apart: 23, of which 12 were waited for; matrix products, arithmetic and copies ran while one was open for 1% of the time, Pallas kernels for 14%

profile of v10, /device:TPU:6, one launch (start us, length us, event | category | flops | bytes accessed | tf_op | source)
XLA Modules:
  0.0 145.0 jit_solution(10503826151464592315)
XLA Ops:
  0.7 2.4 %prep.1 = (bf16[400,384]{1,0:T(8,128)(2,1)S(1)}, f32[1,384]{1,0:T(1,128)S(1)}, f32[2,128]{1,0:T(2,128)S(1)}, s32[8]{0:T(128)S(1)}, s32[5]{0:T(128)S(1)}) custom-call(s32[1]{0:T(128)} %bitcast.frame_ref, s32[1]{0:T(128)} %bitcast.1.head_ref, s32[1]{0:T(128)S(6)} %copy.13.shift_ref, s32[32]{0:T(128)} %ids_ref.1, s32[3]{0:T(128)} %lengths_ref.1, ...), custom_call_target="tpu_custom_call" | custom-call | tf_op jit(solution)/shard_map/prep/pallas_call | solution.py:110
  3.9 2.4 %collective-permute-start.2 = (bf16[400,384]{1,0:T(8,128)(2,1)S(1)}, bf16[400,384]{1,0:T(8,128)(2,1)S(1)}, u32[]{:S(2)}, u32[]{:S(2)}) collective-permute-start(bf16[400,384]{1,0:T(8,128)(2,1)S(1)} %get-tuple-element.38.refs_0_), channel_id=1, source_target_pairs={{0,2},{1,3},{2,4},{3,5},{4,6},{5,7},{6,0},{7,1},{8,10},{9,11},{10,... | collective-permute-start | bytes 921608 | tf_op jit(solution)/shard_map/ppermute | solution.py:615
  6.3 3.2 %collective-permute-start = (bf16[400,384]{1,0:T(8,128)(2,1)S(1)}, bf16[400,384]{1,0:T(8,128)(2,1)S(1)}, u32[]{:S(2)}, u32[]{:S(2)}) collective-permute-start(bf16[400,384]{1,0:T(8,128)(2,1)S(1)} %get-tuple-element.38.refs_0_), channel_id=1, source_target_pairs={{0,1},{1,0},{2,3},{3,2},{4,5},{5,4},{6,7},{7,6},{8,9},{9,8},{10,11... | collective-permute-start | bytes 921608 | tf_op jit(solution)/shard_map/ppermute | solution.py:619
  9.5 3.8 %collective-permute-done.1.refs_2_ = bf16[400,384]{1,0:T(8,128)(2,1)S(1)} collective-permute-done((bf16[400,384]{1,0:T(8,128)(2,1)S(1)}, bf16[400,384]{1,0:T(8,128)(2,1)S(1)}, u32[]{:S(2)}, u32[]{:S(2)}) %collective-permute-start.1) | collective-permute-done | bytes 307232 | tf_op jit(solution)/shard_map/ppermute | solution.py:615
  13.5 3.3 %collective-permute-start.5 = (bf16[192,384]{1,0:T(8,128)(2,1)S(1)}, bf16[192,384]{1,0:T(8,128)(2,1)S(1)}, u32[]{:S(2)}, u32[]{:S(2)}) collective-permute-start(bf16[192,384]{1,0:T(8,128)(2,1)S(1)} %slice.12), channel_id=1, source_target_pairs={{0,2},{1,3},{2,4},{3,5},{4,6},{5,7},{6,0},{7,1},{8,10},{9,11},{10,... | collective-permute-start | bytes 442376 | tf_op jit(solution)/shard_map/ppermute | solution.py:615
  16.8 3.2 %collective-permute-start.4 = (bf16[400,384]{1,0:T(8,128)(2,1)S(1)}, bf16[400,384]{1,0:T(8,128)(2,1)S(1)}, u32[]{:S(2)}, u32[]{:S(2)}) collective-permute-start(bf16[400,384]{1,0:T(8,128)(2,1)S(1)} %collective-permute-done.refs_1_), channel_id=1, source_target_pairs={{0,2},{1,3},{2,4},{3,5},{4,6},{5,7},{6,0},{7,1},{8,10},{9,11},{10,... | collective-permute-start | bytes 921608 | tf_op jit(solution)/shard_map/ppermute | solution.py:615
  20.7 3.2 %collective-permute-start.7 = (bf16[192,384]{1,0:T(8,128)(2,1)S(1)}, bf16[192,384]{1,0:T(8,128)(2,1)S(1)}, u32[]{:S(2)}, u32[]{:S(2)}) collective-permute-start(bf16[192,384]{1,0:T(8,128)(2,1)S(1)} %collective-permute-done.5.refs_6_), channel_id=1, source_target_pairs={{0,1},{1,0},{2,3},{3,2},{4,5},{5,4},{6,7},{7,6},{8,9},{9,8},{10,11... | collective-permute-start | bytes 442376 | tf_op jit(solution)/shard_map/ppermute | solution.py:619
  24.2 1.0 sine_multiply_fusion
  25.3 2.9 %collective-permute-done.7.refs_8_ = bf16[192,384]{1,0:T(8,128)(2,1)S(1)} collective-permute-done((bf16[192,384]{1,0:T(8,128)(2,1)S(1)}, bf16[192,384]{1,0:T(8,128)(2,1)S(1)}, u32[]{:S(2)}, u32[]{:S(2)}) %collective-permute-start.7) | collective-permute-done | bytes 147488 | tf_op jit(solution)/shard_map/ppermute | solution.py:619
  28.2 2.5 %collective-permute-done.8.refs_9_ = bf16[208,384]{1,0:T(8,128)(2,1)S(1)} collective-permute-done((bf16[208,384]{1,0:T(8,128)(2,1)S(1)}, bf16[208,384]{1,0:T(8,128)(2,1)S(1)}, u32[]{:S(2)}, u32[]{:S(2)}) %collective-permute-start.8) | collective-permute-done | bytes 159776 | tf_op jit(solution)/shard_map/ppermute | solution.py:619
  30.7 8.5 %project.1 = (bf16[8,512,128]{2,1,0:T(8,128)(2,1)}, bf16[256,128]{1,0:T(8,128)(2,1)S(1)}) custom-call(s32[8]{0:T(128)S(1)} %get-tuple-element.36.place_ref, bf16[400,384]{1,0:T(8,128)(2,1)S(1)} %get-tuple-element.38.refs_0_, bf16[400,384]{1,0:T(8,128)(2,1)S(1)} %collective-permute-done.refs_1_, bf16[400,384]{1,0:T(8,128)(2,1)S(1)} %collective-permute-done.1.refs_2_, ...), custom_call_target="tpu_custom_call" | custom-call | flops 2717908992 | bytes 12000000 | tf_op jit(solution)/shard_map/project/pallas_call | solution.py:220
  39.1 8.5 %all-to-all-start = ((bf16[8,512,128]{2,1,0:T(8,128)(2,1)}), bf16[8,512,128]{2,1,0:T(8,128)(2,1)S(1)}, u32[]{:S(2)}, u32[]{:S(2)}) async-start(bf16[8,512,128]{2,1,0:T(8,128)(2,1)} %get-tuple-element.42), calls=%async_computation | async-start | bytes 2097152 | tf_op jit(solution)/shard_map/all_to_all | solution.py:686
  48.3 1.5 %collective-permute-start.9 = (bf16[256,128]{1,0:T(8,128)(2,1)S(1)}, bf16[256,128]{1,0:T(8,128)(2,1)S(1)}, u32[]{:S(2)}, u32[]{:S(2)}) collective-permute-start(bf16[256,128]{1,0:T(8,128)(2,1)S(1)} %get-tuple-element.40.refs_0_), channel_id=1, source_target_pairs={{0,8},{8,0},{16,24},{24,16},{32,40},{40,32},{48,56},{56,48},{64,72... | collective-permute-start | bytes 196616 | tf_op jit(solution)/shard_map/ppermute | solution.py:623
  49.8 2.7 %collective-permute-done.10.refs_2_ = bf16[256,128]{1,0:T(8,128)(2,1)S(1)} collective-permute-done((bf16[256,128]{1,0:T(8,128)(2,1)S(1)}, bf16[256,128]{1,0:T(8,128)(2,1)S(1)}, u32[]{:S(2)}, u32[]{:S(2)}) %collective-permute-start.10) | collective-permute-done | bytes 65568 | tf_op jit(solution)/shard_map/ppermute | solution.py:623
  52.7 2.1 %lay_last.1 = (bf16[640,128]{1,0:T(8,128)(2,1)S(1)}, bf16[640,256]{1,0:T(8,128)(2,1)S(1)}, s32[1]{0:T(128)}) custom-call(s32[5]{0:T(128)S(1)} %get-tuple-element.37.where_ref, bf16[256,128]{1,0:T(8,128)(2,1)S(1)} %get-tuple-element.40.refs_0_, bf16[256,128]{1,0:T(8,128)(2,1)S(1)} %collective-permute-done.9.refs_1_, ...), custom_call_target="tpu_custom_call" | custom-call | flops 10000000000 | bytes 10000000 | tf_op jit(solution)/shard_map/lay_last/pallas_call | solution.py:436
  54.8 18.6 %all-to-all-done.q_ref = bf16[8,512,128]{2,1,0:T(8,128)(2,1)S(1)} async-done(((bf16[8,512,128]{2,1,0:T(8,128)(2,1)}), bf16[8,512,128]{2,1,0:T(8,128)(2,1)S(1)}, u32[]{:S(2)}, u32[]{:S(2)}) %all-to-all-start) | async-done | bytes 1048608 | tf_op jit(solution)/shard_map/all_to_all | solution.py:686
  73.6 3.0 %attend_last.1.refs_3_ = bf16[8,144,128]{2,1,0:T(8,128)(2,1)S(1)} custom-call(s32[5]{0:T(128)S(1)} %get-tuple-element.37.where_ref, bf16[8,512,128]{2,1,0:T(8,128)(2,1)S(1)} %all-to-all-done.q_ref, bf16[640,128]{1,0:T(8,128)(2,1)S(1)} %get-tuple-element.47.keys_ref, bf16[640,256]{1,0:T(8,128)(2,1)S(1)} %get-tuple-element.48.value_ref), custom_call_target="tpu_custom_call" | custom-call | flops 335544320 | bytes 1000000 | tf_op jit(solution)/shard_map/attend_last/pallas_call | solution.py:488
  76.7 8.4 %attend_near.1 = (f32[1024,128]{1,0:T(8,128)S(1)}, f32[1024,128]{1,0:T(8,128)S(1)}, f32[1024,128]{1,0:T(8,128)S(1)}, bf16[1024,128]{1,0:T(8,128)(2,1)S(1)}, bf16[384,3072]{1,0:T(8,128)(2,1)S(1)}) custom-call(s32[5]{0:T(128)S(1)} %get-tuple-element.37.where_ref, s32[1]{0:T(128)} %get-tuple-element.41.flag_ref, bf16[8,512,128]{2,1,0:T(8,128)(2,1)S(1)} %all-to-all-done.q_ref, ...), custom_call_target="tpu_custom_call" | custom-call | flops 1207959552 | bytes 3000000 | tf_op jit(solution)/shard_map/attend_near/pallas_call | solution.py:385
  85.1 2.8 %collective-permute-done.13.set_ref = bf16[8,256,128]{2,1,0:T(8,128)(2,1)S(1)} collective-permute-done((bf16[8,256,128]{2,1,0:T(8,128)(2,1)S(1)}, bf16[8,256,128]{2,1,0:T(8,128)(2,1)S(1)}, u32[]{:S(2)}, u32[]{:S(2)}) %collective-permute-start.13) | collective-permute-done | bytes 524320 | tf_op jit(solution)/shard_map/ppermute | solution.py:623
  87.9 4.5 %attend_far.2 = (f32[1024,128]{1,0:T(8,128)S(1)}, f32[1024,128]{1,0:T(8,128)S(1)}, f32[1024,128]{1,0:T(8,128)S(1)}) custom-call(s32[1]{0:T(128)} %get-tuple-element.41.flag_ref, bf16[1024,128]{1,0:T(8,128)(2,1)S(1)} %get-tuple-element.45.q_ref, bf16[8,256,128]{2,1,0:T(8,128)(2,1)S(1)} %collective-permute-done.13.set_ref, ...), custom_call_target="tpu_custom_call" | custom-call | flops 536870912 | bytes 3000000 | tf_op jit(solution)/shard_map/attend_far/pallas_call | solution.py:538
  92.4 4.7 %attend_far.3 = bf16[8,272,128]{2,1,0:T(8,128)(2,1)S(1)} custom-call(s32[1]{0:T(128)} %get-tuple-element.41.flag_ref, bf16[1024,128]{1,0:T(8,128)(2,1)S(1)} %get-tuple-element.45.q_ref, bf16[8,256,128]{2,1,0:T(8,128)(2,1)S(1)} %collective-permute-done.14.set_ref, f32[1024,128]{1,0:T(8,128)S(1)} %get-tuple-element.52.refs_0_, ...), custom_call_target="tpu_custom_call" | custom-call | flops 536870912 | bytes 3000000 | tf_op jit(solution)/shard_map/attend_far/pallas_call | solution.py:538
  97.1 21.5 %all_to_all.10.back_ref = bf16[8,272,128]{2,1,0:T(8,128)(2,1)S(1)} all-to-all(bf16[8,272,128]{2,1,0:T(8,128)(2,1)S(1)} %attend_far.3), channel_id=1, replica_groups={{0,16,32,48,64,80,96,112},{8,24,40,56,72,88,104,120},{128,144,160,176,1..., dimensions={0} | all-to-all | bytes 1114112 | tf_op jit(solution)/shard_map/all_to_all | solution.py:686
  118.6 1.5 %output.2 = (bf16[384,384]{1,0:T(8,128)(2,1)S(1)}, bf16[384,384]{1,0:T(8,128)(2,1)S(1)}, bf16[384,384]{1,0:T(8,128)(2,1)S(1)}, bf16[384,384]{1,0:T(8,128)(2,1)S(1)}) custom-call(s32[8]{0:T(128)S(1)} %get-tuple-element.36.place_ref, bf16[8,272,128]{2,1,0:T(8,128)(2,1)S(1)} %all_to_all.10.back_ref, bf16[384,3072]{1,0:T(8,128)(2,1)S(1)} %get-tuple-element.55.w_ref), custom_call_target="tpu_custom_call" | custom-call | flops 452984832 | bytes 3000000 | tf_op jit(solution)/shard_map/output/pallas_call | solution.py:597
  120.1 1.7 %collective-permute-start.17 = (bf16[384,384]{1,0:T(8,128)(2,1)S(1)}, bf16[384,384]{1,0:T(8,128)(2,1)S(1)}, u32[]{:S(2)}, u32[]{:S(2)}) collective-permute-start(bf16[384,384]{1,0:T(8,128)(2,1)S(1)} %get-tuple-element.61), channel_id=1, source_target_pairs={{0,2},{1,3},{2,4},{3,5},{4,6},{5,7},{6,0},{7,1},{8,10},{9,11},{10,... | collective-permute-start | bytes 884744 | tf_op jit(solution)/shard_map/ppermute | solution.py:615
  122.2 1.8 %collective-permute-start.20 = (bf16[384,384]{1,0:T(8,128)(2,1)S(1)}, bf16[384,384]{1,0:T(8,128)(2,1)S(1)}, u32[]{:S(2)}, u32[]{:S(2)}) collective-permute-start(bf16[384,384]{1,0:T(8,128)(2,1)S(1)} %get-tuple-element.64), channel_id=1, source_target_pairs={{0,1},{1,0},{2,3},{3,2},{4,5},{5,4},{6,7},{7,6},{8,9},{9,8},{10,11... | collective-permute-start | bytes 884744 | tf_op jit(solution)/shard_map/ppermute | solution.py:619
  124.0 1.6 %output.3 = (bf16[384,384]{1,0:T(8,128)(2,1)S(1)}, bf16[384,384]{1,0:T(8,128)(2,1)S(1)}, bf16[384,384]{1,0:T(8,128)(2,1)S(1)}, bf16[384,384]{1,0:T(8,128)(2,1)S(1)}, bf16[384,384]{1,0:T(8,128)(2,1)S(1)}) custom-call(s32[8]{0:T(128)S(1)} %get-tuple-element.36.place_ref, bf16[384,384]{1,0:T(8,128)(2,1)S(1)} %get-tuple-element.56.attn_ref, ...), custom_call_target="tpu_custom_call" | custom-call | flops 566231040 | bytes 3000000 | tf_op jit(solution)/shard_map/output/pallas_call | solution.py:597
  125.6 3.3 %collective-permute-start.15 = (bf16[384,384]{1,0:T(8,128)(2,1)S(1)}, bf16[384,384]{1,0:T(8,128)(2,1)S(1)}, u32[]{:S(2)}, u32[]{:S(2)}) collective-permute-start(bf16[384,384]{1,0:T(8,128)(2,1)S(1)} %get-tuple-element.58), channel_id=1, source_target_pairs={{0,2},{1,3},{2,4},{3,5},{4,6},{5,7},{6,0},{7,1},{8,10},{9,11},{10,... | collective-permute-start | bytes 884744 | tf_op jit(solution)/shard_map/ppermute | solution.py:615
  129.0 1.2 collective-permute-done.17
  130.1 1.3 collective-permute-done.18
  131.5 3.0 %collective-permute-start.19 = (bf16[384,384]{1,0:T(8,128)(2,1)S(1)}, bf16[384,384]{1,0:T(8,128)(2,1)S(1)}, u32[]{:S(2)}, u32[]{:S(2)}) collective-permute-start(bf16[384,384]{1,0:T(8,128)(2,1)S(1)} %add_convert_fusion.2), channel_id=1, source_target_pairs={{0,1},{1,0},{2,3},{3,2},{4,5},{5,4},{6,7},{7,6},{8,9},{9,8},{10,11... | collective-permute-start | bytes 884744 | tf_op jit(solution)/shard_map/ppermute | solution.py:619
  134.7 1.0 collective-permute-done.15
  135.7 8.3 %collective-permute-done.16 = bf16[384,384]{1,0:T(8,128)(2,1)S(1)} collective-permute-done((bf16[384,384]{1,0:T(8,128)(2,1)S(1)}, bf16[384,384]{1,0:T(8,128)(2,1)S(1)}, u32[]{:S(2)}, u32[]{:S(2)}) %collective-permute-start.16) | collective-permute-done | bytes 294944 | tf_op jit(solution)/shard_map/ppermute | solution.py:615
  (36 shorter events, 4.8 us)
Async XLA Ops:
  3.0 10.3 %collective-permute-start.1 = (bf16[400,384]{1,0:T(8,128)(2,1)S(1)}, bf16[400,384]{1,0:T(8,128)(2,1)S(1)}, u32[]{:S(2)}, u32[]{:S(2)}) collective-permute-start(bf16[400,384]{1,0:T(8,128)(2,1)S(1)} %get-tuple-element.38.refs_0_), channel_id=1, source_target_pairs={{0,6},{1,7},{2,0},{3,1},{4,2},{5,3},{6,4},{7,5},{8,14},{9,15},{10,... | collective-permute-start | bytes 921608 | tf_op jit(solution)/shard_map/ppermute | solution.py:615
  3.9 9.5 %collective-permute-start.2 = (bf16[400,384]{1,0:T(8,128)(2,1)S(1)}, bf16[400,384]{1,0:T(8,128)(2,1)S(1)}, u32[]{:S(2)}, u32[]{:S(2)}) collective-permute-start(bf16[400,384]{1,0:T(8,128)(2,1)S(1)} %get-tuple-element.38.refs_0_), channel_id=1, source_target_pairs={{0,2},{1,3},{2,4},{3,5},{4,6},{5,7},{6,0},{7,1},{8,10},{9,11},{10,... | collective-permute-start | bytes 921608 | tf_op jit(solution)/shard_map/ppermute | solution.py:615
  6.3 10.4 %collective-permute-start = (bf16[400,384]{1,0:T(8,128)(2,1)S(1)}, bf16[400,384]{1,0:T(8,128)(2,1)S(1)}, u32[]{:S(2)}, u32[]{:S(2)}) collective-permute-start(bf16[400,384]{1,0:T(8,128)(2,1)S(1)} %get-tuple-element.38.refs_0_), channel_id=1, source_target_pairs={{0,1},{1,0},{2,3},{3,2},{4,5},{5,4},{6,7},{7,6},{8,9},{9,8},{10,11... | collective-permute-start | bytes 921608 | tf_op jit(solution)/shard_map/ppermute | solution.py:619
  13.3 10.5 %collective-permute-start.6 = (bf16[208,384]{1,0:T(8,128)(2,1)S(1)}, bf16[208,384]{1,0:T(8,128)(2,1)S(1)}, u32[]{:S(2)}, u32[]{:S(2)}) collective-permute-start(bf16[208,384]{1,0:T(8,128)(2,1)S(1)} %slice.13), channel_id=1, source_target_pairs={{0,6},{1,7},{2,0},{3,1},{4,2},{5,3},{6,4},{7,5},{8,14},{9,15},{10,... | collective-permute-start | bytes 479240 | tf_op jit(solution)/shard_map/ppermute | solution.py:615
  13.5 7.2 %collective-permute-start.5 = (bf16[192,384]{1,0:T(8,128)(2,1)S(1)}, bf16[192,384]{1,0:T(8,128)(2,1)S(1)}, u32[]{:S(2)}, u32[]{:S(2)}) collective-permute-start(bf16[192,384]{1,0:T(8,128)(2,1)S(1)} %slice.12), channel_id=1, source_target_pairs={{0,2},{1,3},{2,4},{3,5},{4,6},{5,7},{6,0},{7,1},{8,10},{9,11},{10,... | collective-permute-start | bytes 442376 | tf_op jit(solution)/shard_map/ppermute | solution.py:615
  16.8 11.4 %collective-permute-start.3 = (bf16[400,384]{1,0:T(8,128)(2,1)S(1)}, bf16[400,384]{1,0:T(8,128)(2,1)S(1)}, u32[]{:S(2)}, u32[]{:S(2)}) collective-permute-start(bf16[400,384]{1,0:T(8,128)(2,1)S(1)} %collective-permute-done.refs_1_), channel_id=1, source_target_pairs={{0,6},{1,7},{2,0},{3,1},{4,2},{5,3},{6,4},{7,5},{8,14},{9,15},{10,... | collective-permute-start | bytes 921608 | tf_op jit(solution)/shard_map/ppermute | solution.py:615
  16.8 11.4 %collective-permute-start.4 = (bf16[400,384]{1,0:T(8,128)(2,1)S(1)}, bf16[400,384]{1,0:T(8,128)(2,1)S(1)}, u32[]{:S(2)}, u32[]{:S(2)}) collective-permute-start(bf16[400,384]{1,0:T(8,128)(2,1)S(1)} %collective-permute-done.refs_1_), channel_id=1, source_target_pairs={{0,2},{1,3},{2,4},{3,5},{4,6},{5,7},{6,0},{7,1},{8,10},{9,11},{10,... | collective-permute-start | bytes 921608 | tf_op jit(solution)/shard_map/ppermute | solution.py:615
  20.7 7.5 %collective-permute-start.7 = (bf16[192,384]{1,0:T(8,128)(2,1)S(1)}, bf16[192,384]{1,0:T(8,128)(2,1)S(1)}, u32[]{:S(2)}, u32[]{:S(2)}) collective-permute-start(bf16[192,384]{1,0:T(8,128)(2,1)S(1)} %collective-permute-done.5.refs_6_), channel_id=1, source_target_pairs={{0,1},{1,0},{2,3},{3,2},{4,5},{5,4},{6,7},{7,6},{8,9},{9,8},{10,11... | collective-permute-start | bytes 442376 | tf_op jit(solution)/shard_map/ppermute | solution.py:619
  23.9 6.8 %collective-permute-start.8 = (bf16[208,384]{1,0:T(8,128)(2,1)S(1)}, bf16[208,384]{1,0:T(8,128)(2,1)S(1)}, u32[]{:S(2)}, u32[]{:S(2)}) collective-permute-start(bf16[208,384]{1,0:T(8,128)(2,1)S(1)} %collective-permute-done.6.refs_7_), channel_id=1, source_target_pairs={{0,1},{1,0},{2,3},{3,2},{4,5},{5,4},{6,7},{7,6},{8,9},{9,8},{10,11... | collective-permute-start | bytes 479240 | tf_op jit(solution)/shard_map/ppermute | solution.py:619
  39.1 34.3 %all-to-all-start = ((bf16[8,512,128]{2,1,0:T(8,128)(2,1)}), bf16[8,512,128]{2,1,0:T(8,128)(2,1)S(1)}, u32[]{:S(2)}, u32[]{:S(2)}) async-start(bf16[8,512,128]{2,1,0:T(8,128)(2,1)} %get-tuple-element.42), calls=%async_computation | async-start | bytes 2097152 | tf_op jit(solution)/shard_map/all_to_all | solution.py:686
  47.6 4.9 %collective-permute-start.10 = (bf16[256,128]{1,0:T(8,128)(2,1)S(1)}, bf16[256,128]{1,0:T(8,128)(2,1)S(1)}, u32[]{:S(2)}, u32[]{:S(2)}) collective-permute-start(bf16[256,128]{1,0:T(8,128)(2,1)S(1)} %get-tuple-element.40.refs_0_), channel_id=1, source_target_pairs={{0,128},{8,136},{16,144},{24,152},{32,160},{40,168},{48,176},{56,1... | collective-permute-start | bytes 196616 | tf_op jit(solution)/shard_map/ppermute | solution.py:623
  48.3 4.4 %collective-permute-start.11 = (bf16[256,128]{1,0:T(8,128)(2,1)S(1)}, bf16[256,128]{1,0:T(8,128)(2,1)S(1)}, u32[]{:S(2)}, u32[]{:S(2)}) collective-permute-start(bf16[256,128]{1,0:T(8,128)(2,1)S(1)} %get-tuple-element.40.refs_0_), channel_id=1, source_target_pairs={{0,136},{8,128},{16,152},{24,144},{32,168},{40,160},{48,184},{56,1... | collective-permute-start | bytes 196616 | tf_op jit(solution)/shard_map/ppermute | solution.py:623
  48.3 4.4 %collective-permute-start.9 = (bf16[256,128]{1,0:T(8,128)(2,1)S(1)}, bf16[256,128]{1,0:T(8,128)(2,1)S(1)}, u32[]{:S(2)}, u32[]{:S(2)}) collective-permute-start(bf16[256,128]{1,0:T(8,128)(2,1)S(1)} %get-tuple-element.40.refs_0_), channel_id=1, source_target_pairs={{0,8},{8,0},{16,24},{24,16},{32,40},{40,32},{48,56},{56,48},{64,72... | collective-permute-start | bytes 196616 | tf_op jit(solution)/shard_map/ppermute | solution.py:623
  73.4 3.2 %collective-permute-start.12 = (bf16[8,256,128]{2,1,0:T(8,128)(2,1)S(1)}, bf16[8,256,128]{2,1,0:T(8,128)(2,1)S(1)}, u32[]{:S(2)}, u32[]{:S(2)}) collective-permute-start(bf16[8,256,128]{2,1,0:T(8,128)(2,1)S(1)} %slice.14.own_ref), channel_id=1, source_target_pairs={{0,8},{8,0},{16,24},{24,16},{32,40},{40,32},{48,56},{56,48},{64,72... | collective-permute-start | bytes 1572872 | tf_op jit(solution)/shard_map/ppermute | solution.py:623
  73.5 14.3 %collective-permute-start.13 = (bf16[8,256,128]{2,1,0:T(8,128)(2,1)S(1)}, bf16[8,256,128]{2,1,0:T(8,128)(2,1)S(1)}, u32[]{:S(2)}, u32[]{:S(2)}) collective-permute-start(bf16[8,256,128]{2,1,0:T(8,128)(2,1)S(1)} %slice.14.own_ref), channel_id=1, source_target_pairs={{0,128},{8,136},{16,144},{24,152},{32,160},{40,168},{48,176},{56,1... | collective-permute-start | bytes 1572872 | tf_op jit(solution)/shard_map/ppermute | solution.py:623
  87.9 4.5 %collective-permute-start.14 = (bf16[8,256,128]{2,1,0:T(8,128)(2,1)S(1)}, bf16[8,256,128]{2,1,0:T(8,128)(2,1)S(1)}, u32[]{:S(2)}, u32[]{:S(2)}) collective-permute-start(bf16[8,256,128]{2,1,0:T(8,128)(2,1)S(1)} %collective-permute-done.13.set_ref), channel_id=1, source_target_pairs={{0,8},{8,0},{16,24},{24,16},{32,40},{40,32},{48,56},{56,48},{64,72... | collective-permute-start | bytes 1572872 | tf_op jit(solution)/shard_map/ppermute | solution.py:623
  120.1 10.0 %collective-permute-start.17 = (bf16[384,384]{1,0:T(8,128)(2,1)S(1)}, bf16[384,384]{1,0:T(8,128)(2,1)S(1)}, u32[]{:S(2)}, u32[]{:S(2)}) collective-permute-start(bf16[384,384]{1,0:T(8,128)(2,1)S(1)} %get-tuple-element.61), channel_id=1, source_target_pairs={{0,2},{1,3},{2,4},{3,5},{4,6},{5,7},{6,0},{7,1},{8,10},{9,11},{10,... | collective-permute-start | bytes 884744 | tf_op jit(solution)/shard_map/ppermute | solution.py:615
  121.9 9.5 %collective-permute-start.18 = (bf16[384,384]{1,0:T(8,128)(2,1)S(1)}, bf16[384,384]{1,0:T(8,128)(2,1)S(1)}, u32[]{:S(2)}, u32[]{:S(2)}) collective-permute-start(bf16[384,384]{1,0:T(8,128)(2,1)S(1)} %get-tuple-element.62), channel_id=1, source_target_pairs={{0,6},{1,7},{2,0},{3,1},{4,2},{5,3},{6,4},{7,5},{8,14},{9,15},{10,... | collective-permute-start | bytes 884744 | tf_op jit(solution)/shard_map/ppermute | solution.py:615
  122.2 12.3 %collective-permute-start.20 = (bf16[384,384]{1,0:T(8,128)(2,1)S(1)}, bf16[384,384]{1,0:T(8,128)(2,1)S(1)}, u32[]{:S(2)}, u32[]{:S(2)}) collective-permute-start(bf16[384,384]{1,0:T(8,128)(2,1)S(1)} %get-tuple-element.64), channel_id=1, source_target_pairs={{0,1},{1,0},{2,3},{3,2},{4,5},{5,4},{6,7},{7,6},{8,9},{9,8},{10,11... | collective-permute-start | bytes 884744 | tf_op jit(solution)/shard_map/ppermute | solution.py:619
  125.6 18.6 %copy-start = (bf16[3,128,384]{2,1,0:T(8,128)(2,1)S(1)}, bf16[3,128,384]{2,1,0:T(8,128)(2,1)}, u32[]{:S(2)}) copy-start(bf16[3,128,384]{2,1,0:T(8,128)(2,1)} %video_ref.1) | copy-start | bytes 884740
  125.6 10.1 %collective-permute-start.15 = (bf16[384,384]{1,0:T(8,128)(2,1)S(1)}, bf16[384,384]{1,0:T(8,128)(2,1)S(1)}, u32[]{:S(2)}, u32[]{:S(2)}) collective-permute-start(bf16[384,384]{1,0:T(8,128)(2,1)S(1)} %get-tuple-element.58), channel_id=1, source_target_pairs={{0,2},{1,3},{2,4},{3,5},{4,6},{5,7},{6,0},{7,1},{8,10},{9,11},{10,... | collective-permute-start | bytes 884744 | tf_op jit(solution)/shard_map/ppermute | solution.py:615
  128.9 15.1 %collective-permute-start.16 = (bf16[384,384]{1,0:T(8,128)(2,1)S(1)}, bf16[384,384]{1,0:T(8,128)(2,1)S(1)}, u32[]{:S(2)}, u32[]{:S(2)}) collective-permute-start(bf16[384,384]{1,0:T(8,128)(2,1)S(1)} %get-tuple-element.59), channel_id=1, source_target_pairs={{0,6},{1,7},{2,0},{3,1},{4,2},{5,3},{6,4},{7,5},{8,14},{9,15},{10,... | collective-permute-start | bytes 884744 | tf_op jit(solution)/shard_map/ppermute | solution.py:615
  131.5 12.5 %collective-permute-start.19 = (bf16[384,384]{1,0:T(8,128)(2,1)S(1)}, bf16[384,384]{1,0:T(8,128)(2,1)S(1)}, u32[]{:S(2)}, u32[]{:S(2)}) collective-permute-start(bf16[384,384]{1,0:T(8,128)(2,1)S(1)} %add_convert_fusion.2), channel_id=1, source_target_pairs={{0,1},{1,0},{2,3},{3,2},{4,5},{5,4},{6,7},{7,6},{8,9},{9,8},{10,11... | collective-permute-start | bytes 884744 | tf_op jit(solution)/shard_map/ppermute | solution.py:619
  134.6 9.4 %collective-permute-start.21 = (bf16[384,384]{1,0:T(8,128)(2,1)S(1)}, bf16[384,384]{1,0:T(8,128)(2,1)S(1)}, u32[]{:S(2)}, u32[]{:S(2)}) collective-permute-start(bf16[384,384]{1,0:T(8,128)(2,1)S(1)} %add_convert_fusion.1), channel_id=1, source_target_pairs={{0,4},{1,5},{2,6},{3,7},{4,0},{5,1},{6,2},{7,3},{8,12},{9,13},{10,... | collective-permute-start | bytes 884744 | tf_op jit(solution)/shard_map/ppermute | solution.py:615

commit v11 on v8

--- a/solution.py
+++ b/solution.py
@@ -283,11 +283,11 @@
 
 
 def set_keys(ref):
-    return ref[:, 0:TOK, :].reshape(SET, HD)
+    return ref[:, 0:TOK, :].reshape(-1, HD)
 
 
 def set_values(ref):
-    return ref[:, TOK : 2 * TOK, :].reshape(SET, HD)
+    return ref[:, TOK : 2 * TOK, :].reshape(-1, HD)
 
 
 def first_step():
@@ -538,12 +538,12 @@
             grid=(SET // TILE,),
             in_specs=[IN_VMEM] * len(operands),
             out_specs=IN_VMEM if finish else (IN_VMEM,) * 3,
-            scratch_shapes=[pltpu.VMEM((TILE, SET), jnp.float32)]
+            scratch_shapes=[pltpu.VMEM((TILE, keys.shape[0] * TOK), jnp.float32)]
             + [pltpu.VMEM((TILE, 128), jnp.float32)] * 3,
         ),
         compiler_params=pltpu.CompilerParams(vmem_limit_bytes=16 * MIB),
         cost_estimate=pl.CostEstimate(
-            flops=4 * SET * SET * HD, bytes_accessed=3_000_000, transcendentals=SET * SET
+            flops=2 * SET * SET * HD, bytes_accessed=3_000_000, transcendentals=SET * SET // 2
         ),
         name="attend_far",
     )(flag, *map(in_vmem, operands))
@@ -685,16 +685,21 @@
     lasts = [last] + [frame_move(last, flip) for flip in flips]
     last_keys, last_values, flag = lay_last(where, lasts, text_kv, gains)
     near = received[:, : 2 * TOK]
-    over_y = frame_move(near, FRAMES // 2)
+    halves = [near[: RING // 2], near[RING // 2 :]]
+    over_y = [frame_move(half, FRAMES // 2) for half in halves]
     near_later, last_keys = lax.optimization_barrier((near, last_keys))
     over_core = frame_move(near_later, 1)
     ninth = attend_last(where, received, last_keys, last_values)
     *state, queries, w_held = attend_near(
         where, flag, received, near, over_core, text_kv, in_hbm(w_out)
     )
-    over_y, _, _ = lax.optimization_barrier((over_y, state[0], ninth))
-    diagonal = frame_move(over_y, 1)
-    state = attend_far(flag, queries, over_y, state)
+    first, _, _ = lax.optimization_barrier((over_y[0], state[0], ninth))
+    diagonal = frame_move(first, 1)
+    state = attend_far(flag, queries, first, state)
+    state = attend_far(flag, queries, diagonal, state)
+    second, _ = lax.optimization_barrier((over_y[1], state[0]))
+    diagonal = frame_move(second, 1)
+    state = attend_far(flag, queries, second, state)
     returned = attend_far(flag, queries, diagonal, state, ninth)
     back = over_rings(returned)
     proj = scatter_head(places, back, w_held).reshape(video.shape)

time: 145 us -> 150 us (1.034)
  Pallas kernels: 36 us -> 40.2 us
  starting transfers between devices: 37.9 us -> 41.7 us
  waiting for transfers between devices: 46 us -> 42.7 us
    pallas_call x2 -> x4, Pallas kernels: 9.15 us -> 13.4 us  [attend_far(): pl.pallas_call(functools.partial(attend_far_kernel, finish), out_shape=pl...]
    ppermute x6 -> x8, waiting for transfers between devices: 5.77 us -> 3.07 us  [frame_move(): return lax.ppermute(x, 'frame', [(i, i ^ flip) for i in range(FRAMES)])]
    ppermute x6 -> x8, starting transfers between devices: 2.51 us -> 5.02 us  [frame_move(): return lax.ppermute(x, 'frame', [(i, i ^ flip) for i in range(FRAMES)])]
  transfers between devices with their start and end apart: 23 -> 25, of which waited for: 12 -> 11; matrix products, arithmetic and copies ran while one was open for 1% -> 1% of each run, Pallas kernels for 14% -> 17%
where the time goes in v11:
time: 150 us; the launch traced here: 149 us
  waiting for transfers between devices  42.7 us (28%)
  starting transfers between devices  41.7 us (28%)
  Pallas kernels  40.2 us (27%)
  blocking collectives  21.5 us (14%)
  other arithmetic  2.23 us (1%)
    all_to_all x1, blocking collectives, over_rings(): return lax.all_to_all(x, 'frame', 0, 0, axis_index_groups=rings, tiled=True)  21.5 us
    all_to_all x1, waiting for transfers between devices, over_rings(): return lax.all_to_all(x, 'frame', 0, 0, axis_index_groups=rings, tiled=True)  18.6 us
    ppermute x11, waiting for transfers between devices, head_move(): lax.ppermute(x, 'head', [(i, (i + step) % HEAD_AXIS) for i in range(HEAD_...  15.7 us
    ppermute x11, starting transfers between devices, head_move(): lax.ppermute(x, 'head', [(i, (i + step) % HEAD_AXIS) for i in range(HEAD_...  15.6 us
    pallas_call x4, Pallas kernels, attend_far(): pl.pallas_call(functools.partial(attend_far_kernel, finish), out_shape=pl...  13.4 us
    ppermute x5, starting transfers between devices, head_partner(): return lax.ppermute(x, 'head', [(i, i ^ 1) for i in range(HEAD_AXIS)])  12.6 us
    all_to_all x1, starting transfers between devices, over_rings(): return lax.all_to_all(x, 'frame', 0, 0, axis_index_groups=rings, tiled=True)  8.48 us
    pallas_call x1, Pallas kernels, attend_near(): pl.pallas_call(attend_near_kernel, out_shape=STATE + (pltpu.VMEM((SET, HD...  8.37 us
  transfers between devices with their start and end apart: 25, of which 11 were waited for; matrix products, arithmetic and copies ran while one was open for 1% of the time, Pallas kernels for 17%

profile of v11, /device:TPU:6, one launch (start us, length us, event | category | flops | bytes accessed | tf_op | source)
XLA Modules:
  0.0 149.4 jit_solution(9018723917499738171)
XLA Ops:
  0.7 2.4 %prep.1 = (bf16[400,384]{1,0:T(8,128)(2,1)S(1)}, f32[1,384]{1,0:T(1,128)S(1)}, f32[2,128]{1,0:T(2,128)S(1)}, s32[8]{0:T(128)S(1)}, s32[5]{0:T(128)S(1)}) custom-call(s32[1]{0:T(128)} %bitcast.frame_ref, s32[1]{0:T(128)} %bitcast.1.head_ref, s32[1]{0:T(128)S(6)} %copy.13.shift_ref, s32[32]{0:T(128)} %ids_ref.1, s32[3]{0:T(128)} %lengths_ref.1, ...), custom_call_target="tpu_custom_call" | custom-call | tf_op jit(solution)/shard_map/prep/pallas_call | solution.py:110
  3.9 2.4 %collective-permute-start.2 = (bf16[400,384]{1,0:T(8,128)(2,1)S(1)}, bf16[400,384]{1,0:T(8,128)(2,1)S(1)}, u32[]{:S(2)}, u32[]{:S(2)}) collective-permute-start(bf16[400,384]{1,0:T(8,128)(2,1)S(1)} %get-tuple-element.45.refs_0_), channel_id=1, source_target_pairs={{0,2},{1,3},{2,4},{3,5},{4,6},{5,7},{6,0},{7,1},{8,10},{9,11},{10,... | collective-permute-start | bytes 921608 | tf_op jit(solution)/shard_map/ppermute | solution.py:610
  6.3 3.2 %collective-permute-start = (bf16[400,384]{1,0:T(8,128)(2,1)S(1)}, bf16[400,384]{1,0:T(8,128)(2,1)S(1)}, u32[]{:S(2)}, u32[]{:S(2)}) collective-permute-start(bf16[400,384]{1,0:T(8,128)(2,1)S(1)} %get-tuple-element.45.refs_0_), channel_id=1, source_target_pairs={{0,1},{1,0},{2,3},{3,2},{4,5},{5,4},{6,7},{7,6},{8,9},{9,8},{10,11... | collective-permute-start | bytes 921608 | tf_op jit(solution)/shard_map/ppermute | solution.py:614
  9.5 3.8 %collective-permute-done.1.refs_2_ = bf16[400,384]{1,0:T(8,128)(2,1)S(1)} collective-permute-done((bf16[400,384]{1,0:T(8,128)(2,1)S(1)}, bf16[400,384]{1,0:T(8,128)(2,1)S(1)}, u32[]{:S(2)}, u32[]{:S(2)}) %collective-permute-start.1) | collective-permute-done | bytes 307232 | tf_op jit(solution)/shard_map/ppermute | solution.py:610
  13.5 3.3 %collective-permute-start.5 = (bf16[192,384]{1,0:T(8,128)(2,1)S(1)}, bf16[192,384]{1,0:T(8,128)(2,1)S(1)}, u32[]{:S(2)}, u32[]{:S(2)}) collective-permute-start(bf16[192,384]{1,0:T(8,128)(2,1)S(1)} %slice.22), channel_id=1, source_target_pairs={{0,2},{1,3},{2,4},{3,5},{4,6},{5,7},{6,0},{7,1},{8,10},{9,11},{10,... | collective-permute-start | bytes 442376 | tf_op jit(solution)/shard_map/ppermute | solution.py:610
  16.8 3.2 %collective-permute-start.4 = (bf16[400,384]{1,0:T(8,128)(2,1)S(1)}, bf16[400,384]{1,0:T(8,128)(2,1)S(1)}, u32[]{:S(2)}, u32[]{:S(2)}) collective-permute-start(bf16[400,384]{1,0:T(8,128)(2,1)S(1)} %collective-permute-done.refs_1_), channel_id=1, source_target_pairs={{0,2},{1,3},{2,4},{3,5},{4,6},{5,7},{6,0},{7,1},{8,10},{9,11},{10,... | collective-permute-start | bytes 921608 | tf_op jit(solution)/shard_map/ppermute | solution.py:610
  20.7 3.2 %collective-permute-start.7 = (bf16[192,384]{1,0:T(8,128)(2,1)S(1)}, bf16[192,384]{1,0:T(8,128)(2,1)S(1)}, u32[]{:S(2)}, u32[]{:S(2)}) collective-permute-start(bf16[192,384]{1,0:T(8,128)(2,1)S(1)} %collective-permute-done.5.refs_6_), channel_id=1, source_target_pairs={{0,1},{1,0},{2,3},{3,2},{4,5},{5,4},{6,7},{7,6},{8,9},{9,8},{10,11... | collective-permute-start | bytes 442376 | tf_op jit(solution)/shard_map/ppermute | solution.py:614
  25.3 2.9 %collective-permute-done.7.refs_8_ = bf16[192,384]{1,0:T(8,128)(2,1)S(1)} collective-permute-done((bf16[192,384]{1,0:T(8,128)(2,1)S(1)}, bf16[192,384]{1,0:T(8,128)(2,1)S(1)}, u32[]{:S(2)}, u32[]{:S(2)}) %collective-permute-start.7) | collective-permute-done | bytes 147488 | tf_op jit(solution)/shard_map/ppermute | solution.py:614
  28.2 2.5 %collective-permute-done.8.refs_9_ = bf16[208,384]{1,0:T(8,128)(2,1)S(1)} collective-permute-done((bf16[208,384]{1,0:T(8,128)(2,1)S(1)}, bf16[208,384]{1,0:T(8,128)(2,1)S(1)}, u32[]{:S(2)}, u32[]{:S(2)}) %collective-permute-start.8) | collective-permute-done | bytes 159776 | tf_op jit(solution)/shard_map/ppermute | solution.py:614
  30.7 7.9 %project.1 = (bf16[8,512,128]{2,1,0:T(8,128)(2,1)}, bf16[256,128]{1,0:T(8,128)(2,1)S(1)}) custom-call(s32[8]{0:T(128)S(1)} %get-tuple-element.43.place_ref, bf16[400,384]{1,0:T(8,128)(2,1)S(1)} %get-tuple-element.45.refs_0_, bf16[400,384]{1,0:T(8,128)(2,1)S(1)} %collective-permute-done.refs_1_, bf16[400,384]{1,0:T(8,128)(2,1)S(1)} %collective-permute-done.1.refs_2_, ...), custom_call_target="tpu_custom_call" | custom-call | flops 2717908992 | bytes 12000000 | tf_op jit(solution)/shard_map/project/pallas_call | solution.py:216
  38.5 8.5 %all-to-all-start = ((bf16[8,512,128]{2,1,0:T(8,128)(2,1)}), bf16[8,512,128]{2,1,0:T(8,128)(2,1)S(1)}, u32[]{:S(2)}, u32[]{:S(2)}) async-start(bf16[8,512,128]{2,1,0:T(8,128)(2,1)} %get-tuple-element.49), calls=%async_computation | async-start | bytes 2097152 | tf_op jit(solution)/shard_map/all_to_all | solution.py:681
  47.7 1.5 collective-permute-start.9
  49.2 2.7 %collective-permute-done.10.refs_2_ = bf16[256,128]{1,0:T(8,128)(2,1)S(1)} collective-permute-done((bf16[256,128]{1,0:T(8,128)(2,1)S(1)}, bf16[256,128]{1,0:T(8,128)(2,1)S(1)}, u32[]{:S(2)}, u32[]{:S(2)}) %collective-permute-start.10) | collective-permute-done | bytes 65568 | tf_op jit(solution)/shard_map/ppermute | solution.py:618
  52.1 2.1 %lay_last.1 = (bf16[640,128]{1,0:T(8,128)(2,1)S(1)}, bf16[640,256]{1,0:T(8,128)(2,1)S(1)}, s32[1]{0:T(128)}) custom-call(s32[5]{0:T(128)S(1)} %get-tuple-element.44.where_ref, bf16[256,128]{1,0:T(8,128)(2,1)S(1)} %get-tuple-element.47.refs_0_, bf16[256,128]{1,0:T(8,128)(2,1)S(1)} %collective-permute-done.9.refs_1_, ...), custom_call_target="tpu_custom_call" | custom-call | flops 10000000000 | bytes 10000000 | tf_op jit(solution)/shard_map/lay_last/pallas_call | solution.py:431
  54.2 18.6 %all-to-all-done.q_ref = bf16[8,512,128]{2,1,0:T(8,128)(2,1)S(1)} async-done(((bf16[8,512,128]{2,1,0:T(8,128)(2,1)}), bf16[8,512,128]{2,1,0:T(8,128)(2,1)S(1)}, u32[]{:S(2)}, u32[]{:S(2)}) %all-to-all-start) | async-done | bytes 1048608 | tf_op jit(solution)/shard_map/all_to_all | solution.py:681
  73.3 3.0 %attend_last.1.refs_3_ = bf16[8,144,128]{2,1,0:T(8,128)(2,1)S(1)} custom-call(s32[5]{0:T(128)S(1)} %get-tuple-element.44.where_ref, bf16[8,512,128]{2,1,0:T(8,128)(2,1)S(1)} %all-to-all-done.q_ref, bf16[640,128]{1,0:T(8,128)(2,1)S(1)} %get-tuple-element.54.keys_ref, bf16[640,256]{1,0:T(8,128)(2,1)S(1)} %get-tuple-element.55.value_ref), custom_call_target="tpu_custom_call" | custom-call | flops 335544320 | bytes 1000000 | tf_op jit(solution)/shard_map/attend_last/pallas_call | solution.py:483
  76.3 8.4 %attend_near.1 = (f32[1024,128]{1,0:T(8,128)S(1)}, f32[1024,128]{1,0:T(8,128)S(1)}, f32[1024,128]{1,0:T(8,128)S(1)}, bf16[1024,128]{1,0:T(8,128)(2,1)S(1)}, bf16[384,3072]{1,0:T(8,128)(2,1)S(1)}) custom-call(s32[5]{0:T(128)S(1)} %get-tuple-element.44.where_ref, s32[1]{0:T(128)} %get-tuple-element.48.flag_ref, bf16[8,512,128]{2,1,0:T(8,128)(2,1)S(1)} %all-to-all-done.q_ref, ...), custom_call_target="tpu_custom_call" | custom-call | flops 1207959552 | bytes 3000000 | tf_op jit(solution)/shard_map/attend_near/pallas_call | solution.py:380
  85.3 1.7 %collective-permute-start.13 = (bf16[4,256,128]{2,1,0:T(8,128)(2,1)S(1)}, bf16[4,256,128]{2,1,0:T(8,128)(2,1)S(1)}, u32[]{:S(2)}, u32[]{:S(2)}) collective-permute-start(bf16[4,256,128]{2,1,0:T(8,128)(2,1)S(1)} %get-tuple-element.80), channel_id=1, source_target_pairs={{0,128},{8,136},{16,144},{24,152},{32,160},{40,168},{48,176},{56,1... | collective-permute-start | bytes 786440 | tf_op jit(solution)/shard_map/ppermute | solution.py:618
  87.0 3.3 %attend_far.4 = (f32[1024,128]{1,0:T(8,128)S(1)}, f32[1024,128]{1,0:T(8,128)S(1)}, f32[1024,128]{1,0:T(8,128)S(1)}) custom-call(s32[1]{0:T(128)} %get-tuple-element.48.flag_ref, bf16[1024,128]{1,0:T(8,128)(2,1)S(1)} %get-tuple-element.52.q_ref, bf16[4,256,128]{2,1,0:T(8,128)(2,1)S(1)} %collective-permute-done.14.set_ref, ...), custom_call_target="tpu_custom_call" | custom-call | flops 268435456 | bytes 3000000 | tf_op jit(solution)/shard_map/attend_far/pallas_call | solution.py:533
  90.3 3.3 %attend_far.5 = (f32[1024,128]{1,0:T(8,128)S(1)}, f32[1024,128]{1,0:T(8,128)S(1)}, f32[1024,128]{1,0:T(8,128)S(1)}) custom-call(s32[1]{0:T(128)} %get-tuple-element.48.flag_ref, bf16[1024,128]{1,0:T(8,128)(2,1)S(1)} %get-tuple-element.52.q_ref, bf16[4,256,128]{2,1,0:T(8,128)(2,1)S(1)} %collective-permute-done.15.set_ref, ...), custom_call_target="tpu_custom_call" | custom-call | flops 268435456 | bytes 3000000 | tf_op jit(solution)/shard_map/attend_far/pallas_call | solution.py:533
  94.0 3.3 %attend_far.6 = (f32[1024,128]{1,0:T(8,128)S(1)}, f32[1024,128]{1,0:T(8,128)S(1)}, f32[1024,128]{1,0:T(8,128)S(1)}) custom-call(s32[1]{0:T(128)} %get-tuple-element.48.flag_ref, bf16[1024,128]{1,0:T(8,128)(2,1)S(1)} %get-tuple-element.52.q_ref, bf16[4,256,128]{2,1,0:T(8,128)(2,1)S(1)} %collective-permute-done.13.set_ref, ...), custom_call_target="tpu_custom_call" | custom-call | flops 268435456 | bytes 3000000 | tf_op jit(solution)/shard_map/attend_far/pallas_call | solution.py:533
  97.3 3.5 %attend_far.7 = bf16[8,272,128]{2,1,0:T(8,128)(2,1)S(1)} custom-call(s32[1]{0:T(128)} %get-tuple-element.48.flag_ref, bf16[1024,128]{1,0:T(8,128)(2,1)S(1)} %get-tuple-element.52.q_ref, bf16[4,256,128]{2,1,0:T(8,128)(2,1)S(1)} %collective-permute-done.16.set_ref, f32[1024,128]{1,0:T(8,128)S(1)} %get-tuple-element.66.refs_0_, ...), custom_call_target="tpu_custom_call" | custom-call | flops 268435456 | bytes 3000000 | tf_op jit(solution)/shard_map/attend_far/pallas_call | solution.py:533
  100.8 21.5 %all_to_all.10.back_ref = bf16[8,272,128]{2,1,0:T(8,128)(2,1)S(1)} all-to-all(bf16[8,272,128]{2,1,0:T(8,128)(2,1)S(1)} %attend_far.7), channel_id=1, replica_groups={{0,16,32,48,64,80,96,112},{8,24,40,56,72,88,104,120},{128,144,160,176,1..., dimensions={0} | all-to-all | bytes 1114112 | tf_op jit(solution)/shard_map/all_to_all | solution.py:681
  122.3 1.5 %output.2 = (bf16[384,384]{1,0:T(8,128)(2,1)S(1)}, bf16[384,384]{1,0:T(8,128)(2,1)S(1)}, bf16[384,384]{1,0:T(8,128)(2,1)S(1)}, bf16[384,384]{1,0:T(8,128)(2,1)S(1)}) custom-call(s32[8]{0:T(128)S(1)} %get-tuple-element.43.place_ref, bf16[8,272,128]{2,1,0:T(8,128)(2,1)S(1)} %all_to_all.10.back_ref, bf16[384,3072]{1,0:T(8,128)(2,1)S(1)} %get-tuple-element.69.w_ref), custom_call_target="tpu_custom_call" | custom-call | flops 452984832 | bytes 3000000 | tf_op jit(solution)/shard_map/output/pallas_call | solution.py:592
  123.8 2.3 %collective-permute-start.19 = (bf16[384,384]{1,0:T(8,128)(2,1)S(1)}, bf16[384,384]{1,0:T(8,128)(2,1)S(1)}, u32[]{:S(2)}, u32[]{:S(2)}) collective-permute-start(bf16[384,384]{1,0:T(8,128)(2,1)S(1)} %get-tuple-element.75), channel_id=1, source_target_pairs={{0,2},{1,3},{2,4},{3,5},{4,6},{5,7},{6,0},{7,1},{8,10},{9,11},{10,... | collective-permute-start | bytes 884744 | tf_op jit(solution)/shard_map/ppermute | solution.py:610
  126.1 2.4 %collective-permute-start.22 = (bf16[384,384]{1,0:T(8,128)(2,1)S(1)}, bf16[384,384]{1,0:T(8,128)(2,1)S(1)}, u32[]{:S(2)}, u32[]{:S(2)}) collective-permute-start(bf16[384,384]{1,0:T(8,128)(2,1)S(1)} %get-tuple-element.78), channel_id=1, source_target_pairs={{0,1},{1,0},{2,3},{3,2},{4,5},{5,4},{6,7},{7,6},{8,9},{9,8},{10,11... | collective-permute-start | bytes 884744 | tf_op jit(solution)/shard_map/ppermute | solution.py:614
  128.5 1.6 %output.3 = (bf16[384,384]{1,0:T(8,128)(2,1)S(1)}, bf16[384,384]{1,0:T(8,128)(2,1)S(1)}, bf16[384,384]{1,0:T(8,128)(2,1)S(1)}, bf16[384,384]{1,0:T(8,128)(2,1)S(1)}, bf16[384,384]{1,0:T(8,128)(2,1)S(1)}) custom-call(s32[8]{0:T(128)S(1)} %get-tuple-element.43.place_ref, bf16[384,384]{1,0:T(8,128)(2,1)S(1)} %get-tuple-element.70.attn_ref, ...), custom_call_target="tpu_custom_call" | custom-call | flops 566231040 | bytes 3000000 | tf_op jit(solution)/shard_map/output/pallas_call | solution.py:592
  130.1 3.3 %collective-permute-start.17 = (bf16[384,384]{1,0:T(8,128)(2,1)S(1)}, bf16[384,384]{1,0:T(8,128)(2,1)S(1)}, u32[]{:S(2)}, u32[]{:S(2)}) collective-permute-start(bf16[384,384]{1,0:T(8,128)(2,1)S(1)} %get-tuple-element.72), channel_id=1, source_target_pairs={{0,2},{1,3},{2,4},{3,5},{4,6},{5,7},{6,0},{7,1},{8,10},{9,11},{10,... | collective-permute-start | bytes 884744 | tf_op jit(solution)/shard_map/ppermute | solution.py:610
  133.4 2.2 %collective-permute-done.20 = bf16[384,384]{1,0:T(8,128)(2,1)S(1)} collective-permute-done((bf16[384,384]{1,0:T(8,128)(2,1)S(1)}, bf16[384,384]{1,0:T(8,128)(2,1)S(1)}, u32[]{:S(2)}, u32[]{:S(2)}) %collective-permute-start.20) | collective-permute-done | bytes 294944 | tf_op jit(solution)/shard_map/ppermute | solution.py:610
  135.7 3.5 %collective-permute-start.21 = (bf16[384,384]{1,0:T(8,128)(2,1)S(1)}, bf16[384,384]{1,0:T(8,128)(2,1)S(1)}, u32[]{:S(2)}, u32[]{:S(2)}) collective-permute-start(bf16[384,384]{1,0:T(8,128)(2,1)S(1)} %add_convert_fusion.2), channel_id=1, source_target_pairs={{0,1},{1,0},{2,3},{3,2},{4,5},{5,4},{6,7},{7,6},{8,9},{9,8},{10,11... | collective-permute-start | bytes 884744 | tf_op jit(solution)/shard_map/ppermute | solution.py:614
  139.4 5.6 %collective-permute-done.17 = bf16[384,384]{1,0:T(8,128)(2,1)S(1)} collective-permute-done((bf16[384,384]{1,0:T(8,128)(2,1)S(1)}, bf16[384,384]{1,0:T(8,128)(2,1)S(1)}, u32[]{:S(2)}, u32[]{:S(2)}) %collective-permute-start.17) | collective-permute-done | bytes 294944 | tf_op jit(solution)/shard_map/ppermute | solution.py:610
  145.0 3.4 %collective-permute-done.18 = bf16[384,384]{1,0:T(8,128)(2,1)S(1)} collective-permute-done((bf16[384,384]{1,0:T(8,128)(2,1)S(1)}, bf16[384,384]{1,0:T(8,128)(2,1)S(1)}, u32[]{:S(2)}, u32[]{:S(2)}) %collective-permute-start.18) | collective-permute-done | bytes 294944 | tf_op jit(solution)/shard_map/ppermute | solution.py:610
  (43 shorter events, 6.7 us)
Async XLA Ops:
  3.0 10.3 %collective-permute-start.1 = (bf16[400,384]{1,0:T(8,128)(2,1)S(1)}, bf16[400,384]{1,0:T(8,128)(2,1)S(1)}, u32[]{:S(2)}, u32[]{:S(2)}) collective-permute-start(bf16[400,384]{1,0:T(8,128)(2,1)S(1)} %get-tuple-element.45.refs_0_), channel_id=1, source_target_pairs={{0,6},{1,7},{2,0},{3,1},{4,2},{5,3},{6,4},{7,5},{8,14},{9,15},{10,... | collective-permute-start | bytes 921608 | tf_op jit(solution)/shard_map/ppermute | solution.py:610
  3.9 9.5 %collective-permute-start.2 = (bf16[400,384]{1,0:T(8,128)(2,1)S(1)}, bf16[400,384]{1,0:T(8,128)(2,1)S(1)}, u32[]{:S(2)}, u32[]{:S(2)}) collective-permute-start(bf16[400,384]{1,0:T(8,128)(2,1)S(1)} %get-tuple-element.45.refs_0_), channel_id=1, source_target_pairs={{0,2},{1,3},{2,4},{3,5},{4,6},{5,7},{6,0},{7,1},{8,10},{9,11},{10,... | collective-permute-start | bytes 921608 | tf_op jit(solution)/shard_map/ppermute | solution.py:610
  6.3 10.4 %collective-permute-start = (bf16[400,384]{1,0:T(8,128)(2,1)S(1)}, bf16[400,384]{1,0:T(8,128)(2,1)S(1)}, u32[]{:S(2)}, u32[]{:S(2)}) collective-permute-start(bf16[400,384]{1,0:T(8,128)(2,1)S(1)} %get-tuple-element.45.refs_0_), channel_id=1, source_target_pairs={{0,1},{1,0},{2,3},{3,2},{4,5},{5,4},{6,7},{7,6},{8,9},{9,8},{10,11... | collective-permute-start | bytes 921608 | tf_op jit(solution)/shard_map/ppermute | solution.py:614
  13.3 10.5 %collective-permute-start.6 = (bf16[208,384]{1,0:T(8,128)(2,1)S(1)}, bf16[208,384]{1,0:T(8,128)(2,1)S(1)}, u32[]{:S(2)}, u32[]{:S(2)}) collective-permute-start(bf16[208,384]{1,0:T(8,128)(2,1)S(1)} %slice.23), channel_id=1, source_target_pairs={{0,6},{1,7},{2,0},{3,1},{4,2},{5,3},{6,4},{7,5},{8,14},{9,15},{10,... | collective-permute-start | bytes 479240 | tf_op jit(solution)/shard_map/ppermute | solution.py:610
  13.5 7.2 %collective-permute-start.5 = (bf16[192,384]{1,0:T(8,128)(2,1)S(1)}, bf16[192,384]{1,0:T(8,128)(2,1)S(1)}, u32[]{:S(2)}, u32[]{:S(2)}) collective-permute-start(bf16[192,384]{1,0:T(8,128)(2,1)S(1)} %slice.22), channel_id=1, source_target_pairs={{0,2},{1,3},{2,4},{3,5},{4,6},{5,7},{6,0},{7,1},{8,10},{9,11},{10,... | collective-permute-start | bytes 442376 | tf_op jit(solution)/shard_map/ppermute | solution.py:610
  16.8 11.4 %collective-permute-start.3 = (bf16[400,384]{1,0:T(8,128)(2,1)S(1)}, bf16[400,384]{1,0:T(8,128)(2,1)S(1)}, u32[]{:S(2)}, u32[]{:S(2)}) collective-permute-start(bf16[400,384]{1,0:T(8,128)(2,1)S(1)} %collective-permute-done.refs_1_), channel_id=1, source_target_pairs={{0,6},{1,7},{2,0},{3,1},{4,2},{5,3},{6,4},{7,5},{8,14},{9,15},{10,... | collective-permute-start | bytes 921608 | tf_op jit(solution)/shard_map/ppermute | solution.py:610
  16.8 11.4 %collective-permute-start.4 = (bf16[400,384]{1,0:T(8,128)(2,1)S(1)}, bf16[400,384]{1,0:T(8,128)(2,1)S(1)}, u32[]{:S(2)}, u32[]{:S(2)}) collective-permute-start(bf16[400,384]{1,0:T(8,128)(2,1)S(1)} %collective-permute-done.refs_1_), channel_id=1, source_target_pairs={{0,2},{1,3},{2,4},{3,5},{4,6},{5,7},{6,0},{7,1},{8,10},{9,11},{10,... | collective-permute-start | bytes 921608 | tf_op jit(solution)/shard_map/ppermute | solution.py:610
  20.7 7.5 %collective-permute-start.7 = (bf16[192,384]{1,0:T(8,128)(2,1)S(1)}, bf16[192,384]{1,0:T(8,128)(2,1)S(1)}, u32[]{:S(2)}, u32[]{:S(2)}) collective-permute-start(bf16[192,384]{1,0:T(8,128)(2,1)S(1)} %collective-permute-done.5.refs_6_), channel_id=1, source_target_pairs={{0,1},{1,0},{2,3},{3,2},{4,5},{5,4},{6,7},{7,6},{8,9},{9,8},{10,11... | collective-permute-start | bytes 442376 | tf_op jit(solution)/shard_map/ppermute | solution.py:614
  23.9 6.8 %collective-permute-start.8 = (bf16[208,384]{1,0:T(8,128)(2,1)S(1)}, bf16[208,384]{1,0:T(8,128)(2,1)S(1)}, u32[]{:S(2)}, u32[]{:S(2)}) collective-permute-start(bf16[208,384]{1,0:T(8,128)(2,1)S(1)} %collective-permute-done.6.refs_7_), channel_id=1, source_target_pairs={{0,1},{1,0},{2,3},{3,2},{4,5},{5,4},{6,7},{7,6},{8,9},{9,8},{10,11... | collective-permute-start | bytes 479240 | tf_op jit(solution)/shard_map/ppermute | solution.py:614
  38.5 34.3 %all-to-all-start = ((bf16[8,512,128]{2,1,0:T(8,128)(2,1)}), bf16[8,512,128]{2,1,0:T(8,128)(2,1)S(1)}, u32[]{:S(2)}, u32[]{:S(2)}) async-start(bf16[8,512,128]{2,1,0:T(8,128)(2,1)} %get-tuple-element.49), calls=%async_computation | async-start | bytes 2097152 | tf_op jit(solution)/shard_map/all_to_all | solution.py:681
  47.0 4.9 %collective-permute-start.10 = (bf16[256,128]{1,0:T(8,128)(2,1)S(1)}, bf16[256,128]{1,0:T(8,128)(2,1)S(1)}, u32[]{:S(2)}, u32[]{:S(2)}) collective-permute-start(bf16[256,128]{1,0:T(8,128)(2,1)S(1)} %get-tuple-element.47.refs_0_), channel_id=1, source_target_pairs={{0,128},{8,136},{16,144},{24,152},{32,160},{40,168},{48,176},{56,1... | collective-permute-start | bytes 196616 | tf_op jit(solution)/shard_map/ppermute | solution.py:618
  47.7 4.4 %collective-permute-start.11 = (bf16[256,128]{1,0:T(8,128)(2,1)S(1)}, bf16[256,128]{1,0:T(8,128)(2,1)S(1)}, u32[]{:S(2)}, u32[]{:S(2)}) collective-permute-start(bf16[256,128]{1,0:T(8,128)(2,1)S(1)} %get-tuple-element.47.refs_0_), channel_id=1, source_target_pairs={{0,136},{8,128},{16,152},{24,144},{32,168},{40,160},{48,184},{56,1... | collective-permute-start | bytes 196616 | tf_op jit(solution)/shard_map/ppermute | solution.py:618
  47.7 4.4 %collective-permute-start.9 = (bf16[256,128]{1,0:T(8,128)(2,1)S(1)}, bf16[256,128]{1,0:T(8,128)(2,1)S(1)}, u32[]{:S(2)}, u32[]{:S(2)}) collective-permute-start(bf16[256,128]{1,0:T(8,128)(2,1)S(1)} %get-tuple-element.47.refs_0_), channel_id=1, source_target_pairs={{0,8},{8,0},{16,24},{24,16},{32,40},{40,32},{48,56},{56,48},{64,72... | collective-permute-start | bytes 196616 | tf_op jit(solution)/shard_map/ppermute | solution.py:618
  72.9 3.4 %collective-permute-start.12 = (bf16[8,256,128]{2,1,0:T(8,128)(2,1)S(1)}, bf16[8,256,128]{2,1,0:T(8,128)(2,1)S(1)}, u32[]{:S(2)}, u32[]{:S(2)}) collective-permute-start(bf16[8,256,128]{2,1,0:T(8,128)(2,1)S(1)} %slice.24.own_ref), channel_id=1, source_target_pairs={{0,8},{8,0},{16,24},{24,16},{32,40},{40,32},{48,56},{56,48},{64,72... | collective-permute-start | bytes 1572872 | tf_op jit(solution)/shard_map/ppermute | solution.py:618
  73.2 11.5 %collective-permute-start.14 = (bf16[4,256,128]{2,1,0:T(8,128)(2,1)S(1)}, bf16[4,256,128]{2,1,0:T(8,128)(2,1)S(1)}, u32[]{:S(2)}, u32[]{:S(2)}) collective-permute-start(bf16[4,256,128]{2,1,0:T(8,128)(2,1)S(1)} %get-tuple-element.79), channel_id=1, source_target_pairs={{0,128},{8,136},{16,144},{24,152},{32,160},{40,168},{48,176},{56,1... | collective-permute-start | bytes 786440 | tf_op jit(solution)/shard_map/ppermute | solution.py:618
  84.7 5.6 %collective-permute-start.15 = (bf16[4,256,128]{2,1,0:T(8,128)(2,1)S(1)}, bf16[4,256,128]{2,1,0:T(8,128)(2,1)S(1)}, u32[]{:S(2)}, u32[]{:S(2)}) collective-permute-start(bf16[4,256,128]{2,1,0:T(8,128)(2,1)S(1)} %collective-permute-done.14.set_ref), channel_id=1, source_target_pairs={{0,8},{8,0},{16,24},{24,16},{32,40},{40,32},{48,56},{56,48},{64,72... | collective-permute-start | bytes 786440 | tf_op jit(solution)/shard_map/ppermute | solution.py:618
  85.3 8.5 %collective-permute-start.13 = (bf16[4,256,128]{2,1,0:T(8,128)(2,1)S(1)}, bf16[4,256,128]{2,1,0:T(8,128)(2,1)S(1)}, u32[]{:S(2)}, u32[]{:S(2)}) collective-permute-start(bf16[4,256,128]{2,1,0:T(8,128)(2,1)S(1)} %get-tuple-element.80), channel_id=1, source_target_pairs={{0,128},{8,136},{16,144},{24,152},{32,160},{40,168},{48,176},{56,1... | collective-permute-start | bytes 786440 | tf_op jit(solution)/shard_map/ppermute | solution.py:618
  93.8 3.5 %collective-permute-start.16 = (bf16[4,256,128]{2,1,0:T(8,128)(2,1)S(1)}, bf16[4,256,128]{2,1,0:T(8,128)(2,1)S(1)}, u32[]{:S(2)}, u32[]{:S(2)}) collective-permute-start(bf16[4,256,128]{2,1,0:T(8,128)(2,1)S(1)} %collective-permute-done.13.set_ref), channel_id=1, source_target_pairs={{0,8},{8,0},{16,24},{24,16},{32,40},{40,32},{48,56},{56,48},{64,72... | collective-permute-start | bytes 786440 | tf_op jit(solution)/shard_map/ppermute | solution.py:618
  123.8 9.6 %collective-permute-start.19 = (bf16[384,384]{1,0:T(8,128)(2,1)S(1)}, bf16[384,384]{1,0:T(8,128)(2,1)S(1)}, u32[]{:S(2)}, u32[]{:S(2)}) collective-permute-start(bf16[384,384]{1,0:T(8,128)(2,1)S(1)} %get-tuple-element.75), channel_id=1, source_target_pairs={{0,2},{1,3},{2,4},{3,5},{4,6},{5,7},{6,0},{7,1},{8,10},{9,11},{10,... | collective-permute-start | bytes 884744 | tf_op jit(solution)/shard_map/ppermute | solution.py:610
  126.1 9.5 %collective-permute-start.20 = (bf16[384,384]{1,0:T(8,128)(2,1)S(1)}, bf16[384,384]{1,0:T(8,128)(2,1)S(1)}, u32[]{:S(2)}, u32[]{:S(2)}) collective-permute-start(bf16[384,384]{1,0:T(8,128)(2,1)S(1)} %get-tuple-element.76), channel_id=1, source_target_pairs={{0,6},{1,7},{2,0},{3,1},{4,2},{5,3},{6,4},{7,5},{8,14},{9,15},{10,... | collective-permute-start | bytes 884744 | tf_op jit(solution)/shard_map/ppermute | solution.py:610
  126.1 13.2 %collective-permute-start.22 = (bf16[384,384]{1,0:T(8,128)(2,1)S(1)}, bf16[384,384]{1,0:T(8,128)(2,1)S(1)}, u32[]{:S(2)}, u32[]{:S(2)}) collective-permute-start(bf16[384,384]{1,0:T(8,128)(2,1)S(1)} %get-tuple-element.78), channel_id=1, source_target_pairs={{0,1},{1,0},{2,3},{3,2},{4,5},{5,4},{6,7},{7,6},{8,9},{9,8},{10,11... | collective-permute-start | bytes 884744 | tf_op jit(solution)/shard_map/ppermute | solution.py:614
  130.1 18.5 %copy-start = (bf16[3,128,384]{2,1,0:T(8,128)(2,1)S(1)}, bf16[3,128,384]{2,1,0:T(8,128)(2,1)}, u32[]{:S(2)}) copy-start(bf16[3,128,384]{2,1,0:T(8,128)(2,1)} %video_ref.1) | copy-start | bytes 884740
  130.1 14.9 %collective-permute-start.17 = (bf16[384,384]{1,0:T(8,128)(2,1)S(1)}, bf16[384,384]{1,0:T(8,128)(2,1)S(1)}, u32[]{:S(2)}, u32[]{:S(2)}) collective-permute-start(bf16[384,384]{1,0:T(8,128)(2,1)S(1)} %get-tuple-element.72), channel_id=1, source_target_pairs={{0,2},{1,3},{2,4},{3,5},{4,6},{5,7},{6,0},{7,1},{8,10},{9,11},{10,... | collective-permute-start | bytes 884744 | tf_op jit(solution)/shard_map/ppermute | solution.py:610
  133.4 15.0 %collective-permute-start.18 = (bf16[384,384]{1,0:T(8,128)(2,1)S(1)}, bf16[384,384]{1,0:T(8,128)(2,1)S(1)}, u32[]{:S(2)}, u32[]{:S(2)}) collective-permute-start(bf16[384,384]{1,0:T(8,128)(2,1)S(1)} %get-tuple-element.73), channel_id=1, source_target_pairs={{0,6},{1,7},{2,0},{3,1},{4,2},{5,3},{6,4},{7,5},{8,14},{9,15},{10,... | collective-permute-start | bytes 884744 | tf_op jit(solution)/shard_map/ppermute | solution.py:610
  135.7 12.7 %collective-permute-start.21 = (bf16[384,384]{1,0:T(8,128)(2,1)S(1)}, bf16[384,384]{1,0:T(8,128)(2,1)S(1)}, u32[]{:S(2)}, u32[]{:S(2)}) collective-permute-start(bf16[384,384]{1,0:T(8,128)(2,1)S(1)} %add_convert_fusion.2), channel_id=1, source_target_pairs={{0,1},{1,0},{2,3},{3,2},{4,5},{5,4},{6,7},{7,6},{8,9},{9,8},{10,11... | collective-permute-start | bytes 884744 | tf_op jit(solution)/shard_map/ppermute | solution.py:614
  139.3 9.1 %collective-permute-start.23 = (bf16[384,384]{1,0:T(8,128)(2,1)S(1)}, bf16[384,384]{1,0:T(8,128)(2,1)S(1)}, u32[]{:S(2)}, u32[]{:S(2)}) collective-permute-start(bf16[384,384]{1,0:T(8,128)(2,1)S(1)} %add_convert_fusion.1), channel_id=1, source_target_pairs={{0,4},{1,5},{2,6},{3,7},{4,0},{5,1},{6,2},{7,3},{8,12},{9,13},{10,... | collective-permute-start | bytes 884744 | tf_op jit(solution)/shard_map/ppermute | solution.py:610

commit v12 on v8

--- a/solution.py
+++ b/solution.py
@@ -305,7 +305,7 @@
         mixed += jnp.dot(weights.astype(jnp.bfloat16), values, preferred_element_type=jnp.float32)
         return total, mixed
 
-    zeros = jnp.zeros((TILE, 128), jnp.float32)
+    zeros = jnp.zeros((q.shape[0], 128), jnp.float32)
 
     @pl.when(flag_ref[0] == 1)
     def _():
@@ -322,7 +322,7 @@
 
     @pl.when(flag_ref[0] != 1)
     def _():
-        top = jnp.full((TILE, 128), -jnp.inf, jnp.float32)
+        top = jnp.full((q.shape[0], 128), -jnp.inf, jnp.float32)
         column = 0
         for keys, _, valid in pieces:
             if valid is None:
@@ -340,7 +340,7 @@
             weights = jnp.exp2(score_ref[:, column:stop] * EXP_SCALE - top)
             total, mixed = add_up(weights, values, total, mixed)
             column = stop
-        top_ref[...] = jnp.broadcast_to(top, (TILE, 128))
+        top_ref[...] = jnp.broadcast_to(top, (q.shape[0], 128))
         total_ref[...] = total
         mixed_ref[...] = mixed
 
@@ -505,7 +505,7 @@
 def attend_far_kernel(finish, flag_ref, q_ref, set_ref, *refs):
     mixed_in, total_in, top_in, *refs = refs
     score_ref, top_ref, total_ref, mixed_ref = refs[-4:]
-    here = tile_rows()
+    here = slice(None)
     before = top_in[here, 0:1]
     gather_rows(
         flag_ref, q_ref[here, :], [set_piece(set_ref)], before, score_ref,
@@ -517,9 +517,8 @@
     if finish:
         last_ref, out_ref = refs[:2]
         result = (mixed / jnp.sum(total, axis=1, keepdims=True)).astype(jnp.bfloat16)
-        frames = pl.ds(pl.program_id(0) * QUAD, QUAD)
-        out_ref[frames, 0:TOK, :] = result.reshape(QUAD, TOK, HD)
-        out_ref[frames, TOK:RETURN, :] = last_ref[frames]
+        out_ref[:, 0:TOK, :] = result.reshape(RING, TOK, HD)
+        out_ref[:, TOK:RETURN, :] = last_ref[...]
     else:
         mixed_out, total_out, top_out = refs[:3]
         mixed_out[here, :] = mixed
@@ -535,11 +534,11 @@
         out_shape=pltpu.VMEM((RING, RETURN, HD), jnp.bfloat16) if finish else STATE,
         grid_spec=pltpu.PrefetchScalarGridSpec(
             num_scalar_prefetch=1,
-            grid=(SET // TILE,),
+            grid=(1,),
             in_specs=[IN_VMEM] * len(operands),
             out_specs=IN_VMEM if finish else (IN_VMEM,) * 3,
-            scratch_shapes=[pltpu.VMEM((TILE, SET), jnp.float32)]
-            + [pltpu.VMEM((TILE, 128), jnp.float32)] * 3,
+            scratch_shapes=[pltpu.VMEM((SET, SET), jnp.float32)]
+            + [pltpu.VMEM((SET, 128), jnp.float32)] * 3,
         ),
         compiler_params=pltpu.CompilerParams(vmem_limit_bytes=16 * MIB),
         cost_estimate=pl.CostEstimate(

time: 145 us -> 144 us (level)
  transfers between devices with their start and end apart: 23 -> 23, of which waited for: 12 -> 12; matrix products, arithmetic and copies ran while one was open for 1% -> 1% of each run, Pallas kernels for 14% -> 13%
where the time goes in v12:
time: 144 us
  waiting for transfers between devices  46 us (32%)
  starting transfers between devices  37.9 us (26%)
  Pallas kernels  35.3 us (25%)
  blocking collectives  21.5 us (15%)
  other arithmetic  2.23 us (2%)
    all_to_all x1, blocking collectives, over_rings(): return lax.all_to_all(x, 'frame', 0, 0, axis_index_groups=rings, tiled=True)  21.5 us
    all_to_all x1, waiting for transfers between devices, over_rings(): return lax.all_to_all(x, 'frame', 0, 0, axis_index_groups=rings, tiled=True)  18.6 us
    ppermute x11, waiting for transfers between devices, head_move(): lax.ppermute(x, 'head', [(i, (i + step) % HEAD_AXIS) for i in range(HEAD_...  16.3 us
    ppermute x11, starting transfers between devices, head_move(): lax.ppermute(x, 'head', [(i, (i + step) % HEAD_AXIS) for i in range(HEAD_...  15.4 us
    ppermute x5, starting transfers between devices, head_partner(): return lax.ppermute(x, 'head', [(i, i ^ 1) for i in range(HEAD_AXIS)])  11.5 us
    all_to_all x1, starting transfers between devices, over_rings(): return lax.all_to_all(x, 'frame', 0, 0, axis_index_groups=rings, tiled=True)  8.48 us
    pallas_call x2, Pallas kernels, attend_far(): pl.pallas_call(functools.partial(attend_far_kernel, finish), out_shape=pl...  8.41 us
    pallas_call x1, Pallas kernels, attend_near(): pl.pallas_call(attend_near_kernel, out_shape=STATE + (pltpu.VMEM((SET, HD...  8.37 us
  transfers between devices with their start and end apart: 23, of which 12 were waited for; matrix products, arithmetic and copies ran while one was open for 1% of the time, Pallas kernels for 13%

profile of v12, /device:TPU:6, one launch (start us, length us, event | category | flops | bytes accessed | tf_op | source)
XLA Modules:
  0.0 143.9 jit_solution(1435314234027778145)
XLA Ops:
  0.7 2.4 %prep.1 = (bf16[400,384]{1,0:T(8,128)(2,1)S(1)}, f32[1,384]{1,0:T(1,128)S(1)}, f32[2,128]{1,0:T(2,128)S(1)}, s32[8]{0:T(128)S(1)}, s32[5]{0:T(128)S(1)}) custom-call(s32[1]{0:T(128)} %bitcast.frame_ref, s32[1]{0:T(128)} %bitcast.1.head_ref, s32[1]{0:T(128)S(6)} %copy.13.shift_ref, s32[32]{0:T(128)} %ids_ref.1, s32[3]{0:T(128)} %lengths_ref.1, ...), custom_call_target="tpu_custom_call" | custom-call | tf_op jit(solution)/shard_map/prep/pallas_call | solution.py:110
  3.9 2.4 %collective-permute-start.2 = (bf16[400,384]{1,0:T(8,128)(2,1)S(1)}, bf16[400,384]{1,0:T(8,128)(2,1)S(1)}, u32[]{:S(2)}, u32[]{:S(2)}) collective-permute-start(bf16[400,384]{1,0:T(8,128)(2,1)S(1)} %get-tuple-element.38.refs_0_), channel_id=1, source_target_pairs={{0,2},{1,3},{2,4},{3,5},{4,6},{5,7},{6,0},{7,1},{8,10},{9,11},{10,... | collective-permute-start | bytes 921608 | tf_op jit(solution)/shard_map/ppermute | solution.py:609
  6.3 3.2 %collective-permute-start = (bf16[400,384]{1,0:T(8,128)(2,1)S(1)}, bf16[400,384]{1,0:T(8,128)(2,1)S(1)}, u32[]{:S(2)}, u32[]{:S(2)}) collective-permute-start(bf16[400,384]{1,0:T(8,128)(2,1)S(1)} %get-tuple-element.38.refs_0_), channel_id=1, source_target_pairs={{0,1},{1,0},{2,3},{3,2},{4,5},{5,4},{6,7},{7,6},{8,9},{9,8},{10,11... | collective-permute-start | bytes 921608 | tf_op jit(solution)/shard_map/ppermute | solution.py:613
  9.5 3.8 %collective-permute-done.1.refs_2_ = bf16[400,384]{1,0:T(8,128)(2,1)S(1)} collective-permute-done((bf16[400,384]{1,0:T(8,128)(2,1)S(1)}, bf16[400,384]{1,0:T(8,128)(2,1)S(1)}, u32[]{:S(2)}, u32[]{:S(2)}) %collective-permute-start.1) | collective-permute-done | bytes 307232 | tf_op jit(solution)/shard_map/ppermute | solution.py:609
  13.5 3.3 %collective-permute-start.5 = (bf16[192,384]{1,0:T(8,128)(2,1)S(1)}, bf16[192,384]{1,0:T(8,128)(2,1)S(1)}, u32[]{:S(2)}, u32[]{:S(2)}) collective-permute-start(bf16[192,384]{1,0:T(8,128)(2,1)S(1)} %slice.12), channel_id=1, source_target_pairs={{0,2},{1,3},{2,4},{3,5},{4,6},{5,7},{6,0},{7,1},{8,10},{9,11},{10,... | collective-permute-start | bytes 442376 | tf_op jit(solution)/shard_map/ppermute | solution.py:609
  16.8 3.2 %collective-permute-start.4 = (bf16[400,384]{1,0:T(8,128)(2,1)S(1)}, bf16[400,384]{1,0:T(8,128)(2,1)S(1)}, u32[]{:S(2)}, u32[]{:S(2)}) collective-permute-start(bf16[400,384]{1,0:T(8,128)(2,1)S(1)} %collective-permute-done.refs_1_), channel_id=1, source_target_pairs={{0,2},{1,3},{2,4},{3,5},{4,6},{5,7},{6,0},{7,1},{8,10},{9,11},{10,... | collective-permute-start | bytes 921608 | tf_op jit(solution)/shard_map/ppermute | solution.py:609
  20.7 3.2 %collective-permute-start.7 = (bf16[192,384]{1,0:T(8,128)(2,1)S(1)}, bf16[192,384]{1,0:T(8,128)(2,1)S(1)}, u32[]{:S(2)}, u32[]{:S(2)}) collective-permute-start(bf16[192,384]{1,0:T(8,128)(2,1)S(1)} %collective-permute-done.5.refs_6_), channel_id=1, source_target_pairs={{0,1},{1,0},{2,3},{3,2},{4,5},{5,4},{6,7},{7,6},{8,9},{9,8},{10,11... | collective-permute-start | bytes 442376 | tf_op jit(solution)/shard_map/ppermute | solution.py:613
  24.2 1.0 sine_multiply_fusion
  25.3 2.9 %collective-permute-done.7.refs_8_ = bf16[192,384]{1,0:T(8,128)(2,1)S(1)} collective-permute-done((bf16[192,384]{1,0:T(8,128)(2,1)S(1)}, bf16[192,384]{1,0:T(8,128)(2,1)S(1)}, u32[]{:S(2)}, u32[]{:S(2)}) %collective-permute-start.7) | collective-permute-done | bytes 147488 | tf_op jit(solution)/shard_map/ppermute | solution.py:613
  28.2 2.5 %collective-permute-done.8.refs_9_ = bf16[208,384]{1,0:T(8,128)(2,1)S(1)} collective-permute-done((bf16[208,384]{1,0:T(8,128)(2,1)S(1)}, bf16[208,384]{1,0:T(8,128)(2,1)S(1)}, u32[]{:S(2)}, u32[]{:S(2)}) %collective-permute-start.8) | collective-permute-done | bytes 159776 | tf_op jit(solution)/shard_map/ppermute | solution.py:613
  30.7 7.9 %project.1 = (bf16[8,512,128]{2,1,0:T(8,128)(2,1)}, bf16[256,128]{1,0:T(8,128)(2,1)S(1)}) custom-call(s32[8]{0:T(128)S(1)} %get-tuple-element.36.place_ref, bf16[400,384]{1,0:T(8,128)(2,1)S(1)} %get-tuple-element.38.refs_0_, bf16[400,384]{1,0:T(8,128)(2,1)S(1)} %collective-permute-done.refs_1_, bf16[400,384]{1,0:T(8,128)(2,1)S(1)} %collective-permute-done.1.refs_2_, ...), custom_call_target="tpu_custom_call" | custom-call | flops 2717908992 | bytes 12000000 | tf_op jit(solution)/shard_map/project/pallas_call | solution.py:216
  38.6 8.5 %all-to-all-start = ((bf16[8,512,128]{2,1,0:T(8,128)(2,1)}), bf16[8,512,128]{2,1,0:T(8,128)(2,1)S(1)}, u32[]{:S(2)}, u32[]{:S(2)}) async-start(bf16[8,512,128]{2,1,0:T(8,128)(2,1)} %get-tuple-element.42), calls=%async_computation | async-start | bytes 2097152 | tf_op jit(solution)/shard_map/all_to_all | solution.py:680
  47.7 1.5 %collective-permute-start.9 = (bf16[256,128]{1,0:T(8,128)(2,1)S(1)}, bf16[256,128]{1,0:T(8,128)(2,1)S(1)}, u32[]{:S(2)}, u32[]{:S(2)}) collective-permute-start(bf16[256,128]{1,0:T(8,128)(2,1)S(1)} %get-tuple-element.40.refs_0_), channel_id=1, source_target_pairs={{0,8},{8,0},{16,24},{24,16},{32,40},{40,32},{48,56},{56,48},{64,72... | collective-permute-start | bytes 196616 | tf_op jit(solution)/shard_map/ppermute | solution.py:617
  49.2 2.7 %collective-permute-done.10.refs_2_ = bf16[256,128]{1,0:T(8,128)(2,1)S(1)} collective-permute-done((bf16[256,128]{1,0:T(8,128)(2,1)S(1)}, bf16[256,128]{1,0:T(8,128)(2,1)S(1)}, u32[]{:S(2)}, u32[]{:S(2)}) %collective-permute-start.10) | collective-permute-done | bytes 65568 | tf_op jit(solution)/shard_map/ppermute | solution.py:617
  52.1 2.1 %lay_last.1 = (bf16[640,128]{1,0:T(8,128)(2,1)S(1)}, bf16[640,256]{1,0:T(8,128)(2,1)S(1)}, s32[1]{0:T(128)}) custom-call(s32[5]{0:T(128)S(1)} %get-tuple-element.37.where_ref, bf16[256,128]{1,0:T(8,128)(2,1)S(1)} %get-tuple-element.40.refs_0_, bf16[256,128]{1,0:T(8,128)(2,1)S(1)} %collective-permute-done.9.refs_1_, ...), custom_call_target="tpu_custom_call" | custom-call | flops 10000000000 | bytes 10000000 | tf_op jit(solution)/shard_map/lay_last/pallas_call | solution.py:431
  54.2 18.6 %all-to-all-done.q_ref = bf16[8,512,128]{2,1,0:T(8,128)(2,1)S(1)} async-done(((bf16[8,512,128]{2,1,0:T(8,128)(2,1)}), bf16[8,512,128]{2,1,0:T(8,128)(2,1)S(1)}, u32[]{:S(2)}, u32[]{:S(2)}) %all-to-all-start) | async-done | bytes 1048608 | tf_op jit(solution)/shard_map/all_to_all | solution.py:680
  73.2 3.0 %attend_last.1.refs_3_ = bf16[8,144,128]{2,1,0:T(8,128)(2,1)S(1)} custom-call(s32[5]{0:T(128)S(1)} %get-tuple-element.37.where_ref, bf16[8,512,128]{2,1,0:T(8,128)(2,1)S(1)} %all-to-all-done.q_ref, bf16[640,128]{1,0:T(8,128)(2,1)S(1)} %get-tuple-element.47.keys_ref, bf16[640,256]{1,0:T(8,128)(2,1)S(1)} %get-tuple-element.48.value_ref), custom_call_target="tpu_custom_call" | custom-call | flops 335544320 | bytes 1000000 | tf_op jit(solution)/shard_map/attend_last/pallas_call | solution.py:483
  76.3 8.4 %attend_near.1 = (f32[1024,128]{1,0:T(8,128)S(1)}, f32[1024,128]{1,0:T(8,128)S(1)}, f32[1024,128]{1,0:T(8,128)S(1)}, bf16[1024,128]{1,0:T(8,128)(2,1)S(1)}, bf16[384,3072]{1,0:T(8,128)(2,1)S(1)}) custom-call(s32[5]{0:T(128)S(1)} %get-tuple-element.37.where_ref, s32[1]{0:T(128)} %get-tuple-element.41.flag_ref, bf16[8,512,128]{2,1,0:T(8,128)(2,1)S(1)} %all-to-all-done.q_ref, ...), custom_call_target="tpu_custom_call" | custom-call | flops 1207959552 | bytes 3000000 | tf_op jit(solution)/shard_map/attend_near/pallas_call | solution.py:380
  84.6 2.8 %collective-permute-done.13.set_ref = bf16[8,256,128]{2,1,0:T(8,128)(2,1)S(1)} collective-permute-done((bf16[8,256,128]{2,1,0:T(8,128)(2,1)S(1)}, bf16[8,256,128]{2,1,0:T(8,128)(2,1)S(1)}, u32[]{:S(2)}, u32[]{:S(2)}) %collective-permute-start.13) | collective-permute-done | bytes 524320 | tf_op jit(solution)/shard_map/ppermute | solution.py:617
  87.5 4.0 %attend_far.2 = (f32[1024,128]{1,0:T(8,128)S(1)}, f32[1024,128]{1,0:T(8,128)S(1)}, f32[1024,128]{1,0:T(8,128)S(1)}) custom-call(s32[1]{0:T(128)} %get-tuple-element.41.flag_ref, bf16[1024,128]{1,0:T(8,128)(2,1)S(1)} %get-tuple-element.45.q_ref, bf16[8,256,128]{2,1,0:T(8,128)(2,1)S(1)} %collective-permute-done.13.set_ref, ...), custom_call_target="tpu_custom_call" | custom-call | flops 536870912 | bytes 3000000 | tf_op jit(solution)/shard_map/attend_far/pallas_call | solution.py:532
  91.5 4.4 %attend_far.3 = bf16[8,272,128]{2,1,0:T(8,128)(2,1)S(1)} custom-call(s32[1]{0:T(128)} %get-tuple-element.41.flag_ref, bf16[1024,128]{1,0:T(8,128)(2,1)S(1)} %get-tuple-element.45.q_ref, bf16[8,256,128]{2,1,0:T(8,128)(2,1)S(1)} %collective-permute-done.14.set_ref, f32[1024,128]{1,0:T(8,128)S(1)} %get-tuple-element.52.refs_0_, ...), custom_call_target="tpu_custom_call" | custom-call | flops 536870912 | bytes 3000000 | tf_op jit(solution)/shard_map/attend_far/pallas_call | solution.py:532
  95.9 21.5 %all_to_all.10.back_ref = bf16[8,272,128]{2,1,0:T(8,128)(2,1)S(1)} all-to-all(bf16[8,272,128]{2,1,0:T(8,128)(2,1)S(1)} %attend_far.3), channel_id=1, replica_groups={{0,16,32,48,64,80,96,112},{8,24,40,56,72,88,104,120},{128,144,160,176,1..., dimensions={0} | all-to-all | bytes 1114112 | tf_op jit(solution)/shard_map/all_to_all | solution.py:680
  117.5 1.5 %output.2 = (bf16[384,384]{1,0:T(8,128)(2,1)S(1)}, bf16[384,384]{1,0:T(8,128)(2,1)S(1)}, bf16[384,384]{1,0:T(8,128)(2,1)S(1)}, bf16[384,384]{1,0:T(8,128)(2,1)S(1)}) custom-call(s32[8]{0:T(128)S(1)} %get-tuple-element.36.place_ref, bf16[8,272,128]{2,1,0:T(8,128)(2,1)S(1)} %all_to_all.10.back_ref, bf16[384,3072]{1,0:T(8,128)(2,1)S(1)} %get-tuple-element.55.w_ref), custom_call_target="tpu_custom_call" | custom-call | flops 452984832 | bytes 3000000 | tf_op jit(solution)/shard_map/output/pallas_call | solution.py:591
  119.0 1.7 %collective-permute-start.17 = (bf16[384,384]{1,0:T(8,128)(2,1)S(1)}, bf16[384,384]{1,0:T(8,128)(2,1)S(1)}, u32[]{:S(2)}, u32[]{:S(2)}) collective-permute-start(bf16[384,384]{1,0:T(8,128)(2,1)S(1)} %get-tuple-element.61), channel_id=1, source_target_pairs={{0,2},{1,3},{2,4},{3,5},{4,6},{5,7},{6,0},{7,1},{8,10},{9,11},{10,... | collective-permute-start | bytes 884744 | tf_op jit(solution)/shard_map/ppermute | solution.py:609
  121.1 1.8 %collective-permute-start.20 = (bf16[384,384]{1,0:T(8,128)(2,1)S(1)}, bf16[384,384]{1,0:T(8,128)(2,1)S(1)}, u32[]{:S(2)}, u32[]{:S(2)}) collective-permute-start(bf16[384,384]{1,0:T(8,128)(2,1)S(1)} %get-tuple-element.64), channel_id=1, source_target_pairs={{0,1},{1,0},{2,3},{3,2},{4,5},{5,4},{6,7},{7,6},{8,9},{9,8},{10,11... | collective-permute-start | bytes 884744 | tf_op jit(solution)/shard_map/ppermute | solution.py:613
  122.9 1.6 %output.3 = (bf16[384,384]{1,0:T(8,128)(2,1)S(1)}, bf16[384,384]{1,0:T(8,128)(2,1)S(1)}, bf16[384,384]{1,0:T(8,128)(2,1)S(1)}, bf16[384,384]{1,0:T(8,128)(2,1)S(1)}, bf16[384,384]{1,0:T(8,128)(2,1)S(1)}) custom-call(s32[8]{0:T(128)S(1)} %get-tuple-element.36.place_ref, bf16[384,384]{1,0:T(8,128)(2,1)S(1)} %get-tuple-element.56.attn_ref, ...), custom_call_target="tpu_custom_call" | custom-call | flops 566231040 | bytes 3000000 | tf_op jit(solution)/shard_map/output/pallas_call | solution.py:591
  124.5 3.3 %collective-permute-start.15 = (bf16[384,384]{1,0:T(8,128)(2,1)S(1)}, bf16[384,384]{1,0:T(8,128)(2,1)S(1)}, u32[]{:S(2)}, u32[]{:S(2)}) collective-permute-start(bf16[384,384]{1,0:T(8,128)(2,1)S(1)} %get-tuple-element.58), channel_id=1, source_target_pairs={{0,2},{1,3},{2,4},{3,5},{4,6},{5,7},{6,0},{7,1},{8,10},{9,11},{10,... | collective-permute-start | bytes 884744 | tf_op jit(solution)/shard_map/ppermute | solution.py:609
  127.8 1.2 collective-permute-done.17
  129.0 1.3 collective-permute-done.18
  130.4 3.0 %collective-permute-start.19 = (bf16[384,384]{1,0:T(8,128)(2,1)S(1)}, bf16[384,384]{1,0:T(8,128)(2,1)S(1)}, u32[]{:S(2)}, u32[]{:S(2)}) collective-permute-start(bf16[384,384]{1,0:T(8,128)(2,1)S(1)} %add_convert_fusion.2), channel_id=1, source_target_pairs={{0,1},{1,0},{2,3},{3,2},{4,5},{5,4},{6,7},{7,6},{8,9},{9,8},{10,11... | collective-permute-start | bytes 884744 | tf_op jit(solution)/shard_map/ppermute | solution.py:613
  133.6 1.0 collective-permute-done.15
  134.6 8.3 %collective-permute-done.16 = bf16[384,384]{1,0:T(8,128)(2,1)S(1)} collective-permute-done((bf16[384,384]{1,0:T(8,128)(2,1)S(1)}, bf16[384,384]{1,0:T(8,128)(2,1)S(1)}, u32[]{:S(2)}, u32[]{:S(2)}) %collective-permute-start.16) | collective-permute-done | bytes 294944 | tf_op jit(solution)/shard_map/ppermute | solution.py:609
  (36 shorter events, 5.0 us)
Async XLA Ops:
  3.0 10.3 %collective-permute-start.1 = (bf16[400,384]{1,0:T(8,128)(2,1)S(1)}, bf16[400,384]{1,0:T(8,128)(2,1)S(1)}, u32[]{:S(2)}, u32[]{:S(2)}) collective-permute-start(bf16[400,384]{1,0:T(8,128)(2,1)S(1)} %get-tuple-element.38.refs_0_), channel_id=1, source_target_pairs={{0,6},{1,7},{2,0},{3,1},{4,2},{5,3},{6,4},{7,5},{8,14},{9,15},{10,... | collective-permute-start | bytes 921608 | tf_op jit(solution)/shard_map/ppermute | solution.py:609
  3.9 9.5 %collective-permute-start.2 = (bf16[400,384]{1,0:T(8,128)(2,1)S(1)}, bf16[400,384]{1,0:T(8,128)(2,1)S(1)}, u32[]{:S(2)}, u32[]{:S(2)}) collective-permute-start(bf16[400,384]{1,0:T(8,128)(2,1)S(1)} %get-tuple-element.38.refs_0_), channel_id=1, source_target_pairs={{0,2},{1,3},{2,4},{3,5},{4,6},{5,7},{6,0},{7,1},{8,10},{9,11},{10,... | collective-permute-start | bytes 921608 | tf_op jit(solution)/shard_map/ppermute | solution.py:609
  6.3 10.4 %collective-permute-start = (bf16[400,384]{1,0:T(8,128)(2,1)S(1)}, bf16[400,384]{1,0:T(8,128)(2,1)S(1)}, u32[]{:S(2)}, u32[]{:S(2)}) collective-permute-start(bf16[400,384]{1,0:T(8,128)(2,1)S(1)} %get-tuple-element.38.refs_0_), channel_id=1, source_target_pairs={{0,1},{1,0},{2,3},{3,2},{4,5},{5,4},{6,7},{7,6},{8,9},{9,8},{10,11... | collective-permute-start | bytes 921608 | tf_op jit(solution)/shard_map/ppermute | solution.py:613
  13.3 10.5 %collective-permute-start.6 = (bf16[208,384]{1,0:T(8,128)(2,1)S(1)}, bf16[208,384]{1,0:T(8,128)(2,1)S(1)}, u32[]{:S(2)}, u32[]{:S(2)}) collective-permute-start(bf16[208,384]{1,0:T(8,128)(2,1)S(1)} %slice.13), channel_id=1, source_target_pairs={{0,6},{1,7},{2,0},{3,1},{4,2},{5,3},{6,4},{7,5},{8,14},{9,15},{10,... | collective-permute-start | bytes 479240 | tf_op jit(solution)/shard_map/ppermute | solution.py:609
  13.5 7.2 %collective-permute-start.5 = (bf16[192,384]{1,0:T(8,128)(2,1)S(1)}, bf16[192,384]{1,0:T(8,128)(2,1)S(1)}, u32[]{:S(2)}, u32[]{:S(2)}) collective-permute-start(bf16[192,384]{1,0:T(8,128)(2,1)S(1)} %slice.12), channel_id=1, source_target_pairs={{0,2},{1,3},{2,4},{3,5},{4,6},{5,7},{6,0},{7,1},{8,10},{9,11},{10,... | collective-permute-start | bytes 442376 | tf_op jit(solution)/shard_map/ppermute | solution.py:609
  16.8 11.4 %collective-permute-start.3 = (bf16[400,384]{1,0:T(8,128)(2,1)S(1)}, bf16[400,384]{1,0:T(8,128)(2,1)S(1)}, u32[]{:S(2)}, u32[]{:S(2)}) collective-permute-start(bf16[400,384]{1,0:T(8,128)(2,1)S(1)} %collective-permute-done.refs_1_), channel_id=1, source_target_pairs={{0,6},{1,7},{2,0},{3,1},{4,2},{5,3},{6,4},{7,5},{8,14},{9,15},{10,... | collective-permute-start | bytes 921608 | tf_op jit(solution)/shard_map/ppermute | solution.py:609
  16.8 11.4 %collective-permute-start.4 = (bf16[400,384]{1,0:T(8,128)(2,1)S(1)}, bf16[400,384]{1,0:T(8,128)(2,1)S(1)}, u32[]{:S(2)}, u32[]{:S(2)}) collective-permute-start(bf16[400,384]{1,0:T(8,128)(2,1)S(1)} %collective-permute-done.refs_1_), channel_id=1, source_target_pairs={{0,2},{1,3},{2,4},{3,5},{4,6},{5,7},{6,0},{7,1},{8,10},{9,11},{10,... | collective-permute-start | bytes 921608 | tf_op jit(solution)/shard_map/ppermute | solution.py:609
  20.7 7.5 %collective-permute-start.7 = (bf16[192,384]{1,0:T(8,128)(2,1)S(1)}, bf16[192,384]{1,0:T(8,128)(2,1)S(1)}, u32[]{:S(2)}, u32[]{:S(2)}) collective-permute-start(bf16[192,384]{1,0:T(8,128)(2,1)S(1)} %collective-permute-done.5.refs_6_), channel_id=1, source_target_pairs={{0,1},{1,0},{2,3},{3,2},{4,5},{5,4},{6,7},{7,6},{8,9},{9,8},{10,11... | collective-permute-start | bytes 442376 | tf_op jit(solution)/shard_map/ppermute | solution.py:613
  23.9 6.8 %collective-permute-start.8 = (bf16[208,384]{1,0:T(8,128)(2,1)S(1)}, bf16[208,384]{1,0:T(8,128)(2,1)S(1)}, u32[]{:S(2)}, u32[]{:S(2)}) collective-permute-start(bf16[208,384]{1,0:T(8,128)(2,1)S(1)} %collective-permute-done.6.refs_7_), channel_id=1, source_target_pairs={{0,1},{1,0},{2,3},{3,2},{4,5},{5,4},{6,7},{7,6},{8,9},{9,8},{10,11... | collective-permute-start | bytes 479240 | tf_op jit(solution)/shard_map/ppermute | solution.py:613
  38.6 34.3 %all-to-all-start = ((bf16[8,512,128]{2,1,0:T(8,128)(2,1)}), bf16[8,512,128]{2,1,0:T(8,128)(2,1)S(1)}, u32[]{:S(2)}, u32[]{:S(2)}) async-start(bf16[8,512,128]{2,1,0:T(8,128)(2,1)} %get-tuple-element.42), calls=%async_computation | async-start | bytes 2097152 | tf_op jit(solution)/shard_map/all_to_all | solution.py:680
  47.0 4.9 %collective-permute-start.10 = (bf16[256,128]{1,0:T(8,128)(2,1)S(1)}, bf16[256,128]{1,0:T(8,128)(2,1)S(1)}, u32[]{:S(2)}, u32[]{:S(2)}) collective-permute-start(bf16[256,128]{1,0:T(8,128)(2,1)S(1)} %get-tuple-element.40.refs_0_), channel_id=1, source_target_pairs={{0,128},{8,136},{16,144},{24,152},{32,160},{40,168},{48,176},{56,1... | collective-permute-start | bytes 196616 | tf_op jit(solution)/shard_map/ppermute | solution.py:617
  47.7 4.4 %collective-permute-start.11 = (bf16[256,128]{1,0:T(8,128)(2,1)S(1)}, bf16[256,128]{1,0:T(8,128)(2,1)S(1)}, u32[]{:S(2)}, u32[]{:S(2)}) collective-permute-start(bf16[256,128]{1,0:T(8,128)(2,1)S(1)} %get-tuple-element.40.refs_0_), channel_id=1, source_target_pairs={{0,136},{8,128},{16,152},{24,144},{32,168},{40,160},{48,184},{56,1... | collective-permute-start | bytes 196616 | tf_op jit(solution)/shard_map/ppermute | solution.py:617
  47.7 4.4 %collective-permute-start.9 = (bf16[256,128]{1,0:T(8,128)(2,1)S(1)}, bf16[256,128]{1,0:T(8,128)(2,1)S(1)}, u32[]{:S(2)}, u32[]{:S(2)}) collective-permute-start(bf16[256,128]{1,0:T(8,128)(2,1)S(1)} %get-tuple-element.40.refs_0_), channel_id=1, source_target_pairs={{0,8},{8,0},{16,24},{24,16},{32,40},{40,32},{48,56},{56,48},{64,72... | collective-permute-start | bytes 196616 | tf_op jit(solution)/shard_map/ppermute | solution.py:617
  72.9 3.4 %collective-permute-start.12 = (bf16[8,256,128]{2,1,0:T(8,128)(2,1)S(1)}, bf16[8,256,128]{2,1,0:T(8,128)(2,1)S(1)}, u32[]{:S(2)}, u32[]{:S(2)}) collective-permute-start(bf16[8,256,128]{2,1,0:T(8,128)(2,1)S(1)} %slice.14.own_ref), channel_id=1, source_target_pairs={{0,8},{8,0},{16,24},{24,16},{32,40},{40,32},{48,56},{56,48},{64,72... | collective-permute-start | bytes 1572872 | tf_op jit(solution)/shard_map/ppermute | solution.py:617
  73.1 14.3 %collective-permute-start.13 = (bf16[8,256,128]{2,1,0:T(8,128)(2,1)S(1)}, bf16[8,256,128]{2,1,0:T(8,128)(2,1)S(1)}, u32[]{:S(2)}, u32[]{:S(2)}) collective-permute-start(bf16[8,256,128]{2,1,0:T(8,128)(2,1)S(1)} %slice.14.own_ref), channel_id=1, source_target_pairs={{0,128},{8,136},{16,144},{24,152},{32,160},{40,168},{48,176},{56,1... | collective-permute-start | bytes 1572872 | tf_op jit(solution)/shard_map/ppermute | solution.py:617
  87.5 4.0 %collective-permute-start.14 = (bf16[8,256,128]{2,1,0:T(8,128)(2,1)S(1)}, bf16[8,256,128]{2,1,0:T(8,128)(2,1)S(1)}, u32[]{:S(2)}, u32[]{:S(2)}) collective-permute-start(bf16[8,256,128]{2,1,0:T(8,128)(2,1)S(1)} %collective-permute-done.13.set_ref), channel_id=1, source_target_pairs={{0,8},{8,0},{16,24},{24,16},{32,40},{40,32},{48,56},{56,48},{64,72... | collective-permute-start | bytes 1572872 | tf_op jit(solution)/shard_map/ppermute | solution.py:617
  119.0 10.0 %collective-permute-start.17 = (bf16[384,384]{1,0:T(8,128)(2,1)S(1)}, bf16[384,384]{1,0:T(8,128)(2,1)S(1)}, u32[]{:S(2)}, u32[]{:S(2)}) collective-permute-start(bf16[384,384]{1,0:T(8,128)(2,1)S(1)} %get-tuple-element.61), channel_id=1, source_target_pairs={{0,2},{1,3},{2,4},{3,5},{4,6},{5,7},{6,0},{7,1},{8,10},{9,11},{10,... | collective-permute-start | bytes 884744 | tf_op jit(solution)/shard_map/ppermute | solution.py:609
  120.7 9.5 %collective-permute-start.18 = (bf16[384,384]{1,0:T(8,128)(2,1)S(1)}, bf16[384,384]{1,0:T(8,128)(2,1)S(1)}, u32[]{:S(2)}, u32[]{:S(2)}) collective-permute-start(bf16[384,384]{1,0:T(8,128)(2,1)S(1)} %get-tuple-element.62), channel_id=1, source_target_pairs={{0,6},{1,7},{2,0},{3,1},{4,2},{5,3},{6,4},{7,5},{8,14},{9,15},{10,... | collective-permute-start | bytes 884744 | tf_op jit(solution)/shard_map/ppermute | solution.py:609
  121.1 12.3 %collective-permute-start.20 = (bf16[384,384]{1,0:T(8,128)(2,1)S(1)}, bf16[384,384]{1,0:T(8,128)(2,1)S(1)}, u32[]{:S(2)}, u32[]{:S(2)}) collective-permute-start(bf16[384,384]{1,0:T(8,128)(2,1)S(1)} %get-tuple-element.64), channel_id=1, source_target_pairs={{0,1},{1,0},{2,3},{3,2},{4,5},{5,4},{6,7},{7,6},{8,9},{9,8},{10,11... | collective-permute-start | bytes 884744 | tf_op jit(solution)/shard_map/ppermute | solution.py:613
  124.5 18.6 %copy-start = (bf16[3,128,384]{2,1,0:T(8,128)(2,1)S(1)}, bf16[3,128,384]{2,1,0:T(8,128)(2,1)}, u32[]{:S(2)}) copy-start(bf16[3,128,384]{2,1,0:T(8,128)(2,1)} %video_ref.1) | copy-start | bytes 884740
  124.5 10.1 %collective-permute-start.15 = (bf16[384,384]{1,0:T(8,128)(2,1)S(1)}, bf16[384,384]{1,0:T(8,128)(2,1)S(1)}, u32[]{:S(2)}, u32[]{:S(2)}) collective-permute-start(bf16[384,384]{1,0:T(8,128)(2,1)S(1)} %get-tuple-element.58), channel_id=1, source_target_pairs={{0,2},{1,3},{2,4},{3,5},{4,6},{5,7},{6,0},{7,1},{8,10},{9,11},{10,... | collective-permute-start | bytes 884744 | tf_op jit(solution)/shard_map/ppermute | solution.py:609
  127.8 15.1 %collective-permute-start.16 = (bf16[384,384]{1,0:T(8,128)(2,1)S(1)}, bf16[384,384]{1,0:T(8,128)(2,1)S(1)}, u32[]{:S(2)}, u32[]{:S(2)}) collective-permute-start(bf16[384,384]{1,0:T(8,128)(2,1)S(1)} %get-tuple-element.59), channel_id=1, source_target_pairs={{0,6},{1,7},{2,0},{3,1},{4,2},{5,3},{6,4},{7,5},{8,14},{9,15},{10,... | collective-permute-start | bytes 884744 | tf_op jit(solution)/shard_map/ppermute | solution.py:609
  130.4 12.5 %collective-permute-start.19 = (bf16[384,384]{1,0:T(8,128)(2,1)S(1)}, bf16[384,384]{1,0:T(8,128)(2,1)S(1)}, u32[]{:S(2)}, u32[]{:S(2)}) collective-permute-start(bf16[384,384]{1,0:T(8,128)(2,1)S(1)} %add_convert_fusion.2), channel_id=1, source_target_pairs={{0,1},{1,0},{2,3},{3,2},{4,5},{5,4},{6,7},{7,6},{8,9},{9,8},{10,11... | collective-permute-start | bytes 884744 | tf_op jit(solution)/shard_map/ppermute | solution.py:613
  133.5 9.4 %collective-permute-start.21 = (bf16[384,384]{1,0:T(8,128)(2,1)S(1)}, bf16[384,384]{1,0:T(8,128)(2,1)S(1)}, u32[]{:S(2)}, u32[]{:S(2)}) collective-permute-start(bf16[384,384]{1,0:T(8,128)(2,1)S(1)} %add_convert_fusion.1), channel_id=1, source_target_pairs={{0,4},{1,5},{2,6},{3,7},{4,0},{5,1},{6,2},{7,3},{8,12},{9,13},{10,... | collective-permute-start | bytes 884744 | tf_op jit(solution)/shard_map/ppermute | solution.py:609
